TPU v7x, 32 devices: a whole 2x2x4 slice. The times are simulated.
32 devices in a mesh: rep: 8 (over z, y), fsdp: 4 (over x, core).
Axes of the slice: x: 2, y: 2, z: 4, core: 2. Of those that a mesh axis runs over, the one named last changes fastest.
Arguments:
- tokens: bfloat16 [8192, 2304], P(('rep', 'fsdp')), may hold values from -6 to 6
- cotangent: bfloat16 [8192, 2304], P(('rep', 'fsdp')), may hold values from -6 to 6
- gain_attn: float32 [2304], replicated, may hold values from 0.25 to 1.75
- gain_ffn: float32 [2304], replicated, may hold values from 0.25 to 1.75
- w_query: bfloat16 [2304, 2304], P(None, 'fsdp'), may hold values from -0.125 to 0.125
- w_key: bfloat16 [2304, 2304], P(None, 'fsdp'), may hold values from -0.125 to 0.125
- w_value: bfloat16 [2304, 2304], P(None, 'fsdp'), may hold values from -0.125 to 0.125
- w_out: bfloat16 [2304, 2304], P(None, 'fsdp'), may hold values from -3 to 3
- w_gate: bfloat16 [2304, 5760], P(None, 'fsdp'), may hold values from -0.125 to 0.125
- w_up: bfloat16 [2304, 5760], P(None, 'fsdp'), may hold values from -0.125 to 0.125
- w_down: bfloat16 [5760, 2304], P(None, 'fsdp'), may hold values from -0.375 to 0.375
Outputs:
- output: bfloat16 [8192, 2304], P(('rep', 'fsdp'))
- d_tokens: float32 [8192, 2304], P(('rep', 'fsdp'))
- grad_gain_attn: float32 [2304], replicated
- grad_gain_ffn: float32 [2304], replicated
- grad_query: float32 [2304, 2304], P('rep', 'fsdp')
- grad_key: float32 [2304, 2304], P('rep', 'fsdp')
- grad_value: float32 [2304, 2304], P('rep', 'fsdp')
- grad_out: float32 [2304, 2304], P('rep', 'fsdp')
- grad_gate: float32 [2304, 5760], P('rep', 'fsdp')
- grad_up: float32 [2304, 5760], P('rep', 'fsdp')
- grad_down: float32 [5760, 2304], P('rep', 'fsdp')
All inputs are finite; a program needn't handle non-finite values.
Results may differ from a plain program's by a relative error of at most 0.015.
Values may be sent and summed in bfloat16 or wider, within the bound.
No kernel may reach another device: no remote copies, remote signals or barrier semaphores. Data moves between devices by JAX's collectives and lax.ppermute only.
A program may use at most 384 MiB of HBM per device.

v0:
```python
import math

import jax
import jax.numpy as jnp
from jax import lax
from jax.sharding import PartitionSpec as P

H = 36
HD = 64
FF = 5760
BLK = 256


epsilon = 1e-05
branch_scale = 1.4 / math.sqrt(40.0)


def rotate(field, positions, direction):
    half = field.shape[-1] // 2
    frequency = 10000.0 ** (-(jnp.arange(half, dtype=jnp.float32) * 2.0 / field.shape[-1]))
    angles = positions.astype(jnp.float32)[:, None] * frequency[None, :]
    cosine = jnp.cos(angles)[:, None, :]
    sine = direction * jnp.sin(angles)[:, None, :]
    first = field[..., :half]
    second = field[..., half:]
    return jnp.concatenate(
        [first * cosine - second * sine, second * cosine + first * sine], axis=-1
    )


def split_lanes(field):
    return field.reshape(field.shape[0], 4, field.shape[1] // 4).transpose(1, 0, 2)


def join_lanes(field):
    return field.transpose(1, 0, 2).reshape(field.shape[1], field.shape[0] * field.shape[2])


def body(
    tokens, cotangent, gain_attn, gain_ffn, w_query, w_key, w_value, w_out, w_gate, w_up, w_down
):
    rows = tokens.shape[0]
    width = tokens.shape[1]
    groups = lax.axis_size("fsdp")
    span = rows * groups
    head_size = HD
    lane_heads = H // 4
    factor_scale = HD ** (-0.5)
    owner = lax.axis_index("fsdp")
    width_cols = width // groups
    hidden_cols = FF // groups
    width_start = owner * width_cols
    hidden_start = owner * hidden_cols
    positions = owner * rows + jnp.arange(rows, dtype=jnp.int32)
    query_blocks = positions // BLK
    key_blocks = jnp.arange(span, dtype=jnp.int32) // BLK
    allowed = key_blocks[None, :] <= query_blocks[:, None]
    x_full = tokens.astype(jnp.float32)
    factor_attn = lax.rsqrt(jnp.mean(x_full * x_full, axis=-1, keepdims=True) + epsilon)
    unit_attn = x_full * factor_attn
    normed = (unit_attn * gain_attn).astype(jnp.bfloat16)
    attn_stack = jnp.stack((w_query, w_key, w_value, w_out))
    attn_full = lax.all_gather(attn_stack, "fsdp", axis=2, tiled=True)
    projected = jnp.einsum("td,cde->cte", normed, attn_full[:3], preferred_element_type=jnp.float32)
    query_rot = (
        rotate(projected[0].reshape(rows, H, head_size), positions, 1.0)
        .reshape(rows, width)
        .astype(jnp.bfloat16)
    )
    key_rot = (
        rotate(projected[1].reshape(rows, H, head_size), positions, 1.0)
        .reshape(rows, width)
        .astype(jnp.bfloat16)
    )
    value_low = projected[2].astype(jnp.bfloat16)
    key_all, value_all = (
        lax.all_gather(key_rot, "fsdp", axis=0, tiled=True),
        lax.all_gather(value_low, "fsdp", axis=0, tiled=True),
    )

    def lane_scores(query_lane, key_lane):
        query_heads = query_lane.reshape(rows, lane_heads, head_size)
        key_heads = key_lane.reshape(span, lane_heads, head_size)
        raw_scores = (
            jnp.einsum("thd,shd->hts", query_heads, key_heads, preferred_element_type=jnp.float32)
            * factor_scale
        )
        return jnp.where(allowed[None], raw_scores, -1e30)

    def lane_forward(operands):
        query_lane, key_lane, value_lane = operands
        masked = lane_scores(query_lane, key_lane)
        row_max = jnp.max(masked, axis=-1, keepdims=True)
        expo = jnp.exp(masked - row_max)
        totals = jnp.sum(expo, axis=-1, keepdims=True)
        probs_low = (expo / totals).astype(jnp.bfloat16)
        value_heads = value_lane.reshape(span, lane_heads, head_size)
        mixed = jnp.einsum(
            "hts,shd->thd", probs_low, value_heads, preferred_element_type=jnp.float32
        )
        return (mixed.reshape(rows, lane_heads * head_size), (row_max + jnp.log(totals))[..., 0])

    mixed_lanes, logsum_lanes = lax.map(
        lane_forward, (split_lanes(query_rot), split_lanes(key_all), split_lanes(value_all))
    )
    attended = join_lanes(mixed_lanes).astype(jnp.bfloat16)
    attn_result = jnp.dot(attended, attn_full[3], preferred_element_type=jnp.float32)
    hidden_state = x_full + branch_scale * attn_result
    factor_ffn = lax.rsqrt(jnp.mean(hidden_state * hidden_state, axis=-1, keepdims=True) + epsilon)
    unit_ffn = hidden_state * factor_ffn
    normed_ffn = (unit_ffn * gain_ffn).astype(jnp.bfloat16)
    ffn_stack = jnp.stack((w_gate, w_up))
    ffn_full = lax.all_gather(ffn_stack, "fsdp", axis=2, tiled=True)
    down_full = lax.all_gather(w_down, "fsdp", axis=1, tiled=True)
    gate_up = jnp.einsum("td,cdf->ctf", normed_ffn, ffn_full, preferred_element_type=jnp.float32)
    gate_value = gate_up[0]
    up_value = gate_up[1]
    sigmoid_gate = jax.nn.sigmoid(gate_value)
    activated = gate_value * sigmoid_gate
    inner = (activated * up_value).astype(jnp.bfloat16)
    ffn_result = jnp.dot(inner, down_full, preferred_element_type=jnp.float32)
    output = (hidden_state + branch_scale * ffn_result).astype(jnp.bfloat16)
    upstream = cotangent.astype(jnp.float32)
    d_ffn = (branch_scale * upstream).astype(jnp.bfloat16)
    inner_piece = lax.all_gather(inner, "fsdp", axis=0, tiled=True)
    grad_piece = lax.all_gather(d_ffn, "fsdp", axis=0, tiled=True)
    own_part = lax.dynamic_slice_in_dim(grad_piece, width_start, width_cols, 1)
    down_grad = jnp.einsum("tf,te->fe", inner_piece, own_part, preferred_element_type=jnp.float32)
    column_part = d_ffn
    d_inner = jnp.einsum(
        "te,fe->tf",
        column_part,
        lax.all_gather(w_down, "fsdp", axis=1, tiled=True),
        preferred_element_type=jnp.float32,
    )
    d_gate = d_inner * up_value * sigmoid_gate * (1.0 + gate_value * (1.0 - sigmoid_gate))
    d_up = d_inner * activated
    d_gate_low = d_gate.astype(jnp.bfloat16)
    d_up_low = d_up.astype(jnp.bfloat16)
    d_gate_up = jnp.stack((d_gate_low, d_up_low))
    normed_piece = lax.all_gather(normed_ffn, "fsdp", axis=0, tiled=True)
    gate_piece = lax.all_gather(d_gate_low, "fsdp", axis=0, tiled=True)
    up_piece = lax.all_gather(d_up_low, "fsdp", axis=0, tiled=True)
    own_gate = lax.dynamic_slice_in_dim(gate_piece, hidden_start, hidden_cols, 1)
    own_up = lax.dynamic_slice_in_dim(up_piece, hidden_start, hidden_cols, 1)
    gate_grad = jnp.einsum("td,tf->df", normed_piece, own_gate, preferred_element_type=jnp.float32)
    up_grad = jnp.einsum("td,tf->df", normed_piece, own_up, preferred_element_type=jnp.float32)
    column_part = d_gate_up
    d_normed_ffn = jnp.einsum(
        "ctf,cdf->td",
        column_part,
        lax.all_gather(ffn_stack, "fsdp", axis=2, tiled=True),
        preferred_element_type=jnp.float32,
    )
    attn_back = lax.all_gather(attn_stack, "fsdp", axis=2, tiled=True)
    gain_ffn_term = jnp.sum(d_normed_ffn * unit_ffn, axis=0)
    scaled_ffn = d_normed_ffn * gain_ffn
    d_hidden = upstream + factor_ffn * (
        scaled_ffn - unit_ffn * jnp.mean(scaled_ffn * unit_ffn, axis=-1, keepdims=True)
    )
    d_attn = (branch_scale * d_hidden).astype(jnp.bfloat16)
    d_attended = jnp.einsum(
        "te,de->td", d_attn, attn_back[3], preferred_element_type=jnp.float32
    ).astype(jnp.bfloat16)

    def lane_backward(operands):
        query_lane, key_lane, value_lane, grad_lane, logsum_lane = operands
        masked = lane_scores(query_lane, key_lane)
        probs = jnp.exp(masked - logsum_lane[..., None])
        probs_low = probs.astype(jnp.bfloat16)
        grad_heads = grad_lane.reshape(rows, lane_heads, head_size)
        value_heads = value_lane.reshape(span, lane_heads, head_size)
        d_probs = jnp.einsum(
            "thd,shd->hts", grad_heads, value_heads, preferred_element_type=jnp.float32
        )
        row_delta = jnp.sum(probs * d_probs, axis=-1, keepdims=True)
        d_scores = (probs * (d_probs - row_delta)).astype(jnp.bfloat16)
        query_heads = query_lane.reshape(rows, lane_heads, head_size)
        key_heads = key_lane.reshape(span, lane_heads, head_size)
        d_query_lane = (
            jnp.einsum("hts,shd->thd", d_scores, key_heads, preferred_element_type=jnp.float32)
            * factor_scale
        )
        d_key_lane = (
            jnp.einsum("hts,thd->shd", d_scores, query_heads, preferred_element_type=jnp.float32)
            * factor_scale
        )
        d_value_lane = jnp.einsum(
            "hts,thd->shd", probs_low, grad_heads, preferred_element_type=jnp.float32
        )
        lane_width = lane_heads * head_size
        return (
            d_query_lane.reshape(rows, lane_width),
            d_key_lane.reshape(span, lane_width),
            d_value_lane.reshape(span, lane_width),
        )

    d_query_lanes, d_key_lanes, d_value_lanes = lax.map(
        lane_backward,
        (
            split_lanes(query_rot),
            split_lanes(key_all),
            split_lanes(value_all),
            split_lanes(d_attended),
            logsum_lanes,
        ),
    )
    d_key_own, d_value_own = (
        lax.psum_scatter(join_lanes(d_key_lanes), "fsdp", scatter_dimension=0, tiled=True),
        lax.psum_scatter(join_lanes(d_value_lanes), "fsdp", scatter_dimension=0, tiled=True),
    )
    d_query_low = (
        rotate(join_lanes(d_query_lanes).reshape(rows, H, head_size), positions, -1.0)
        .reshape(rows, width)
        .astype(jnp.bfloat16)
    )
    d_key_low = (
        rotate(d_key_own.reshape(rows, H, head_size), positions, -1.0)
        .reshape(rows, width)
        .astype(jnp.bfloat16)
    )
    d_value_low = d_value_own.astype(jnp.bfloat16)
    d_project = jnp.stack((d_query_low, d_key_low, d_value_low))
    normed_piece = lax.all_gather(normed, "fsdp", axis=0, tiled=True)
    attended_piece = lax.all_gather(attended, "fsdp", axis=0, tiled=True)
    query_piece = lax.all_gather(d_query_low, "fsdp", axis=0, tiled=True)
    key_piece = lax.all_gather(d_key_low, "fsdp", axis=0, tiled=True)
    value_piece = lax.all_gather(d_value_low, "fsdp", axis=0, tiled=True)
    out_piece = lax.all_gather(d_attn, "fsdp", axis=0, tiled=True)

    def own_columns(field):
        return lax.dynamic_slice_in_dim(field, width_start, width_cols, 1)

    query_grad = jnp.einsum(
        "td,te->de", normed_piece, own_columns(query_piece), preferred_element_type=jnp.float32
    )
    key_grad = jnp.einsum(
        "td,te->de", normed_piece, own_columns(key_piece), preferred_element_type=jnp.float32
    )
    value_grad = jnp.einsum(
        "td,te->de", normed_piece, own_columns(value_piece), preferred_element_type=jnp.float32
    )
    out_grad = jnp.einsum(
        "td,te->de", attended_piece, own_columns(out_piece), preferred_element_type=jnp.float32
    )
    d_normed = jnp.einsum(
        "cte,cde->td", d_project, attn_back[:3], preferred_element_type=jnp.float32
    )
    gain_attn_term = jnp.sum(d_normed * unit_attn, axis=0)
    scaled_attn = d_normed * gain_attn
    d_tokens = d_hidden + factor_attn * (
        scaled_attn - unit_attn * jnp.mean(scaled_attn * unit_attn, axis=-1, keepdims=True)
    )
    grad_gain_attn, grad_gain_ffn = lax.psum((gain_attn_term, gain_ffn_term), ("rep", "fsdp"))
    summed = (
        lax.psum_scatter(query_grad, "rep", scatter_dimension=0, tiled=True),
        lax.psum_scatter(key_grad, "rep", scatter_dimension=0, tiled=True),
        lax.psum_scatter(value_grad, "rep", scatter_dimension=0, tiled=True),
        lax.psum_scatter(out_grad, "rep", scatter_dimension=0, tiled=True),
        lax.psum_scatter(gate_grad, "rep", scatter_dimension=0, tiled=True),
        lax.psum_scatter(up_grad, "rep", scatter_dimension=0, tiled=True),
        lax.psum_scatter(down_grad, "rep", scatter_dimension=0, tiled=True),
    )
    return (
        output,
        d_tokens,
        grad_gain_attn,
        grad_gain_ffn,
        summed[0],
        summed[1],
        summed[2],
        summed[3],
        summed[4],
        summed[5],
        summed[6],
    )


def solution(mesh):
    placed = (
        P(("rep", "fsdp"), None),
        P(("rep", "fsdp"), None),
        P(),
        P(),
        P(None, "fsdp"),
        P(None, "fsdp"),
        P(None, "fsdp"),
        P(None, "fsdp"),
        P(None, "fsdp"),
        P(None, "fsdp"),
        P(None, "fsdp"),
    )
    return jax.shard_map(
        body,
        mesh=mesh,
        in_specs=placed,
        out_specs=(
            P(("rep", "fsdp"), None),
            P(("rep", "fsdp"), None),
            P(),
            P(),
            P("rep", "fsdp"),
            P("rep", "fsdp"),
            P("rep", "fsdp"),
            P("rep", "fsdp"),
            P("rep", "fsdp"),
            P("rep", "fsdp"),
            P("rep", "fsdp"),
        ),
        check_vma=False,
    )
```

profile of v0, /device:TPU:0, one launch (start us, length us, event | category | flops | bytes accessed | tf_op | source)
XLA Modules:
  0.0 2888.3 jit_solution(10226551414120788478)
XLA Ops:
  7.2 9.6 pad_maximum_fusion.1
  19.6 252.5 %all-gather.18.cloned.1.call-done = bf16[4,2304,2304]{1,2,0:T(8,128)(2,1)} async-done(((bf16[4,2304,576]{1,2,0:T(8,128)(2,1)}), bf16[4,2304,2304]{1,2,0:T(8,128)(2,1)}) %all-gather.18.cloned.1.call-update) | async-done | bytes 42467344 | tf_op jit(solution)/shard_map/all_gather | solution.py:63
  272.1 14.3 convolution_bitcast_fusion.1
  291.2 2.8 slice.122
  294.1 11.1 pad_maximum_fusion
  306.3 23.1 all-gather.20.cloned.1.call-done
  329.4 40.2 %all-gather.48.cloned.1.call-done = bf16[1,1024,2304]{1,2,0:T(8,128)(2,1)} async-done(((bf16[1,256,2304]{1,2,0:T(8,128)(2,1)}), bf16[1,1024,2304]{1,2,0:T(8,128)(2,1)}) %all-gather.48.cloned.1.call-update) | async-done | bytes 4718608 | tf_op jit(solution)/shard_map/all_gather | solution.py:78
  369.6 42.6 %while.30 = (s32[]{:T(128)}, bf16[4,256,576]{1,2,0:T(8,128)(2,1)S(1)}, f32[4,9,256]{2,1,0:T(8,128)}, bf16[4,1024,576]{1,2,0:T(8,128)(2,1)}, bf16[4,256,576]{1,2,...) while((s32[]{:T(128)}, ...), condition=%wide.region_4.5_spmd.clone.clone, body=%wide.region_1.4_spmd.clone.sunk.clone | while | flops 632551168 | bytes 38294112 | solution.py:103
  376.7 3.1 fusion.153
  387.7 3.1 fusion.153
  398.6 3.1 fusion.153
  409.0 3.1 fusion.153
  413.2 7.7 multiply_reduce_fusion.3
  422.8 261.9 %all-gather.22.cloned.1.call-done = bf16[2,2304,5760]{1,2,0:T(8,128)(2,1)} async-done(((bf16[2,2304,1440]{1,2,0:T(8,128)(2,1)}), bf16[2,2304,5760]{1,2,0:T(8,128)(2,1)}) %all-gather.22.cloned.1.call-update) | async-done | bytes 53084176 | tf_op jit(solution)/shard_map/all_gather | solution.py:113
  684.7 33.6 %convolution_bitcast_fusion = f32[2,256,5760]{1,2,0:T(8,128)} fusion(bf16[2,2304,5760]{1,2,0:T(8,128)(2,1)} %all-gather.22.cloned.1.call-done, bf16[256,2304]{1,0:T(8,128)(2,1)} %multiply_convert_fusion.5), kind=kOutput, calls=%fused_computation.40 | convolution fusion | flops 13589544960 | bytes 66060288 | tf_op jit(solution)/shard_map/td,cdf->ctf/dot_general | solution.py:115
  718.4 130.2 %all-gather.24.cloned.1.call-done = bf16[5760,2304]{0,1:T(8,128)(2,1)} async-done(((bf16[5760,576]{0,1:T(8,128)(2,1)}), bf16[5760,2304]{0,1:T(8,128)(2,1)}) %all-gather.24.cloned.1.call-update) | async-done | bytes 26542096 | tf_op jit(solution)/shard_map/all_gather | solution.py:114
  848.6 22.2 multiply_convert_fusion.2
  870.9 26.2 multiply_reduce_fusion.1
  898.3 3.8 multiply_convert_fusion.4
  902.1 7.3 fusion.34
  910.1 80.1 %while.31 = (s32[]{:T(128)}, f32[4,256,576]{1,2,0:T(8,128)}, f32[4,1024,576]{1,2,0:T(8,128)}, f32[4,1024,576]{1,2,0:T(8,128)}, bf16[4,1024,576]{1,2,0:T(8,128)(2...) while((s32[]{:T(128)}, f32[4,256,576]{1,2,0:T(8,128)}, ...), condition=%wide.region_9.10_spmd.clone.clone, body=%wide.region_7.9_spmd.clone.sunk.clone | while | flops 1546336000 | bytes 98440320 | solution.py:198
  915.4 3.6 multiply_reduce_fusion.6
  919.0 2.8 multiply_convert_fusion.8
  935.3 3.6 multiply_reduce_fusion.6
  938.9 2.8 multiply_convert_fusion.8
  955.3 3.6 multiply_reduce_fusion.6
  958.9 2.8 multiply_convert_fusion.8
  975.3 3.6 multiply_reduce_fusion.6
  978.9 2.8 multiply_convert_fusion.8
  990.3 10.0 copy.42
  1001.1 67.7 %reduce-scatter.12.cloned.1.call-done = f32[256,2304]{0,1:T(8,128)} async-done(((f32[1024,2304]{0,1:T(8,128)}), f32[256,2304]{0,1:T(8,128)}) %reduce-scatter.12.cloned.1.call-update) | async-done | bytes 2359312 | tf_op jit(solution)/shard_map/reduce_scatter | solution.py:209
  1068.8 3.1 multiply_subtract_fusion.1
  1075.5 74.4 %reduce-scatter.14.cloned.1.call-done = f32[256,2304]{1,0:T(8,128)} async-done(((f32[1024,2304]{1,0:T(8,128)}), f32[256,2304]{1,0:T(8,128)}) %reduce-scatter.14.cloned.1.call-update) | async-done | bytes 2359312 | tf_op jit(solution)/shard_map/reduce_scatter | solution.py:210
  1149.9 2.8 convert_bitcast_fusion
  1152.7 21.6 fusion.54
  1175.0 6.5 fusion.48
  1184.8 2.8 convert_element_type.133
  1189.4 41.2 %all-gather.44.cloned.1.call-done = bf16[1024,5760]{0,1:T(8,128)(2,1)} async-done(((bf16[256,5760]{0,1:T(8,128)(2,1)}), bf16[1024,5760]{0,1:T(8,128)(2,1)}) %all-gather.44.cloned.1.call-update) | async-done | bytes 11796496 | tf_op jit(solution)/shard_map/all_gather | solution.py:125
  1230.7 39.6 %all-gather.46.cloned.1.call-done = bf16[1024,2304]{1,0:T(8,128)(2,1)} async-done(((bf16[256,2304]{1,0:T(8,128)(2,1)}), bf16[1024,2304]{1,0:T(8,128)(2,1)}) %all-gather.46.cloned.1.call-update) | async-done | bytes 4718608 | tf_op jit(solution)/shard_map/all_gather | solution.py:126
  1270.3 16.2 fusion.56
  1286.6 23.8 all-gather.34.cloned.1.call-done
  1310.4 39.6 %all-gather.36.cloned.1.call-done = bf16[1024,2304]{1,0:T(8,128)(2,1)} async-done(((bf16[256,2304]{1,0:T(8,128)(2,1)}), bf16[1024,2304]{1,0:T(8,128)(2,1)}) %all-gather.36.cloned.1.call-update) | async-done | bytes 4718608 | tf_op jit(solution)/shard_map/all_gather | solution.py:229
  1350.0 9.5 fusion.58
  1360.0 28.9 %all-gather.26.cloned.1.call-done = bf16[1024,2304]{1,0:T(8,128)(2,1)} async-done(((bf16[256,2304]{1,0:T(8,128)(2,1)}), bf16[1024,2304]{1,0:T(8,128)(2,1)}) %all-gather.26.cloned.1.call-update) | async-done | bytes 4718608 | tf_op jit(solution)/shard_map/all_gather | solution.py:224
  1388.9 39.7 %all-gather.28.cloned.1.call-done = bf16[1024,2304]{0,1:T(8,128)(2,1)} async-done(((bf16[256,2304]{0,1:T(8,128)(2,1)}), bf16[1024,2304]{0,1:T(8,128)(2,1)}) %all-gather.28.cloned.1.call-update) | async-done | bytes 4718608 | tf_op jit(solution)/shard_map/all_gather | solution.py:226
  1428.6 9.2 fusion.66
  1437.9 30.2 %all-gather.30.cloned.1.call-done = bf16[1024,2304]{0,1:T(8,128)(2,1)} async-done(((bf16[256,2304]{0,1:T(8,128)(2,1)}), bf16[1024,2304]{0,1:T(8,128)(2,1)}) %all-gather.30.cloned.1.call-update) | async-done | bytes 4718608 | tf_op jit(solution)/shard_map/all_gather | solution.py:227
  1468.1 9.2 fusion.64
  1477.6 29.4 %all-gather.32.cloned.1.call-done = bf16[1024,2304]{1,0:T(8,128)(2,1)} async-done(((bf16[256,2304]{1,0:T(8,128)(2,1)}), bf16[1024,2304]{1,0:T(8,128)(2,1)}) %all-gather.32.cloned.1.call-update) | async-done | bytes 4718608 | tf_op jit(solution)/shard_map/all_gather | solution.py:228
  1507.0 9.6 fusion.60
  1516.7 29.8 %all-gather.38.cloned.1.call-done = bf16[1024,2304]{1,0:T(8,128)(2,1)} async-done(((bf16[256,2304]{1,0:T(8,128)(2,1)}), bf16[1024,2304]{1,0:T(8,128)(2,1)}) %all-gather.38.cloned.1.call-update) | async-done | bytes 4718608 | tf_op jit(solution)/shard_map/all_gather | solution.py:141
  1546.5 80.6 %all-gather.40.cloned.1.call-done = bf16[1024,5760]{0,1:T(8,128)(2,1)} async-done(((bf16[256,5760]{0,1:T(8,128)(2,1)}), bf16[1024,5760]{0,1:T(8,128)(2,1)}) %all-gather.40.cloned.1.call-update) | async-done | bytes 11796496 | tf_op jit(solution)/shard_map/all_gather | solution.py:142
  1627.1 14.3 fusion.46
  1641.7 66.1 %all-gather.42.cloned.1.call-done = bf16[1024,5760]{0,1:T(8,128)(2,1)} async-done(((bf16[256,5760]{0,1:T(8,128)(2,1)}), bf16[1024,5760]{0,1:T(8,128)(2,1)}) %all-gather.42.cloned.1.call-update) | async-done | bytes 11796496 | tf_op jit(solution)/shard_map/all_gather | solution.py:143
  1707.8 13.6 fusion.44
  1721.4 14.7 fusion.33
  1736.1 45.5 %all-reduce = (f32[2304]{0:T(1024)}, f32[2304]{0:T(1024)}) all-reduce(f32[2304]{0:T(1024)S(1)} %copy-done.19, f32[2304]{0:T(1024)S(1)} %copy-done.18), channel_id=1, replica_groups=mesh['rep'=8,'fsdp'=4] {'rep','fsdp'}, use_global_device_ids=true, to_apply=%region_14.15 | all-reduce | flops 4608 | bytes 36864 | tf_op jit(solution)/shard_map/psum | solution.py:254
  1781.6 168.9 %reduce-scatter.28.cloned.1.call-done = f32[720,576]{1,0:T(8,128)} async-done(((f32[5760,576]{1,0:T(8,128)}), f32[720,576]{1,0:T(8,128)}) %reduce-scatter.28.cloned.1.call-update) | async-done | bytes 1658896
  1953.2 112.7 %reduce-scatter.22.cloned.1.call-done = f32[288,576]{1,0:T(8,128)} async-done(((f32[2304,576]{1,0:T(8,128)}), f32[288,576]{1,0:T(8,128)}) %reduce-scatter.22.cloned.1.call-update) | async-done | bytes 663568 | tf_op jit(solution)/shard_map/reduce_scatter | solution.py:259
  2066.0 116.3 %reduce-scatter.16.cloned.1.call-done = f32[288,576]{1,0:T(8,128)} async-done(((f32[2304,576]{1,0:T(8,128)}), f32[288,576]{1,0:T(8,128)}) %reduce-scatter.16.cloned.1.call-update) | async-done | bytes 663568 | tf_op jit(solution)/shard_map/reduce_scatter | solution.py:256
  2182.3 116.3 %reduce-scatter.18.cloned.1.call-done = f32[288,576]{1,0:T(8,128)} async-done(((f32[2304,576]{1,0:T(8,128)}), f32[288,576]{1,0:T(8,128)}) %reduce-scatter.18.cloned.1.call-update) | async-done | bytes 663568 | tf_op jit(solution)/shard_map/reduce_scatter | solution.py:257
  2298.6 116.3 %reduce-scatter.20.cloned.1.call-done = f32[288,576]{1,0:T(8,128)} async-done(((f32[2304,576]{1,0:T(8,128)}), f32[288,576]{1,0:T(8,128)}) %reduce-scatter.20.cloned.1.call-update) | async-done | bytes 663568 | tf_op jit(solution)/shard_map/reduce_scatter | solution.py:258
  2415.0 233.6 %reduce-scatter.24.cloned.1.call-done = f32[288,1440]{1,0:T(8,128)} async-done(((f32[2304,1440]{1,0:T(8,128)}), f32[288,1440]{1,0:T(8,128)}) %reduce-scatter.24.cloned.1.call-update) | async-done | bytes 1658896 | tf_op jit(solution)/shard_map/reduce_scatter | solution.py:260
  2648.5 233.0 %reduce-scatter.26.cloned.1.call-done = f32[288,1440]{1,0:T(8,128)} async-done(((f32[2304,1440]{1,0:T(8,128)}), f32[288,1440]{1,0:T(8,128)}) %reduce-scatter.26.cloned.1.call-update) | async-done | bytes 1658896 | tf_op jit(solution)/shard_map/reduce_scatter | solution.py:261
  (197 shorter events, 111.9 us)
Async XLA Ops:
  7.2 264.9 %all-gather.18.cloned.1.call-start = ((), (), s32[]{:S(2)}) async-start(), calls=%async_computation.9 | async-start | bytes 53084160 | tf_op jit(solution)/shard_map/all_gather | solution.py:63
  16.8 1.3 copy-start.4
  16.8 2.4 copy-start.15
  16.8 312.6 %all-gather.20.cloned.1.call-start = ((), (), s32[]{:S(2)}) async-start(), calls=%async_computation.10 | async-start | bytes 5898240 | tf_op jit(solution)/shard_map/all_gather | solution.py:77
  18.4 0.8 copy-start.20
  19.2 270.0 %copy-start.8 = (f32[256,32]{0,1:T(8,128)}, f32[256,32]{0,1:T(8,128)S(1)}, u32[]{:S(2)}) copy-start(f32[256,32]{0,1:T(8,128)S(1)} %get-tuple-element.227) | copy-start | bytes 98308
  19.6 266.9 %copy-start.6 = (bf16[256,2304]{1,0:T(8,128)(2,1)}, bf16[256,2304]{1,0:T(8,128)(2,1)S(1)}, u32[]{:S(2)}) copy-start(bf16[256,2304]{1,0:T(8,128)(2,1)S(1)} %fusion.49) | copy-start | bytes 3538948
  286.4 2.8 copy-start.5
  291.1 78.5 %all-gather.48.cloned.1.call-start = ((), (), s32[]{:S(2)}) async-start(), calls=%async_computation.32 | async-start | bytes 5898240 | tf_op jit(solution)/shard_map/all_gather | solution.py:78
  294.0 390.7 %all-gather.22.cloned.1.call-start = ((), (), s32[]{:S(2)}) async-start(), calls=%async_computation.11 | async-start | bytes 66355200 | tf_op jit(solution)/shard_map/all_gather | solution.py:113
  305.2 543.4 %all-gather.24.cloned.1.call-start = ((), (), s32[]{:S(2)}) async-start(), calls=%async_computation.12 | async-start | bytes 33177600 | tf_op jit(solution)/shard_map/all_gather | solution.py:114
  305.8 763.0 %reduce-scatter.12.cloned.1.call-start = ((), (), s32[]{:S(2)}) async-start(), calls=%async_computation.13 | async-start | bytes 11796480 | tf_op jit(solution)/shard_map/reduce_scatter | solution.py:209
  412.2 1.0 copy-start.7
  412.2 1.0 copy-start.13
  413.2 8.3 copy-start.11
  420.9 476.8 %copy-start = (f32[256,2304]{1,0:T(8,128)}, f32[256,2304]{1,0:T(8,128)S(1)}, u32[]{:S(2)}) copy-start(f32[256,2304]{1,0:T(8,128)S(1)} %get-tuple-element.229) | copy-start | bytes 7077892
  420.9 0.6 copy-start.16
  897.7 0.6 copy-start.21
  909.4 0.7 copy-start.14
  990.2 159.6 %reduce-scatter.14.cloned.1.call-start = ((), (), s32[]{:S(2)}) async-start(), calls=%async_computation.14 | async-start | bytes 11796480 | tf_op jit(solution)/shard_map/reduce_scatter | solution.py:210
  1000.3 68.5 %copy-start.9 = (f32[256,32]{0,1:T(8,128)S(1)}, f32[256,32]{0,1:T(8,128)}, u32[]{:S(2)}) copy-start(f32[256,32]{0,1:T(8,128)} %copy-done.8) | copy-start | bytes 98308
  1000.3 68.5 %copy-start.10 = (f32[256,32]{0,1:T(8,128)S(1)}, f32[256,32]{0,1:T(8,128)}, u32[]{:S(2)}) copy-start(f32[256,32]{0,1:T(8,128)} %get-tuple-element.225) | copy-start | bytes 98308
  1000.3 230.3 %all-gather.44.cloned.1.call-start = ((), (), s32[]{:S(2)}) async-start(), calls=%async_computation.30 | async-start | bytes 14745600 | tf_op jit(solution)/shard_map/all_gather | solution.py:125
  1001.1 269.2 %all-gather.46.cloned.1.call-start = ((), (), s32[]{:S(2)}) async-start(), calls=%async_computation.31 | async-start | bytes 5898240 | tf_op jit(solution)/shard_map/all_gather | solution.py:126
  1072.0 1.9 copy-start.3
  1073.9 78.7 %copy-start.2 = (bf16[256,36,64]{0,2,1:T(8,128)(2,1)}, bf16[256,36,64]{0,2,1:T(8,128)(2,1)S(1)}, u32[]{:S(2)}) copy-start(bf16[256,36,64]{0,2,1:T(8,128)(2,1)S(1)} %maximum_convert_fusion.1) | copy-start | bytes 3538948
  1152.7 22.3 copy-start.1
  1152.7 22.3 copy-start.12
  1152.7 22.3 copy-start.17
  1181.5 128.9 %all-gather.34.cloned.1.call-start = ((), (), s32[]{:S(2)}) async-start(), calls=%async_computation.22 | async-start | bytes 5898240 | tf_op jit(solution)/shard_map/all_gather | solution.py:225
  1182.1 167.9 %all-gather.36.cloned.1.call-start = ((), (), s32[]{:S(2)}) async-start(), calls=%async_computation.23 | async-start | bytes 5898240 | tf_op jit(solution)/shard_map/all_gather | solution.py:229
  1182.8 206.1 %all-gather.26.cloned.1.call-start = ((), (), s32[]{:S(2)}) async-start(), calls=%async_computation.15 | async-start | bytes 5898240 | tf_op jit(solution)/shard_map/all_gather | solution.py:224
  1183.4 245.2 %all-gather.28.cloned.1.call-start = ((), (), s32[]{:S(2)}) async-start(), calls=%async_computation.16 | async-start | bytes 5898240 | tf_op jit(solution)/shard_map/all_gather | solution.py:226
  1184.1 284.0 %all-gather.30.cloned.1.call-start = ((), (), s32[]{:S(2)}) async-start(), calls=%async_computation.18 | async-start | bytes 5898240 | tf_op jit(solution)/shard_map/all_gather | solution.py:227
  1184.7 322.3 %all-gather.32.cloned.1.call-start = ((), (), s32[]{:S(2)}) async-start(), calls=%async_computation.20 | async-start | bytes 5898240 | tf_op jit(solution)/shard_map/all_gather | solution.py:228
  1187.6 358.9 %all-gather.38.cloned.1.call-start = ((), (), s32[]{:S(2)}) async-start(), calls=%async_computation.25 | async-start | bytes 5898240 | tf_op jit(solution)/shard_map/all_gather | solution.py:141
  1188.2 438.9 %all-gather.40.cloned.1.call-start = ((), (), s32[]{:S(2)}) async-start(), calls=%async_computation.26 | async-start | bytes 14745600 | tf_op jit(solution)/shard_map/all_gather | solution.py:142
  1188.8 519.0 %all-gather.42.cloned.1.call-start = ((), (), s32[]{:S(2)}) async-start(), calls=%async_computation.28 | async-start | bytes 14745600 | tf_op jit(solution)/shard_map/all_gather | solution.py:143
  1189.4 761.1 %reduce-scatter.28.cloned.1.call-start = ((), (), s32[]{:S(2)}) async-start(), calls=%async_computation.33 | async-start | bytes 16588800
  1286.5 779.4 %reduce-scatter.22.cloned.1.call-start = ((), (), s32[]{:S(2)}) async-start(), calls=%async_computation.24 | async-start | bytes 6635520 | tf_op jit(solution)/shard_map/reduce_scatter | solution.py:259
  1359.5 822.8 %reduce-scatter.16.cloned.1.call-start = ((), (), s32[]{:S(2)}) async-start(), calls=%async_computation.17 | async-start | bytes 6635520 | tf_op jit(solution)/shard_map/reduce_scatter | solution.py:256
  1437.8 860.8 %reduce-scatter.18.cloned.1.call-start = ((), (), s32[]{:S(2)}) async-start(), calls=%async_computation.19 | async-start | bytes 6635520 | tf_op jit(solution)/shard_map/reduce_scatter | solution.py:257
  1477.4 937.6 %reduce-scatter.20.cloned.1.call-start = ((), (), s32[]{:S(2)}) async-start(), calls=%async_computation.21 | async-start | bytes 6635520 | tf_op jit(solution)/shard_map/reduce_scatter | solution.py:258
  1516.6 1131.9 %reduce-scatter.24.cloned.1.call-start = ((), (), s32[]{:S(2)}) async-start(), calls=%async_computation.27 | async-start | bytes 15925248 | tf_op jit(solution)/shard_map/reduce_scatter | solution.py:260
  1641.4 1240.1 %reduce-scatter.26.cloned.1.call-start = ((), (), s32[]{:S(2)}) async-start(), calls=%async_computation.29 | async-start | bytes 15925248 | tf_op jit(solution)/shard_map/reduce_scatter | solution.py:261
  1721.4 14.7 copy-start.18
  1721.4 14.7 copy-start.19
Sparse Core Ops, SparseCore 0:
  16.9 255.1 all-gather.17
  291.3 38.0 all-gather.19
  331.5 38.0 all-gather.47
  371.0 313.6 all-gather.21
  686.2 162.4 all-gather.23
  990.4 78.3 reduce-scatter.11
  1071.4 78.4 reduce-scatter.13
  1151.4 79.2 all-gather.43
  1232.8 37.4 all-gather.45
  1272.3 38.0 all-gather.33
  1312.5 37.4 all-gather.35
  1351.4 37.4 all-gather.25
  1390.5 38.0 all-gather.27
  1430.0 38.0 all-gather.29
  1469.5 37.4 all-gather.31
  1509.0 37.4 all-gather.37
  1547.9 79.2 all-gather.39
  1628.6 79.2 all-gather.41
  1711.4 239.0 reduce-scatter.27
  1955.0 110.9 reduce-scatter.21
  2070.7 111.6 reduce-scatter.15
  2187.0 111.6 reduce-scatter.17
  2303.3 111.6 reduce-scatter.19
  2419.5 228.9 reduce-scatter.23
  2653.2 228.2 reduce-scatter.25
where the time goes:
time: 2890 us
  waiting for transfers between devices  2400 us (83%)
  matrix products  289 us (10%)
  other arithmetic  71.3 us (2%)
  local copies, waits for them, and re-layouts  62.6 us (2%)
  blocking collectives  45.5 us (2%)
    all_gather x1, waiting for transfers between devices, body(): ffn_full = lax.all_gather(ffn_stack, 'fsdp', axis=2, tiled=True)  262 us
    all_gather x1, waiting for transfers between devices, body(): attn_full = lax.all_gather(attn_stack, 'fsdp', axis=2, tiled=True)  253 us
    reduce_scatter x1, waiting for transfers between devices, body(): lax.psum_scatter(gate_grad, 'rep', scatter_dimension=0, tiled=True)  234 us
    reduce_scatter x1, waiting for transfers between devices, body(): lax.psum_scatter(up_grad, 'rep', scatter_dimension=0, tiled=True)  233 us
    unnamed x26, waiting for transfers between devices  175 us
    all_gather x1, waiting for transfers between devices, body(): down_full = lax.all_gather(w_down, 'fsdp', axis=1, tiled=True)  130 us
    reduce_scatter x1, waiting for transfers between devices, body(): lax.psum_scatter(value_grad, 'rep', scatter_dimension=0, tiled=True)  116 us
    reduce_scatter x1, waiting for transfers between devices, body(): lax.psum_scatter(query_grad, 'rep', scatter_dimension=0, tiled=True)  116 us
  transfers between devices with their start and end apart: 25, of which 25 were waited for; matrix products, arithmetic and copies ran while one was open for 9% of the time, Pallas kernels for 0%

commit v1 on v0

v1 whole, which is shorter than its diff:
```python
import math

import jax
import jax.numpy as jnp
from jax import lax
from jax.experimental import pallas as pl
from jax.experimental.pallas import tpu as pltpu
from jax.sharding import PartitionSpec as P

HD = 64
BLK = 256
NT = (((1,), (1,)), ((), ()))

epsilon = 1e-05
branch_scale = 1.4 / math.sqrt(40.0)
low = jnp.bfloat16
full = jnp.float32


def turn(field, cosine, sine):
    half = field.shape[0] // 2
    first, second = field[:half], field[half:]
    return jnp.concatenate(
        [first * cosine - second * sine, second * cosine + first * sine], axis=0
    )


def forward_kernel(
    q_ref, k_ref, v_ref, cos_ref, sin_ref, out_ref, ql_ref, kl_ref, vl_ref, lse_ref
):
    cosine, sine = cos_ref[...], sin_ref[...]
    span = q_ref.shape[2]
    q_low = turn(q_ref[0], cosine, sine).astype(low)
    k_low = turn(k_ref[0], cosine, sine).astype(low)
    v_low = v_ref[0].astype(low)
    ql_ref[0] = q_low
    kl_ref[0] = k_low
    vl_ref[0] = v_low
    q_scaled = (q_low * (HD ** (-0.5))).astype(low)
    k_rows = k_low.T
    for j in range(span // BLK):
        kv = (j + 1) * BLK
        cols = slice(j * BLK, kv)
        scores = jnp.dot(k_rows[:kv], q_scaled[:, cols], preferred_element_type=full)
        top = jnp.max(scores, axis=0, keepdims=True)
        expo = jnp.exp(scores - top)
        total = jnp.sum(expo, axis=0, keepdims=True)
        probs = (expo * (1.0 / total)).astype(low)
        out_ref[0, :, cols] = jnp.dot(
            v_low[:, :kv], probs, preferred_element_type=full
        ).astype(low)
        lse_ref[0, :, cols] = top + jnp.log(total)


def attention_forward(query, key, value, cosine, sine):
    heads, _, span = query.shape
    spec = pl.BlockSpec((1, HD, span), lambda h: (h, 0, 0))
    table = pl.BlockSpec((HD // 2, span), lambda h: (0, 0))
    field = jax.ShapeDtypeStruct((heads, HD, span), low)
    row = pl.BlockSpec((1, 1, span), lambda h: (h, 0, 0))
    return pl.pallas_call(
        forward_kernel,
        grid=(heads,),
        in_specs=[spec, spec, spec, table, table],
        out_specs=[spec, spec, spec, spec, row],
        out_shape=[field, field, field, field, jax.ShapeDtypeStruct((heads, 1, span), full)],
        compiler_params=pltpu.CompilerParams(vmem_limit_bytes=48 * 2**20),
        cost_estimate=pl.CostEstimate(
            flops=heads * span * span * HD * 10, bytes_accessed=heads * HD * span * 20,
            transcendentals=heads * span * span,
        ),
        name="attention_forward",
    )(query, key, value, cosine, sine)


def backward_kernel(
    q_ref, k_ref, v_ref, g_ref, lse_ref, cos_ref, sin_ref, dq_ref, dk_ref, dv_ref, dk_acc, dv_acc
):
    cosine, sine = cos_ref[...], sin_ref[...]
    span = q_ref.shape[2]
    q_scaled = (q_ref[0] * (HD ** (-0.5))).astype(low)
    k_low, v_low, grad = k_ref[0], v_ref[0], g_ref[0]
    k_rows, v_rows = k_low.T, v_low.T
    dk_acc[...] = jnp.zeros_like(dk_acc)
    dv_acc[...] = jnp.zeros_like(dv_acc)
    for j in range(span // BLK):
        kv = (j + 1) * BLK
        cols = slice(j * BLK, kv)
        q_j, g_j = q_scaled[:, cols], grad[:, cols]
        scores = jnp.dot(k_rows[:kv], q_j, preferred_element_type=full)
        probs = jnp.exp(scores - lse_ref[0, :, cols])
        probs_low = probs.astype(low)
        d_probs = jnp.dot(v_rows[:kv], g_j, preferred_element_type=full)
        delta = jnp.sum(probs * d_probs, axis=0, keepdims=True)
        d_scores = (probs * (d_probs - delta)).astype(low)
        dq = jnp.dot(k_low[:, :kv], d_scores, preferred_element_type=full) * (HD ** (-0.5))
        dq_ref[0, :, cols] = turn(dq, cosine[:, cols], -sine[:, cols]).astype(low)
        dk_acc[:, :kv] += lax.dot_general(q_j, d_scores, NT, preferred_element_type=full)
        dv_acc[:, :kv] += lax.dot_general(g_j, probs_low, NT, preferred_element_type=full)
    dk_ref[0] = turn(dk_acc[...], cosine, -sine).astype(low)
    dv_ref[0] = dv_acc[...].astype(low)


def attention_backward(query, key, value, grad, lse, cosine, sine):
    heads, _, span = query.shape
    spec = pl.BlockSpec((1, HD, span), lambda h: (h, 0, 0))
    table = pl.BlockSpec((HD // 2, span), lambda h: (0, 0))
    row = pl.BlockSpec((1, 1, span), lambda h: (h, 0, 0))
    field = jax.ShapeDtypeStruct((heads, HD, span), low)
    return pl.pallas_call(
        backward_kernel,
        grid=(heads,),
        in_specs=[spec, spec, spec, spec, row, table, table],
        out_specs=[spec, spec, spec],
        out_shape=[field, field, field],
        scratch_shapes=[pltpu.VMEM((HD, span), full), pltpu.VMEM((HD, span), full)],
        compiler_params=pltpu.CompilerParams(vmem_limit_bytes=48 * 2**20),
        cost_estimate=pl.CostEstimate(
            flops=heads * span * span * HD * 20, bytes_accessed=heads * HD * span * 14,
            transcendentals=heads * span * span,
        ),
        name="attention_backward",
    )(query, key, value, grad, lse, cosine, sine)


def swap(array, j):
    size = lax.axis_size("fsdp")
    return lax.ppermute(array, "fsdp", [(i, i ^ j) for i in range(size)])


def place_kernel(*refs):
    *blocks, out, held, arrived, left = refs
    me = lax.axis_index("fsdp")
    into = [
        pltpu.make_async_copy(block, held.at[j], arrived.at[j]) for j, block in enumerate(blocks)
    ]
    back = [
        pltpu.make_async_copy(
            held.at[j], out.at[lax.bitwise_xor(me, jnp.int32(j))], left.at[j]
        )
        for j in range(len(blocks))
    ]
    for copy in into:
        copy.start()
    for copy, then in zip(into, back):
        copy.wait()
        then.start()
    for copy in back:
        copy.wait()


def place(blocks):
    count = len(blocks)
    first = blocks[0]
    whole = pl.pallas_call(
        place_kernel,
        in_specs=[pl.BlockSpec(memory_space=pl.ANY)] * count,
        out_specs=pl.BlockSpec(memory_space=pl.ANY),
        out_shape=jax.ShapeDtypeStruct((count,) + first.shape, first.dtype),
        scratch_shapes=[
            pltpu.VMEM((count,) + first.shape, first.dtype),
            pltpu.SemaphoreType.DMA((count,)),
            pltpu.SemaphoreType.DMA((count,)),
        ],
        compiler_params=pltpu.CompilerParams(vmem_limit_bytes=16 * 2**20),
        cost_estimate=pl.CostEstimate(
            flops=0, bytes_accessed=2 * count * first.size * first.dtype.itemsize, transcendentals=0
        ),
        name="place",
    )(*blocks)
    return whole.reshape((count * first.shape[0],) + first.shape[1:])


def gather(array):
    core = swap(array, 1)
    chip = swap(array, 2)
    return place([array, core, chip, swap(chip, 1)])


def scatter_sum(chunk):
    far = swap(chunk(3), 1)
    across = swap((chunk(2) + far).astype(low), 2)
    near = swap(chunk(1), 1)
    return chunk(0).astype(full) + near.astype(full) + across.astype(full)


def total_of(array):
    array = array + swap(array, 1)
    return array + swap(array, 2)


def to_rows(field, rows):
    me = lax.axis_index("fsdp")
    size = lax.axis_size("fsdp")
    blocks = []
    for j in range(size):
        block = lax.dynamic_slice_in_dim(field, (me ^ j) * rows, rows, 1)
        blocks.append(block if j == 0 else swap(block, j))
    return place(blocks).T


def rep_dims(size):
    return {8: (4, 2), 32: (2, 4, 4)}.get(size, (size,))


def coordinate(index, dims, at):
    stride = math.prod(dims[at + 1 :])
    return (index // stride) % dims[at], stride


def line_sum(part, dims, at):
    count = dims[at]
    size = math.prod(dims)
    me, stride = coordinate(lax.axis_index("rep"), dims, at)

    def piece(index):
        return lax.dynamic_index_in_dim(part, jnp.clip(index, 0, count - 1), 1, False)

    def run(sign):
        moving = None
        for step in range(1, count):
            mine = piece(me + sign * (count - step))
            if moving is not None:
                mine = (mine.astype(full) + moving.astype(full)).astype(low)
            pairs = []
            for index in range(size):
                here, _ = coordinate(index, dims, at)
                far = here if sign > 0 else count - 1 - here
                if far <= step - 1:
                    pairs.append((index, index + sign * stride))
            moving = lax.ppermute(mine, "rep", pairs)
        return moving

    return piece(me).astype(full) + run(1).astype(full) + run(-1).astype(full)


def halves(act):
    size = lax.axis_size("rep")
    dims = rep_dims(size)
    if dims[-1] != 2:
        return None, act
    side = lax.axis_index("rep") % 2
    view = act.reshape(size // 2, 2, act.shape[0] // size, act.shape[1])
    rows = act.shape[0] // 2
    return (
        lax.dynamic_index_in_dim(view, 1 - side, 1, False).reshape(rows, -1),
        lax.dynamic_index_in_dim(view, side, 1, False).reshape(rows, -1),
    )


def grad_sum(parts, grad):
    other, own = parts
    size = lax.axis_size("rep")
    dims = rep_dims(size)
    columns = grad.shape[0]

    def outer(rows):
        return jnp.einsum("dt,ft->df", rows, grad, preferred_element_type=full)

    last = len(dims) - 1
    if other is not None:
        neighbours = [(i, i ^ 1) for i in range(size)]
        sent = lax.ppermute(outer(other).astype(low), "rep", neighbours)
        part = outer(own) + sent.astype(full)
        rows = 2 * own.shape[0] // size
        last -= 1
    else:
        part = outer(own)
        rows = own.shape[0] // size
    for at in range(last, -1, -1):
        part = line_sum(part.astype(low).reshape(-1, dims[at], rows, columns), dims, at)
    return part.reshape(rows, columns)


def body(
    tokens, cotangent, gain_attn, gain_ffn, w_query, w_key, w_value, w_out, w_gate, w_up, w_down
):
    rows, width = tokens.shape
    size = lax.axis_size("fsdp")
    reps = lax.axis_size("rep")
    span = rows * size
    me = lax.axis_index("fsdp")
    replica = lax.axis_index("rep")
    width_cols = width // size
    hidden_cols = w_gate.shape[1]
    heads = width_cols // HD

    half = HD // 2
    frequency = 10000.0 ** (-(jnp.arange(half, dtype=full) * 2.0 / HD))
    angles = frequency[:, None] * jnp.arange(span, dtype=jnp.int32).astype(full)[None, :]
    cosine, sine = jnp.cos(angles), jnp.sin(angles)

    def own_columns(field):
        return lax.dynamic_slice_in_dim(field, me * width_cols, width_cols, 1)

    def own_gain(gain):
        return lax.dynamic_slice_in_dim(gain, me * width_cols, width_cols, 0)[:, None]

    tokens_all = gather(tokens)
    x_all = tokens_all.astype(full)
    factor_all = lax.rsqrt(jnp.mean(x_all * x_all, axis=-1, keepdims=True) + epsilon)
    normed = (x_all * factor_all * gain_attn).astype(low)
    cotangent_all = gather(cotangent)
    d_ffn = (branch_scale * cotangent_all.astype(full)).astype(low)

    share = hidden_cols // reps

    def down_part(j):
        return lax.dynamic_slice_in_dim(w_down, (me ^ j) * hidden_cols + replica * share, share, 0)

    def down_rows(j):
        return lax.dynamic_slice_in_dim(w_down, (me ^ j) * hidden_cols, hidden_cols, 0)

    part_chip = swap(down_part(2), 2)
    part_both = swap(swap(down_part(3), 2), 1)
    down_blocks = [
        down_rows(0),
        swap(down_rows(1), 1),
        lax.all_gather(part_chip, "rep", axis=0, tiled=True),
        lax.all_gather(part_both, "rep", axis=0, tiled=True),
    ]
    down_own = place([block.T for block in down_blocks])
    d_inner = jnp.einsum("ef,te->ft", down_own, d_ffn, preferred_element_type=full)

    def project(weight):
        field = jnp.einsum("de,td->et", weight, normed, preferred_element_type=full)
        return field.reshape(heads, HD, span)

    attended, query_low, key_low, value_low, lse = attention_forward(
        project(w_query), project(w_key), project(w_value), cosine, sine
    )
    attended_all = gather(attended.reshape(width_cols, span))

    attn_result = jnp.einsum("de,dt->et", w_out, attended_all, preferred_element_type=full)
    hidden = own_columns(tokens_all).astype(full).T + branch_scale * attn_result
    squares = total_of(jnp.sum(hidden * hidden, axis=0, keepdims=True))
    factor = lax.rsqrt(squares / width + epsilon)
    gain_own = own_gain(gain_ffn)
    scaled_all = gather((hidden * gain_own).astype(low))

    gate = factor * jnp.einsum("df,dt->ft", w_gate, scaled_all, preferred_element_type=full)
    up = factor * jnp.einsum("df,dt->ft", w_up, scaled_all, preferred_element_type=full)
    sigmoid = jax.nn.sigmoid(gate)
    activated = gate * sigmoid
    inner = (activated * up).astype(low)
    d_gate_full = factor * d_inner * up * sigmoid * (1.0 + gate * (1.0 - sigmoid))
    d_up_full = factor * d_inner * activated
    d_gate = d_gate_full.astype(low)
    d_up = d_up_full.astype(low)
    mean_ffn = total_of(jnp.sum(d_gate_full * gate + d_up_full * up, axis=0, keepdims=True)) / width

    scaled_halves = halves(scaled_all)
    grad_gate = grad_sum(scaled_halves, d_gate)
    grad_up = grad_sum(scaled_halves, d_up)

    def ffn_chunk(j):
        at = (me ^ j) * width_cols
        gate_rows = lax.dynamic_slice_in_dim(w_gate, at, width_cols, 0)
        up_rows = lax.dynamic_slice_in_dim(w_up, at, width_cols, 0)
        return (
            jnp.einsum("df,ft->dt", gate_rows, d_gate, preferred_element_type=full)
            + jnp.einsum("df,ft->dt", up_rows, d_up, preferred_element_type=full)
        ).astype(low)

    d_scaled = scatter_sum(ffn_chunk)
    gain_ffn_term = jnp.sum(d_scaled * hidden, axis=1)
    d_hidden = (
        own_columns(cotangent_all).astype(full).T
        + gain_own * d_scaled
        - hidden * (factor * mean_ffn)
    )
    d_attn = (branch_scale * d_hidden).astype(low)

    def out_chunk(j):
        out_rows = lax.dynamic_slice_in_dim(w_out, (me ^ j) * width_cols, width_cols, 0)
        return jnp.einsum("de,et->dt", out_rows, d_attn, preferred_element_type=full).astype(low)

    d_attended = scatter_sum(out_chunk).astype(low).reshape(heads, HD, span)

    inner_all = gather(inner)
    ffn_result = jnp.einsum("fe,ft->et", w_down, inner_all, preferred_element_type=full)
    output = to_rows((hidden + branch_scale * ffn_result).astype(low), rows)
    grad_down = grad_sum(halves(inner_all), own_columns(d_ffn).T)
    grad_out = grad_sum(halves(attended_all), d_attn)

    d_query, d_key, d_value = (
        field.reshape(width_cols, span)
        for field in attention_backward(
            query_low, key_low, value_low, d_attended, lse, cosine, sine
        )
    )
    normed_halves = halves(normed.T)
    grad_query = grad_sum(normed_halves, d_query)
    grad_key = grad_sum(normed_halves, d_key)
    grad_value = grad_sum(normed_halves, d_value)

    def token_chunk(j):
        def product(grad, weight):
            block = lax.dynamic_slice_in_dim(grad, (me ^ j) * rows, rows, 1)
            return jnp.einsum("et,de->td", block, weight, preferred_element_type=full)

        return (product(d_query, w_query) + product(d_key, w_key) + product(d_value, w_value)).astype(low)

    d_normed = scatter_sum(token_chunk)
    x_own = tokens.astype(full)
    factor_own = lax.rsqrt(jnp.mean(x_own * x_own, axis=-1, keepdims=True) + epsilon)
    unit_own = x_own * factor_own
    scaled = d_normed * gain_attn
    d_tokens = to_rows(d_hidden.astype(low), rows).astype(full) + factor_own * (
        scaled - unit_own * jnp.mean(scaled * unit_own, axis=-1, keepdims=True)
    )
    gain_attn_term = jnp.sum(d_normed * unit_own, axis=0)
    gain_ffn_wide = lax.dynamic_update_slice_in_dim(
        jnp.zeros((width,), full), gain_ffn_term, me * width_cols, 0
    )
    grad_gain_attn, grad_gain_ffn = lax.psum((gain_attn_term, gain_ffn_wide), ("rep", "fsdp"))
    return (
        output,
        d_tokens,
        grad_gain_attn,
        grad_gain_ffn,
        grad_query,
        grad_key,
        grad_value,
        grad_out,
        grad_gate,
        grad_up,
        grad_down,
    )


def solution(mesh):
    rows = P(("rep", "fsdp"), None)
    columns = P(None, "fsdp")
    both = P("rep", "fsdp")
    return jax.shard_map(
        body,
        mesh=mesh,
        in_specs=(rows, rows, P(), P()) + (columns,) * 7,
        out_specs=(rows, rows, P(), P()) + (both,) * 7,
        check_vma=False,
    )
```

time: 2890 us -> 978 us (0.34)
  waiting for transfers between devices: 2400 us -> 280 us
  starting transfers between devices: 2.07 us -> 156 us
  matrix products: 289 us -> 199 us
  local copies, waits for them, and re-layouts: 62.6 us -> 141 us
  Pallas kernels: 0 us -> 68.8 us
    all_gather x16 -> x2, waiting for transfers between devices: 1160 us -> 7.19 us  [the longest x1 7.18 us: body(): lax.all_gather(part_both, 'rep', axis=0, tiled=True)]
    reduce_scatter x8 -> x0, waiting for transfers between devices: 1070 us -> none  [the longest x1 234 us: body(): lax.psum_scatter(gate_grad, 'rep', scatter_dimension=0, tiled=True)]
    ppermute x0 -> x87, waiting for transfers between devices: none -> 273 us  [the longest x7 121 us: grad_sum(): sent = lax.ppermute(outer(other).astype(low), 'rep', neighbours)]
    unnamed x26 -> x2, waiting for transfers between devices: 175 us -> 0.03 us
    ppermute x0 -> x87, starting transfers between devices: none -> 156 us  [the longest x42 128 us: run(): moving = lax.ppermute(mine, 'rep', pairs)]
    dot_general x42 -> x46, matrix products: 273 us -> 199 us  [the longest x14 75.6 us: outer(): return jnp.einsum('dt,ft->df', rows, grad, preferred_element_type=full)]
    pallas_call x0 -> x10, Pallas kernels: none -> 68.8 us  [the longest x1 25.8 us: attention_backward(): pl.pallas_call(backward_kernel, grid=(heads,), in_specs=[spec, spec, spec...]
    dynamic_slice x24 -> x11, local copies, waits for them, and re-layouts: 20.2 us -> 50.2 us  [the longest x1 20.8 us: piece(): lax.dynamic_index_in_dim(part, jnp.clip(index, 0, count - 1), 1, False)]
  transfers between devices with their start and end apart: 25 -> 89, of which waited for: 25 -> 24; matrix products, arithmetic and copies ran while one was open for 9% -> 37% of each run, Pallas kernels for 0% -> 7%
where the time goes in v1:
time: 978 us; the launch traced here: 967 us
  waiting for transfers between devices  280 us (29%)
  matrix products  199 us (20%)
  starting transfers between devices  156 us (16%)
  local copies, waits for them, and re-layouts  141 us (14%)
  Pallas kernels  68.8 us (7%)
  other arithmetic  64.5 us (7%)
  blocking collectives  41 us (4%)
  between operations  15.7 us (2%)
    ppermute x42, starting transfers between devices, run(): moving = lax.ppermute(mine, 'rep', pairs)  128 us
    ppermute x7, waiting for transfers between devices, grad_sum(): sent = lax.ppermute(outer(other).astype(low), 'rep', neighbours)  121 us
    ppermute x38, waiting for transfers between devices, swap(): return lax.ppermute(array, 'fsdp', [(i, i ^ j) for i in range(size)])  84.7 us
    dot_general x14, matrix products, outer(): return jnp.einsum('dt,ft->df', rows, grad, preferred_element_type=full)  75.6 us
    ppermute x42, waiting for transfers between devices, run(): moving = lax.ppermute(mine, 'rep', pairs)  67.5 us
    psum x1, blocking collectives, body(): lax.psum((gain_attn_term, gain_ffn_wide), ('rep', 'fsdp'))  41 us
    unnamed x182, local copies, waits for them, and re-layouts  34.6 us
    convert_element_type x22, other arithmetic, run(): mine = (mine.astype(full) + moving.astype(full)).astype(low)  28.4 us
  transfers between devices with their start and end apart: 89, of which 24 were waited for; matrix products, arithmetic and copies ran while one was open for 37% of the time, Pallas kernels for 7%

profile of v1, /device:TPU:0, one launch (start us, length us, event | category | flops | bytes accessed | tf_op | source)
XLA Modules:
  0.0 966.6 jit_solution(3938566427748158298)
XLA Ops:
  10.2 26.3 %collective-permute-done.1.refs_2_ = bf16[256,2304]{1,0:T(8,128)(2,1)} collective-permute-done((bf16[256,2304]{1,0:T(8,128)(2,1)}, bf16[256,2304]{1,0:T(8,128)(2,1)}, u32[]{:S(2)}, u32[]{:S(2)}) %collective-permute-start.1) | collective-permute-done | bytes 1179680 | tf_op jit(solution)/shard_map/ppermute | solution.py:128
  41.4 6.1 collective-permute-done.21
  54.3 6.7 copy.117
  64.6 4.3 fusion.156
  68.9 4.4 fusion.157
  73.3 4.4 fusion.158
  77.7 22.9 %attention_forward.1 = (bf16[9,64,1024]{2,1,0:T(8,128)(2,1)}, bf16[9,64,1024]{2,1,0:T(8,128)(2,1)S(1)}, bf16[9,64,1024]{2,1,0:T(8,128)(2,1)S(1)}, bf16[9,64,1024]{2,1,0:T(8,128)(2,1)S(1)}, f32[9,1,1024]{2,1,0:T(1,128)S(1)}) custom-call(f32[9,64,1024]{2,1,0:T(8,128)} %bitcast.470, f32[9,64,1024]{2,1,0:T(8,128)} %bitcast.471, f32[9,64,1024]{2,1,0:T(8,128)} %bitcast.472, ...), custom_call_target="tpu_custom_call" | custom-call | flops 6039797760 | bytes 11796480 | tf_op jit(solution)/shard_map/attention_forward/pallas_call | solution.py:61
  107.1 26.4 %collective-permute-done.4.refs_2_ = bf16[576,1024]{1,0:T(8,128)(2,1)} collective-permute-done((bf16[576,1024]{1,0:T(8,128)(2,1)}, bf16[576,1024]{1,0:T(8,128)(2,1)}, u32[]{:S(2)}, u32[]{:S(2)}) %collective-permute-start.4) | collective-permute-done | bytes 1179680 | tf_op jit(solution)/shard_map/ppermute | solution.py:128
  139.0 5.7 constant_dynamic-slice_fusion.21
  159.7 6.3 fusion.31
  176.5 3.8 copy.100
  180.3 7.2 all-gather.7.cloned.1.call-done
  190.4 3.9 copy.102
  202.6 10.2 %fusion.155 = f32[1440,1024]{1,0:T(8,128)} fusion(bf16[2304,1440]{1,0:T(8,128)(2,1)S(1)} %bitcast.377, bf16[1024,2304]{1,0:T(8,128)(2,1)S(1)} %bitcast.438), kind=kOutput, calls=%fused_computation.289 | convolution fusion | flops 6794772480 | bytes 17252352 | tf_op jit(solution)/shard_map/ef,te->ft/dot_general | solution.py:323
  221.7 8.9 fusion.159
  230.6 15.1 %fusion.151 = (bf16[1440,1024]{1,0:T(8,128)(2,1)S(1)}, f32[1024]{0:T(1024)S(1)}, bf16[1440,1024]{1,0:T(8,128)(2,1)}, bf16[1440,1024]{1,0:T(8,128)(2,1)}) fusion(f32[1024,1440]{0,1:T(8,128)} %fusion.159, f32[1024]{0:T(1024)S(1)} %bitcast.461, f32[1440,1024]{1,0:T(8,128)} %fusion.155, bf16[2304,1440]{0,1:T(8,128)(2,1)S(1)} %bitcast.433, ...), kind=kOutput, calls=%fused_computation.286 | convolution fusion | flops 6827211776 | bytes 32006144 | tf_op jit(solution)/shard_map/df,dt->ft/dot_general | solution.py:341
  246.0 5.4 fusion.35
  254.1 3.8 fusion.43
  260.5 5.5 convolution_convert_fusion.1
  268.3 5.9 convolution_convert_fusion
  285.3 19.5 %collective-permute-done.28 = f32[1,1024]{1,0:T(1,128)S(1)} collective-permute-done((f32[1,1024]{1,0:T(1,128)S(1)}, f32[1,1024]{1,0:T(1,128)S(1)}, u32[]{:S(2)}, u32[]{:S(2)}) %collective-permute-start.28) | collective-permute-done | bytes 4128 | tf_op jit(solution)/shard_map/ppermute | solution.py:128
  329.0 25.6 %collective-permute-done.73 = bf16[1152,1440]{0,1:T(8,128)(2,1)} collective-permute-done((bf16[1152,1440]{0,1:T(8,128)(2,1)}, bf16[1152,1440]{0,1:T(8,128)(2,1)}, u32[]{:S(2)}, u32[]{:S(2)}) %collective-permute-start.73) | collective-permute-done | bytes 3317792 | tf_op jit(solution)/shard_map/ppermute | solution.py:263
  355.1 9.2 fusion.1
  364.4 5.7 copy.109
  373.0 52.6 %collective-permute-done.66 = bf16[1152,1440]{0,1:T(8,128)(2,1)} collective-permute-done((bf16[1152,1440]{0,1:T(8,128)(2,1)}, bf16[1152,1440]{0,1:T(8,128)(2,1)}, u32[]{:S(2)}, u32[]{:S(2)}) %collective-permute-start.66) | collective-permute-done | bytes 3317792 | tf_op jit(solution)/shard_map/ppermute | solution.py:263
  425.7 4.9 collective-permute-start.74
  430.6 7.7 fusion
  438.3 5.7 copy.108
  444.0 8.9 collective-permute-done.59
  452.9 5.2 fusion.17
  461.9 4.0 collective-permute-start.60
  477.3 4.4 collective-permute-start.61
  484.3 15.4 %collective-permute-done.61 = bf16[1,288,576]{2,1,0:T(8,128)(2,1)S(1)} collective-permute-done((bf16[1,288,576]{2,1,0:T(8,128)(2,1)S(1)}, bf16[1,288,576]{2,1,0:T(8,128)(2,1)S(1)}, u32[]{:S(2)}, u32[]{:S(2)}) %collective-permute-start.61) | collective-permute-done | bytes 331808 | tf_op jit(solution)/shard_map/ppermute | solution.py:231
  507.2 15.2 %collective-permute-start.75 = (bf16[1,288,1440]{2,1,0:T(8,128)(2,1)}, bf16[1,288,1440]{2,1,0:T(8,128)(2,1)}, u32[]{:S(2)}, u32[]{:S(2)}) collective-permute-start(bf16[1,288,1440]{2,1,0:T(8,128)(2,1)} %fusion.59), channel_id=1, source_target_pairs={{0,8},{4,12},{8,16},{12,20},{1,9},{5,13},{9,17},{13,21},{2,10},{6,... | collective-permute-start | bytes 2488328 | tf_op jit(solution)/shard_map/ppermute | solution.py:231
  525.5 25.8 %attention_backward.1 = (bf16[9,64,1024]{2,1,0:T(8,128)(2,1)S(1)}, bf16[9,64,1024]{2,1,0:T(8,128)(2,1)S(1)}, bf16[9,64,1024]{2,1,0:T(8,128)(2,1)S(1)}) custom-call(bf16[9,64,1024]{2,1,0:T(8,128)(2,1)S(1)} %copy-done.21, bf16[9,64,1024]{2,1,0:T(8,128)(2,1)S(1)} %copy-done.23, bf16[9,64,1024]{2,1,0:T(8,128)(2,1)} %copy-done.24, ...), custom_call_target="tpu_custom_call" | custom-call | flops 12079595520 | bytes 8257536 | tf_op jit(solution)/shard_map/attention_backward/pallas_call | solution.py:110
  551.3 4.2 fusion.113
  585.2 11.7 %collective-permute-done.68 = bf16[1,288,1440]{2,1,0:T(8,128)(2,1)S(1)} collective-permute-done((bf16[1,288,1440]{2,1,0:T(8,128)(2,1)S(1)}, bf16[1,288,1440]{2,1,0:T(8,128)(2,1)S(1)}, u32[]{:S(2)}, u32[]{:S(2)}) %collective-permute-start.68) | collective-permute-done | bytes 829472 | tf_op jit(solution)/shard_map/ppermute | solution.py:231
  612.4 3.8 place.11
  616.4 9.6 fusion.30
  628.3 10.2 %constant_dynamic-slice_fusion.8 = (bf16[4,1,720,1024]{3,2,1,0:T(8,128)(2,1)}, bf16[4,1,720,1024]{3,2,1,0:T(8,128)(2,1)}) fusion(bf16[4,2,720,1024]{3,2,1,0:T(8,128)(2,1)} %bitcast.365, s32[]{:T(128)S(6)} %select_n.183, s32[]{:T(128)S(6)} %select_n.184), kind=kLoop, calls=%fused_computation.236 | loop fusion | bytes 23592968 | tf_op jit(solution)/shard_map/jit(dynamic_index_in_dim)/dynamic_slice | solution.py:247
  638.4 8.7 convolution_convert_fusion.2
  647.7 4.1 add_convert_fusion.1
  656.5 10.8 %collective-permute-done.38 = bf16[1152,576]{0,1:T(8,128)(2,1)} collective-permute-done((bf16[1152,576]{0,1:T(8,128)(2,1)}, bf16[1152,576]{0,1:T(8,128)(2,1)}, u32[]{:S(2)}, u32[]{:S(2)}) %collective-permute-start.38) | collective-permute-done | bytes 1327136 | tf_op jit(solution)/shard_map/ppermute | solution.py:263
  667.3 5.3 add_convert_fusion.3
  673.2 22.5 %collective-permute-done.45 = bf16[1152,576]{0,1:T(8,128)(2,1)} collective-permute-done((bf16[1152,576]{0,1:T(8,128)(2,1)}, bf16[1152,576]{0,1:T(8,128)(2,1)}, u32[]{:S(2)}, u32[]{:S(2)}) %collective-permute-start.45) | collective-permute-done | bytes 1327136 | tf_op jit(solution)/shard_map/ppermute | solution.py:263
  695.7 5.9 collective-permute-start.53
  701.6 4.1 add_convert_fusion.2
  718.7 5.3 collective-permute-start.39
  726.1 4.3 fusion.16
  736.4 8.4 collective-permute-done.39
  744.8 4.4 collective-permute-start.69
  761.8 5.1 collective-permute-done.69
  766.9 4.3 collective-permute-start.54
  779.7 5.2 collective-permute-start.47
  789.1 8.6 add_convert_fusion
  797.7 9.2 reshape.715
  806.9 20.8 %constant_dynamic-slice_fusion.5 = (bf16[1,1,720,576]{2,1,3,0:T(2,128)(2,1)}, bf16[1,1,720,576]{2,1,3,0:T(2,128)(2,1)S(1)}, bf16[1,1,720,576]{2,1,3,0:T(2,128)(2...) fusion(bf16[1,4,720,576]{2,1,3,0:T(4,128)(2,1)} %reshape.715, ...), kind=kLoop, calls=%fused_computation.233 | loop fusion | bytes 11612188 | tf_op jit(solution)/shard_map/jit(dynamic_index_in_dim)/dynamic_slice | solution.py:217
  841.8 6.8 collective-permute-start.55
  849.5 15.6 %collective-permute-start.41 = (bf16[1,288,576]{2,1,0:T(8,128)(2,1)}, bf16[1,288,576]{2,1,0:T(8,128)(2,1)}, u32[]{:S(2)}, u32[]{:S(2)}) collective-permute-start(bf16[1,288,576]{2,1,0:T(8,128)(2,1)} %get-tuple-element.79), channel_id=1, source_target_pairs={{0,8},{4,12},{8,16},{12,20},{16,24},{20,28},{1,9},{5,13},{9,17},{1... | collective-permute-start | bytes 995336 | tf_op jit(solution)/shard_map/ppermute | solution.py:231
  867.9 4.6 collective-permute-start.82
  877.4 9.3 collective-permute-done.82
  889.1 7.3 collective-permute-start.83
  900.1 41.0 %all-reduce = (f32[2304]{0:T(1024)}, f32[2304]{0:T(1024)}) all-reduce(f32[2304]{0:T(1024)S(1)} %get-tuple-element.27, f32[2304]{0:T(1024)} %copy-done.67), channel_id=1, replica_groups=mesh['rep'=8,'fsdp'=4] {'rep','fsdp'}, use_global_device_ids=true, to_apply=%region_6.7 | all-reduce | flops 4608 | bytes 36864 | tf_op jit(solution)/shard_map/psum | solution.py:416
  950.7 4.0 collective-permute-done.51
  (439 shorter events, 292.7 us)
Async XLA Ops:
  7.2 166.3 %all-gather.5.cloned.1.call-start = ((), (), s32[]{:S(2)}) async-start(), calls=%async_computation | async-start | bytes 2119680 | tf_op jit(solution)/shard_map/all_gather | solution.py:319
  7.2 29.3 %collective-permute-start.1 = (bf16[256,2304]{1,0:T(8,128)(2,1)}, bf16[256,2304]{1,0:T(8,128)(2,1)}, u32[]{:S(2)}, u32[]{:S(2)}) collective-permute-start(bf16[256,2304]{1,0:T(8,128)(2,1)} %refs_0_.2), channel_id=1, source_target_pairs={{0,2},{1,3},{2,0},{3,1},{4,6},{5,7},{6,4},{7,5},{8,10},{9,11},{10,... | collective-permute-start | bytes 3538952 | tf_op jit(solution)/shard_map/ppermute | solution.py:128
  10.2 38.1 %collective-permute-start = (bf16[256,2304]{1,0:T(8,128)(2,1)}, bf16[256,2304]{1,0:T(8,128)(2,1)}, u32[]{:S(2)}, u32[]{:S(2)}) collective-permute-start(bf16[256,2304]{1,0:T(8,128)(2,1)} %refs_0_.2), channel_id=1, source_target_pairs={{0,1},{1,0},{2,3},{3,2},{4,5},{5,4},{6,7},{7,6},{8,9},{9,8},{10,11... | collective-permute-start | bytes 3538952 | tf_op jit(solution)/shard_map/ppermute | solution.py:128
  40.5 65.5 %collective-permute-start.18 = (bf16[256,2304]{1,0:T(8,128)(2,1)}, bf16[256,2304]{1,0:T(8,128)(2,1)}, u32[]{:S(2)}, u32[]{:S(2)}) collective-permute-start(bf16[256,2304]{1,0:T(8,128)(2,1)} %refs_0_.3), channel_id=1, source_target_pairs={{0,2},{1,3},{2,0},{3,1},{4,6},{5,7},{6,4},{7,5},{8,10},{9,11},{10,... | collective-permute-start | bytes 3538952 | tf_op jit(solution)/shard_map/ppermute | solution.py:128
  48.3 139.2 %all-gather.7.cloned.1.call-start = ((), (), s32[]{:S(2)}) async-start(), calls=%async_computation.1 | async-start | bytes 2119680 | tf_op jit(solution)/shard_map/all_gather | solution.py:320
  104.3 29.2 %collective-permute-start.4 = (bf16[576,1024]{1,0:T(8,128)(2,1)}, bf16[576,1024]{1,0:T(8,128)(2,1)}, u32[]{:S(2)}, u32[]{:S(2)}) collective-permute-start(bf16[576,1024]{1,0:T(8,128)(2,1)} %bitcast.7.refs_0_), channel_id=1, source_target_pairs={{0,2},{1,3},{2,0},{3,1},{4,6},{5,7},{6,4},{7,5},{8,10},{9,11},{10,... | collective-permute-start | bytes 3538952 | tf_op jit(solution)/shard_map/ppermute | solution.py:128
  106.1 41.7 %collective-permute-start.17 = (bf16[256,2304]{1,0:T(8,128)(2,1)}, bf16[256,2304]{1,0:T(8,128)(2,1)}, u32[]{:S(2)}, u32[]{:S(2)}) collective-permute-start(bf16[256,2304]{1,0:T(8,128)(2,1)} %refs_0_.3), channel_id=1, source_target_pairs={{0,1},{1,0},{2,3},{3,2},{4,5},{5,4},{6,7},{7,6},{8,9},{9,8},{10,11... | collective-permute-start | bytes 3538952 | tf_op jit(solution)/shard_map/ppermute | solution.py:128
  106.1 41.7 %collective-permute-start.19 = (bf16[256,2304]{1,0:T(8,128)(2,1)}, bf16[256,2304]{1,0:T(8,128)(2,1)}, u32[]{:S(2)}, u32[]{:S(2)}) collective-permute-start(bf16[256,2304]{1,0:T(8,128)(2,1)} %collective-permute-done.18.refs_2_), channel_id=1, source_target_pairs={{0,1},{1,0},{2,3},{3,2},{4,5},{5,4},{6,7},{7,6},{8,9},{9,8},{10,11... | collective-permute-start | bytes 3538952 | tf_op jit(solution)/shard_map/ppermute | solution.py:128
  106.8 30.1 %collective-permute-start.22 = (bf16[180,576]{1,0:T(8,128)(2,1)S(1)}, bf16[180,576]{1,0:T(8,128)(2,1)S(1)}, u32[]{:S(2)}, u32[]{:S(2)}) collective-permute-start(bf16[180,576]{1,0:T(8,128)(2,1)S(1)} %copy.120), channel_id=1, source_target_pairs={{0,2},{1,3},{2,0},{3,1},{4,6},{5,7},{6,4},{7,5},{8,10},{9,11},{10,... | collective-permute-start | bytes 622088 | tf_op jit(solution)/shard_map/ppermute | solution.py:128
  107.1 49.7 %collective-permute-start.3 = (bf16[576,1024]{1,0:T(8,128)(2,1)}, bf16[576,1024]{1,0:T(8,128)(2,1)}, u32[]{:S(2)}, u32[]{:S(2)}) collective-permute-start(bf16[576,1024]{1,0:T(8,128)(2,1)} %bitcast.7.refs_0_), channel_id=1, source_target_pairs={{0,1},{1,0},{2,3},{3,2},{4,5},{5,4},{6,7},{7,6},{8,9},{9,8},{10,11... | collective-permute-start | bytes 3538952 | tf_op jit(solution)/shard_map/ppermute | solution.py:128
  133.6 23.2 %collective-permute-start.5 = (bf16[576,1024]{1,0:T(8,128)(2,1)}, bf16[576,1024]{1,0:T(8,128)(2,1)}, u32[]{:S(2)}, u32[]{:S(2)}) collective-permute-start(bf16[576,1024]{1,0:T(8,128)(2,1)} %collective-permute-done.4.refs_2_), channel_id=1, source_target_pairs={{0,1},{1,0},{2,3},{3,2},{4,5},{5,4},{6,7},{7,6},{8,9},{9,8},{10,11... | collective-permute-start | bytes 3538952 | tf_op jit(solution)/shard_map/ppermute | solution.py:128
  144.7 49.6 %collective-permute-start.20 = (bf16[1440,576]{0,1:T(8,128)(2,1)}, bf16[1440,576]{0,1:T(8,128)(2,1)}, u32[]{:S(2)}, u32[]{:S(2)}) collective-permute-start(bf16[1440,576]{0,1:T(8,128)(2,1)} %get-tuple-element.41), channel_id=1, source_target_pairs={{0,1},{1,0},{2,3},{3,2},{4,5},{5,4},{6,7},{7,6},{8,9},{9,8},{10,11... | collective-permute-start | bytes 4976648 | tf_op jit(solution)/shard_map/ppermute | solution.py:128
  166.0 36.5 %collective-permute-start.9 = (bf16[576,1024]{1,0:T(8,128)(2,1)}, bf16[576,1024]{1,0:T(8,128)(2,1)}, u32[]{:S(2)}, u32[]{:S(2)}) collective-permute-start(bf16[576,1024]{1,0:T(8,128)(2,1)} %get-tuple-element.66.refs_0_), channel_id=1, source_target_pairs={{0,2},{1,3},{2,0},{3,1},{4,6},{5,7},{6,4},{7,5},{8,10},{9,11},{10,... | collective-permute-start | bytes 3538952 | tf_op jit(solution)/shard_map/ppermute | solution.py:128
  245.8 34.4 %collective-permute-start.27 = (f32[1,1024]{1,0:T(1,128)S(1)}, f32[1,1024]{1,0:T(1,128)S(1)}, u32[]{:S(2)}, u32[]{:S(2)}) collective-permute-start(f32[1,1024]{1,0:T(1,128)S(1)} %bitcast.464), channel_id=1, source_target_pairs={{0,1},{1,0},{2,3},{3,2},{4,5},{5,4},{6,7},{7,6},{8,9},{9,8},{10,11... | collective-permute-start | bytes 12296 | tf_op jit(solution)/shard_map/ppermute | solution.py:128
  253.7 20.4 %collective-permute-start.25 = (bf16[576,1024]{1,0:T(8,128)(2,1)S(1)}, bf16[576,1024]{1,0:T(8,128)(2,1)S(1)}, u32[]{:S(2)}, u32[]{:S(2)}) collective-permute-start(bf16[576,1024]{1,0:T(8,128)(2,1)S(1)} %add_convert_fusion.5), channel_id=1, source_target_pairs={{0,1},{1,0},{2,3},{3,2},{4,5},{5,4},{6,7},{7,6},{8,9},{9,8},{10,11... | collective-permute-start | bytes 3538952 | tf_op jit(solution)/shard_map/ppermute | solution.py:128
  260.2 44.5 %collective-permute-start.24 = (bf16[576,1024]{1,0:T(8,128)(2,1)S(1)}, bf16[576,1024]{1,0:T(8,128)(2,1)S(1)}, u32[]{:S(2)}, u32[]{:S(2)}) collective-permute-start(bf16[576,1024]{1,0:T(8,128)(2,1)S(1)} %add_convert_fusion.7), channel_id=1, source_target_pairs={{0,1},{1,0},{2,3},{3,2},{4,5},{5,4},{6,7},{7,6},{8,9},{9,8},{10,11... | collective-permute-start | bytes 3538952 | tf_op jit(solution)/shard_map/ppermute | solution.py:128
  276.4 28.3 %collective-permute-start.26 = (bf16[576,1024]{1,0:T(8,128)(2,1)S(1)}, bf16[576,1024]{1,0:T(8,128)(2,1)S(1)}, u32[]{:S(2)}, u32[]{:S(2)}) collective-permute-start(bf16[576,1024]{1,0:T(8,128)(2,1)S(1)} %fusion.78), channel_id=1, source_target_pairs={{0,2},{1,3},{2,0},{3,1},{4,6},{5,7},{6,4},{7,5},{8,10},{9,11},{10,... | collective-permute-start | bytes 3538952 | tf_op jit(solution)/shard_map/ppermute | solution.py:128
  279.5 75.1 %collective-permute-start.73 = (bf16[1152,1440]{0,1:T(8,128)(2,1)}, bf16[1152,1440]{0,1:T(8,128)(2,1)}, u32[]{:S(2)}, u32[]{:S(2)}) collective-permute-start(bf16[1152,1440]{0,1:T(8,128)(2,1)} %convolution_convert_fusion), channel_id=1, source_target_pairs={{0,4},{4,0},{8,12},{12,8},{16,20},{20,16},{24,28},{28,24},{1,5},{5... | collective-permute-start | bytes 9953288 | tf_op jit(solution)/shard_map/ppermute | solution.py:263
  280.2 24.6 %collective-permute-start.28 = (f32[1,1024]{1,0:T(1,128)S(1)}, f32[1,1024]{1,0:T(1,128)S(1)}, u32[]{:S(2)}, u32[]{:S(2)}) collective-permute-start(f32[1,1024]{1,0:T(1,128)S(1)} %add.522), channel_id=1, source_target_pairs={{0,2},{1,3},{2,0},{3,1},{4,6},{5,7},{6,4},{7,5},{8,10},{9,11},{10,... | collective-permute-start | bytes 12296 | tf_op jit(solution)/shard_map/ppermute | solution.py:128
  283.8 141.9 %collective-permute-start.66 = (bf16[1152,1440]{0,1:T(8,128)(2,1)}, bf16[1152,1440]{0,1:T(8,128)(2,1)}, u32[]{:S(2)}, u32[]{:S(2)}) collective-permute-start(bf16[1152,1440]{0,1:T(8,128)(2,1)} %convolution_convert_fusion.1), channel_id=1, source_target_pairs={{0,4},{4,0},{8,12},{12,8},{16,20},{20,16},{24,28},{28,24},{1,5},{5... | collective-permute-start | bytes 9953288 | tf_op jit(solution)/shard_map/ppermute | solution.py:263
  320.4 156.1 %collective-permute-start.12 = (bf16[1440,1024]{1,0:T(8,128)(2,1)}, bf16[1440,1024]{1,0:T(8,128)(2,1)}, u32[]{:S(2)}, u32[]{:S(2)}) collective-permute-start(bf16[1440,1024]{1,0:T(8,128)(2,1)} %get-tuple-element.36.refs_0_), channel_id=1, source_target_pairs={{0,2},{1,3},{2,0},{3,1},{4,6},{5,7},{6,4},{7,5},{8,10},{9,11},{10,... | collective-permute-start | bytes 8847368 | tf_op jit(solution)/shard_map/ppermute | solution.py:128
  322.5 182.9 %collective-permute-start.32 = (bf16[576,1024]{1,0:T(8,128)(2,1)}, bf16[576,1024]{1,0:T(8,128)(2,1)}, u32[]{:S(2)}, u32[]{:S(2)}) collective-permute-start(bf16[576,1024]{1,0:T(8,128)(2,1)} %convolution_convert_fusion.9), channel_id=1, source_target_pairs={{0,1},{1,0},{2,3},{3,2},{4,5},{5,4},{6,7},{7,6},{8,9},{9,8},{10,11... | collective-permute-start | bytes 3538952 | tf_op jit(solution)/shard_map/ppermute | solution.py:128
  323.0 145.5 %collective-permute-start.33 = (bf16[576,1024]{1,0:T(8,128)(2,1)}, bf16[576,1024]{1,0:T(8,128)(2,1)}, u32[]{:S(2)}, u32[]{:S(2)}) collective-permute-start(bf16[576,1024]{1,0:T(8,128)(2,1)} %convolution_convert_fusion.7), channel_id=1, source_target_pairs={{0,1},{1,0},{2,3},{3,2},{4,5},{5,4},{6,7},{7,6},{8,9},{9,8},{10,11... | collective-permute-start | bytes 3538952 | tf_op jit(solution)/shard_map/ppermute | solution.py:128
  354.6 98.3 %collective-permute-start.59 = (bf16[1152,576]{0,1:T(8,128)(2,1)}, bf16[1152,576]{0,1:T(8,128)(2,1)}, u32[]{:S(2)}, u32[]{:S(2)}) collective-permute-start(bf16[1152,576]{0,1:T(8,128)(2,1)} %convolution_convert_fusion.3), channel_id=1, source_target_pairs={{0,4},{4,0},{8,12},{12,8},{16,20},{20,16},{24,28},{28,24},{1,5},{5... | collective-permute-start | bytes 3981320 | tf_op jit(solution)/shard_map/ppermute | solution.py:263
  425.7 51.6 %collective-permute-start.74 = (bf16[1,288,1440]{2,1,0:T(8,128)(2,1)}, bf16[1,288,1440]{2,1,0:T(8,128)(2,1)}, u32[]{:S(2)}, u32[]{:S(2)}) collective-permute-start(bf16[1,288,1440]{2,1,0:T(8,128)(2,1)} %get-tuple-element.59), channel_id=1, source_target_pairs={{0,8},{4,12},{1,9},{5,13},{2,10},{6,14},{3,11},{7,15}} | collective-permute-start | bytes 2488328 | tf_op jit(solution)/shard_map/ppermute | solution.py:231
  468.5 31.4 %collective-permute-start.67 = (bf16[1,288,1440]{2,1,0:T(8,128)(2,1)S(1)}, bf16[1,288,1440]{2,1,0:T(8,128)(2,1)S(1)}, u32[]{:S(2)}, u32[]{:S(2)}) collective-permute-start(bf16[1,288,1440]{2,1,0:T(8,128)(2,1)S(1)} %get-tuple-element.63), channel_id=1, source_target_pairs={{0,8},{4,12},{1,9},{5,13},{2,10},{6,14},{3,11},{7,15}} | collective-permute-start | bytes 2488328 | tf_op jit(solution)/shard_map/ppermute | solution.py:231
  475.0 32.3 %collective-permute-start.34 = (bf16[576,1024]{1,0:T(8,128)(2,1)S(1)}, bf16[576,1024]{1,0:T(8,128)(2,1)S(1)}, u32[]{:S(2)}, u32[]{:S(2)}) collective-permute-start(bf16[576,1024]{1,0:T(8,128)(2,1)S(1)} %fusion.77), channel_id=1, source_target_pairs={{0,2},{1,3},{2,0},{3,1},{4,6},{5,7},{6,4},{7,5},{8,10},{9,11},{10,... | collective-permute-start | bytes 3538952 | tf_op jit(solution)/shard_map/ppermute | solution.py:128
  477.3 22.4 %collective-permute-start.61 = (bf16[1,288,576]{2,1,0:T(8,128)(2,1)S(1)}, bf16[1,288,576]{2,1,0:T(8,128)(2,1)S(1)}, u32[]{:S(2)}, u32[]{:S(2)}) collective-permute-start(bf16[1,288,576]{2,1,0:T(8,128)(2,1)S(1)} %fusion.85), channel_id=1, source_target_pairs={{0,8},{4,12},{8,16},{12,20},{1,9},{5,13},{9,17},{13,21},{2,10},{6,... | collective-permute-start | bytes 995336 | tf_op jit(solution)/shard_map/ppermute | solution.py:231
  484.3 128.1 %collective-permute-start.11 = (bf16[1440,1024]{1,0:T(8,128)(2,1)}, bf16[1440,1024]{1,0:T(8,128)(2,1)S(1)}, u32[]{:S(2)}, u32[]{:S(2)}) collective-permute-start(bf16[1440,1024]{1,0:T(8,128)(2,1)} %get-tuple-element.36.refs_0_), channel_id=1, source_target_pairs={{0,1},{1,0},{2,3},{3,2},{4,5},{5,4},{6,7},{7,6},{8,9},{9,8},{10,11... | collective-permute-start | bytes 8847368 | tf_op jit(solution)/shard_map/ppermute | solution.py:128
  499.7 112.6 %collective-permute-start.13 = (bf16[1440,1024]{1,0:T(8,128)(2,1)}, bf16[1440,1024]{1,0:T(8,128)(2,1)S(1)}, u32[]{:S(2)}, u32[]{:S(2)}) collective-permute-start(bf16[1440,1024]{1,0:T(8,128)(2,1)} %collective-permute-done.12.refs_2_), channel_id=1, source_target_pairs={{0,1},{1,0},{2,3},{3,2},{4,5},{5,4},{6,7},{7,6},{8,9},{9,8},{10,11... | collective-permute-start | bytes 8847368 | tf_op jit(solution)/shard_map/ppermute | solution.py:128
  503.1 72.2 %collective-permute-start.77 = (bf16[1,288,1440]{2,1,0:T(8,128)(2,1)}, bf16[1,288,1440]{2,1,0:T(8,128)(2,1)}, u32[]{:S(2)}, u32[]{:S(2)}) collective-permute-start(bf16[1,288,1440]{2,1,0:T(8,128)(2,1)} %get-tuple-element.60), channel_id=1, source_target_pairs={{24,16},{28,20},{25,17},{29,21},{26,18},{30,22},{27,19},{31,23}} | collective-permute-start | bytes 2488328 | tf_op jit(solution)/shard_map/ppermute | solution.py:231
  505.5 78.4 %collective-permute-start.70 = (bf16[1,288,1440]{2,1,0:T(8,128)(2,1)}, bf16[1,288,1440]{2,1,0:T(8,128)(2,1)}, u32[]{:S(2)}, u32[]{:S(2)}) collective-permute-start(bf16[1,288,1440]{2,1,0:T(8,128)(2,1)} %get-tuple-element.64), channel_id=1, source_target_pairs={{24,16},{28,20},{25,17},{29,21},{26,18},{30,22},{27,19},{31,23}} | collective-permute-start | bytes 2488328 | tf_op jit(solution)/shard_map/ppermute | solution.py:231
  507.2 72.0 %collective-permute-start.75 = (bf16[1,288,1440]{2,1,0:T(8,128)(2,1)}, bf16[1,288,1440]{2,1,0:T(8,128)(2,1)}, u32[]{:S(2)}, u32[]{:S(2)}) collective-permute-start(bf16[1,288,1440]{2,1,0:T(8,128)(2,1)} %fusion.59), channel_id=1, source_target_pairs={{0,8},{4,12},{8,16},{12,20},{1,9},{5,13},{9,17},{13,21},{2,10},{6,... | collective-permute-start | bytes 2488328 | tf_op jit(solution)/shard_map/ppermute | solution.py:231
  575.3 21.6 %collective-permute-start.68 = (bf16[1,288,1440]{2,1,0:T(8,128)(2,1)S(1)}, bf16[1,288,1440]{2,1,0:T(8,128)(2,1)S(1)}, u32[]{:S(2)}, u32[]{:S(2)}) collective-permute-start(bf16[1,288,1440]{2,1,0:T(8,128)(2,1)S(1)} %copy-done.59), channel_id=1, source_target_pairs={{0,8},{4,12},{8,16},{12,20},{1,9},{5,13},{9,17},{13,21},{2,10},{6,... | collective-permute-start | bytes 2488328 | tf_op jit(solution)/shard_map/ppermute | solution.py:231
  579.3 24.3 %collective-permute-start.62 = (bf16[1,288,576]{2,1,0:T(8,128)(2,1)S(1)}, bf16[1,288,576]{2,1,0:T(8,128)(2,1)S(1)}, u32[]{:S(2)}, u32[]{:S(2)}) collective-permute-start(bf16[1,288,576]{2,1,0:T(8,128)(2,1)S(1)} %get-tuple-element.67), channel_id=1, source_target_pairs={{0,8},{4,12},{8,16},{12,20},{16,24},{20,28},{1,9},{5,13},{9,17},{1... | collective-permute-start | bytes 995336 | tf_op jit(solution)/shard_map/ppermute | solution.py:231
  583.9 22.5 %collective-permute-start.65 = (bf16[1,288,576]{2,1,0:T(8,128)(2,1)S(1)}, bf16[1,288,576]{2,1,0:T(8,128)(2,1)S(1)}, u32[]{:S(2)}, u32[]{:S(2)}) collective-permute-start(bf16[1,288,576]{2,1,0:T(8,128)(2,1)S(1)} %copy-done.62), channel_id=1, source_target_pairs={{8,0},{12,4},{16,8},{20,12},{24,16},{28,20},{9,1},{13,5},{17,9},{2... | collective-permute-start | bytes 995336 | tf_op jit(solution)/shard_map/ppermute | solution.py:231
  606.5 40.7 %collective-permute-start.52 = (bf16[1152,576]{0,1:T(8,128)(2,1)}, bf16[1152,576]{0,1:T(8,128)(2,1)}, u32[]{:S(2)}, u32[]{:S(2)}) collective-permute-start(bf16[1152,576]{0,1:T(8,128)(2,1)} %convolution_convert_fusion.4), channel_id=1, source_target_pairs={{0,4},{4,0},{8,12},{12,8},{16,20},{20,16},{24,28},{28,24},{1,5},{5... | collective-permute-start | bytes 3981320 | tf_op jit(solution)/shard_map/ppermute | solution.py:263
  608.0 59.3 %collective-permute-start.38 = (bf16[1152,576]{0,1:T(8,128)(2,1)}, bf16[1152,576]{0,1:T(8,128)(2,1)}, u32[]{:S(2)}, u32[]{:S(2)}) collective-permute-start(bf16[1152,576]{0,1:T(8,128)(2,1)} %convolution_convert_fusion.6), channel_id=1, source_target_pairs={{0,4},{4,0},{8,12},{12,8},{16,20},{20,16},{24,28},{28,24},{1,5},{5... | collective-permute-start | bytes 3981320 | tf_op jit(solution)/shard_map/ppermute | solution.py:263
  610.6 85.1 %collective-permute-start.45 = (bf16[1152,576]{0,1:T(8,128)(2,1)}, bf16[1152,576]{0,1:T(8,128)(2,1)}, u32[]{:S(2)}, u32[]{:S(2)}) collective-permute-start(bf16[1152,576]{0,1:T(8,128)(2,1)} %convolution_convert_fusion.5), channel_id=1, source_target_pairs={{0,4},{4,0},{8,12},{12,8},{16,20},{20,16},{24,28},{28,24},{1,5},{5... | collective-permute-start | bytes 3981320 | tf_op jit(solution)/shard_map/ppermute | solution.py:263
  612.3 60.3 %collective-permute-start.36 = (bf16[256,2304]{1,0:T(8,128)(2,1)}, bf16[256,2304]{1,0:T(8,128)(2,1)}, u32[]{:S(2)}, u32[]{:S(2)}) collective-permute-start(bf16[256,2304]{1,0:T(8,128)(2,1)} %fusion.15), channel_id=1, source_target_pairs={{0,1},{1,0},{2,3},{3,2},{4,5},{5,4},{6,7},{7,6},{8,9},{9,8},{10,11... | collective-permute-start | bytes 3538952 | tf_op jit(solution)/shard_map/ppermute | solution.py:128
  627.1 88.1 %collective-permute-start.16 = (bf16[576,256]{1,0:T(8,128)(2,1)}, bf16[576,256]{1,0:T(8,128)(2,1)S(1)}, u32[]{:S(2)}, u32[]{:S(2)}) collective-permute-start(bf16[576,256]{1,0:T(8,128)(2,1)} %get-tuple-element.87), channel_id=1, source_target_pairs={{0,3},{1,2},{2,1},{3,0},{4,7},{5,6},{6,5},{7,4},{8,11},{9,10},{10,... | collective-permute-start | bytes 884744 | tf_op jit(solution)/shard_map/ppermute | solution.py:128
  647.2 70.2 %collective-permute-start.15 = (bf16[576,256]{1,0:T(8,128)(2,1)}, bf16[576,256]{1,0:T(8,128)(2,1)S(1)}, u32[]{:S(2)}, u32[]{:S(2)}) collective-permute-start(bf16[576,256]{1,0:T(8,128)(2,1)} %get-tuple-element.88), channel_id=1, source_target_pairs={{0,2},{1,3},{2,0},{3,1},{4,6},{5,7},{6,4},{7,5},{8,10},{9,11},{10,... | collective-permute-start | bytes 884744 | tf_op jit(solution)/shard_map/ppermute | solution.py:128
  667.3 51.4 %collective-permute-start.14 = (bf16[576,256]{1,0:T(8,128)(2,1)}, bf16[576,256]{1,0:T(8,128)(2,1)}, u32[]{:S(2)}, u32[]{:S(2)}) collective-permute-start(bf16[576,256]{1,0:T(8,128)(2,1)} %get-tuple-element.89), channel_id=1, source_target_pairs={{0,1},{1,0},{2,3},{3,2},{4,5},{5,4},{6,7},{7,6},{8,9},{9,8},{10,11... | collective-permute-start | bytes 884744 | tf_op jit(solution)/shard_map/ppermute | solution.py:128
  672.6 114.7 %collective-permute-start.80 = (bf16[2880,576]{0,1:T(8,128)(2,1)}, bf16[2880,576]{0,1:T(8,128)(2,1)}, u32[]{:S(2)}, u32[]{:S(2)}) collective-permute-start(bf16[2880,576]{0,1:T(8,128)(2,1)} %convolution_convert_fusion.2), channel_id=1, source_target_pairs={{0,4},{4,0},{8,12},{12,8},{16,20},{20,16},{24,28},{28,24},{1,5},{5... | collective-permute-start | bytes 9953288 | tf_op jit(solution)/shard_map/ppermute | solution.py:263
  695.7 28.3 %collective-permute-start.53 = (bf16[1,288,576]{2,1,0:T(8,128)(2,1)}, bf16[1,288,576]{2,1,0:T(8,128)(2,1)}, u32[]{:S(2)}, u32[]{:S(2)}) collective-permute-start(bf16[1,288,576]{2,1,0:T(8,128)(2,1)} %get-tuple-element.73), channel_id=1, source_target_pairs={{0,8},{4,12},{1,9},{5,13},{2,10},{6,14},{3,11},{7,15}} | collective-permute-start | bytes 995336 | tf_op jit(solution)/shard_map/ppermute | solution.py:231
  715.2 41.9 %collective-permute-start.76 = (bf16[1,288,1440]{2,1,0:T(8,128)(2,1)}, bf16[1,288,1440]{2,1,0:T(8,128)(2,1)}, u32[]{:S(2)}, u32[]{:S(2)}) collective-permute-start(bf16[1,288,1440]{2,1,0:T(8,128)(2,1)} %get-tuple-element.57), channel_id=1, source_target_pairs={{0,8},{4,12},{8,16},{12,20},{16,24},{20,28},{1,9},{5,13},{9,17},{1... | collective-permute-start | bytes 2488328 | tf_op jit(solution)/shard_map/ppermute | solution.py:231
  717.4 40.4 %collective-permute-start.79 = (bf16[1,288,1440]{2,1,0:T(8,128)(2,1)}, bf16[1,288,1440]{2,1,0:T(8,128)(2,1)}, u32[]{:S(2)}, u32[]{:S(2)}) collective-permute-start(bf16[1,288,1440]{2,1,0:T(8,128)(2,1)} %fusion.58), channel_id=1, source_target_pairs={{8,0},{12,4},{16,8},{20,12},{24,16},{28,20},{9,1},{13,5},{17,9},{2... | collective-permute-start | bytes 2488328 | tf_op jit(solution)/shard_map/ppermute | solution.py:231
  718.7 26.1 %collective-permute-start.39 = (bf16[1,288,576]{2,1,0:T(8,128)(2,1)}, bf16[1,288,576]{2,1,0:T(8,128)(2,1)}, u32[]{:S(2)}, u32[]{:S(2)}) collective-permute-start(bf16[1,288,576]{2,1,0:T(8,128)(2,1)} %get-tuple-element.81), channel_id=1, source_target_pairs={{0,8},{4,12},{1,9},{5,13},{2,10},{6,14},{3,11},{7,15}} | collective-permute-start | bytes 995336 | tf_op jit(solution)/shard_map/ppermute | solution.py:231
  724.0 28.7 %collective-permute-start.46 = (bf16[1,288,576]{2,1,0:T(8,128)(2,1)}, bf16[1,288,576]{2,1,0:T(8,128)(2,1)}, u32[]{:S(2)}, u32[]{:S(2)}) collective-permute-start(bf16[1,288,576]{2,1,0:T(8,128)(2,1)} %get-tuple-element.77), channel_id=1, source_target_pairs={{0,8},{4,12},{1,9},{5,13},{2,10},{6,14},{3,11},{7,15}} | collective-permute-start | bytes 995336 | tf_op jit(solution)/shard_map/ppermute | solution.py:231
  744.8 22.1 %collective-permute-start.69 = (bf16[1,288,1440]{2,1,0:T(8,128)(2,1)}, bf16[1,288,1440]{2,1,0:T(8,128)(2,1)S(1)}, u32[]{:S(2)}, u32[]{:S(2)}) collective-permute-start(bf16[1,288,1440]{2,1,0:T(8,128)(2,1)} %get-tuple-element.61), channel_id=1, source_target_pairs={{0,8},{4,12},{8,16},{12,20},{16,24},{20,28},{1,9},{5,13},{9,17},{1... | collective-permute-start | bytes 2488328 | tf_op jit(solution)/shard_map/ppermute | solution.py:231
  757.8 21.9 %collective-permute-start.42 = (bf16[1,288,576]{2,1,0:T(8,128)(2,1)S(1)}, bf16[1,288,576]{2,1,0:T(8,128)(2,1)S(1)}, u32[]{:S(2)}, u32[]{:S(2)}) collective-permute-start(bf16[1,288,576]{2,1,0:T(8,128)(2,1)S(1)} %copy-done.61), channel_id=1, source_target_pairs={{24,16},{28,20},{25,17},{29,21},{26,18},{30,22},{27,19},{31,23}} | collective-permute-start | bytes 995336 | tf_op jit(solution)/shard_map/ppermute | solution.py:231
  775.8 90.6 %collective-permute-start.35 = (bf16[256,2304]{1,0:T(8,128)(2,1)}, bf16[256,2304]{1,0:T(8,128)(2,1)}, u32[]{:S(2)}, u32[]{:S(2)}) collective-permute-start(bf16[256,2304]{1,0:T(8,128)(2,1)} %fusion.13), channel_id=1, source_target_pairs={{0,1},{1,0},{2,3},{3,2},{4,5},{5,4},{6,7},{7,6},{8,9},{9,8},{10,11... | collective-permute-start | bytes 3538952 | tf_op jit(solution)/shard_map/ppermute | solution.py:128
  778.1 49.8 %collective-permute-start.49 = (bf16[1,288,576]{2,1,0:T(8,128)(2,1)}, bf16[1,288,576]{2,1,0:T(8,128)(2,1)S(1)}, u32[]{:S(2)}, u32[]{:S(2)}) collective-permute-start(bf16[1,288,576]{2,1,0:T(8,128)(2,1)} %get-tuple-element.78), channel_id=1, source_target_pairs={{24,16},{28,20},{25,17},{29,21},{26,18},{30,22},{27,19},{31,23}} | collective-permute-start | bytes 995336 | tf_op jit(solution)/shard_map/ppermute | solution.py:231
  779.7 51.0 %collective-permute-start.47 = (bf16[1,288,576]{2,1,0:T(8,128)(2,1)}, bf16[1,288,576]{2,1,0:T(8,128)(2,1)}, u32[]{:S(2)}, u32[]{:S(2)}) collective-permute-start(bf16[1,288,576]{2,1,0:T(8,128)(2,1)} %fusion.97), channel_id=1, source_target_pairs={{0,8},{4,12},{8,16},{12,20},{1,9},{5,13},{9,17},{13,21},{2,10},{6,... | collective-permute-start | bytes 995336 | tf_op jit(solution)/shard_map/ppermute | solution.py:231
  784.9 48.6 %collective-permute-start.57 = (bf16[1,288,576]{2,1,0:T(8,128)(2,1)S(1)}, bf16[1,288,576]{2,1,0:T(8,128)(2,1)}, u32[]{:S(2)}, u32[]{:S(2)}) collective-permute-start(bf16[1,288,576]{2,1,0:T(8,128)(2,1)S(1)} %get-tuple-element.72), channel_id=1, source_target_pairs={{16,8},{20,12},{24,16},{28,20},{17,9},{21,13},{25,17},{29,21},{18,... | collective-permute-start | bytes 995336 | tf_op jit(solution)/shard_map/ppermute | solution.py:231
  787.3 46.9 %collective-permute-start.43 = (bf16[1,288,576]{2,1,0:T(8,128)(2,1)}, bf16[1,288,576]{2,1,0:T(8,128)(2,1)}, u32[]{:S(2)}, u32[]{:S(2)}) collective-permute-start(bf16[1,288,576]{2,1,0:T(8,128)(2,1)} %get-tuple-element.80), channel_id=1, source_target_pairs={{16,8},{20,12},{24,16},{28,20},{17,9},{21,13},{25,17},{29,21},{18,... | collective-permute-start | bytes 995336 | tf_op jit(solution)/shard_map/ppermute | solution.py:231
  829.0 38.8 %collective-permute-start.37 = (bf16[256,2304]{1,0:T(8,128)(2,1)S(1)}, bf16[256,2304]{1,0:T(8,128)(2,1)S(1)}, u32[]{:S(2)}, u32[]{:S(2)}) collective-permute-start(bf16[256,2304]{1,0:T(8,128)(2,1)S(1)} %copy-done.57), channel_id=1, source_target_pairs={{0,2},{1,3},{2,0},{3,1},{4,6},{5,7},{6,4},{7,5},{8,10},{9,11},{10,... | collective-permute-start | bytes 3538952 | tf_op jit(solution)/shard_map/ppermute | solution.py:128
  834.2 31.2 %collective-permute-start.81 = (bf16[1,720,576]{1,2,0:T(8,128)(2,1)S(1)}, bf16[1,720,576]{1,2,0:T(8,128)(2,1)S(1)}, u32[]{:S(2)}, u32[]{:S(2)}) collective-permute-start(bf16[1,720,576]{1,2,0:T(8,128)(2,1)S(1)} %bitcast.456), channel_id=1, source_target_pairs={{0,8},{4,12},{1,9},{5,13},{2,10},{6,14},{3,11},{7,15}} | collective-permute-start | bytes 2488328 | tf_op jit(solution)/shard_map/ppermute | solution.py:231
  841.8 47.2 %collective-permute-start.55 = (bf16[1,288,576]{2,1,0:T(8,128)(2,1)}, bf16[1,288,576]{2,1,0:T(8,128)(2,1)}, u32[]{:S(2)}, u32[]{:S(2)}) collective-permute-start(bf16[1,288,576]{2,1,0:T(8,128)(2,1)} %get-tuple-element.71), channel_id=1, source_target_pairs={{0,8},{4,12},{8,16},{12,20},{16,24},{20,28},{1,9},{5,13},{9,17},{1... | collective-permute-start | bytes 995336 | tf_op jit(solution)/shard_map/ppermute | solution.py:231
  849.5 91.6 %collective-permute-start.41 = (bf16[1,288,576]{2,1,0:T(8,128)(2,1)}, bf16[1,288,576]{2,1,0:T(8,128)(2,1)}, u32[]{:S(2)}, u32[]{:S(2)}) collective-permute-start(bf16[1,288,576]{2,1,0:T(8,128)(2,1)} %get-tuple-element.79), channel_id=1, source_target_pairs={{0,8},{4,12},{8,16},{12,20},{16,24},{20,28},{1,9},{5,13},{9,17},{1... | collective-permute-start | bytes 995336 | tf_op jit(solution)/shard_map/ppermute | solution.py:231
  866.4 76.6 %collective-permute-start.58 = (bf16[1,288,576]{2,1,0:T(8,128)(2,1)}, bf16[1,288,576]{2,1,0:T(8,128)(2,1)}, u32[]{:S(2)}, u32[]{:S(2)}) collective-permute-start(bf16[1,288,576]{2,1,0:T(8,128)(2,1)} %fusion.90), channel_id=1, source_target_pairs={{8,0},{12,4},{16,8},{20,12},{24,16},{28,20},{9,1},{13,5},{17,9},{2... | collective-permute-start | bytes 995336 | tf_op jit(solution)/shard_map/ppermute | solution.py:231
  875.9 70.6 %collective-permute-start.44 = (bf16[1,288,576]{2,1,0:T(8,128)(2,1)}, bf16[1,288,576]{2,1,0:T(8,128)(2,1)}, u32[]{:S(2)}, u32[]{:S(2)}) collective-permute-start(bf16[1,288,576]{2,1,0:T(8,128)(2,1)} %fusion.102), channel_id=1, source_target_pairs={{8,0},{12,4},{16,8},{20,12},{24,16},{28,20},{9,1},{13,5},{17,9},{2... | collective-permute-start | bytes 995336 | tf_op jit(solution)/shard_map/ppermute | solution.py:231
  886.7 70.0 %collective-permute-start.86 = (bf16[1,720,576]{1,2,0:T(8,128)(2,1)S(1)}, bf16[1,720,576]{1,2,0:T(8,128)(2,1)}, u32[]{:S(2)}, u32[]{:S(2)}) collective-permute-start(bf16[1,720,576]{1,2,0:T(8,128)(2,1)S(1)} %fusion.52), channel_id=1, source_target_pairs={{8,0},{12,4},{16,8},{20,12},{24,16},{28,20},{9,1},{13,5},{17,9},{2... | collective-permute-start | bytes 2488328 | tf_op jit(solution)/shard_map/ppermute | solution.py:231
  889.1 67.6 %collective-permute-start.83 = (bf16[1,720,576]{1,2,0:T(8,128)(2,1)}, bf16[1,720,576]{1,2,0:T(8,128)(2,1)}, u32[]{:S(2)}, u32[]{:S(2)}) collective-permute-start(bf16[1,720,576]{1,2,0:T(8,128)(2,1)} %fusion.54), channel_id=1, source_target_pairs={{0,8},{4,12},{8,16},{12,20},{16,24},{20,28},{1,9},{5,13},{9,17},{1... | collective-permute-start | bytes 2488328 | tf_op jit(solution)/shard_map/ppermute | solution.py:231
  (111 other events, 1435.5 us)
Sparse Core Ops, SparseCore 0:
  48.4 48.2 all-gather.4
  139.1 48.2 all-gather.6

commit v2 on v1

v2 whole, which is shorter than its diff:
```python
import math

import jax
import jax.numpy as jnp
from jax import lax
from jax.experimental import pallas as pl
from jax.experimental.pallas import tpu as pltpu
from jax.sharding import PartitionSpec as P

HD = 64
BLK = 256
NT = (((1,), (1,)), ((), ()))

epsilon = 1e-05
branch_scale = 1.4 / math.sqrt(40.0)
low = jnp.bfloat16
full = jnp.float32

SMALL = pl.CostEstimate(flops=0, bytes_accessed=0, transcendentals=0)


def turn(field, cosine, sine):
    half = field.shape[0] // 2
    first, second = field[:half], field[half:]
    return jnp.concatenate(
        [first * cosine - second * sine, second * cosine + first * sine], axis=0
    )


def forward_kernel(
    q_here, k_here, v_here, q_there, k_there, v_there, cos_ref, sin_ref,
    out_ref, ql_ref, kl_ref, vl_ref, lse_ref,
):
    cosine, sine = cos_ref[...], sin_ref[...]
    span = cosine.shape[1]
    chip = lax.axis_index("fsdp") // 2

    def join(here, there):
        return jnp.concatenate(
            [jnp.where(chip == 0, here[0], there[0]), jnp.where(chip == 0, there[0], here[0])],
            axis=1,
        )

    q_low = turn(join(q_here, q_there), cosine, sine).astype(low)
    k_low = turn(join(k_here, k_there), cosine, sine).astype(low)
    v_low = join(v_here, v_there).astype(low)
    ql_ref[0] = q_low
    kl_ref[0] = k_low
    vl_ref[0] = v_low
    q_scaled = (q_low * (HD ** (-0.5))).astype(low)
    k_rows = k_low.T
    for j in range(span // BLK):
        kv = (j + 1) * BLK
        cols = slice(j * BLK, kv)
        scores = jnp.dot(k_rows[:kv], q_scaled[:, cols], preferred_element_type=full)
        top = jnp.max(scores, axis=0, keepdims=True)
        expo = jnp.exp(scores - top)
        total = jnp.sum(expo, axis=0, keepdims=True)
        probs = (expo * (1.0 / total)).astype(low)
        out_ref[0, :, cols] = jnp.dot(
            v_low[:, :kv], probs, preferred_element_type=full
        ).astype(low)
        lse_ref[0, :, cols] = top + jnp.log(total)


def attention_forward(here, there, cosine, sine):
    heads, _, part = here[0].shape
    span = cosine.shape[1]
    half = pl.BlockSpec((1, HD, part), lambda h: (h, 0, 0))
    spec = pl.BlockSpec((1, HD, span), lambda h: (h, 0, 0))
    table = pl.BlockSpec((HD // 2, span), lambda h: (0, 0))
    field = jax.ShapeDtypeStruct((heads, HD, span), low)
    row = pl.BlockSpec((1, 1, span), lambda h: (h, 0, 0))
    return pl.pallas_call(
        forward_kernel,
        grid=(heads,),
        in_specs=[half] * 6 + [table, table],
        out_specs=[spec, spec, spec, spec, row],
        out_shape=[field, field, field, field, jax.ShapeDtypeStruct((heads, 1, span), full)],
        compiler_params=pltpu.CompilerParams(vmem_limit_bytes=60 * 2**20),
        cost_estimate=SMALL,
        name="attention_forward",
    )(*here, *there, cosine, sine)


def backward_kernel(
    q_ref, k_ref, v_ref, g_ref, lse_ref, cos_ref, sin_ref, dq_ref, dk_ref, dv_ref, dk_acc, dv_acc
):
    cosine, sine = cos_ref[...], sin_ref[...]
    span = q_ref.shape[2]
    q_scaled = (q_ref[0] * (HD ** (-0.5))).astype(low)
    k_low, v_low, grad = k_ref[0], v_ref[0], g_ref[0]
    k_rows, v_rows = k_low.T, v_low.T
    dk_acc[...] = jnp.zeros_like(dk_acc)
    dv_acc[...] = jnp.zeros_like(dv_acc)
    for j in range(span // BLK):
        kv = (j + 1) * BLK
        cols = slice(j * BLK, kv)
        q_j, g_j = q_scaled[:, cols], grad[:, cols]
        scores = jnp.dot(k_rows[:kv], q_j, preferred_element_type=full)
        probs = jnp.exp(scores - lse_ref[0, :, cols])
        probs_low = probs.astype(low)
        d_probs = jnp.dot(v_rows[:kv], g_j, preferred_element_type=full)
        delta = jnp.sum(probs * d_probs, axis=0, keepdims=True)
        d_scores = (probs * (d_probs - delta)).astype(low)
        dq = jnp.dot(k_low[:, :kv], d_scores, preferred_element_type=full) * (HD ** (-0.5))
        dq_ref[0, :, cols] = turn(dq, cosine[:, cols], -sine[:, cols]).astype(low)
        dk_acc[:, :kv] += lax.dot_general(q_j, d_scores, NT, preferred_element_type=full)
        dv_acc[:, :kv] += lax.dot_general(g_j, probs_low, NT, preferred_element_type=full)
    dk_ref[0] = turn(dk_acc[...], cosine, -sine).astype(low)
    dv_ref[0] = dv_acc[...].astype(low)


def attention_backward(query, key, value, grad, lse, cosine, sine):
    heads, _, span = query.shape
    spec = pl.BlockSpec((1, HD, span), lambda h: (h, 0, 0))
    table = pl.BlockSpec((HD // 2, span), lambda h: (0, 0))
    row = pl.BlockSpec((1, 1, span), lambda h: (h, 0, 0))
    field = jax.ShapeDtypeStruct((heads, HD, span), low)
    return pl.pallas_call(
        backward_kernel,
        grid=(heads,),
        in_specs=[spec, spec, spec, spec, row, table, table],
        out_specs=[spec, spec, spec],
        out_shape=[field, field, field],
        scratch_shapes=[pltpu.VMEM((HD, span), full), pltpu.VMEM((HD, span), full)],
        compiler_params=pltpu.CompilerParams(vmem_limit_bytes=60 * 2**20),
        cost_estimate=SMALL,
        name="attention_backward",
    )(query, key, value, grad, lse, cosine, sine)


def swap(array, j):
    size = lax.axis_size("fsdp")
    return lax.ppermute(array, "fsdp", [(i, i ^ j) for i in range(size)])


def after(value, *earlier):
    return lax.optimization_barrier((value, *earlier))[0]


def place_kernel(*refs):
    *blocks, out, held, arrived, left = refs
    me = lax.axis_index("fsdp")
    into = [
        pltpu.make_async_copy(block, held.at[j], arrived.at[j]) for j, block in enumerate(blocks)
    ]
    back = [
        pltpu.make_async_copy(
            held.at[j], out.at[lax.bitwise_xor(me, jnp.int32(j))], left.at[j]
        )
        for j in range(len(blocks))
    ]
    for copy in into:
        copy.start()
    for copy, then in zip(into, back):
        copy.wait()
        then.start()
    for copy in back:
        copy.wait()


def place(blocks):
    count = len(blocks)
    first = blocks[0]
    whole = pl.pallas_call(
        place_kernel,
        in_specs=[pl.BlockSpec(memory_space=pl.ANY)] * count,
        out_specs=pl.BlockSpec(memory_space=pl.ANY),
        out_shape=jax.ShapeDtypeStruct((count,) + first.shape, first.dtype),
        scratch_shapes=[
            pltpu.VMEM((count,) + first.shape, first.dtype),
            pltpu.SemaphoreType.DMA((count,)),
            pltpu.SemaphoreType.DMA((count,)),
        ],
        compiler_params=pltpu.CompilerParams(vmem_limit_bytes=16 * 2**20),
        cost_estimate=SMALL,
        name="place",
    )(*blocks)
    return whole.reshape((count * first.shape[0],) + first.shape[1:])


def gather(array, *before_last):
    core = swap(array, 1)
    chip = swap(array, 2)
    return [array, core, chip, swap(after(chip, *before_last) if before_last else chip, 1)]


def bring(blocks, held, arrived, rest=None):
    me = lax.axis_index("fsdp")
    cols = held.shape[1]
    count = len(blocks)
    copies = []
    for j, block in enumerate(blocks):
        to = held.at[lax.bitwise_xor(me, jnp.int32(j))]
        if rest is None:
            copies.append(pltpu.make_async_copy(block, to, arrived.at[j]))
        else:
            copies.append(pltpu.make_async_copy(block.at[pl.ds(0, cols)], to, arrived.at[j]))
            copies.append(
                pltpu.make_async_copy(
                    block.at[pl.ds(cols, 16)], rest.at[j], arrived.at[count + j]
                )
            )
    for copy in copies:
        copy.start()
    for copy in copies:
        copy.wait()


def spread_kernel(index, *refs, count, kept, normalize):
    step = pl.program_id(0)
    blocks, gain = refs[:count], refs[count]
    outs = refs[count + 1 + kept :]
    me = index[count]
    for j, block in enumerate(blocks):

        @pl.when(step == j)
        def _():
            x = block[...].astype(full)
            cols = outs[1].shape[0]
            if normalize:
                factor = lax.rsqrt(jnp.mean(x * x, axis=-1, keepdims=True) + epsilon)
                wide = (x * factor * gain[...]).astype(low)
                outs[2][...] = wide.T
            else:
                wide = (branch_scale * x).astype(low)
            outs[0][...] = wide
            for g in range(x.shape[1] // cols):

                @pl.when(me == g)
                def _():
                    outs[1][...] = x[:, g * cols : (g + 1) * cols].T


def spread(blocks, partners, gain, normalize, earlier=None):
    rows, width = blocks[0].shape
    size = lax.axis_size("fsdp")
    count = len(blocks)
    me = lax.axis_index("fsdp")
    tokens = [me ^ j for j in partners]
    local = [block % count for block in tokens]
    index = jnp.stack([jnp.asarray(v, jnp.int32) for v in (*local, me, *tokens)])
    const = lambda shape: pl.BlockSpec(shape, lambda i, index: (0,) * len(shape))
    kept = len(earlier) if earlier else 0
    outs = [
        (
            pl.BlockSpec((rows, width), lambda i, index: (index[i], 0)),
            jax.ShapeDtypeStruct((count * rows, width), low),
        ),
        (
            pl.BlockSpec((width // size, rows), lambda i, index: (0, index[count + 1 + i])),
            jax.ShapeDtypeStruct((width // size, size * rows), full),
        ),
    ]
    if normalize:
        outs.append(
            (
                pl.BlockSpec((width, rows), lambda i, index: (0, index[count + 1 + i])),
                jax.ShapeDtypeStruct((width, size * rows), low),
            )
        )
    return pl.pallas_call(
        lambda *refs: spread_kernel(*refs, count=count, kept=kept, normalize=normalize),
        grid_spec=pltpu.PrefetchScalarGridSpec(
            num_scalar_prefetch=1,
            grid=(count,),
            in_specs=[const((rows, width))] * count
            + [const((1, width))]
            + [pl.BlockSpec(memory_space=pl.ANY)] * kept,
            out_specs=[spec for spec, _ in outs],
        ),
        out_shape=[shape for _, shape in outs],
        input_output_aliases={count + 2 + i: 1 + i for i in range(kept)},
        compiler_params=pltpu.CompilerParams(vmem_limit_bytes=32 * 2**20),
        cost_estimate=SMALL,
        name="spread",
    )(index, *blocks, gain[None, :], *(earlier or ()))


def hidden_kernel(
    own, core, chip, both, weight, tokens, gain, hidden_ref, scaled_ref, all_ref,
    squares_ref, held, arrived, left,
):
    step = pl.program_id(0)
    out = pltpu.make_async_copy(held, all_ref, left.at[0])

    @pl.when(step == 0)
    def _():
        bring((own, core, chip, both), held, arrived)
        out.start()

    span = held.shape[2]
    result = jnp.dot(
        weight[...], held[...].reshape(-1, span), preferred_element_type=full
    )
    hidden = tokens[...] + branch_scale * result
    tile = hidden.shape[0]
    at = pl.multiple_of(step * tile, tile)
    hidden_ref[pl.ds(at, tile), :] = hidden
    scaled_ref[pl.ds(at, tile), :] = (hidden * gain[...]).astype(low)
    squares = jnp.sum(hidden * hidden, axis=0, keepdims=True)

    @pl.when(step == 0)
    def _():
        squares_ref[...] = squares

    @pl.when(step != 0)
    def _():
        squares_ref[...] += squares

    @pl.when(step == pl.num_programs(0) - 1)
    def _():
        total = squares_ref[...]
        high = total.astype(low)
        rest = (total - high.astype(full)).astype(low)
        cols = hidden_ref.shape[0]
        scaled_ref[cols : cols + 8] = jnp.broadcast_to(high, (8, high.shape[1]))
        scaled_ref[cols + 8 :] = jnp.broadcast_to(rest, (8, high.shape[1]))
        out.wait()


def hidden_state(blocks, weight, tokens, gain):
    cols, span = blocks[0].shape
    size = len(blocks)
    tiles = 2
    tile = cols // tiles
    hbm = pl.BlockSpec(memory_space=pl.ANY)
    rows = lambda wide: pl.BlockSpec((tile, wide), lambda i: (i, 0))
    const = lambda shape: pl.BlockSpec(shape, lambda i: (0, 0))
    hidden, scaled, whole = pl.pallas_call(
        hidden_kernel,
        grid=(tiles,),
        in_specs=[hbm] * 4 + [rows(size * cols), rows(span), rows(1)],
        out_specs=[const((cols, span)), const((cols + 16, span)), hbm],
        out_shape=[
            jax.ShapeDtypeStruct((cols, span), full),
            jax.ShapeDtypeStruct((cols + 16, span), low),
            jax.ShapeDtypeStruct((size, cols, span), low),
        ],
        scratch_shapes=[
            pltpu.VMEM((1, span), full),
            pltpu.VMEM((size, cols, span), low),
            pltpu.SemaphoreType.DMA((size,)),
            pltpu.SemaphoreType.DMA((1,)),
        ],
        compiler_params=pltpu.CompilerParams(vmem_limit_bytes=60 * 2**20),
        cost_estimate=SMALL,
        name="hidden_state",
    )(*blocks, weight, tokens, gain)
    return hidden, scaled, whole.reshape(size * cols, span)


def inner_kernel(
    own, core, chip, both, w_gate, w_up, d_inner, inner_ref, d_gate_ref, d_up_ref, mean_ref, factor_ref,
    all_ref, held, rest, arrived, left,
):
    step = pl.program_id(0)
    out = pltpu.make_async_copy(held, all_ref, left.at[0])
    span = held.shape[2]

    @pl.when(step == 0)
    def _():
        bring((own, core, chip, both), held, arrived, rest)
        out.start()
        squares = [
            rest[j, 0:1].astype(full) + rest[j, 8:9].astype(full) for j in range(held.shape[0])
        ]
        total = (squares[0] + squares[1]) + (squares[2] + squares[3])
        factor_ref[...] = lax.rsqrt(total / (held.shape[0] * held.shape[1]) + epsilon)

        mean_ref[...] = jnp.zeros_like(mean_ref)

    wide = span // 4
    for part in range(4):
        cut = slice(part * wide, (part + 1) * wide)
        scaled = held[:, :, cut].reshape(-1, wide)
        factor = factor_ref[:, cut]
        gate = factor * jnp.dot(w_gate[...], scaled, preferred_element_type=full)
        up = factor * jnp.dot(w_up[...], scaled, preferred_element_type=full)
        sigmoid = 0.5 * jnp.tanh(0.5 * gate) + 0.5
        activated = gate * sigmoid
        inner_ref[:, cut] = (activated * up).astype(low)
        grad = factor * d_inner[:, cut].astype(full)
        d_up = grad * activated
        d_gate = grad * up * (sigmoid + activated * (1.0 - sigmoid))
        d_gate_ref[:, cut] = d_gate.astype(low)
        d_up_ref[:, cut] = d_up.astype(low)
        mean_ref[:, cut] += jnp.sum(d_gate * gate + d_up * up, axis=0, keepdims=True)

    @pl.when(step == pl.num_programs(0) - 1)
    def _():
        out.wait()


def inner_part(blocks, w_gate, w_up, d_inner):
    tall, span = blocks[0].shape
    cols = tall - 16
    size = len(blocks)
    units = w_gate.shape[0]
    tile = units // 3
    hbm = pl.BlockSpec(memory_space=pl.ANY)
    rows = lambda wide: pl.BlockSpec((tile, wide), lambda i: (i, 0))
    row = pl.BlockSpec((1, span), lambda i: (0, 0))
    field = jax.ShapeDtypeStruct((units, span), low)
    inner, d_gate, d_up, mean, factor, whole = pl.pallas_call(
        inner_kernel,
        grid=(units // tile,),
        in_specs=[hbm] * 4 + [rows(size * cols), rows(size * cols), rows(span)],
        out_specs=[rows(span), rows(span), rows(span), row, row, hbm],
        out_shape=[
            field,
            field,
            field,
            jax.ShapeDtypeStruct((1, span), full),
            jax.ShapeDtypeStruct((1, span), full),
            jax.ShapeDtypeStruct((size, cols, span), low),
        ],
        scratch_shapes=[
            pltpu.VMEM((size, cols, span), low),
            pltpu.VMEM((size, 16, span), low),
            pltpu.SemaphoreType.DMA((2 * size,)),
            pltpu.SemaphoreType.DMA((1,)),
        ],
        compiler_params=pltpu.CompilerParams(vmem_limit_bytes=60 * 2**20),
        cost_estimate=SMALL,
        name="inner_part",
    )(*blocks, w_gate, w_up, d_inner)
    return inner, d_gate, d_up, mean, factor, whole.reshape(size * cols, span)


def to_rows(field, rows):
    me = lax.axis_index("fsdp")
    size = lax.axis_size("fsdp")
    blocks = []
    for j in range(size):
        block = lax.dynamic_slice_in_dim(field, (me ^ j) * rows, rows, 1)
        blocks.append(block if j == 0 else swap(block, j))
    return place(blocks).T


def product_kernel(index, act, *refs, count, adds, turned):
    grads = refs[:count]
    added = refs[count] if adds else None
    out = refs[-1]
    rows = act[:, 0].reshape(-1, act.shape[-1])
    for k in range(count):
        pair = (grads[k][...], rows) if turned else (rows, grads[k][...])
        total = lax.dot_general(*pair, NT, preferred_element_type=full)
        if turned:
            if adds:
                total = total + added[0, k].astype(full)
            out[0, k] = total.astype(low)
            continue
        total = total.reshape((act.shape[0], act.shape[2]) + total.shape[1:])
        if adds:
            total = total + added[:, k].astype(full)
        out[:, k] = total.astype(low)


def half_product(act, grads, side, added=None, turned=False, earlier=()):
    size = lax.axis_size("rep")
    count = len(grads)
    columns, tokens = grads[0].shape
    lines, rows = size // 2, act.shape[0] // size
    index = jnp.asarray(side, jnp.int32)[None]
    if earlier:
        index = after(index, *earlier)
    steps = lines
    some = lines // steps
    shape = (columns, rows) if turned else (rows, columns)
    piece = pl.BlockSpec((some, count) + shape, lambda i, index: (i, 0, 0, 0))
    return pl.pallas_call(
        lambda *refs: product_kernel(*refs, count=count, adds=added is not None, turned=turned),
        grid_spec=pltpu.PrefetchScalarGridSpec(
            num_scalar_prefetch=1,
            grid=(steps,),
            in_specs=[pl.BlockSpec((some, 1, rows, tokens), lambda i, index: (i, index[0], 0, 0))]
            + [pl.BlockSpec((columns, tokens), lambda i, index: (0, 0))] * count
            + ([] if added is None else [piece]),
            out_specs=piece,
        ),
        out_shape=jax.ShapeDtypeStruct((lines, count) + shape, low),
        compiler_params=pltpu.CompilerParams(vmem_limit_bytes=60 * 2**20),
        cost_estimate=SMALL,
        name="half_product",
    )(index, act.reshape(lines, 2, rows, tokens), *grads, *(() if added is None else (added,)))


def whole_kernel(act, grad, out):
    out[0] = lax.dot_general(act[0], grad[...], NT, preferred_element_type=full).astype(low)


def whole_product(act, grad):
    lines = lax.axis_size("rep") // 2
    columns, tokens = grad.shape
    rows = act.shape[0] // lines
    return pl.pallas_call(
        whole_kernel,
        grid=(lines,),
        in_specs=[
            pl.BlockSpec((1, rows, tokens), lambda i: (i, 0, 0)),
            pl.BlockSpec((columns, tokens), lambda i: (0, 0)),
        ],
        out_specs=pl.BlockSpec((1, rows, columns), lambda i: (i, 0, 0)),
        out_shape=jax.ShapeDtypeStruct((lines, rows, columns), low),
        compiler_params=pltpu.CompilerParams(vmem_limit_bytes=60 * 2**20),
        cost_estimate=SMALL,
        name="whole_product",
    )(act.reshape(lines, rows, tokens), grad)


def neighbour(array):
    return lax.ppermute(array, "rep", [(i, i ^ 1) for i in range(lax.axis_size("rep"))])


def line_scatter(array):
    size = lax.axis_size("rep")
    groups = [list(range(side, size, 2)) for side in range(2)]
    return lax.psum_scatter(
        array, "rep", scatter_dimension=0, tiled=True, axis_index_groups=groups
    )


class GradSum:
    def __init__(self, act, grads, turned=False):
        self.act, self.grads, self.turned = act, grads, turned
        self.side = lax.axis_index("rep") % 2

    def send(self, earlier=()):
        sent = half_product(
            self.act, self.grads, 1 - self.side, turned=self.turned, earlier=earlier
        )
        self.arrived = neighbour(sent)
        return sent

    def keep(self, earlier=(), last=None):
        kept = half_product(
            self.act, self.grads, self.side, self.arrived, turned=self.turned, earlier=earlier
        )
        self.sums = line_scatter(kept if last is None else after(kept, last.sums))
        return kept

    def line_first(self, earlier=()):
        whole = whole_product(self.act, after(self.grads[0], *earlier))
        self.sums = line_scatter(whole)
        return whole

    def sides_last(self, earlier=()):
        _, rows, columns = self.sums.shape
        parts = self.sums.reshape(2, rows // 2, columns)
        side = after(self.side, *earlier)
        sent = lax.dynamic_index_in_dim(parts, 1 - side, 0, False)
        kept = lax.dynamic_index_in_dim(parts, side, 0, False)
        return kept.astype(full) + neighbour(sent).astype(full)

    def result(self):
        return [self.sums[0, k].astype(full) for k in range(len(self.grads))]


def sum_everywhere(array):
    array = (array + swap(array, 1)) + (swap(array, 2) + swap(array, 3))
    size = lax.axis_size("rep")
    far = 1
    while far < size:
        array = array + lax.ppermute(array, "rep", [(i, i ^ far) for i in range(size)])
        far *= 2
    return array


def flip_kernel(*refs):
    count = len(refs) // 2
    for wide, tall in zip(refs[:count], refs[count:]):
        tall[...] = wide[...].T


def flip(arrays, tiles, earlier=()):
    width = arrays[0].shape[1]
    tile = width // tiles
    index = jnp.zeros((1,), jnp.int32)
    if earlier:
        index = after(index, *earlier)
    return pl.pallas_call(
        lambda index, *refs: flip_kernel(*refs),
        grid_spec=pltpu.PrefetchScalarGridSpec(
            num_scalar_prefetch=1,
            grid=(tiles,),
            in_specs=[pl.BlockSpec((a.shape[0], tile), lambda i, index: (0, i)) for a in arrays],
            out_specs=[pl.BlockSpec((tile, a.shape[0]), lambda i, index: (i, 0)) for a in arrays],
        ),
        out_shape=[jax.ShapeDtypeStruct((width, a.shape[0]), a.dtype) for a in arrays],
        compiler_params=pltpu.CompilerParams(vmem_limit_bytes=60 * 2**20),
        cost_estimate=SMALL,
        name="flip",
    )(index, *arrays)


def chunks_kernel(index, *refs, count, ways, added, extra):
    step = pl.program_id(0)
    weights, refs = refs[:count], refs[count:]
    grads, refs = refs[:count], refs[count:]
    plus, refs = refs[:added], refs[added:]
    row, outs = refs[:extra], refs[extra:]
    total = None
    for weight, grad in zip(weights, grads):
        term = jnp.dot(weight[...], grad[...], preferred_element_type=full)
        total = term if total is None else total + term
    cols = total.shape[0]
    for way, out in enumerate(outs):

        @pl.when(step == way)
        def _():
            found = total + plus[way][:cols].astype(full) if plus else total
            out[:cols] = found.astype(out.dtype)
            if row:
                found = row[0][...]
                if plus:
                    found = found + plus[way][cols : cols + 1].astype(full)
                out[cols:] = jnp.broadcast_to(
                    found.astype(out.dtype), (out.shape[0] - cols, found.shape[1])
                )


def feature_chunks(weights, grads, partners, plus=(), extra=None, dtype=low, earlier=()):
    me = lax.axis_index("fsdp")
    span = grads[0].shape[1]
    cols = weights[0].shape[0] // lax.axis_size("fsdp")
    tall = cols + (0 if extra is None else 16)
    index = jnp.stack([jnp.asarray(me ^ j, jnp.int32) for j in partners])
    if earlier:
        index = after(index, *earlier)
    extra = () if extra is None else (extra,)
    const = lambda shape: pl.BlockSpec(shape, lambda i, index: (0, 0))
    return pl.pallas_call(
        lambda *refs: chunks_kernel(
            *refs, count=len(weights), ways=len(partners), added=len(plus), extra=len(extra)
        ),
        grid_spec=pltpu.PrefetchScalarGridSpec(
            num_scalar_prefetch=1,
            grid=(len(partners),),
            in_specs=[
                pl.BlockSpec((cols, w.shape[1]), lambda i, index: (index[i], 0)) for w in weights
            ]
            + [const(a.shape) for a in (*grads, *plus, *extra)],
            out_specs=[const((tall, span))] * len(partners),
        ),
        out_shape=[jax.ShapeDtypeStruct((tall, span), dtype)] * len(partners),
        compiler_params=pltpu.CompilerParams(vmem_limit_bytes=60 * 2**20),
        cost_estimate=SMALL,
        name="feature_chunks",
    )(index, *weights, *grads, *plus, *extra)


def blocks_kernel(index, *refs, count, added):
    step = pl.program_id(0)
    weights, refs = refs[:count], refs[count:]
    grads, refs = refs[:count], refs[count:]
    plus, outs = refs[:added], refs[added:]
    total = None
    for weight, grad in zip(weights, grads):
        term = jnp.dot(grad[...].T, weight[...], preferred_element_type=full)
        total = term if total is None else total + term
    for way, out in enumerate(outs):

        @pl.when(step == way)
        def _():
            found = total + plus[way][...].astype(full) if plus else total
            out[...] = found.astype(out.dtype)


def token_chunks(weights, grads, partners, rows, plus=(), dtype=low, earlier=()):
    me = lax.axis_index("fsdp")
    width = weights[0].shape[1]
    index = jnp.stack([jnp.asarray(me ^ j, jnp.int32) for j in partners])
    if earlier:
        index = after(index, *earlier)
    const = lambda shape: pl.BlockSpec(shape, lambda i, index: (0, 0))
    return pl.pallas_call(
        lambda *refs: blocks_kernel(*refs, count=len(weights), added=len(plus)),
        grid_spec=pltpu.PrefetchScalarGridSpec(
            num_scalar_prefetch=1,
            grid=(len(partners),),
            in_specs=[const(w.shape) for w in weights]
            + [pl.BlockSpec((g.shape[0], rows), lambda i, index: (0, index[i])) for g in grads]
            + [const(a.shape) for a in plus],
            out_specs=[const((rows, width))] * len(partners),
        ),
        out_shape=[jax.ShapeDtypeStruct((rows, width), dtype)] * len(partners),
        compiler_params=pltpu.CompilerParams(vmem_limit_bytes=60 * 2**20),
        cost_estimate=SMALL,
        name="token_chunks",
    )(index, *weights, *grads, *plus)


def body(
    tokens, cotangent, gain_attn, gain_ffn, w_query, w_key, w_value, w_out, w_gate, w_up, w_down
):
    rows, width = tokens.shape
    size = lax.axis_size("fsdp")
    reps = lax.axis_size("rep")
    span = rows * size
    me = lax.axis_index("fsdp")
    replica = lax.axis_index("rep")
    width_cols = width // size
    hidden_cols = w_gate.shape[1]
    heads = width_cols // HD

    half = HD // 2
    frequency = 10000.0 ** (-(jnp.arange(half, dtype=full) * 2.0 / HD))
    angles = frequency[:, None] * jnp.arange(span, dtype=jnp.int32).astype(full)[None, :]
    cosine, sine = jnp.cos(angles), jnp.sin(angles)

    def own_gain(gain):
        return lax.dynamic_slice_in_dim(gain, me * width_cols, width_cols, 0)[:, None]

    down_turned = w_down.T
    share = width_cols // reps

    def down_part(j):
        return lax.dynamic_slice(
            down_turned, (replica * share, (me ^ j) * hidden_cols), (share, hidden_cols)
        )

    parts = [down_part(2), down_part(3)]

    def project(normed):
        found = []
        for weight in (w_query, w_key, w_value):
            field = jnp.einsum("de,td->et", weight, normed, preferred_element_type=full)
            found.append(field.reshape(heads, HD, normed.shape[0]))
        return found

    tokens_chip = swap(tokens, 2)
    normed_here, tokens_part, normed_part = spread(
        [tokens, swap(tokens, 1)], (0, 1), gain_attn, True
    )
    here = project(normed_here)
    tokens_chip = after(tokens_chip, *here)
    parts = [swap(after(part, tokens_chip), 2) for part in parts]
    normed_there, tokens_own, normed_turned = spread(
        [tokens_chip, swap(tokens_chip, 1)],
        (2, 3),
        gain_attn,
        True,
        (tokens_part, normed_part),
    )
    there = project(normed_there)
    parts = [after(part, *there) for part in parts]
    cotangent_chip = swap(after(cotangent, *parts), 2)
    parts_all = lax.all_gather(
        jnp.stack([parts[0], swap(parts[1], 1)]), "rep", axis=1, tiled=True
    )
    attended, query_low, key_low, value_low, lse = attention_forward(here, there, cosine, sine)

    cotangent_blocks = [
        cotangent, swap(cotangent, 1), cotangent_chip, swap(after(cotangent_chip, attended), 1)
    ]
    d_ffn, cotangent_own = spread(cotangent_blocks, (0, 1, 2, 3), gain_attn, False)
    d_ffn_own = (branch_scale * cotangent_own).astype(low)
    me_later = after(me, d_ffn)

    def down_block(j):
        return lax.dynamic_slice_in_dim(
            down_turned, (me_later ^ j) * hidden_cols, hidden_cols, 1
        )

    down_near = [down_block(0), swap(down_block(1), 1)]
    gate_tall, up_tall = flip([w_gate.T, w_up.T], 6, [down_near[0]])
    (out_tall,) = flip([w_out.T], 6, [gate_tall])
    attended_blocks = gather(attended.reshape(width_cols, span), out_tall)

    gain_own = own_gain(gain_ffn)
    hidden, scaled, attended_all = hidden_state(attended_blocks, w_out.T, tokens_own, gain_own)
    down_own = place([after(down_near[0], scaled), down_near[1], parts_all[0], parts_all[1]])
    d_inner = jnp.einsum("ef,te->ft", down_own, d_ffn, preferred_element_type=full).astype(low)
    scaled_blocks = gather(scaled, d_inner)

    inner, d_gate, d_up, mean, factor, scaled_all = inner_part(
        scaled_blocks, w_gate.T, w_up.T, d_inner
    )

    sum_up = GradSum(scaled_all, [d_up])
    sum_gate = GradSum(scaled_all, [d_gate])
    ffn_weights, ffn_grads = (gate_tall, up_tall), (d_gate, d_up)
    token = sum_up.line_first()
    far, near = feature_chunks(ffn_weights, ffn_grads, (3, 1), extra=mean, earlier=[token])
    token = sum_gate.send([far])
    far, near = swap(far, 1), swap(near, 1)
    (chunk,) = feature_chunks(
        ffn_weights, ffn_grads, (2,), plus=[far], extra=mean, earlier=[token]
    )
    across = swap(chunk, 2)
    (own,) = feature_chunks(
        ffn_weights, ffn_grads, (0,), plus=[near], extra=mean, dtype=full, earlier=[chunk]
    )
    d_scaled = own + across.astype(full)
    mean_ffn = d_scaled[width_cols : width_cols + 1] / width
    d_scaled = d_scaled[:width_cols]
    gain_ffn_term = jnp.sum(d_scaled * hidden, axis=1)
    d_hidden = cotangent_own + gain_own * d_scaled - hidden * (factor * mean_ffn)
    d_attn = (branch_scale * d_hidden).astype(low)

    far, near = feature_chunks([out_tall], [d_attn], (3, 1))
    far, near = swap(far, 1), swap(near, 1)
    (chunk,) = feature_chunks([out_tall], [d_attn], (2,), plus=[far])
    across = swap(chunk, 2)
    (own,) = feature_chunks(
        [out_tall], [d_attn], (0,), plus=[near], dtype=full, earlier=[chunk]
    )
    sum_out = GradSum(attended_all, [d_attn])
    token = sum_out.send([own])
    d_attended = own + after(across, token).astype(full)
    d_attended = d_attended.astype(low).reshape(heads, HD, span)
    inner_chip = swap(after(inner, d_attended), 2)
    token = sum_gate.keep([d_attended], sum_up)

    d_query, d_key, d_value = (
        field.reshape(width_cols, span)
        for field in attention_backward(
            query_low, key_low, value_low, d_attended, after(lse, token), cosine, sine
        )
    )
    attn_weights, attn_grads = (w_query.T, w_key.T, w_value.T), (d_query, d_key, d_value)
    far, near = token_chunks(attn_weights, attn_grads, (3, 1), rows)
    sum_attn = GradSum(normed_turned, [d_query, d_key, d_value])
    token = sum_attn.send([far])
    far, near = swap(far, 1), swap(near, 1)
    (chunk,) = token_chunks(attn_weights, attn_grads, (2,), rows, plus=[far], earlier=[token])
    across = swap(chunk, 2)
    (own,) = token_chunks(
        attn_weights, attn_grads, (0,), rows, plus=[near], dtype=full, earlier=[chunk]
    )
    token = sum_out.keep([own], sum_gate)

    inner_both = swap(after(inner_chip, token), 1)
    inner_all = place([inner, swap(inner, 1), inner_chip, inner_both])
    sum_down = GradSum(inner_all, [d_ffn_own], turned=True)
    token = sum_down.send()
    ffn_result = jnp.einsum(
        "fe,ft->et", w_down, after(inner_all, token), preferred_element_type=full
    )
    output_turned = (hidden + branch_scale * ffn_result).astype(low)
    output = to_rows(output_turned, rows)
    hidden_rows = to_rows(after(d_hidden.astype(low), output_turned), rows).astype(full)

    d_normed = own + after(across, output_turned).astype(full)
    x_own = tokens.astype(full)
    factor_own = lax.rsqrt(jnp.mean(x_own * x_own, axis=-1, keepdims=True) + epsilon)
    unit_own = x_own * factor_own
    part = d_normed * gain_attn
    gain_attn_term = jnp.sum(d_normed * unit_own, axis=0)
    gain_ffn_wide = lax.dynamic_update_slice_in_dim(
        jnp.zeros((width,), full), gain_ffn_term, me * width_cols, 0
    )
    d_tokens = hidden_rows + factor_own * (
        part - unit_own * jnp.mean(part * unit_own, axis=-1, keepdims=True)
    )
    grad_up = sum_up.sides_last([output_turned])
    token = sum_attn.keep([gain_attn_term], sum_out)
    grad_gain_attn, grad_gain_ffn = sum_everywhere(
        jnp.stack([after(gain_attn_term, token), gain_ffn_wide])
    )
    token = sum_down.keep([token, d_tokens], sum_attn)
    grad_query, grad_key, grad_value = sum_attn.result()
    (grad_out,) = sum_out.result()
    (grad_gate,) = sum_gate.result()
    (grad_down,) = sum_down.result()
    return (
        output,
        d_tokens,
        grad_gain_attn,
        grad_gain_ffn,
        grad_query,
        grad_key,
        grad_value,
        grad_out,
        grad_gate,
        grad_up,
        grad_down.T,
    )


def solution(mesh):
    rows = P(("rep", "fsdp"), None)
    columns = P(None, "fsdp")
    both = P("rep", "fsdp")
    return jax.shard_map(
        body,
        mesh=mesh,
        in_specs=(rows, rows, P(), P()) + (columns,) * 7,
        out_specs=(rows, rows, P(), P()) + (both,) * 7,
        check_vma=False,
    )
```

time: 978 us -> 683 us (0.70)
  Pallas kernels: 68.8 us -> 271 us
  matrix products: 199 us -> 42 us
  starting transfers between devices: 156 us -> 35.3 us
  local copies, waits for them, and re-layouts: 141 us -> 42.9 us
  blocking collectives: 41 us -> 0 us
  waiting for transfers between devices: 280 us -> 239 us
  other arithmetic: 64.5 us -> 29.7 us
    pallas_call x1 -> x26, Pallas kernels: 22.9 us -> 235 us  [the longest x8 63.7 us: half_product(): pl.pallas_call(lambda *refs: product_kernel(*refs, count=count, adds=adde...]
    dot_general x42 -> x1, matrix products: 176 us -> 13.3 us  [body(): jnp.einsum('fe,ft->et', w_down, after(inner_all, token), preferred_elemen...]
    ppermute x49 -> x8, starting transfers between devices: 134 us -> 9.22 us  [the longest x3 4.84 us: sum_everywhere(): lax.ppermute(array, 'rep', [(i, i ^ far) for i in range(size)])]
    ppermute x49 -> x8, waiting for transfers between devices: 188 us -> 142 us  [the longest x5 114 us: neighbour(): lax.ppermute(array, 'rep', [(i, i ^ 1) for i in range(lax.axis_size('rep'...]
    psum x1 -> x0, blocking collectives: 41 us -> none  [body(): lax.psum((gain_attn_term, gain_ffn_wide), ('rep', 'fsdp'))]
    dynamic_slice x8 -> x2, local copies, waits for them, and re-layouts: 47.2 us -> 6.35 us  [the longest x1 5.07 us: down_block(): lax.dynamic_slice_in_dim(down_turned, (me_later ^ j) * hidden_cols, hidde...]
    convert_element_type x26 -> x6, other arithmetic: 39.7 us -> 8.89 us  [the longest x3 3.72 us: result(): return [self.sums[0, k].astype(full) for k in range(len(self.grads))]]
    convert_element_type x7 -> x1, local copies, waits for them, and re-layouts: 24.9 us -> 3.11 us  [body(): to_rows(after(d_hidden.astype(low), output_turned), rows).astype(full)]
  transfers between devices with their start and end apart: 89 -> 51, of which waited for: 24 -> 21; matrix products, arithmetic and copies ran while one was open for 37% -> 13% of each run, Pallas kernels for 7% -> 35%
where the time goes in v2:
time: 683 us; the launch traced here: 675 us
  Pallas kernels  271 us (40%)
  waiting for transfers between devices  239 us (35%)
  local copies, waits for them, and re-layouts  42.9 us (6%)
  matrix products  42 us (6%)
  starting transfers between devices  35.3 us (5%)
  other arithmetic  29.7 us (4%)
  between operations  15 us (2%)
    ppermute x5, waiting for transfers between devices, neighbour(): lax.ppermute(array, 'rep', [(i, i ^ 1) for i in range(lax.axis_size('rep'...  114 us
    ppermute x37, waiting for transfers between devices, swap(): return lax.ppermute(array, 'fsdp', [(i, i ^ j) for i in range(size)])  77.9 us
    pallas_call x8, Pallas kernels, half_product(): pl.pallas_call(lambda *refs: product_kernel(*refs, count=count, adds=adde...  63.7 us
    pallas_call x6, Pallas kernels, feature_chunks(): pl.pallas_call(lambda *refs: chunks_kernel(*refs, count=len(weights), way...  46.7 us
    pallas_call x3, Pallas kernels, token_chunks(): pl.pallas_call(lambda *refs: blocks_kernel(*refs, count=len(weights), add...  28.1 us
    ppermute x3, waiting for transfers between devices, sum_everywhere(): lax.ppermute(array, 'rep', [(i, i ^ far) for i in range(size)])  27.9 us
    pallas_call x1, Pallas kernels, attention_backward(): pl.pallas_call(backward_kernel, grid=(heads,), in_specs=[spec, spec, spec...  26.7 us
    ppermute x37, starting transfers between devices, swap(): return lax.ppermute(array, 'fsdp', [(i, i ^ j) for i in range(size)])  25.9 us
  transfers between devices with their start and end apart: 51, of which 21 were waited for; matrix products, arithmetic and copies ran while one was open for 13% of the time, Pallas kernels for 35%

profile of v2, /device:TPU:0, one launch (start us, length us, event | category | flops | bytes accessed | tf_op | source)
XLA Modules:
  0.0 674.8 jit_solution(1280153160949476333)
XLA Ops:
  7.7 2.6 collective-permute-start.1
  14.7 2.7 spread.3
  17.4 6.1 fusion.17
  23.5 2.6 fusion.16
  26.0 2.6 fusion.15
  28.6 8.5 %collective-permute-done.1.refs_1_ = bf16[256,2304]{1,0:T(8,128)(2,1)S(1)} collective-permute-done((bf16[256,2304]{1,0:T(8,128)(2,1)}, bf16[256,2304]{1,0:T(8,128)(2,1)S(1)}, u32[]{:S(2)}, u32[]{:S(2)}) %collective-permute-start.1) | collective-permute-done | bytes 1179680 | tf_op jit(solution)/shard_map/ppermute | solution.py:135
  40.5 2.3 copy-done.2
  42.9 4.4 spread.4
  47.3 2.6 fusion.20
  51.1 2.6 fusion.19
  53.6 2.6 fusion.18
  61.7 23.2 %attention_forward.1 = (bf16[9,64,1024]{2,1,0:T(8,128)(2,1)}, bf16[9,64,1024]{2,1,0:T(8,128)(2,1)}, bf16[9,64,1024]{2,1,0:T(8,128)(2,1)}, bf16[9,64,1024]{2,1,0:T(8,128)(2,1)}, f32[9,1,1024]{2,1,0:T(1,128)}) custom-call(f32[9,64,512]{2,1,0:T(8,128)} %bitcast.174, f32[9,64,512]{2,1,0:T(8,128)} %bitcast.173, f32[9,64,512]{2,1,0:T(8,128)} %bitcast.172, ...), custom_call_target="tpu_custom_call" | custom-call | tf_op jit(solution)/shard_map/attention_forward/pallas_call | solution.py:74
  89.8 3.9 spread.5
  97.1 5.1 dynamic-slice_bitcast_fusion
  102.2 11.5 %flip.2 = (bf16[2304,1440]{1,0:T(8,128)(2,1)}, bf16[2304,1440]{1,0:T(8,128)(2,1)}) custom-call(s32[1]{0:T(128)} %constant.100.clone.1.index, bf16[1440,2304]{1,0:T(8,128)(2,1)} %bitcast.149, bf16[1440,2304]{1,0:T(8,128)(2,1)} %bitcast.151), custom_call_target="tpu_custom_call" | custom-call | tf_op jit(solution)/shard_map/flip/pallas_call | solution.py:583
  113.7 5.6 flip.3.refs_1_
  122.8 9.6 %hidden_state.1 = (f32[576,1024]{1,0:T(8,128)}, bf16[592,1024]{1,0:T(8,128)(2,1)}, bf16[4,576,1024]{2,1,0:T(8,128)(2,1)}) custom-call(bf16[576,1024]{1,0:T(8,128)(2,1)} %bitcast.171, bf16[576,1024]{1,0:T(8,128)(2,1)} %collective-permute-done.3.core, bf16[576,1024]{1,0:T(8,128)(2,1)} %collective-permute-done.4.chip, ...), custom_call_target="tpu_custom_call" | custom-call | tf_op jit(solution)/shard_map/hidden_state/pallas_call | solution.py:331
  132.4 2.4 collective-permute-start.12
  134.9 2.4 slice_bitcast_fusion
  137.3 3.0 place.4
  140.3 9.7 %convolution_convert_fusion.d_inner = bf16[1440,1024]{1,0:T(8,128)(2,1)} fusion(bf16[2304,1440]{1,0:T(8,128)(2,1)S(1)} %bitcast.128, bf16[1024,2304]{1,0:T(8,128)(2,1)S(1)} %bitcast.131), kind=kOutput, calls=%fused_computation | convolution fusion | flops 6796247040 | bytes 14303232 | tf_op jit(solution)/shard_map/ef,te->ft/dot_general | solution.py:775
  150.0 12.3 %collective-permute-done.12.chip = bf16[592,1024]{1,0:T(8,128)(2,1)} collective-permute-done((bf16[592,1024]{1,0:T(8,128)(2,1)}, bf16[592,1024]{1,0:T(8,128)(2,1)}, u32[]{:S(2)}, u32[]{:S(2)}) %collective-permute-start.12) | collective-permute-done | bytes 1212448 | tf_op jit(solution)/shard_map/ppermute | solution.py:135
  162.3 3.1 collective-permute-done.15.both
  166.4 24.5 %inner_part.1 = (bf16[1440,1024]{1,0:T(8,128)(2,1)}, bf16[1440,1024]{1,0:T(8,128)(2,1)}, bf16[1440,1024]{1,0:T(8,128)(2,1)}, f32[1,1024]{1,0:T(1,128)}, f32[1,10...) custom-call(bf16[592,1024]{1,0:T(8,128)(2,1)} %get-tuple-element.103.own, bf16[592,1024]{1,0:T(8,128)(2,1)} %collective-permute-done.11.core, ...), custom_call_target="tpu_custom_call" | custom-call | tf_op jit(solution)/shard_map/inner_part/pallas_call | solution.py:406
  190.9 11.6 %whole_product.1 = bf16[4,576,1440]{2,1,0:T(8,128)(2,1)} custom-call(bf16[4,576,1024]{2,1,0:T(8,128)(2,1)} %get-tuple-element.108.act, bf16[1440,1024]{1,0:T(8,128)(2,1)} %get-tuple-element.109.grad.refs_4_), custom_call_target="tpu_custom_call" | custom-call | tf_op jit(solution)/shard_map/whole_product/pallas_call | solution.py:498
  203.2 13.9 %feature_chunks.6 = (bf16[592,1024]{1,0:T(8,128)(2,1)}, bf16[592,1024]{1,0:T(8,128)(2,1)}) custom-call(s32[2]{0:T(128)} %pad_add_fusion.refs_0_, bf16[2304,1440]{1,0:T(8,128)(2,1)} %get-tuple-element.98.refs_1_, bf16[2304,1440]{1,0:T(8,128)(2,1)} %get-tuple-element.111.refs_2_, bf16[1440,1024]{1,0:T(8,128)(2,1)} %get-tuple-element.112.refs_3_.refs_2_, ...), custom_call_target="tpu_custom_call" | custom-call | tf_op jit(solution)/shard_map/feature_chunks/pallas_call | solution.py:634
  217.6 7.8 %half_product.8 = bf16[4,1,288,1440]{3,2,1,0:T(8,128)(2,1)} custom-call(s32[1]{0:T(128)} %bitcast.43.refs_0_, bf16[4,2,288,1024]{3,2,1,0:T(8,128)(2,1)} %bitcast.132, bf16[1440,1024]{1,0:T(8,128)(2,1)} %get-tuple-element.112.refs_3_.refs_2_), custom_call_target="tpu_custom_call" | custom-call | tf_op jit(solution)/shard_map/half_product/pallas_call | solution.py:473
  226.5 8.9 %feature_chunks.7 = bf16[592,1024]{1,0:T(8,128)(2,1)} custom-call(s32[1]{0:T(128)} %bitcast.12.refs_0_, bf16[2304,1440]{1,0:T(8,128)(2,1)} %get-tuple-element.98.refs_1_, bf16[2304,1440]{1,0:T(8,128)(2,1)} %get-tuple-element.111.refs_2_, bf16[1440,1024]{1,0:T(8,128)(2,1)} %get-tuple-element.112.refs_3_.refs_2_, ...), custom_call_target="tpu_custom_call" | custom-call | tf_op jit(solution)/shard_map/feature_chunks/pallas_call | solution.py:634
  239.7 9.4 %feature_chunks.8 = f32[592,1024]{1,0:T(8,128)} custom-call(s32[1]{0:T(128)} %bitcast.2.refs_0_, bf16[2304,1440]{1,0:T(8,128)(2,1)} %get-tuple-element.98.refs_1_, bf16[2304,1440]{1,0:T(8,128)(2,1)} %get-tuple-element.111.refs_2_, bf16[1440,1024]{1,0:T(8,128)(2,1)} %get-tuple-element.112.refs_3_.refs_2_, bf16[1440,1024]{1,0:T(8,128)(2,1)} %get-tuple-element.109.grad.refs_4_, ...), custom_call_target="tpu_custom_call" | custom-call | tf_op jit(solution)/shard_map/feature_chunks/pallas_call | solution.py:634
  249.2 15.2 %collective-permute-done.19 = bf16[592,1024]{1,0:T(8,128)(2,1)S(1)} collective-permute-done((bf16[592,1024]{1,0:T(8,128)(2,1)}, bf16[592,1024]{1,0:T(8,128)(2,1)S(1)}, u32[]{:S(2)}, u32[]{:S(2)}) %collective-permute-start.19) | collective-permute-done | bytes 1212448 | tf_op jit(solution)/shard_map/ppermute | solution.py:135
  269.8 6.0 feature_chunks.9
  276.3 2.5 collective-permute-done.20.refs_3_
  279.9 3.9 feature_chunks.10
  286.6 4.5 feature_chunks.11
  291.1 5.6 half_product.9
  296.7 15.4 %collective-permute-done.22 = bf16[576,1024]{1,0:T(8,128)(2,1)S(1)} collective-permute-done((bf16[576,1024]{1,0:T(8,128)(2,1)}, bf16[576,1024]{1,0:T(8,128)(2,1)S(1)}, u32[]{:S(2)}, u32[]{:S(2)}) %collective-permute-start.22) | collective-permute-done | bytes 1179680 | tf_op jit(solution)/shard_map/ppermute | solution.py:135
  315.8 8.4 %half_product.10 = bf16[4,1,288,1440]{3,2,1,0:T(8,128)(2,1)} custom-call(s32[1]{0:T(128)} %bitcast.48.refs_0_, bf16[4,2,288,1024]{3,2,1,0:T(8,128)(2,1)} %bitcast.133, bf16[1440,1024]{1,0:T(8,128)(2,1)} %get-tuple-element.112.refs_3_.refs_2_, bf16[4,1,288,1440]{3,2,1,0:T(8,128)(2,1)} %collective-permute-done.24.refs_3_), custom_call_target="tpu_custom_call" | custom-call | tf_op jit(solution)/shard_map/half_product/pallas_call | solution.py:473
  324.1 3.8 reduce-scatter.6.cloned.1.call-done
  331.0 26.7 %attention_backward.1 = (bf16[9,64,1024]{2,1,0:T(8,128)(2,1)}, bf16[9,64,1024]{2,1,0:T(8,128)(2,1)}, bf16[9,64,1024]{2,1,0:T(8,128)(2,1)}) custom-call(bf16[9,64,1024]{2,1,0:T(8,128)(2,1)} %get-tuple-element.127.q_ref, bf16[9,64,1024]{2,1,0:T(8,128)(2,1)} %get-tuple-element.128.k_ref, bf16[9,64,1024]{2,1,0:T(8,128)(2,1)} %get-tuple-element.129.v_ref, ...), custom_call_target="tpu_custom_call" | custom-call | tf_op jit(solution)/shard_map/attention_backward/pallas_call | solution.py:120
  357.7 11.9 %token_chunks.3 = (bf16[256,2304]{1,0:T(8,128)(2,1)}, bf16[256,2304]{1,0:T(8,128)(2,1)}) custom-call(s32[2]{0:T(128)} %pad_add_fusion.refs_0_, bf16[576,2304]{1,0:T(8,128)(2,1)} %bitcast.153, bf16[576,2304]{1,0:T(8,128)(2,1)} %bitcast.156, bf16[576,2304]{1,0:T(8,128)(2,1)} %bitcast.159, bf16[576,1024]{1,0:T(8,128)(2,1)} %bitcast.134, ...), custom_call_target="tpu_custom_call" | custom-call | tf_op jit(solution)/shard_map/token_chunks/pallas_call | solution.py:678
  370.1 9.6 %half_product.11 = bf16[4,3,288,576]{3,2,1,0:T(8,128)(2,1)} custom-call(s32[1]{0:T(128)} %bitcast.43.refs_0_, bf16[4,2,288,1024]{3,2,1,0:T(8,128)(2,1)} %bitcast.126, bf16[576,1024]{1,0:T(8,128)(2,1)} %bitcast.135, bf16[576,1024]{1,0:T(8,128)(2,1)} %bitcast.140, bf16[576,1024]{1,0:T(8,128)(2,1)} %bitcast.145), custom_call_target="tpu_custom_call" | custom-call | tf_op jit(solution)/shard_map/half_product/pallas_call | solution.py:473
  379.8 7.9 %token_chunks.4 = bf16[256,2304]{1,0:T(8,128)(2,1)} custom-call(s32[1]{0:T(128)} %bitcast.12.refs_0_, bf16[576,2304]{1,0:T(8,128)(2,1)} %bitcast.154, bf16[576,2304]{1,0:T(8,128)(2,1)} %bitcast.157, bf16[576,2304]{1,0:T(8,128)(2,1)} %bitcast.160, bf16[576,1024]{1,0:T(8,128)(2,1)} %bitcast.136, bf16[576,1024]{1,0:T(8,128)(2,1)} %bitcast.141, ...), custom_call_target="tpu_custom_call" | custom-call | tf_op jit(solution)/shard_map/token_chunks/pallas_call | solution.py:678
  388.7 8.2 %token_chunks.5 = f32[256,2304]{1,0:T(8,128)} custom-call(s32[1]{0:T(128)} %bitcast.2.refs_0_, bf16[576,2304]{1,0:T(8,128)(2,1)} %bitcast.155, bf16[576,2304]{1,0:T(8,128)(2,1)} %bitcast.158, bf16[576,2304]{1,0:T(8,128)(2,1)} %bitcast.161, bf16[576,1024]{1,0:T(8,128)(2,1)} %bitcast.137, bf16[576,1024]{1,0:T(8,128)(2,1)} %bitcast.142, ...), custom_call_target="tpu_custom_call" | custom-call | tf_op jit(solution)/shard_map/token_chunks/pallas_call | solution.py:678
  398.1 5.7 half_product.12
  405.7 3.9 collective-permute-done.28.refs_3_
  409.7 5.0 place.5
  414.7 4.3 copy-done
  419.0 7.8 %half_product.13 = bf16[4,1,576,720]{3,2,1,0:T(8,128)(2,1)} custom-call(s32[1]{0:T(128)} %bitcast.43.refs_0_, bf16[4,2,720,1024]{3,2,1,0:T(8,128)(2,1)} %bitcast.123, bf16[576,1024]{1,0:T(8,128)(2,1)} %get-tuple-element.168.refs_2_), custom_call_target="tpu_custom_call" | custom-call | tf_op jit(solution)/shard_map/half_product/pallas_call | solution.py:473
  426.9 13.3 %fusion.9 = bf16[576,1024]{1,0:T(8,128)(2,1)} fusion(f32[576,1024]{1,0:T(8,128)} %get-tuple-element.102, bf16[5760,576]{0,1:T(8,128)(2,1)} %param.21, bf16[5760,1024]{1,0:T(8,128)(2,1)} %bitcast.124), kind=kOutput, calls=%fused_computation.14 | convolution fusion | flops 6796541952 | bytes 21970944 | tf_op jit(solution)/shard_map/fe,ft->et/dot_general | solution.py:839
  440.2 2.8 fusion.7
  443.0 59.1 %collective-permute-done.36.refs_5_ = bf16[4,3,288,576]{3,2,1,0:T(8,128)(2,1)} collective-permute-done((bf16[4,3,288,576]{3,2,1,0:T(8,128)(2,1)}, bf16[4,3,288,576]{3,2,1,0:T(8,128)(2,1)}, u32[]{:S(2)}, u32[]{:S(2)}) %collective-permute-start.36) | collective-permute-done | bytes 3981344 | tf_op jit(solution)/shard_map/ppermute | solution.py:514
  502.1 10.2 %half_product.14 = bf16[4,3,288,576]{3,2,1,0:T(8,128)(2,1)} custom-call(s32[1]{0:T(128)} %bitcast.48.refs_0_, bf16[4,2,288,1024]{3,2,1,0:T(8,128)(2,1)} %bitcast.127, bf16[576,1024]{1,0:T(8,128)(2,1)} %bitcast.138, bf16[576,1024]{1,0:T(8,128)(2,1)} %bitcast.143, bf16[576,1024]{1,0:T(8,128)(2,1)} %bitcast.148, ...), custom_call_target="tpu_custom_call" | custom-call | tf_op jit(solution)/shard_map/half_product/pallas_call | solution.py:473
  516.7 6.9 %collective-permute-done.34.refs_3_ = bf16[576,256]{1,0:T(8,128)(2,1)S(1)} collective-permute-done((bf16[576,256]{1,0:T(8,128)(2,1)S(1)}, bf16[576,256]{1,0:T(8,128)(2,1)S(1)}, u32[]{:S(2)}, u32[]{:S(2)}) %collective-permute-start.34) | collective-permute-done | bytes 294944 | tf_op jit(solution)/shard_map/ppermute | solution.py:135
  523.6 4.6 collective-permute-done.33.refs_2_
  530.4 3.1 copy.28
  533.6 4.2 fusion.6
  537.7 52.7 %collective-permute-done.44.refs_3_ = bf16[4,1,576,720]{3,2,1,0:T(8,128)(2,1)} collective-permute-done((bf16[4,1,576,720]{3,2,1,0:T(8,128)(2,1)}, bf16[4,1,576,720]{3,2,1,0:T(8,128)(2,1)}, u32[]{:S(2)}, u32[]{:S(2)}) %collective-permute-start.44) | collective-permute-done | bytes 3317792 | tf_op jit(solution)/shard_map/ppermute | solution.py:514
  590.4 8.5 %half_product.15 = bf16[4,1,576,720]{3,2,1,0:T(8,128)(2,1)} custom-call(s32[1]{0:T(128)} %bitcast.48.refs_0_, bf16[4,2,720,1024]{3,2,1,0:T(8,128)(2,1)} %bitcast.125, bf16[576,1024]{1,0:T(8,128)(2,1)} %get-tuple-element.168.refs_2_, bf16[4,1,576,720]{3,2,1,0:T(8,128)(2,1)} %collective-permute-done.44.refs_3_), custom_call_target="tpu_custom_call" | custom-call | tf_op jit(solution)/shard_map/half_product/pallas_call | solution.py:473
  609.5 19.3 %collective-permute-done.40 = f32[2,2304]{1,0:T(2,128)S(1)} collective-permute-done((f32[2,2304]{1,0:T(2,128)S(1)}, f32[2,2304]{1,0:T(2,128)S(1)}, u32[]{:S(2)}, u32[]{:S(2)}) %collective-permute-start.40) | collective-permute-done | bytes 18464 | tf_op jit(solution)/shard_map/ppermute | solution.py:566
  630.4 4.3 collective-permute-done.41
  636.3 4.3 collective-permute-done.42
  643.4 3.0 convert_add_fusion.2
  650.2 14.9 %reduce-scatter.14.cloned.1.call-done = bf16[1,1,576,720]{3,2,1,0:T(8,128)(2,1)} async-done(((bf16[4,1,576,720]{3,2,1,0:T(8,128)(2,1)}), bf16[1,1,576,720]{3,2,1,0:T(8,128)(2,1)}) %reduce-scatter.14.cloned.1.call-update) | async-done | bytes 829456 | tf_op jit(solution)/shard_map/reduce_scatter | solution.py:520
  665.0 2.5 convert_bitcast_fusion
  (209 shorter events, 82.4 us)
Async XLA Ops:
  7.2 127.7 %all-gather.2.cloned.1.call-start = ((), (), s32[]{:S(2)}) async-start(), calls=%async_computation.5 | async-start | bytes 3981312 | tf_op jit(solution)/shard_map/all_gather | solution.py:750
  7.2 3.9 collective-permute-start
  7.7 29.3 %collective-permute-start.1 = (bf16[256,2304]{1,0:T(8,128)(2,1)}, bf16[256,2304]{1,0:T(8,128)(2,1)S(1)}, u32[]{:S(2)}, u32[]{:S(2)}) collective-permute-start(bf16[256,2304]{1,0:T(8,128)(2,1)} %refs_1_.2), channel_id=1, source_target_pairs={{0,2},{1,3},{2,0},{3,1},{4,6},{5,7},{6,4},{7,5},{8,10},{9,11},{10,... | collective-permute-start | bytes 3538952 | tf_op jit(solution)/shard_map/ppermute | solution.py:135
  17.4 6.1 copy-start.1
  17.4 6.1 copy-start.15
  37.1 3.5 collective-permute-start.2
  38.4 18.1 %collective-permute-start.6 = (bf16[72,1440]{1,0:T(8,128)(2,1)S(1)}, bf16[72,1440]{1,0:T(8,128)(2,1)S(1)}, u32[]{:S(2)}, u32[]{:S(2)}) collective-permute-start(bf16[72,1440]{1,0:T(8,128)(2,1)S(1)} %get-tuple-element.89), channel_id=1, source_target_pairs={{0,2},{1,3},{2,0},{3,1},{4,6},{5,7},{6,4},{7,5},{8,10},{9,11},{10,... | collective-permute-start | bytes 622088 | tf_op jit(solution)/shard_map/ppermute | solution.py:135
  40.3 15.9 %collective-permute-start.7 = (bf16[72,1440]{1,0:T(8,128)(2,1)S(1)}, bf16[72,1440]{1,0:T(8,128)(2,1)S(1)}, u32[]{:S(2)}, u32[]{:S(2)}) collective-permute-start(bf16[72,1440]{1,0:T(8,128)(2,1)S(1)} %get-tuple-element.91), channel_id=1, source_target_pairs={{0,2},{1,3},{2,0},{3,1},{4,6},{5,7},{6,4},{7,5},{8,10},{9,11},{10,... | collective-permute-start | bytes 622088 | tf_op jit(solution)/shard_map/ppermute | solution.py:135
  56.2 1.5 collective-permute-start.14
  58.5 269.4 %reduce-scatter.6.cloned.1.call-start = ((), (), s32[]{:S(2)}) async-start(), calls=%async_computation.6 | async-start | bytes 8847360 | tf_op jit(solution)/shard_map/reduce_scatter | solution.py:520
  58.6 28.2 %collective-permute-start.8 = (bf16[256,2304]{1,0:T(8,128)(2,1)S(1)}, bf16[256,2304]{1,0:T(8,128)(2,1)S(1)}, u32[]{:S(2)}, u32[]{:S(2)}) collective-permute-start(bf16[256,2304]{1,0:T(8,128)(2,1)S(1)} %copy-done.11), channel_id=1, source_target_pairs={{0,2},{1,3},{2,0},{3,1},{4,6},{5,7},{6,4},{7,5},{8,10},{9,11},{10,... | collective-permute-start | bytes 3538952 | tf_op jit(solution)/shard_map/ppermute | solution.py:135
  60.5 28.3 %collective-permute-start.5 = (bf16[256,2304]{1,0:T(8,128)(2,1)S(1)}, bf16[256,2304]{1,0:T(8,128)(2,1)S(1)}, u32[]{:S(2)}, u32[]{:S(2)}) collective-permute-start(bf16[256,2304]{1,0:T(8,128)(2,1)S(1)} %copy-done.11), channel_id=1, source_target_pairs={{0,1},{1,0},{2,3},{3,2},{4,5},{5,4},{6,7},{7,6},{8,9},{9,8},{10,11... | collective-permute-start | bytes 3538952 | tf_op jit(solution)/shard_map/ppermute | solution.py:135
  86.8 3.0 collective-permute-start.9
  86.8 32.4 %collective-permute-start.4 = (bf16[576,1024]{1,0:T(8,128)(2,1)}, bf16[576,1024]{1,0:T(8,128)(2,1)}, u32[]{:S(2)}, u32[]{:S(2)}) collective-permute-start(bf16[576,1024]{1,0:T(8,128)(2,1)} %bitcast.169), channel_id=1, source_target_pairs={{0,2},{1,3},{2,0},{3,1},{4,6},{5,7},{6,4},{7,5},{8,10},{9,11},{10,... | collective-permute-start | bytes 3538952 | tf_op jit(solution)/shard_map/ppermute | solution.py:135
  88.6 32.8 %collective-permute-start.3 = (bf16[576,1024]{1,0:T(8,128)(2,1)}, bf16[576,1024]{1,0:T(8,128)(2,1)}, u32[]{:S(2)}, u32[]{:S(2)}) collective-permute-start(bf16[576,1024]{1,0:T(8,128)(2,1)} %bitcast.170), channel_id=1, source_target_pairs={{0,1},{1,0},{2,3},{3,2},{4,5},{5,4},{6,7},{7,6},{8,9},{9,8},{10,11... | collective-permute-start | bytes 3538952 | tf_op jit(solution)/shard_map/ppermute | solution.py:135
  119.2 3.5 collective-permute-start.10
  119.6 17.6 %collective-permute-start.13 = (bf16[576,1440]{1,0:T(8,128)(2,1)}, bf16[576,1440]{1,0:T(8,128)(2,1)S(1)}, u32[]{:S(2)}, u32[]{:S(2)}) collective-permute-start(bf16[576,1440]{1,0:T(8,128)(2,1)} %get-tuple-element.161), channel_id=1, source_target_pairs={{0,1},{1,0},{2,3},{3,2},{4,5},{5,4},{6,7},{7,6},{8,9},{9,8},{10,11... | collective-permute-start | bytes 4976648 | tf_op jit(solution)/shard_map/ppermute | solution.py:135
  132.4 29.9 %collective-permute-start.12 = (bf16[592,1024]{1,0:T(8,128)(2,1)}, bf16[592,1024]{1,0:T(8,128)(2,1)}, u32[]{:S(2)}, u32[]{:S(2)}) collective-permute-start(bf16[592,1024]{1,0:T(8,128)(2,1)} %get-tuple-element.103.own), channel_id=1, source_target_pairs={{0,2},{1,3},{2,0},{3,1},{4,6},{5,7},{6,4},{7,5},{8,10},{9,11},{10,... | collective-permute-start | bytes 3637256 | tf_op jit(solution)/shard_map/ppermute | solution.py:135
  134.8 27.5 %collective-permute-start.11 = (bf16[592,1024]{1,0:T(8,128)(2,1)}, bf16[592,1024]{1,0:T(8,128)(2,1)}, u32[]{:S(2)}, u32[]{:S(2)}) collective-permute-start(bf16[592,1024]{1,0:T(8,128)(2,1)} %get-tuple-element.103.own), channel_id=1, source_target_pairs={{0,1},{1,0},{2,3},{3,2},{4,5},{5,4},{6,7},{7,6},{8,9},{9,8},{10,11... | collective-permute-start | bytes 3637256 | tf_op jit(solution)/shard_map/ppermute | solution.py:135
  134.8 5.4 slice-start
  162.3 3.1 collective-permute-start.15
  202.5 202.3 %reduce-scatter.8.cloned.1.call-start = ((), (), s32[]{:S(2)}) async-start(), calls=%async_computation.7 | async-start | bytes 4423680 | tf_op jit(solution)/shard_map/reduce_scatter | solution.py:520
  217.1 8.3 %collective-permute-start.17 = (bf16[592,1024]{1,0:T(8,128)(2,1)}, bf16[592,1024]{1,0:T(8,128)(2,1)S(1)}, u32[]{:S(2)}, u32[]{:S(2)}) collective-permute-start(bf16[592,1024]{1,0:T(8,128)(2,1)} %get-tuple-element.114), channel_id=1, source_target_pairs={{0,1},{1,0},{2,3},{3,2},{4,5},{5,4},{6,7},{7,6},{8,9},{9,8},{10,11... | collective-permute-start | bytes 3637256 | tf_op jit(solution)/shard_map/ppermute | solution.py:135
  217.3 21.4 %collective-permute-start.18 = (bf16[592,1024]{1,0:T(8,128)(2,1)}, bf16[592,1024]{1,0:T(8,128)(2,1)S(1)}, u32[]{:S(2)}, u32[]{:S(2)}) collective-permute-start(bf16[592,1024]{1,0:T(8,128)(2,1)} %get-tuple-element.118), channel_id=1, source_target_pairs={{0,1},{1,0},{2,3},{3,2},{4,5},{5,4},{6,7},{7,6},{8,9},{9,8},{10,11... | collective-permute-start | bytes 3637256 | tf_op jit(solution)/shard_map/ppermute | solution.py:135
  235.4 29.0 %collective-permute-start.19 = (bf16[592,1024]{1,0:T(8,128)(2,1)}, bf16[592,1024]{1,0:T(8,128)(2,1)S(1)}, u32[]{:S(2)}, u32[]{:S(2)}) collective-permute-start(bf16[592,1024]{1,0:T(8,128)(2,1)} %feature_chunks.7), channel_id=1, source_target_pairs={{0,2},{1,3},{2,0},{3,1},{4,6},{5,7},{6,4},{7,5},{8,10},{9,11},{10,... | collective-permute-start | bytes 3637256 | tf_op jit(solution)/shard_map/ppermute | solution.py:135
  237.2 78.5 %collective-permute-start.24 = (bf16[4,1,288,1440]{3,2,1,0:T(8,128)(2,1)}, bf16[4,1,288,1440]{3,2,1,0:T(8,128)(2,1)}, u32[]{:S(2)}, u32[]{:S(2)}) collective-permute-start(bf16[4,1,288,1440]{3,2,1,0:T(8,128)(2,1)} %half_product.8), channel_id=1, source_target_pairs={{0,4},{4,0},{8,12},{12,8},{16,20},{20,16},{24,28},{28,24},{1,5},{5... | collective-permute-start | bytes 9953288 | tf_op jit(solution)/shard_map/ppermute | solution.py:514
  249.2 17.2 %copy-start.37 = (f32[1,1024]{1,0:T(1,128)S(1)}, f32[1,1024]{1,0:T(1,128)}, u32[]{:S(2)}) copy-start(f32[1,1024]{1,0:T(1,128)} %get-tuple-element.119) | copy-start | bytes 12292
  249.2 17.2 %copy-start.8 = (f32[576,1024]{1,0:T(8,128)S(1)}, f32[576,1024]{1,0:T(8,128)}, u32[]{:S(2)}) copy-start(f32[576,1024]{1,0:T(8,128)} %copy-done.7) | copy-start | bytes 7077892
  249.2 17.3 %copy-start.20 = (f32[576,1024]{1,0:T(8,128)S(1)}, f32[576,1024]{1,0:T(8,128)}, u32[]{:S(2)}) copy-start(f32[576,1024]{1,0:T(8,128)} %get-tuple-element.102) | copy-start | bytes 7077892
  275.8 3.1 collective-permute-start.20
  275.8 9.8 %collective-permute-start.21 = (bf16[576,1024]{1,0:T(8,128)(2,1)}, bf16[576,1024]{1,0:T(8,128)(2,1)S(1)}, u32[]{:S(2)}, u32[]{:S(2)}) collective-permute-start(bf16[576,1024]{1,0:T(8,128)(2,1)} %get-tuple-element.122), channel_id=1, source_target_pairs={{0,1},{1,0},{2,3},{3,2},{4,5},{5,4},{6,7},{7,6},{8,9},{9,8},{10,11... | collective-permute-start | bytes 3538952 | tf_op jit(solution)/shard_map/ppermute | solution.py:135
  283.8 28.2 %collective-permute-start.22 = (bf16[576,1024]{1,0:T(8,128)(2,1)}, bf16[576,1024]{1,0:T(8,128)(2,1)S(1)}, u32[]{:S(2)}, u32[]{:S(2)}) collective-permute-start(bf16[576,1024]{1,0:T(8,128)(2,1)} %feature_chunks.10), channel_id=1, source_target_pairs={{0,2},{1,3},{2,0},{3,1},{4,6},{5,7},{6,4},{7,5},{8,10},{9,11},{10,... | collective-permute-start | bytes 3538952 | tf_op jit(solution)/shard_map/ppermute | solution.py:135
  291.1 21.0 %copy-start.19 = (f32[576,1024]{1,0:T(8,128)S(1)}, f32[576,1024]{1,0:T(8,128)}, u32[]{:S(2)}) copy-start(f32[576,1024]{1,0:T(8,128)} %feature_chunks.11) | copy-start | bytes 7077892
  328.0 184.3 %reduce-scatter.10.cloned.1.call-start = ((), (), s32[]{:S(2)}) async-start(), calls=%async_computation.8 | async-start | bytes 1843200 | tf_op jit(solution)/shard_map/reduce_scatter | solution.py:520
  328.0 75.8 %collective-permute-start.23 = (bf16[1440,1024]{1,0:T(8,128)(2,1)}, bf16[1440,1024]{1,0:T(8,128)(2,1)}, u32[]{:S(2)}, u32[]{:S(2)}) collective-permute-start(bf16[1440,1024]{1,0:T(8,128)(2,1)} %get-tuple-element.126.refs_0_), channel_id=1, source_target_pairs={{0,2},{1,3},{2,0},{3,1},{4,6},{5,7},{6,4},{7,5},{8,10},{9,11},{10,... | collective-permute-start | bytes 8847368 | tf_op jit(solution)/shard_map/ppermute | solution.py:135
  329.5 67.4 %collective-permute-start.27 = (bf16[4,1,288,576]{3,2,1,0:T(8,128)(2,1)}, bf16[4,1,288,576]{3,2,1,0:T(8,128)(2,1)S(1)}, u32[]{:S(2)}, u32[]{:S(2)}) collective-permute-start(bf16[4,1,288,576]{3,2,1,0:T(8,128)(2,1)} %half_product.9), channel_id=1, source_target_pairs={{0,4},{4,0},{8,12},{12,8},{16,20},{20,16},{24,28},{28,24},{1,5},{5... | collective-permute-start | bytes 3981320 | tf_op jit(solution)/shard_map/ppermute | solution.py:514
  369.6 10.2 %collective-permute-start.25 = (bf16[256,2304]{1,0:T(8,128)(2,1)}, bf16[256,2304]{1,0:T(8,128)(2,1)}, u32[]{:S(2)}, u32[]{:S(2)}) collective-permute-start(bf16[256,2304]{1,0:T(8,128)(2,1)} %get-tuple-element.136), channel_id=1, source_target_pairs={{0,1},{1,0},{2,3},{3,2},{4,5},{5,4},{6,7},{7,6},{8,9},{9,8},{10,11... | collective-permute-start | bytes 3538952 | tf_op jit(solution)/shard_map/ppermute | solution.py:135
  369.6 18.1 %collective-permute-start.26 = (bf16[256,2304]{1,0:T(8,128)(2,1)}, bf16[256,2304]{1,0:T(8,128)(2,1)S(1)}, u32[]{:S(2)}, u32[]{:S(2)}) collective-permute-start(bf16[256,2304]{1,0:T(8,128)(2,1)} %get-tuple-element.141), channel_id=1, source_target_pairs={{0,1},{1,0},{2,3},{3,2},{4,5},{5,4},{6,7},{7,6},{8,9},{9,8},{10,11... | collective-permute-start | bytes 3538952 | tf_op jit(solution)/shard_map/ppermute | solution.py:135
  370.1 35.6 %collective-permute-start.16 = (bf16[1440,1024]{1,0:T(8,128)(2,1)}, bf16[1440,1024]{1,0:T(8,128)(2,1)}, u32[]{:S(2)}, u32[]{:S(2)}) collective-permute-start(bf16[1440,1024]{1,0:T(8,128)(2,1)} %get-tuple-element.126.refs_0_), channel_id=1, source_target_pairs={{0,1},{1,0},{2,3},{3,2},{4,5},{5,4},{6,7},{7,6},{8,9},{9,8},{10,11... | collective-permute-start | bytes 8847368 | tf_op jit(solution)/shard_map/ppermute | solution.py:135
  397.0 7.9 %copy-start.5 = (bf16[256,2304]{1,0:T(8,128)(2,1)S(1)}, bf16[256,2304]{1,0:T(8,128)(2,1)}, u32[]{:S(2)}) copy-start(bf16[256,2304]{1,0:T(8,128)(2,1)} %refs_1_.2) | copy-start | bytes 3538948
  403.8 5.9 collective-permute-start.28
  404.3 97.8 %collective-permute-start.36 = (bf16[4,3,288,576]{3,2,1,0:T(8,128)(2,1)}, bf16[4,3,288,576]{3,2,1,0:T(8,128)(2,1)}, u32[]{:S(2)}, u32[]{:S(2)}) collective-permute-start(bf16[4,3,288,576]{3,2,1,0:T(8,128)(2,1)} %half_product.11), channel_id=1, source_target_pairs={{0,4},{4,0},{8,12},{12,8},{16,20},{20,16},{24,28},{28,24},{1,5},{5... | collective-permute-start | bytes 11943944 | tf_op jit(solution)/shard_map/ppermute | solution.py:514
  404.8 194.1 %reduce-scatter.12.cloned.1.call-start = ((), (), s32[]{:S(2)}) async-start(), calls=%async_computation.9 | async-start | bytes 5529600 | tf_op jit(solution)/shard_map/reduce_scatter | solution.py:520
  405.2 35.0 %copy-start.35 = (f32[256]{0:T(256)}, f32[256]{0:T(256)S(1)}, u32[]{:S(2)}) copy-start(f32[256]{0:T(256)S(1)} %add_rsqrt_fusion) | copy-start | bytes 3076
  405.2 34.9 %collective-permute-start.35 = (bf16[256,2304]{1,0:T(8,128)(2,1)}, bf16[256,2304]{1,0:T(8,128)(2,1)}, u32[]{:S(2)}, u32[]{:S(2)}) collective-permute-start(bf16[256,2304]{1,0:T(8,128)(2,1)} %token_chunks.4), channel_id=1, source_target_pairs={{0,2},{1,3},{2,0},{3,1},{4,6},{5,7},{6,4},{7,5},{8,10},{9,11},{10,... | collective-permute-start | bytes 3538952 | tf_op jit(solution)/shard_map/ppermute | solution.py:135
  426.9 13.3 %copy-start.18 = (f32[256,2304]{1,0:T(8,128)S(1)}, f32[256,2304]{1,0:T(8,128)}, u32[]{:S(2)}) copy-start(f32[256,2304]{1,0:T(8,128)} %token_chunks.5) | copy-start | bytes 7077892
  426.9 13.3 %copy-start.32 = (f32[2304]{0:T(1024)S(1)}, f32[2304]{0:T(1024)}, u32[]{:S(2)}) copy-start(f32[2304]{0:T(1024)} %param.13) | copy-start | bytes 27652
  512.3 152.7 %reduce-scatter.14.cloned.1.call-start = ((), (), s32[]{:S(2)}) async-start(), calls=%async_computation.10 | async-start | bytes 4423680 | tf_op jit(solution)/shard_map/reduce_scatter | solution.py:520
  512.4 78.0 %collective-permute-start.44 = (bf16[4,1,576,720]{3,2,1,0:T(8,128)(2,1)}, bf16[4,1,576,720]{3,2,1,0:T(8,128)(2,1)}, u32[]{:S(2)}, u32[]{:S(2)}) collective-permute-start(bf16[4,1,576,720]{3,2,1,0:T(8,128)(2,1)} %half_product.13), channel_id=1, source_target_pairs={{0,4},{4,0},{8,12},{12,8},{16,20},{20,16},{24,28},{28,24},{1,5},{5... | collective-permute-start | bytes 9953288 | tf_op jit(solution)/shard_map/ppermute | solution.py:514
  514.2 9.3 %collective-permute-start.34 = (bf16[576,256]{1,0:T(8,128)(2,1)S(1)}, bf16[576,256]{1,0:T(8,128)(2,1)S(1)}, u32[]{:S(2)}, u32[]{:S(2)}) collective-permute-start(bf16[576,256]{1,0:T(8,128)(2,1)S(1)} %get-tuple-element.169), channel_id=1, source_target_pairs={{0,3},{1,2},{2,1},{3,0},{4,7},{5,6},{6,5},{7,4},{8,11},{9,10},{10,... | collective-permute-start | bytes 884744 | tf_op jit(solution)/shard_map/ppermute | solution.py:135
  514.3 13.9 %collective-permute-start.33 = (bf16[576,256]{1,0:T(8,128)(2,1)S(1)}, bf16[576,256]{1,0:T(8,128)(2,1)S(1)}, u32[]{:S(2)}, u32[]{:S(2)}) collective-permute-start(bf16[576,256]{1,0:T(8,128)(2,1)S(1)} %get-tuple-element.170), channel_id=1, source_target_pairs={{0,2},{1,3},{2,0},{3,1},{4,6},{5,7},{6,4},{7,5},{8,10},{9,11},{10,... | collective-permute-start | bytes 884744 | tf_op jit(solution)/shard_map/ppermute | solution.py:135
  514.9 13.3 %collective-permute-start.32 = (bf16[576,256]{1,0:T(8,128)(2,1)S(1)}, bf16[576,256]{1,0:T(8,128)(2,1)S(1)}, u32[]{:S(2)}, u32[]{:S(2)}) collective-permute-start(bf16[576,256]{1,0:T(8,128)(2,1)S(1)} %get-tuple-element.171), channel_id=1, source_target_pairs={{0,1},{1,0},{2,3},{3,2},{4,5},{5,4},{6,7},{7,6},{8,9},{9,8},{10,11... | collective-permute-start | bytes 884744 | tf_op jit(solution)/shard_map/ppermute | solution.py:135
  598.9 7.3 %copy-start.21 = (bf16[1,576,1440]{2,1,0:T(8,128)(2,1)S(1)}, bf16[1,576,1440]{2,1,0:T(8,128)(2,1)}, u32[]{:S(2)}) copy-start(bf16[1,576,1440]{2,1,0:T(8,128)(2,1)} %reduce-scatter.6.cloned.1.call-done) | copy-start | bytes 4976644
  599.7 6.6 copy-start.33
  600.3 6.0 collective-permute-start.38
  600.7 5.9 collective-permute-start.39
  600.7 6.3 collective-permute-start.37
  604.6 36.6 %collective-permute-start.31 = (bf16[576,256]{1,0:T(8,128)(2,1)}, bf16[576,256]{1,0:T(8,128)(2,1)S(1)}, u32[]{:S(2)}, u32[]{:S(2)}) collective-permute-start(bf16[576,256]{1,0:T(8,128)(2,1)} %get-tuple-element.173), channel_id=1, source_target_pairs={{0,3},{1,2},{2,1},{3,0},{4,7},{5,6},{6,5},{7,4},{8,11},{9,10},{10,... | collective-permute-start | bytes 884744 | tf_op jit(solution)/shard_map/ppermute | solution.py:135
  604.6 36.6 %collective-permute-start.30 = (bf16[576,256]{1,0:T(8,128)(2,1)}, bf16[576,256]{1,0:T(8,128)(2,1)S(1)}, u32[]{:S(2)}, u32[]{:S(2)}) collective-permute-start(bf16[576,256]{1,0:T(8,128)(2,1)} %get-tuple-element.174), channel_id=1, source_target_pairs={{0,2},{1,3},{2,0},{3,1},{4,6},{5,7},{6,4},{7,5},{8,10},{9,11},{10,... | collective-permute-start | bytes 884744 | tf_op jit(solution)/shard_map/ppermute | solution.py:135
  606.3 35.0 %collective-permute-start.29 = (bf16[576,256]{1,0:T(8,128)(2,1)}, bf16[576,256]{1,0:T(8,128)(2,1)S(1)}, u32[]{:S(2)}, u32[]{:S(2)}) collective-permute-start(bf16[576,256]{1,0:T(8,128)(2,1)} %get-tuple-element.175), channel_id=1, source_target_pairs={{0,1},{1,0},{2,3},{3,2},{4,5},{5,4},{6,7},{7,6},{8,9},{9,8},{10,11... | collective-permute-start | bytes 884744 | tf_op jit(solution)/shard_map/ppermute | solution.py:135
  606.6 36.8 %collective-permute-start.43 = (bf16[288,1440]{1,0:T(8,128)(2,1)S(1)}, bf16[288,1440]{1,0:T(8,128)(2,1)}, u32[]{:S(2)}, u32[]{:S(2)}) collective-permute-start(bf16[288,1440]{1,0:T(8,128)(2,1)S(1)} %dynamic-slice_bitcast_fusion.2), channel_id=1, source_target_pairs={{0,4},{4,0},{8,12},{12,8},{16,20},{20,16},{24,28},{28,24},{1,5},{5... | collective-permute-start | bytes 2488328 | tf_op jit(solution)/shard_map/ppermute | solution.py:514
  607.8 21.1 %collective-permute-start.40 = (f32[2,2304]{1,0:T(2,128)S(1)}, f32[2,2304]{1,0:T(2,128)S(1)}, u32[]{:S(2)}, u32[]{:S(2)}) collective-permute-start(f32[2,2304]{1,0:T(2,128)S(1)} %add_add_fusion), channel_id=1, source_target_pairs={{0,4},{4,0},{8,12},{12,8},{16,20},{20,16},{24,28},{28,24},{1,5},{5... | collective-permute-start | bytes 55304 | tf_op jit(solution)/shard_map/ppermute | solution.py:566
  628.9 5.9 collective-permute-start.41
  634.8 5.8 collective-permute-start.42
  (27 other events, 62.5 us)
Sparse Core Ops, SparseCore 0:
  58.7 66.7 all-gather.1
  202.7 125.2 reduce-scatter.5
  330.3 66.8 reduce-scatter.7
  405.0 33.4 reduce-scatter.9
  512.4 79.1 reduce-scatter.11
  599.1 65.8 reduce-scatter.13

commit v3 on v2

--- a/solution.py
+++ b/solution.py
@@ -84,12 +84,13 @@
 
 
 def backward_kernel(
-    q_ref, k_ref, v_ref, g_ref, lse_ref, cos_ref, sin_ref, dq_ref, dk_ref, dv_ref, dk_acc, dv_acc
+    q_ref, k_ref, v_ref, g_ref, h_ref, lse_ref, cos_ref, sin_ref, dq_ref, dk_ref, dv_ref, dk_acc, dv_acc
 ):
     cosine, sine = cos_ref[...], sin_ref[...]
     span = q_ref.shape[2]
     q_scaled = (q_ref[0] * (HD ** (-0.5))).astype(low)
-    k_low, v_low, grad = k_ref[0], v_ref[0], g_ref[0]
+    k_low, v_low = k_ref[0], v_ref[0]
+    grad = (g_ref[0] + h_ref[0].astype(full)).astype(low)
     k_rows, v_rows = k_low.T, v_low.T
     dk_acc[...] = jnp.zeros_like(dk_acc)
     dv_acc[...] = jnp.zeros_like(dv_acc)
@@ -111,7 +112,7 @@
     dv_ref[0] = dv_acc[...].astype(low)
 
 
-def attention_backward(query, key, value, grad, lse, cosine, sine):
+def attention_backward(query, key, value, grad, rest, lse, cosine, sine):
     heads, _, span = query.shape
     spec = pl.BlockSpec((1, HD, span), lambda h: (h, 0, 0))
     table = pl.BlockSpec((HD // 2, span), lambda h: (0, 0))
@@ -120,14 +121,14 @@
     return pl.pallas_call(
         backward_kernel,
         grid=(heads,),
-        in_specs=[spec, spec, spec, spec, row, table, table],
+        in_specs=[spec, spec, spec, spec, spec, row, table, table],
         out_specs=[spec, spec, spec],
         out_shape=[field, field, field],
         scratch_shapes=[pltpu.VMEM((HD, span), full), pltpu.VMEM((HD, span), full)],
         compiler_params=pltpu.CompilerParams(vmem_limit_bytes=60 * 2**20),
         cost_estimate=SMALL,
         name="attention_backward",
-    )(query, key, value, grad, lse, cosine, sine)
+    )(query, key, value, grad, rest, lse, cosine, sine)
 
 
 def swap(array, j):
@@ -139,45 +140,59 @@
     return lax.optimization_barrier((value, *earlier))[0]
 
 
-def place_kernel(*refs):
+def stage(run, *earlier):
+    blank = lambda: jax.tree.map(lambda a: jnp.zeros(a.shape, a.dtype), jax.eval_shape(run))
+    return lax.cond(after(jnp.bool_(True), *earlier), run, blank)
+
+
+def place_kernel(*refs, parts):
     *blocks, out, held, arrived, left = refs
     me = lax.axis_index("fsdp")
-    into = [
-        pltpu.make_async_copy(block, held.at[j], arrived.at[j]) for j, block in enumerate(blocks)
-    ]
-    back = [
-        pltpu.make_async_copy(
-            held.at[j], out.at[lax.bitwise_xor(me, jnp.int32(j))], left.at[j]
+    into, back = [], []
+    for j in range(held.shape[0]):
+        at = 0
+        for i in range(j * parts, (j + 1) * parts):
+            rows = blocks[i].shape[0]
+            into.append(
+                pltpu.make_async_copy(blocks[i], held.at[j, pl.ds(at, rows)], arrived.at[i])
+            )
+            at += rows
+        back.append(
+            pltpu.make_async_copy(
+                held.at[j], out.at[lax.bitwise_xor(me, jnp.int32(j))], left.at[j]
+            )
         )
-        for j in range(len(blocks))
-    ]
     for copy in into:
         copy.start()
-    for copy, then in zip(into, back):
-        copy.wait()
-        then.start()
+    for j, copy in enumerate(back):
+        for part in into[j * parts : (j + 1) * parts]:
+            part.wait()
+        copy.start()
     for copy in back:
         copy.wait()
 
 
-def place(blocks):
+def place(blocks, parts=1):
     count = len(blocks)
-    first = blocks[0]
+    size = count // parts
+    rows = sum(block.shape[0] for block in blocks[:parts])
+    shape = (size, rows, blocks[0].shape[1])
+    dtype = blocks[0].dtype
     whole = pl.pallas_call(
-        place_kernel,
+        lambda *refs: place_kernel(*refs, parts=parts),
         in_specs=[pl.BlockSpec(memory_space=pl.ANY)] * count,
         out_specs=pl.BlockSpec(memory_space=pl.ANY),
-        out_shape=jax.ShapeDtypeStruct((count,) + first.shape, first.dtype),
+        out_shape=jax.ShapeDtypeStruct(shape, dtype),
         scratch_shapes=[
-            pltpu.VMEM((count,) + first.shape, first.dtype),
+            pltpu.VMEM(shape, dtype),
             pltpu.SemaphoreType.DMA((count,)),
-            pltpu.SemaphoreType.DMA((count,)),
+            pltpu.SemaphoreType.DMA((size,)),
         ],
-        compiler_params=pltpu.CompilerParams(vmem_limit_bytes=16 * 2**20),
+        compiler_params=pltpu.CompilerParams(vmem_limit_bytes=60 * 2**20),
         cost_estimate=SMALL,
         name="place",
     )(*blocks)
-    return whole.reshape((count * first.shape[0],) + first.shape[1:])
+    return whole.reshape(size * rows, shape[2])
 
 
 def gather(array, *before_last):
@@ -352,7 +367,7 @@
 
 
 def inner_kernel(
-    own, core, chip, both, w_gate, w_up, d_inner, inner_ref, d_gate_ref, d_up_ref, mean_ref, factor_ref,
+    own, core, chip, both, w_gate, w_up, d_inner, inner_ref, grads_ref, mean_ref, factor_ref,
     all_ref, held, rest, arrived, left,
 ):
     step = pl.program_id(0)
@@ -384,8 +399,8 @@
         grad = factor * d_inner[:, cut].astype(full)
         d_up = grad * activated
         d_gate = grad * up * (sigmoid + activated * (1.0 - sigmoid))
-        d_gate_ref[:, cut] = d_gate.astype(low)
-        d_up_ref[:, cut] = d_up.astype(low)
+        grads_ref[0, :, cut] = d_gate.astype(low)
+        grads_ref[1, :, cut] = d_up.astype(low)
         mean_ref[:, cut] += jnp.sum(d_gate * gate + d_up * up, axis=0, keepdims=True)
 
     @pl.when(step == pl.num_programs(0) - 1)
@@ -402,16 +417,14 @@
     hbm = pl.BlockSpec(memory_space=pl.ANY)
     rows = lambda wide: pl.BlockSpec((tile, wide), lambda i: (i, 0))
     row = pl.BlockSpec((1, span), lambda i: (0, 0))
-    field = jax.ShapeDtypeStruct((units, span), low)
-    inner, d_gate, d_up, mean, factor, whole = pl.pallas_call(
+    inner, grads, mean, factor, whole = pl.pallas_call(
         inner_kernel,
         grid=(units // tile,),
         in_specs=[hbm] * 4 + [rows(size * cols), rows(size * cols), rows(span)],
-        out_specs=[rows(span), rows(span), rows(span), row, row, hbm],
+        out_specs=[rows(span), pl.BlockSpec((2, tile, span), lambda i: (0, i, 0)), row, row, hbm],
         out_shape=[
-            field,
-            field,
-            field,
+            jax.ShapeDtypeStruct((units, span), low),
+            jax.ShapeDtypeStruct((2, units, span), low),
             jax.ShapeDtypeStruct((1, span), full),
             jax.ShapeDtypeStruct((1, span), full),
             jax.ShapeDtypeStruct((size, cols, span), low),
@@ -426,7 +439,7 @@
         cost_estimate=SMALL,
         name="inner_part",
     )(*blocks, w_gate, w_up, d_inner)
-    return inner, d_gate, d_up, mean, factor, whole.reshape(size * cols, span)
+    return inner, grads.reshape(2 * units, span), mean, factor, whole.reshape(size * cols, span)
 
 
 def to_rows(field, rows):
@@ -458,10 +471,11 @@
         out[:, k] = total.astype(low)
 
 
-def half_product(act, grads, side, added=None, turned=False, earlier=()):
+def half_product(act, grads, side, added=None, turned=False, columns=None, earlier=()):
     size = lax.axis_size("rep")
     count = len(grads)
-    columns, tokens = grads[0].shape
+    tokens = grads[0].shape[1]
+    columns = columns or grads[0].shape[0]
     lines, rows = size // 2, act.shape[0] // size
     index = jnp.asarray(side, jnp.int32)[None]
     if earlier:
@@ -491,16 +505,17 @@
     out[0] = lax.dot_general(act[0], grad[...], NT, preferred_element_type=full).astype(low)
 
 
-def whole_product(act, grad):
+def whole_product(act, grad, columns):
     lines = lax.axis_size("rep") // 2
-    columns, tokens = grad.shape
+    tokens = grad.shape[1]
+    last = grad.shape[0] // columns - 1
     rows = act.shape[0] // lines
     return pl.pallas_call(
         whole_kernel,
         grid=(lines,),
         in_specs=[
             pl.BlockSpec((1, rows, tokens), lambda i: (i, 0, 0)),
-            pl.BlockSpec((columns, tokens), lambda i: (0, 0)),
+            pl.BlockSpec((columns, tokens), lambda i: (last, 0)),
         ],
         out_specs=pl.BlockSpec((1, rows, columns), lambda i: (i, 0, 0)),
         out_shape=jax.ShapeDtypeStruct((lines, rows, columns), low),
@@ -523,26 +538,39 @@
 
 
 class GradSum:
-    def __init__(self, act, grads, turned=False):
-        self.act, self.grads, self.turned = act, grads, turned
+    def __init__(self, act, grads, turned=False, columns=None):
+        self.act, self.grads, self.turned, self.columns = act, grads, turned, columns
         self.side = lax.axis_index("rep") % 2
 
     def send(self, earlier=()):
         sent = half_product(
-            self.act, self.grads, 1 - self.side, turned=self.turned, earlier=earlier
+            self.act,
+            self.grads,
+            1 - self.side,
+            turned=self.turned,
+            columns=self.columns,
+            earlier=earlier,
         )
+        return sent
+
+    def transfer(self, sent):
         self.arrived = neighbour(sent)
-        return sent
 
     def keep(self, earlier=(), last=None):
         kept = half_product(
-            self.act, self.grads, self.side, self.arrived, turned=self.turned, earlier=earlier
+            self.act,
+            self.grads,
+            self.side,
+            self.arrived,
+            turned=self.turned,
+            columns=self.columns,
+            earlier=earlier,
         )
         self.sums = line_scatter(kept if last is None else after(kept, last.sums))
         return kept
 
     def line_first(self, earlier=()):
-        whole = whole_product(self.act, after(self.grads[0], *earlier))
+        whole = whole_product(self.act, after(self.grads[0], *earlier), self.columns)
         self.sums = line_scatter(whole)
         return whole
 
@@ -597,14 +625,15 @@
 
 def chunks_kernel(index, *refs, count, ways, added, extra):
     step = pl.program_id(0)
-    weights, refs = refs[:count], refs[count:]
-    grads, refs = refs[:count], refs[count:]
+    weights, grads, refs = refs[:count], refs[count], refs[count + 1 :]
     plus, refs = refs[:added], refs[added:]
     row, outs = refs[:extra], refs[extra:]
-    total = None
-    for weight, grad in zip(weights, grads):
-        term = jnp.dot(weight[...], grad[...], preferred_element_type=full)
+    total, at = None, 0
+    for weight in weights:
+        units = weight.shape[1]
+        term = jnp.dot(weight[...], grads[at : at + units], preferred_element_type=full)
         total = term if total is None else total + term
+        at += units
     cols = total.shape[0]
     for way, out in enumerate(outs):
 
@@ -623,7 +652,7 @@
 
 def feature_chunks(weights, grads, partners, plus=(), extra=None, dtype=low, earlier=()):
     me = lax.axis_index("fsdp")
-    span = grads[0].shape[1]
+    span = grads.shape[1]
     cols = weights[0].shape[0] // lax.axis_size("fsdp")
     tall = cols + (0 if extra is None else 16)
     index = jnp.stack([jnp.asarray(me ^ j, jnp.int32) for j in partners])
@@ -641,14 +670,55 @@
             in_specs=[
                 pl.BlockSpec((cols, w.shape[1]), lambda i, index: (index[i], 0)) for w in weights
             ]
-            + [const(a.shape) for a in (*grads, *plus, *extra)],
+            + [const(a.shape) for a in (grads, *plus, *extra)],
             out_specs=[const((tall, span))] * len(partners),
         ),
         out_shape=[jax.ShapeDtypeStruct((tall, span), dtype)] * len(partners),
         compiler_params=pltpu.CompilerParams(vmem_limit_bytes=60 * 2**20),
         cost_estimate=SMALL,
         name="feature_chunks",
-    )(index, *weights, *grads, *plus, *extra)
+    )(index, *weights, grads, *plus, *extra)
+
+
+def attn_grad_kernel(
+    own, across, cotangent, hidden, gain, factor, attn_ref, hidden_ref, term_ref, *, width
+):
+    cols = hidden.shape[0]
+    mean = (own[cols : cols + 1] + across[cols : cols + 1].astype(full)) * (1.0 / width)
+    scaled = own[:cols] + across[:cols].astype(full)
+    state = hidden[...]
+    term = jnp.sum(scaled * state, axis=1, keepdims=True)
+    step = pl.program_id(0)
+
+    @pl.when(step == 0)
+    def _():
+        term_ref[...] = term
+
+    @pl.when(step != 0)
+    def _():
+        term_ref[...] += term
+
+    grad = cotangent[...] + gain[...] * scaled - state * (factor[...] * mean)
+    hidden_ref[...] = grad.astype(low)
+    attn_ref[...] = (branch_scale * grad).astype(low)
+
+
+def attn_grad(own, across, cotangent, hidden, gain, factor, width):
+    cols, span = hidden.shape
+    field = jax.ShapeDtypeStruct((cols, span), low)
+    tiles = 4
+    tile = lambda rows: pl.BlockSpec((rows, span // tiles), lambda i: (0, i))
+    once = pl.BlockSpec((cols, 1), lambda i: (0, 0))
+    return pl.pallas_call(
+        lambda *refs: attn_grad_kernel(*refs, width=width),
+        grid=(tiles,),
+        in_specs=[tile(cols + 16), tile(cols + 16), tile(cols), tile(cols), once, tile(1)],
+        out_specs=[tile(cols), tile(cols), once],
+        out_shape=[field, field, jax.ShapeDtypeStruct((cols, 1), full)],
+        compiler_params=pltpu.CompilerParams(vmem_limit_bytes=60 * 2**20),
+        cost_estimate=SMALL,
+        name="attn_grad",
+    )(own, across, cotangent, hidden, gain, factor)
 
 
 def blocks_kernel(index, *refs, count, added):
@@ -775,95 +845,111 @@
     d_inner = jnp.einsum("ef,te->ft", down_own, d_ffn, preferred_element_type=full).astype(low)
     scaled_blocks = gather(scaled, d_inner)
 
-    inner, d_gate, d_up, mean, factor, scaled_all = inner_part(
+    inner, ffn_grads, mean, factor, scaled_all = inner_part(
         scaled_blocks, w_gate.T, w_up.T, d_inner
     )
 
-    sum_up = GradSum(scaled_all, [d_up])
-    sum_gate = GradSum(scaled_all, [d_gate])
-    ffn_weights, ffn_grads = (gate_tall, up_tall), (d_gate, d_up)
-    token = sum_up.line_first()
-    far, near = feature_chunks(ffn_weights, ffn_grads, (3, 1), extra=mean, earlier=[token])
-    token = sum_gate.send([far])
+    third = 2 * hidden_cols // 3
+    sum_most = GradSum(scaled_all, [ffn_grads], columns=2 * third)
+    sum_rest = GradSum(scaled_all, [ffn_grads], columns=third)
+    token = sum_rest.line_first()
+    token = sum_most.send([token])
+    sum_most.transfer(token)
+    inner_chip = swap(inner, 2)
+    inner_core = swap(inner, 1)
+    ffn_weights = (gate_tall, up_tall)
+
+    def first_stage():
+        far, near = feature_chunks(ffn_weights, ffn_grads, (3, 1), extra=mean)
+        far, near = swap(far, 1), swap(near, 1)
+        (chunk,) = feature_chunks(ffn_weights, ffn_grads, (2,), plus=[far], extra=mean)
+        return chunk, near
+
+    chunk, near = stage(first_stage, token)
+    across = swap(chunk, 2)
+    (own,) = feature_chunks(ffn_weights, ffn_grads, (0,), plus=[near], extra=mean, dtype=full)
+    inner_late = after(inner_chip, own)
+    inner_all = place([inner, inner_core, inner_late, swap(inner_late, 1)])
+    sum_down = GradSum(inner_all, [d_ffn_own], turned=True)
+    token = sum_down.send()
+    sum_down.transfer(token)
+    d_attn, d_hidden, gain_ffn_term = attn_grad(
+        own, after(across, token), cotangent_own, hidden, gain_own, factor, width
+    )
+
+    far, near = feature_chunks([out_tall], d_attn, (3, 1))
     far, near = swap(far, 1), swap(near, 1)
-    (chunk,) = feature_chunks(
-        ffn_weights, ffn_grads, (2,), plus=[far], extra=mean, earlier=[token]
-    )
+    (chunk,) = feature_chunks([out_tall], d_attn, (2,), plus=[far])
     across = swap(chunk, 2)
-    (own,) = feature_chunks(
-        ffn_weights, ffn_grads, (0,), plus=[near], extra=mean, dtype=full, earlier=[chunk]
-    )
-    d_scaled = own + across.astype(full)
-    mean_ffn = d_scaled[width_cols : width_cols + 1] / width
-    d_scaled = d_scaled[:width_cols]
-    gain_ffn_term = jnp.sum(d_scaled * hidden, axis=1)
-    d_hidden = cotangent_own + gain_own * d_scaled - hidden * (factor * mean_ffn)
-    d_attn = (branch_scale * d_hidden).astype(low)
-
-    far, near = feature_chunks([out_tall], [d_attn], (3, 1))
-    far, near = swap(far, 1), swap(near, 1)
-    (chunk,) = feature_chunks([out_tall], [d_attn], (2,), plus=[far])
-    across = swap(chunk, 2)
-    (own,) = feature_chunks(
-        [out_tall], [d_attn], (0,), plus=[near], dtype=full, earlier=[chunk]
-    )
+    token = sum_most.keep([chunk], sum_rest)
+    (own,) = feature_chunks([out_tall], d_attn, (0,), plus=[near], dtype=full, earlier=[token])
     sum_out = GradSum(attended_all, [d_attn])
     token = sum_out.send([own])
-    d_attended = own + after(across, token).astype(full)
-    d_attended = d_attended.astype(low).reshape(heads, HD, span)
-    inner_chip = swap(after(inner, d_attended), 2)
-    token = sum_gate.keep([d_attended], sum_up)
-
-    d_query, d_key, d_value = (
-        field.reshape(width_cols, span)
-        for field in attention_backward(
-            query_low, key_low, value_low, d_attended, after(lse, token), cosine, sine
+    sum_out.transfer(token)
+    across = after(across, token)
+
+    def second_stage():
+        d_query, d_key, d_value = (
+            field.reshape(width_cols, span)
+            for field in attention_backward(
+                query_low,
+                key_low,
+                value_low,
+                own.reshape(heads, HD, span),
+                across.reshape(heads, HD, span),
+                lse,
+                cosine,
+                sine,
+            )
         )
-    )
-    attn_weights, attn_grads = (w_query.T, w_key.T, w_value.T), (d_query, d_key, d_value)
-    far, near = token_chunks(attn_weights, attn_grads, (3, 1), rows)
+        sent = GradSum(normed_turned, [d_query, d_key, d_value]).send()
+        return d_query, d_key, d_value, sent
+
+    d_query, d_key, d_value, sent = second_stage()
     sum_attn = GradSum(normed_turned, [d_query, d_key, d_value])
-    token = sum_attn.send([far])
-    far, near = swap(far, 1), swap(near, 1)
-    (chunk,) = token_chunks(attn_weights, attn_grads, (2,), rows, plus=[far], earlier=[token])
-    across = swap(chunk, 2)
-    (own,) = token_chunks(
-        attn_weights, attn_grads, (0,), rows, plus=[near], dtype=full, earlier=[chunk]
-    )
-    token = sum_out.keep([own], sum_gate)
-
-    inner_both = swap(after(inner_chip, token), 1)
-    inner_all = place([inner, swap(inner, 1), inner_chip, inner_both])
-    sum_down = GradSum(inner_all, [d_ffn_own], turned=True)
-    token = sum_down.send()
+    sum_attn.transfer(sent)
+    token = sum_down.keep([sent], sum_most)
+
+    def third_stage():
+        attn_weights, attn_grads = (w_query.T, w_key.T, w_value.T), (d_query, d_key, d_value)
+        far, near = token_chunks(attn_weights, attn_grads, (3, 1), rows)
+        far, near = swap(far, 1), swap(near, 1)
+        (chunk,) = token_chunks(attn_weights, attn_grads, (2,), rows, plus=[far])
+        across = swap(chunk, 2)
+        (own,) = token_chunks(
+            attn_weights, attn_grads, (0,), rows, plus=[near], dtype=full, earlier=[chunk]
+        )
+        return own, across
+
+    own, across = stage(third_stage, token)
+    token = sum_out.keep([own], sum_down)
     ffn_result = jnp.einsum(
         "fe,ft->et", w_down, after(inner_all, token), preferred_element_type=full
     )
     output_turned = (hidden + branch_scale * ffn_result).astype(low)
     output = to_rows(output_turned, rows)
-    hidden_rows = to_rows(after(d_hidden.astype(low), output_turned), rows).astype(full)
-
-    d_normed = own + after(across, output_turned).astype(full)
+    hidden_rows = to_rows(after(d_hidden, output_turned), rows)
+    d_normed = own + after(across, token).astype(full)
     x_own = tokens.astype(full)
     factor_own = lax.rsqrt(jnp.mean(x_own * x_own, axis=-1, keepdims=True) + epsilon)
     unit_own = x_own * factor_own
     part = d_normed * gain_attn
     gain_attn_term = jnp.sum(d_normed * unit_own, axis=0)
     gain_ffn_wide = lax.dynamic_update_slice_in_dim(
-        jnp.zeros((width,), full), gain_ffn_term, me * width_cols, 0
-    )
-    d_tokens = hidden_rows + factor_own * (
+        jnp.zeros((width,), full), gain_ffn_term[:, 0], me * width_cols, 0
+    )
+    d_tokens = hidden_rows.astype(full) + factor_own * (
         part - unit_own * jnp.mean(part * unit_own, axis=-1, keepdims=True)
     )
-    grad_up = sum_up.sides_last([output_turned])
-    token = sum_attn.keep([gain_attn_term], sum_out)
-    grad_gain_attn, grad_gain_ffn = sum_everywhere(
-        jnp.stack([after(gain_attn_term, token), gain_ffn_wide])
-    )
-    token = sum_down.keep([token, d_tokens], sum_attn)
+    grad_rest = sum_rest.sides_last([token])
+    token = sum_attn.keep([d_tokens, output], sum_out)
+    grad_gain_attn, grad_gain_ffn = sum_everywhere(jnp.stack([gain_attn_term, gain_ffn_wide]))
+    grad_rest = sum_rest.sides_last([token])
     grad_query, grad_key, grad_value = sum_attn.result()
     (grad_out,) = sum_out.result()
-    (grad_gate,) = sum_gate.result()
+    (grad_most,) = sum_most.result()
+    grad_gate = grad_most[:, :hidden_cols]
+    grad_up = jnp.concatenate([grad_most[:, hidden_cols:], grad_rest], axis=1)
     (grad_down,) = sum_down.result()
     return (
         output,

time: 683 us -> 657 us (0.962)
  waiting for transfers between devices: 239 us -> 198 us
  Pallas kernels: 271 us -> 286 us
    ppermute x5, waiting for transfers between devices: 114 us -> 25.9 us  [neighbour(): lax.ppermute(array, 'rep', [(i, i ^ 1) for i in range(lax.axis_size('rep'...]
    ppermute x37, waiting for transfers between devices: 77.9 us -> 108 us  [swap(): return lax.ppermute(array, 'fsdp', [(i, i ^ j) for i in range(size)])]
    reduce_scatter x5, waiting for transfers between devices: 18.7 us -> 42.6 us  [line_scatter(): lax.psum_scatter(array, 'rep', scatter_dimension=0, tiled=True, axis_inde...]
    pallas_call x4 -> x5, Pallas kernels: 9.16 us -> 24.7 us  [the longest x4 18.5 us: place(): pl.pallas_call(lambda *refs: place_kernel(*refs, parts=parts), in_specs=[...]
    unnamed x80 -> x70, local copies, waits for them, and re-layouts: 22.5 us -> 19.6 us
  transfers between devices with their start and end apart: 51 -> 51, of which waited for: 21 -> 24; matrix products, arithmetic and copies ran while one was open for 13% -> 14% of each run, Pallas kernels for 35% -> 39%
where the time goes in v3:
time: 657 us; the launch traced here: 648 us
  Pallas kernels  286 us (44%)
  waiting for transfers between devices  198 us (30%)
  local copies, waits for them, and re-layouts  45.7 us (7%)
  matrix products  44.6 us (7%)
  starting transfers between devices  32.2 us (5%)
  other arithmetic  26.4 us (4%)
  between operations  15 us (2%)
    ppermute x37, waiting for transfers between devices, swap(): return lax.ppermute(array, 'fsdp', [(i, i ^ j) for i in range(size)])  108 us
    pallas_call x8, Pallas kernels, half_product(): pl.pallas_call(lambda *refs: product_kernel(*refs, count=count, adds=adde...  65.4 us
    pallas_call x6, Pallas kernels, feature_chunks(): pl.pallas_call(lambda *refs: chunks_kernel(*refs, count=len(weights), way...  46.9 us
    reduce_scatter x5, waiting for transfers between devices, line_scatter(): lax.psum_scatter(array, 'rep', scatter_dimension=0, tiled=True, axis_inde...  42.6 us
    pallas_call x3, Pallas kernels, token_chunks(): pl.pallas_call(lambda *refs: blocks_kernel(*refs, count=len(weights), add...  28.6 us
    pallas_call x1, Pallas kernels, attention_backward(): pl.pallas_call(backward_kernel, grid=(heads,), in_specs=[spec, spec, spec...  25.9 us
    ppermute x5, waiting for transfers between devices, neighbour(): lax.ppermute(array, 'rep', [(i, i ^ 1) for i in range(lax.axis_size('rep'...  25.9 us
    pallas_call x1, Pallas kernels, inner_part(): pl.pallas_call(inner_kernel, grid=(units // tile,), in_specs=[hbm] * 4 +...  24.6 us
  transfers between devices with their start and end apart: 51, of which 24 were waited for; matrix products, arithmetic and copies ran while one was open for 14% of the time, Pallas kernels for 39%

profile of v3, /device:TPU:0, one launch (start us, length us, event | category | flops | bytes accessed | tf_op | source)
XLA Modules:
  0.0 647.6 jit_solution(8263316554689157008)
XLA Ops:
  14.7 2.7 spread.3
  17.4 6.1 fusion.15
  28.6 8.5 %collective-permute-done.6.refs_1_ = bf16[256,2304]{1,0:T(8,128)(2,1)S(1)} collective-permute-done((bf16[256,2304]{1,0:T(8,128)(2,1)}, bf16[256,2304]{1,0:T(8,128)(2,1)S(1)}, u32[]{:S(2)}, u32[]{:S(2)}) %collective-permute-start.6) | collective-permute-done | bytes 1179680 | tf_op jit(solution)/shard_map/ppermute | solution.py:136
  42.9 4.4 spread.4
  51.0 2.6 fusion.17
  61.7 23.2 %attention_forward.1 = (bf16[9,64,1024]{2,1,0:T(8,128)(2,1)}, bf16[9,64,1024]{2,1,0:T(8,128)(2,1)}, bf16[9,64,1024]{2,1,0:T(8,128)(2,1)}, bf16[9,64,1024]{2,1,0:T(8,128)(2,1)}, f32[9,1,1024]{2,1,0:T(1,128)}) custom-call(f32[9,64,512]{2,1,0:T(8,128)} %bitcast.177, f32[9,64,512]{2,1,0:T(8,128)} %bitcast.176, f32[9,64,512]{2,1,0:T(8,128)} %bitcast.175, ...), custom_call_target="tpu_custom_call" | custom-call | tf_op jit(solution)/shard_map/attention_forward/pallas_call | solution.py:74
  93.6 3.6 spread.5
  99.3 6.5 %dynamic-slice_bitcast_fusion = (bf16[576,1440]{1,0:T(8,128)(2,1)}, bf16[576,1440]{1,0:T(8,128)(2,1)}) fusion(bf16[5760,576]{0,1:T(8,128)(2,1)} %param.25, s32[]{:T(128)S(6)} %select_n.105, s32[]{:T(128)S(6)} %select_n.103), kind=kLoop, calls=%fused_computation.22 | loop fusion | bytes 6635528 | tf_op jit(solution)/shard_map/dynamic_slice | solution.py:833
  105.8 11.4 %flip.2 = (bf16[2304,1440]{1,0:T(8,128)(2,1)}, bf16[2304,1440]{1,0:T(8,128)(2,1)}) custom-call(s32[1]{0:T(128)} %constant.127.clone.1.index, bf16[1440,2304]{1,0:T(8,128)(2,1)} %bitcast.152, bf16[1440,2304]{1,0:T(8,128)(2,1)} %bitcast.154), custom_call_target="tpu_custom_call" | custom-call | tf_op jit(solution)/shard_map/flip/pallas_call | solution.py:611
  117.3 5.5 flip.3.refs_1_
  128.2 9.7 %hidden_state.1 = (f32[576,1024]{1,0:T(8,128)}, bf16[592,1024]{1,0:T(8,128)(2,1)}, bf16[4,576,1024]{2,1,0:T(8,128)(2,1)}) custom-call(bf16[576,1024]{1,0:T(8,128)(2,1)} %bitcast.174, bf16[576,1024]{1,0:T(8,128)(2,1)} %collective-permute-done.8.core, bf16[576,1024]{1,0:T(8,128)(2,1)} %collective-permute-done.9.chip, bf16[576,1024]{1,0:T(8,128)(2,1)} %copy-done.21, ...), custom_call_target="tpu_custom_call" | custom-call | tf_op jit(solution)/shard_map/hidden_state/pallas_call | solution.py:346
  138.5 4.0 slice_bitcast_fusion
  142.5 5.9 place.4
  148.4 13.2 %convolution_convert_fusion.d_inner = bf16[1440,1024]{1,0:T(8,128)(2,1)} fusion(bf16[2304,1440]{1,0:T(8,128)(2,1)} %bitcast.170, bf16[1024,2304]{1,0:T(8,128)(2,1)} %copy-done.14), kind=kOutput, calls=%fused_computation.2 | convolution fusion | flops 6796247040 | bytes 14303232 | tf_op jit(solution)/shard_map/ef,te->ft/dot_general | solution.py:845
  161.6 5.7 collective-permute-done.17.chip
  167.3 3.2 collective-permute-done.20.both
  170.5 24.6 %inner_part.1 = (bf16[1440,1024]{1,0:T(8,128)(2,1)}, bf16[2,1440,1024]{2,1,0:T(8,128)(2,1)}, f32[1,1024]{1,0:T(1,128)S(1)}, f32[1,1024]{1,0:T(1,128)}, bf16[4,576,1024]{2,1,0:T(8,128)(2,1)}) custom-call(bf16[592,1024]{1,0:T(8,128)(2,1)} %get-tuple-element.134.own, bf16[592,1024]{1,0:T(8,128)(2,1)} %collective-permute-done.16.core, ...), custom_call_target="tpu_custom_call" | custom-call | tf_op jit(solution)/shard_map/inner_part/pallas_call | solution.py:420
  195.1 9.0 %whole_product.1 = bf16[4,576,960]{2,1,0:T(8,128)(2,1)} custom-call(bf16[4,576,1024]{2,1,0:T(8,128)(2,1)} %get-tuple-element.140.act, bf16[2880,1024]{1,0:T(8,128)(2,1)} %bitcast.133), custom_call_target="tpu_custom_call" | custom-call | tf_op jit(solution)/shard_map/whole_product/pallas_call | solution.py:513
  204.5 9.3 %half_product.8 = bf16[4,1,288,1920]{3,2,1,0:T(8,128)(2,1)} custom-call(s32[1]{0:T(128)} %bitcast.54.refs_0_, bf16[4,2,288,1024]{3,2,1,0:T(8,128)(2,1)} %bitcast.141, bf16[2880,1024]{1,0:T(8,128)(2,1)} %bitcast.134), custom_call_target="tpu_custom_call" | custom-call | tf_op jit(solution)/shard_map/half_product/pallas_call | solution.py:487
  215.4 26.7 %conditional.2 = (bf16[592,1024]{1,0:T(8,128)(2,1)}, bf16[592,1024]{1,0:T(8,128)(2,1)}) conditional(s32[]{:T(128)} %convert_element_type.88, () %tuple.73, (bf16[2304,1440]{1,0:T(8,128)(2,1)}, bf16[2304,1440]{1,0:T(8,128)(2,1)}, bf16[2880,1024]{1,0:T(8,128)(2,1)}, f32[1,1024]{1,0:T(1,128)S(1)}) %tuple.126), branch_computations={%region_0.1_spmd, %region_1.2_spmd} | conditional | flops 7 | bytes 9699496 | solution.py:145
  216.0 13.8 %feature_chunks.6 = (bf16[592,1024]{1,0:T(8,128)(2,1)}, bf16[592,1024]{1,0:T(8,128)(2,1)}) custom-call(s32[2]{0:T(128)} %pad_add_fusion.refs_0_, bf16[2304,1440]{1,0:T(8,128)(2,1)} %get-tuple-element.20.refs_1_, bf16[2304,1440]{1,0:T(8,128)(2,1)} %get-tuple-element.21.refs_2_, bf16[2880,1024]{1,0:T(8,128)(2,1)} %get-tuple-element.22.refs_3_, ...), custom_call_target="tpu_custom_call" | custom-call | tf_op jit(solution)/shard_map/cond/branch_1_fun/feature_chunks/pallas_call | solution.py:663
  230.4 2.9 collective-permute-done.refs_4_
  233.2 8.9 %feature_chunks.7 = bf16[592,1024]{1,0:T(8,128)(2,1)} custom-call(s32[1]{0:T(128)} %bitcast.refs_0_, bf16[2304,1440]{1,0:T(8,128)(2,1)} %get-tuple-element.20.refs_1_, bf16[2304,1440]{1,0:T(8,128)(2,1)} %get-tuple-element.21.refs_2_, bf16[2880,1024]{1,0:T(8,128)(2,1)} %get-tuple-element.22.refs_3_, bf16[592,1024]{1,0:T(8,128)(2,1)} %collective-permute-done.refs_4_, ...), custom_call_target="tpu_custom_call" | custom-call | tf_op jit(solution)/shard_map/cond/branch_1_fun/feature_chunks/pallas_call | solution.py:663
  242.1 9.4 %feature_chunks.8.refs_0_ = f32[592,1024]{1,0:T(8,128)} custom-call(s32[1]{0:T(128)} %bitcast.12.refs_0_, bf16[2304,1440]{1,0:T(8,128)(2,1)} %get-tuple-element.129.refs_1_, bf16[2304,1440]{1,0:T(8,128)(2,1)} %get-tuple-element.138.refs_2_, bf16[2880,1024]{1,0:T(8,128)(2,1)} %bitcast.136, bf16[592,1024]{1,0:T(8,128)(2,1)} %get-tuple-element.144.refs_4_, ...), custom_call_target="tpu_custom_call" | custom-call | tf_op jit(solution)/shard_map/feature_chunks/pallas_call | solution.py:663
  251.5 18.9 %collective-permute-done.22.refs_2_ = bf16[1440,1024]{1,0:T(8,128)(2,1)} collective-permute-done((bf16[1440,1024]{1,0:T(8,128)(2,1)}, bf16[1440,1024]{1,0:T(8,128)(2,1)}, u32[]{:S(2)}, u32[]{:S(2)}) %collective-permute-start.22) | collective-permute-done | bytes 2949152 | tf_op jit(solution)/shard_map/ppermute | solution.py:136
  272.7 3.5 collective-permute-done.23.refs_3_
  276.2 8.6 %place.5 = bf16[4,1440,1024]{2,1,0:T(8,128)(2,1)} custom-call(bf16[1440,1024]{1,0:T(8,128)(2,1)} %get-tuple-element.137.refs_0_, bf16[1440,1024]{1,0:T(8,128)(2,1)} %collective-permute-done.21.refs_1_, bf16[1440,1024]{1,0:T(8,128)(2,1)} %collective-permute-done.22.refs_2_, bf16[1440,1024]{1,0:T(8,128)(2,1)} %collective-permute-done.23.refs_3_), custom_call_target="tpu_custom_call" | custom-call | tf_op jit(solution)/shard_map/place/pallas_call | solution.py:181
  284.7 7.9 %half_product.9 = bf16[4,1,576,720]{3,2,1,0:T(8,128)(2,1)} custom-call(s32[1]{0:T(128)} %bitcast.54.refs_0_, bf16[4,2,720,1024]{3,2,1,0:T(8,128)(2,1)} %bitcast.138, bf16[576,1024]{1,0:T(8,128)(2,1)} %multiply_convert_fusion.refs_2_), custom_call_target="tpu_custom_call" | custom-call | tf_op jit(solution)/shard_map/half_product/pallas_call | solution.py:487
  292.7 7.2 %collective-permute-done.24.refs_1_ = bf16[592,1024]{1,0:T(8,128)(2,1)} collective-permute-done((bf16[592,1024]{1,0:T(8,128)(2,1)}, bf16[592,1024]{1,0:T(8,128)(2,1)}, u32[]{:S(2)}, u32[]{:S(2)}) %collective-permute-start.24) | collective-permute-done | bytes 1212448 | tf_op jit(solution)/shard_map/ppermute | solution.py:136
  299.8 6.2 attn_grad.1
  306.0 6.0 feature_chunks.9
  312.0 3.1 collective-permute-done.25.refs_3_
  316.1 3.9 feature_chunks.10
  320.0 10.1 %half_product.10 = bf16[4,1,288,1920]{3,2,1,0:T(8,128)(2,1)} custom-call(s32[1]{0:T(128)} %bitcast.57.refs_0_, bf16[4,2,288,1024]{3,2,1,0:T(8,128)(2,1)} %bitcast.142, bf16[2880,1024]{1,0:T(8,128)(2,1)} %bitcast.137, bf16[4,1,288,1920]{3,2,1,0:T(8,128)(2,1)} %collective-permute-done.26.refs_3_), custom_call_target="tpu_custom_call" | custom-call | tf_op jit(solution)/shard_map/half_product/pallas_call | solution.py:487
  332.2 2.7 collective-permute-done.27.refs_3_
  335.9 5.0 feature_chunks.11
  340.9 5.5 half_product.11
  346.4 13.9 %collective-permute-done.28 = bf16[576,1024]{1,0:T(8,128)(2,1)S(1)} collective-permute-done((bf16[576,1024]{1,0:T(8,128)(2,1)S(1)}, bf16[576,1024]{1,0:T(8,128)(2,1)S(1)}, u32[]{:S(2)}, u32[]{:S(2)}) %collective-permute-start.28) | collective-permute-done | bytes 1179680 | tf_op jit(solution)/shard_map/ppermute | solution.py:136
  361.3 25.9 %attention_backward.1 = (bf16[9,64,1024]{2,1,0:T(8,128)(2,1)S(1)}, bf16[9,64,1024]{2,1,0:T(8,128)(2,1)S(1)}, bf16[9,64,1024]{2,1,0:T(8,128)(2,1)S(1)}) custom-call(bf16[9,64,1024]{2,1,0:T(8,128)(2,1)} %get-tuple-element.147.q_ref, bf16[9,64,1024]{2,1,0:T(8,128)(2,1)} %get-tuple-element.148.k_ref, bf16[9,64,1024]{2,1,0:T(8,128)(2,1)} %get-tuple-element.149.v_ref, ...), custom_call_target="tpu_custom_call" | custom-call | tf_op jit(solution)/shard_map/attention_backward/pallas_call | solution.py:121
  387.2 8.9 %half_product.12 = bf16[4,3,288,576]{3,2,1,0:T(8,128)(2,1)} custom-call(s32[1]{0:T(128)} %bitcast.54.refs_0_, bf16[4,2,288,1024]{3,2,1,0:T(8,128)(2,1)} %bitcast.131, bf16[576,1024]{1,0:T(8,128)(2,1)S(1)} %bitcast.143, bf16[576,1024]{1,0:T(8,128)(2,1)S(1)} %bitcast.146, bf16[576,1024]{1,0:T(8,128)(2,1)S(1)} %bitcast.149), custom_call_target="tpu_custom_call" | custom-call | tf_op jit(solution)/shard_map/half_product/pallas_call | solution.py:487
  396.1 13.1 %collective-permute-done.29.refs_3_ = bf16[4,1,576,720]{3,2,1,0:T(8,128)(2,1)} collective-permute-done((bf16[4,1,576,720]{3,2,1,0:T(8,128)(2,1)}, bf16[4,1,576,720]{3,2,1,0:T(8,128)(2,1)}, u32[]{:S(2)}, u32[]{:S(2)}) %collective-permute-start.29) | collective-permute-done | bytes 3317792 | tf_op jit(solution)/shard_map/ppermute | solution.py:529
  409.1 8.5 %half_product.13 = bf16[4,1,576,720]{3,2,1,0:T(8,128)(2,1)} custom-call(s32[1]{0:T(128)} %bitcast.57.refs_0_, bf16[4,2,720,1024]{3,2,1,0:T(8,128)(2,1)} %bitcast.139, bf16[576,1024]{1,0:T(8,128)(2,1)} %multiply_convert_fusion.refs_2_, bf16[4,1,576,720]{3,2,1,0:T(8,128)(2,1)} %collective-permute-done.29.refs_3_), custom_call_target="tpu_custom_call" | custom-call | tf_op jit(solution)/shard_map/half_product/pallas_call | solution.py:487
  421.4 52.5 %conditional.3 = (f32[256,2304]{1,0:T(8,128)}, bf16[256,2304]{1,0:T(8,128)(2,1)}) conditional(s32[]{:T(128)} %convert_element_type.90, () %tuple.83, (bf16[2304,576]{0,1:T(8,128)(2,1)}, bf16[2304,576]{0,1:T(8,128)(2,1)}, bf16[2304,576]{0,1:T(8,128)(2,1)}, bf16[576,1024]{1,0:T(8,128)(2,1)S(1)}, bf16[576,1024]{1,0:T(8,128)(2,1)S(1)}, ...), branch_computations={%region_2.3_spmd, %region_3.4_spmd} | conditional | flops 7 | bytes 14155984 | solution.py:145
  422.0 12.7 %token_chunks.3 = (bf16[256,2304]{1,0:T(8,128)(2,1)}, bf16[256,2304]{1,0:T(8,128)(2,1)}) custom-call(s32[2]{0:T(128)} %pad_add_fusion.1.refs_0_, bf16[576,2304]{1,0:T(8,128)(2,1)} %bitcast.156, bf16[576,2304]{1,0:T(8,128)(2,1)} %bitcast.159, bf16[576,2304]{1,0:T(8,128)(2,1)} %bitcast.162, bf16[576,1024]{1,0:T(8,128)(2,1)S(1)} %get-tuple-element.29.refs_4_, ...), custom_call_target="tpu_custom_call" | custom-call | tf_op jit(solution)/shard_map/cond/branch_1_fun/token_chunks/pallas_call | solution.py:748
  435.2 2.7 collective-permute-done.2.refs_7_
  437.9 7.7 %token_chunks.4 = bf16[256,2304]{1,0:T(8,128)(2,1)} custom-call(s32[1]{0:T(128)} %bitcast.4.refs_0_, bf16[576,2304]{1,0:T(8,128)(2,1)} %bitcast.157, bf16[576,2304]{1,0:T(8,128)(2,1)} %bitcast.160, bf16[576,2304]{1,0:T(8,128)(2,1)} %bitcast.163, bf16[576,1024]{1,0:T(8,128)(2,1)S(1)} %get-tuple-element.29.refs_4_, ...), custom_call_target="tpu_custom_call" | custom-call | tf_op jit(solution)/shard_map/cond/branch_1_fun/token_chunks/pallas_call | solution.py:748
  445.8 8.2 %token_chunks.5 = f32[256,2304]{1,0:T(8,128)} custom-call(s32[1]{0:T(128)} %bitcast.3.refs_0_, bf16[576,2304]{1,0:T(8,128)(2,1)} %bitcast.158, bf16[576,2304]{1,0:T(8,128)(2,1)} %bitcast.161, bf16[576,2304]{1,0:T(8,128)(2,1)} %bitcast.164, bf16[576,1024]{1,0:T(8,128)(2,1)S(1)} %get-tuple-element.29.refs_4_, bf16[576,1024]{1,0:T(8,128)(2,1)S(1)} %get-tuple-element.30.refs_5_, ...), custom_call_target="tpu_custom_call" | custom-call | tf_op jit(solution)/shard_map/cond/branch_1_fun/token_chunks/pallas_call | solution.py:748
  454.1 19.8 %collective-permute-done.4 = bf16[256,2304]{1,0:T(8,128)(2,1)} collective-permute-done((bf16[256,2304]{1,0:T(8,128)(2,1)}, bf16[256,2304]{1,0:T(8,128)(2,1)}, u32[]{:S(2)}, u32[]{:S(2)}) %collective-permute-start.4) | collective-permute-done | bytes 1179680 | tf_op jit(solution)/shard_map/cond/branch_1_fun/ppermute | solution.py:136
  473.9 5.8 half_product.14
  479.7 12.3 %fusion.9 = bf16[576,1024]{1,0:T(8,128)(2,1)S(1)} fusion(f32[576,1024]{1,0:T(8,128)} %get-tuple-element.133.refs_3_, bf16[5760,576]{0,1:T(8,128)(2,1)} %param.25, bf16[5760,1024]{1,0:T(8,128)(2,1)} %bitcast.140), kind=kOutput, calls=%fused_computation.15 | convolution fusion | flops 6796541952 | bytes 21970944 | tf_op jit(solution)/shard_map/fe,ft->et/dot_general | solution.py:926
  499.7 3.0 collective-permute-done.33.refs_3_
  502.6 5.4 collective-permute-done.32.refs_2_
  509.1 3.5 fusion.7
  515.9 2.7 copy.28
  522.7 2.9 bitcast_convert_fusion
  525.6 3.1 copy.29
  528.7 4.9 fusion.6
  533.5 12.8 %collective-permute-done.43.refs_5_ = bf16[4,3,288,576]{3,2,1,0:T(8,128)(2,1)} collective-permute-done((bf16[4,3,288,576]{3,2,1,0:T(8,128)(2,1)}, bf16[4,3,288,576]{3,2,1,0:T(8,128)(2,1)}, u32[]{:S(2)}, u32[]{:S(2)}) %collective-permute-start.43) | collective-permute-done | bytes 3981344 | tf_op jit(solution)/shard_map/ppermute | solution.py:529
  546.4 9.5 %half_product.15 = bf16[4,3,288,576]{3,2,1,0:T(8,128)(2,1)} custom-call(s32[1]{0:T(128)} %bitcast.57.refs_0_, bf16[4,2,288,1024]{3,2,1,0:T(8,128)(2,1)} %bitcast.132, bf16[576,1024]{1,0:T(8,128)(2,1)S(1)} %bitcast.145, bf16[576,1024]{1,0:T(8,128)(2,1)S(1)} %bitcast.148, bf16[576,1024]{1,0:T(8,128)(2,1)} %bitcast.151, ...), custom_call_target="tpu_custom_call" | custom-call | tf_op jit(solution)/shard_map/half_product/pallas_call | solution.py:487
  563.5 11.7 %collective-permute-done.40 = f32[2,2304]{1,0:T(2,128)S(1)} collective-permute-done((f32[2,2304]{1,0:T(2,128)S(1)}, f32[2,2304]{1,0:T(2,128)S(1)}, u32[]{:S(2)}, u32[]{:S(2)}) %collective-permute-start.40) | collective-permute-done | bytes 18464 | tf_op jit(solution)/shard_map/ppermute | solution.py:594
  576.9 5.1 collective-permute-done.41
  583.3 5.2 collective-permute-done.42
  595.1 42.6 %reduce-scatter.14.cloned.1.call-done = bf16[1,3,288,576]{3,2,1,0:T(8,128)(2,1)} async-done(((bf16[4,3,288,576]{3,2,1,0:T(8,128)(2,1)}), bf16[1,3,288,576]{3,2,1,0:T(8,128)(2,1)}) %reduce-scatter.14.cloned.1.call-update) | async-done | bytes 995344 | tf_op jit(solution)/shard_map/reduce_scatter | solution.py:535
  637.7 2.6 fusion.10
  (203 shorter events, 95.9 us)
Async XLA Ops:
  7.2 131.3 %all-gather.2.cloned.1.call-start = ((), (), s32[]{:S(2)}) async-start(), calls=%async_computation.5 | async-start | bytes 3981312 | tf_op jit(solution)/shard_map/all_gather | solution.py:820
  7.2 3.9 collective-permute-start.5
  7.7 29.3 %collective-permute-start.6 = (bf16[256,2304]{1,0:T(8,128)(2,1)}, bf16[256,2304]{1,0:T(8,128)(2,1)S(1)}, u32[]{:S(2)}, u32[]{:S(2)}) collective-permute-start(bf16[256,2304]{1,0:T(8,128)(2,1)} %refs_1_.2), channel_id=1, source_target_pairs={{0,2},{1,3},{2,0},{3,1},{4,6},{5,7},{6,4},{7,5},{8,10},{9,11},{10,... | collective-permute-start | bytes 3538952 | tf_op jit(solution)/shard_map/ppermute | solution.py:136
  17.4 6.1 copy-start
  17.4 6.1 copy-start.18
  37.1 3.5 collective-permute-start.7
  38.4 18.1 %collective-permute-start.11 = (bf16[72,1440]{1,0:T(8,128)(2,1)S(1)}, bf16[72,1440]{1,0:T(8,128)(2,1)S(1)}, u32[]{:S(2)}, u32[]{:S(2)}) collective-permute-start(bf16[72,1440]{1,0:T(8,128)(2,1)S(1)} %get-tuple-element.120), channel_id=1, source_target_pairs={{0,2},{1,3},{2,0},{3,1},{4,6},{5,7},{6,4},{7,5},{8,10},{9,11},{10,... | collective-permute-start | bytes 622088 | tf_op jit(solution)/shard_map/ppermute | solution.py:136
  40.3 16.0 %collective-permute-start.12 = (bf16[72,1440]{1,0:T(8,128)(2,1)S(1)}, bf16[72,1440]{1,0:T(8,128)(2,1)S(1)}, u32[]{:S(2)}, u32[]{:S(2)}) collective-permute-start(bf16[72,1440]{1,0:T(8,128)(2,1)S(1)} %get-tuple-element.122), channel_id=1, source_target_pairs={{0,2},{1,3},{2,0},{3,1},{4,6},{5,7},{6,4},{7,5},{8,10},{9,11},{10,... | collective-permute-start | bytes 622088 | tf_op jit(solution)/shard_map/ppermute | solution.py:136
  42.9 4.4 copy-start.20
  47.3 3.6 copy-start.5
  47.3 3.7 copy-start.19
  53.6 4.9 copy-start.9
  56.2 1.5 collective-permute-start.19
  58.5 271.6 %reduce-scatter.6.cloned.1.call-start = ((), (), s32[]{:S(2)}) async-start(), calls=%async_computation.6 | async-start | bytes 5898240 | tf_op jit(solution)/shard_map/reduce_scatter | solution.py:535
  58.6 28.2 %collective-permute-start.13 = (bf16[256,2304]{1,0:T(8,128)(2,1)S(1)}, bf16[256,2304]{1,0:T(8,128)(2,1)S(1)}, u32[]{:S(2)}, u32[]{:S(2)}) collective-permute-start(bf16[256,2304]{1,0:T(8,128)(2,1)S(1)} %copy-done.9), channel_id=1, source_target_pairs={{0,2},{1,3},{2,0},{3,1},{4,6},{5,7},{6,4},{7,5},{8,10},{9,11},{10,... | collective-permute-start | bytes 3538952 | tf_op jit(solution)/shard_map/ppermute | solution.py:136
  60.5 29.4 %collective-permute-start.10 = (bf16[256,2304]{1,0:T(8,128)(2,1)S(1)}, bf16[256,2304]{1,0:T(8,128)(2,1)S(1)}, u32[]{:S(2)}, u32[]{:S(2)}) collective-permute-start(bf16[256,2304]{1,0:T(8,128)(2,1)S(1)} %copy-done.9), channel_id=1, source_target_pairs={{0,1},{1,0},{2,3},{3,2},{4,5},{5,4},{6,7},{7,6},{8,9},{9,8},{10,11... | collective-permute-start | bytes 3538952 | tf_op jit(solution)/shard_map/ppermute | solution.py:136
  86.8 4.0 collective-permute-start.14
  87.8 35.0 %collective-permute-start.9 = (bf16[576,1024]{1,0:T(8,128)(2,1)}, bf16[576,1024]{1,0:T(8,128)(2,1)}, u32[]{:S(2)}, u32[]{:S(2)}) collective-permute-start(bf16[576,1024]{1,0:T(8,128)(2,1)} %bitcast.172), channel_id=1, source_target_pairs={{0,2},{1,3},{2,0},{3,1},{4,6},{5,7},{6,4},{7,5},{8,10},{9,11},{10,... | collective-permute-start | bytes 3538952 | tf_op jit(solution)/shard_map/ppermute | solution.py:136
  89.6 35.6 %collective-permute-start.8 = (bf16[576,1024]{1,0:T(8,128)(2,1)}, bf16[576,1024]{1,0:T(8,128)(2,1)}, u32[]{:S(2)}, u32[]{:S(2)}) collective-permute-start(bf16[576,1024]{1,0:T(8,128)(2,1)} %bitcast.173), channel_id=1, source_target_pairs={{0,1},{1,0},{2,3},{3,2},{4,5},{5,4},{6,7},{7,6},{8,9},{9,8},{10,11... | collective-permute-start | bytes 3538952 | tf_op jit(solution)/shard_map/ppermute | solution.py:136
  99.3 172.0 %copy-start.6 = (f32[576,1024]{1,0:T(8,128)}, f32[576,1024]{1,0:T(8,128)S(1)}, u32[]{:S(2)}) copy-start(f32[576,1024]{1,0:T(8,128)S(1)} %get-tuple-element.151.refs_2_) | copy-start | bytes 7077892
  122.8 4.4 collective-permute-start.15
  123.5 19.0 %collective-permute-start.18 = (bf16[576,1440]{1,0:T(8,128)(2,1)}, bf16[576,1440]{1,0:T(8,128)(2,1)}, u32[]{:S(2)}, u32[]{:S(2)}) collective-permute-start(bf16[576,1440]{1,0:T(8,128)(2,1)} %get-tuple-element.186), channel_id=1, source_target_pairs={{0,1},{1,0},{2,3},{3,2},{4,5},{5,4},{6,7},{7,6},{8,9},{9,8},{10,11... | collective-permute-start | bytes 4976648 | tf_op jit(solution)/shard_map/ppermute | solution.py:136
  137.9 29.3 %collective-permute-start.17 = (bf16[592,1024]{1,0:T(8,128)(2,1)}, bf16[592,1024]{1,0:T(8,128)(2,1)}, u32[]{:S(2)}, u32[]{:S(2)}) collective-permute-start(bf16[592,1024]{1,0:T(8,128)(2,1)} %get-tuple-element.134.own), channel_id=1, source_target_pairs={{0,2},{1,3},{2,0},{3,1},{4,6},{5,7},{6,4},{7,5},{8,10},{9,11},{10,... | collective-permute-start | bytes 3637256 | tf_op jit(solution)/shard_map/ppermute | solution.py:136
  138.1 29.1 %collective-permute-start.16 = (bf16[592,1024]{1,0:T(8,128)(2,1)}, bf16[592,1024]{1,0:T(8,128)(2,1)}, u32[]{:S(2)}, u32[]{:S(2)}) collective-permute-start(bf16[592,1024]{1,0:T(8,128)(2,1)} %get-tuple-element.134.own), channel_id=1, source_target_pairs={{0,1},{1,0},{2,3},{3,2},{4,5},{5,4},{6,7},{7,6},{8,9},{9,8},{10,11... | collective-permute-start | bytes 3637256 | tf_op jit(solution)/shard_map/ppermute | solution.py:136
  167.3 3.2 collective-permute-start.20
  204.1 213.6 %reduce-scatter.8.cloned.1.call-start = ((), (), s32[]{:S(2)}) async-start(), calls=%async_computation.7 | async-start | bytes 5529600 | tf_op jit(solution)/shard_map/reduce_scatter | solution.py:535
  204.1 66.3 %collective-permute-start.22 = (bf16[1440,1024]{1,0:T(8,128)(2,1)}, bf16[1440,1024]{1,0:T(8,128)(2,1)}, u32[]{:S(2)}, u32[]{:S(2)}) collective-permute-start(bf16[1440,1024]{1,0:T(8,128)(2,1)} %get-tuple-element.137.refs_0_), channel_id=1, source_target_pairs={{0,2},{1,3},{2,0},{3,1},{4,6},{5,7},{6,4},{7,5},{8,10},{9,11},{10,... | collective-permute-start | bytes 8847368 | tf_op jit(solution)/shard_map/ppermute | solution.py:136
  213.8 106.3 %collective-permute-start.26 = (bf16[4,1,288,1920]{3,2,1,0:T(8,128)(2,1)}, bf16[4,1,288,1920]{3,2,1,0:T(8,128)(2,1)}, u32[]{:S(2)}, u32[]{:S(2)}) collective-permute-start(bf16[4,1,288,1920]{3,2,1,0:T(8,128)(2,1)} %half_product.8), channel_id=1, source_target_pairs={{0,4},{4,0},{8,12},{12,8},{16,20},{20,16},{24,28},{28,24},{1,5},{5... | collective-permute-start | bytes 13271048 | tf_op jit(solution)/shard_map/ppermute | solution.py:529
  215.4 57.2 %collective-permute-start.21 = (bf16[1440,1024]{1,0:T(8,128)(2,1)}, bf16[1440,1024]{1,0:T(8,128)(2,1)}, u32[]{:S(2)}, u32[]{:S(2)}) collective-permute-start(bf16[1440,1024]{1,0:T(8,128)(2,1)} %get-tuple-element.137.refs_0_), channel_id=1, source_target_pairs={{0,1},{1,0},{2,3},{3,2},{4,5},{5,4},{6,7},{7,6},{8,9},{9,8},{10,11... | collective-permute-start | bytes 8847368 | tf_op jit(solution)/shard_map/ppermute | solution.py:136
  229.8 3.5 collective-permute-start
  230.4 11.7 %collective-permute-start.1 = (bf16[592,1024]{1,0:T(8,128)(2,1)}, bf16[592,1024]{1,0:T(8,128)(2,1)}, u32[]{:S(2)}, u32[]{:S(2)}) collective-permute-start(bf16[592,1024]{1,0:T(8,128)(2,1)} %get-tuple-element.25), channel_id=1, source_target_pairs={{0,1},{1,0},{2,3},{3,2},{4,5},{5,4},{6,7},{7,6},{8,9},{9,8},{10,11... | collective-permute-start | bytes 3637256 | tf_op jit(solution)/shard_map/cond/branch_1_fun/ppermute | solution.py:136
  270.4 5.7 collective-permute-start.23
  270.4 29.4 %collective-permute-start.24 = (bf16[592,1024]{1,0:T(8,128)(2,1)}, bf16[592,1024]{1,0:T(8,128)(2,1)}, u32[]{:S(2)}, u32[]{:S(2)}) collective-permute-start(bf16[592,1024]{1,0:T(8,128)(2,1)} %get-tuple-element.150), channel_id=1, source_target_pairs={{0,2},{1,3},{2,0},{3,1},{4,6},{5,7},{6,4},{7,5},{8,10},{9,11},{10,... | collective-permute-start | bytes 3637256 | tf_op jit(solution)/shard_map/ppermute | solution.py:136
  312.0 3.1 collective-permute-start.25
  330.2 163.8 %reduce-scatter.10.cloned.1.call-start = ((), (), s32[]{:S(2)}) async-start(), calls=%async_computation.8 | async-start | bytes 4423680 | tf_op jit(solution)/shard_map/reduce_scatter | solution.py:535
  330.2 78.9 %collective-permute-start.29 = (bf16[4,1,576,720]{3,2,1,0:T(8,128)(2,1)}, bf16[4,1,576,720]{3,2,1,0:T(8,128)(2,1)}, u32[]{:S(2)}, u32[]{:S(2)}) collective-permute-start(bf16[4,1,576,720]{3,2,1,0:T(8,128)(2,1)} %half_product.9), channel_id=1, source_target_pairs={{0,4},{4,0},{8,12},{12,8},{16,20},{20,16},{24,28},{28,24},{1,5},{5... | collective-permute-start | bytes 9953288 | tf_op jit(solution)/shard_map/ppermute | solution.py:529
  331.9 3.1 collective-permute-start.27
  331.9 28.4 %collective-permute-start.28 = (bf16[576,1024]{1,0:T(8,128)(2,1)S(1)}, bf16[576,1024]{1,0:T(8,128)(2,1)S(1)}, u32[]{:S(2)}, u32[]{:S(2)}) collective-permute-start(bf16[576,1024]{1,0:T(8,128)(2,1)S(1)} %copy-done.22), channel_id=1, source_target_pairs={{0,2},{1,3},{2,0},{3,1},{4,6},{5,7},{6,4},{7,5},{8,10},{9,11},{10,... | collective-permute-start | bytes 3538952 | tf_op jit(solution)/shard_map/ppermute | solution.py:136
  387.2 8.9 %copy-start.15 = (bf16[9,64,1024]{2,1,0:T(8,128)(2,1)}, bf16[9,64,1024]{2,1,0:T(8,128)(2,1)S(1)}, u32[]{:S(2)}) copy-start(bf16[9,64,1024]{2,1,0:T(8,128)(2,1)S(1)} %get-tuple-element.165) | copy-start | bytes 3538948
  417.6 138.2 %reduce-scatter.12.cloned.1.call-start = ((), (), s32[]{:S(2)}) async-start(), calls=%async_computation.9 | async-start | bytes 1843200 | tf_op jit(solution)/shard_map/reduce_scatter | solution.py:535
  417.7 56.2 %collective-permute-start.30 = (bf16[4,1,288,576]{3,2,1,0:T(8,128)(2,1)}, bf16[4,1,288,576]{3,2,1,0:T(8,128)(2,1)}, u32[]{:S(2)}, u32[]{:S(2)}) collective-permute-start(bf16[4,1,288,576]{3,2,1,0:T(8,128)(2,1)} %half_product.11), channel_id=1, source_target_pairs={{0,4},{4,0},{8,12},{12,8},{16,20},{20,16},{24,28},{28,24},{1,5},{5... | collective-permute-start | bytes 3981320 | tf_op jit(solution)/shard_map/ppermute | solution.py:529
  420.3 126.1 %collective-permute-start.43 = (bf16[4,3,288,576]{3,2,1,0:T(8,128)(2,1)}, bf16[4,3,288,576]{3,2,1,0:T(8,128)(2,1)}, u32[]{:S(2)}, u32[]{:S(2)}) collective-permute-start(bf16[4,3,288,576]{3,2,1,0:T(8,128)(2,1)} %half_product.12), channel_id=1, source_target_pairs={{0,4},{4,0},{8,12},{12,8},{16,20},{20,16},{24,28},{28,24},{1,5},{5... | collective-permute-start | bytes 11943944 | tf_op jit(solution)/shard_map/ppermute | solution.py:529
  434.7 3.2 collective-permute-start.2
  434.7 11.2 %collective-permute-start.3 = (bf16[256,2304]{1,0:T(8,128)(2,1)}, bf16[256,2304]{1,0:T(8,128)(2,1)}, u32[]{:S(2)}, u32[]{:S(2)}) collective-permute-start(bf16[256,2304]{1,0:T(8,128)(2,1)} %get-tuple-element.34), channel_id=1, source_target_pairs={{0,1},{1,0},{2,3},{3,2},{4,5},{5,4},{6,7},{7,6},{8,9},{9,8},{10,11... | collective-permute-start | bytes 3538952 | tf_op jit(solution)/shard_map/cond/branch_1_fun/ppermute | solution.py:136
  445.6 28.3 %collective-permute-start.4 = (bf16[256,2304]{1,0:T(8,128)(2,1)}, bf16[256,2304]{1,0:T(8,128)(2,1)}, u32[]{:S(2)}, u32[]{:S(2)}) collective-permute-start(bf16[256,2304]{1,0:T(8,128)(2,1)} %token_chunks.4), channel_id=1, source_target_pairs={{0,2},{1,3},{2,0},{3,1},{4,6},{5,7},{6,4},{7,5},{8,10},{9,11},{10,... | collective-permute-start | bytes 3538952 | tf_op jit(solution)/shard_map/cond/branch_1_fun/ppermute | solution.py:136
  493.1 16.0 %copy-start.33 = (f32[2304]{0:T(1024)S(1)}, f32[2304]{0:T(1024)}, u32[]{:S(2)}) copy-start(f32[2304]{0:T(1024)} %param.17) | copy-start | bytes 27652
  493.1 9.6 %collective-permute-start.33 = (bf16[576,256]{1,0:T(8,128)(2,1)}, bf16[576,256]{1,0:T(8,128)(2,1)}, u32[]{:S(2)}, u32[]{:S(2)}) collective-permute-start(bf16[576,256]{1,0:T(8,128)(2,1)} %get-tuple-element.196), channel_id=1, source_target_pairs={{0,3},{1,2},{2,1},{3,0},{4,7},{5,6},{6,5},{7,4},{8,11},{9,10},{10,... | collective-permute-start | bytes 884744 | tf_op jit(solution)/shard_map/ppermute | solution.py:136
  493.1 14.9 %collective-permute-start.32 = (bf16[576,256]{1,0:T(8,128)(2,1)}, bf16[576,256]{1,0:T(8,128)(2,1)}, u32[]{:S(2)}, u32[]{:S(2)}) collective-permute-start(bf16[576,256]{1,0:T(8,128)(2,1)} %get-tuple-element.197), channel_id=1, source_target_pairs={{0,2},{1,3},{2,0},{3,1},{4,6},{5,7},{6,4},{7,5},{8,10},{9,11},{10,... | collective-permute-start | bytes 884744 | tf_op jit(solution)/shard_map/ppermute | solution.py:136
  494.0 143.7 %reduce-scatter.14.cloned.1.call-start = ((), (), s32[]{:S(2)}) async-start(), calls=%async_computation.10 | async-start | bytes 5529600 | tf_op jit(solution)/shard_map/reduce_scatter | solution.py:535
  494.1 14.0 %copy-start.32 = (bf16[576,256]{1,0:T(8,128)(2,1)S(1)}, bf16[576,256]{1,0:T(8,128)(2,1)}, u32[]{:S(2)}) copy-start(bf16[576,256]{1,0:T(8,128)(2,1)} %get-tuple-element.198) | copy-start | bytes 884740
  497.1 21.5 %collective-permute-start.36 = (bf16[576,256]{1,0:T(8,128)(2,1)}, bf16[576,256]{1,0:T(8,128)(2,1)}, u32[]{:S(2)}, u32[]{:S(2)}) collective-permute-start(bf16[576,256]{1,0:T(8,128)(2,1)} %get-tuple-element.192), channel_id=1, source_target_pairs={{0,3},{1,2},{2,1},{3,0},{4,7},{5,6},{6,5},{7,4},{8,11},{9,10},{10,... | collective-permute-start | bytes 884744 | tf_op jit(solution)/shard_map/ppermute | solution.py:136
  498.0 22.7 %collective-permute-start.35 = (bf16[576,256]{1,0:T(8,128)(2,1)}, bf16[576,256]{1,0:T(8,128)(2,1)}, u32[]{:S(2)}, u32[]{:S(2)}) collective-permute-start(bf16[576,256]{1,0:T(8,128)(2,1)} %get-tuple-element.193), channel_id=1, source_target_pairs={{0,2},{1,3},{2,0},{3,1},{4,6},{5,7},{6,4},{7,5},{8,10},{9,11},{10,... | collective-permute-start | bytes 884744 | tf_op jit(solution)/shard_map/ppermute | solution.py:136
  502.6 18.0 %collective-permute-start.34 = (bf16[576,256]{1,0:T(8,128)(2,1)}, bf16[576,256]{1,0:T(8,128)(2,1)}, u32[]{:S(2)}, u32[]{:S(2)}) collective-permute-start(bf16[576,256]{1,0:T(8,128)(2,1)} %get-tuple-element.194), channel_id=1, source_target_pairs={{0,1},{1,0},{2,3},{3,2},{4,5},{5,4},{6,7},{7,6},{8,9},{9,8},{10,11... | collective-permute-start | bytes 884744 | tf_op jit(solution)/shard_map/ppermute | solution.py:136
  508.0 5.1 collective-permute-start.31
  555.8 3.6 copy-start.25
  555.9 33.5 %copy-start.27 = (bf16[1,1,288,1920]{3,2,1,0:T(8,128)(2,1)S(1)}, bf16[1,1,288,1920]{3,2,1,0:T(8,128)(2,1)}, u32[]{:S(2)}) copy-start(bf16[1,1,288,1920]{3,2,1,0:T(8,128)(2,1)} %reduce-scatter.8.cloned.1.call-done) | copy-start | bytes 3317764
  557.2 3.9 collective-permute-start.38
  557.6 3.6 collective-permute-start.39
  557.6 3.6 collective-permute-start.37
  559.5 29.7 %collective-permute-start.44 = (bf16[288,960]{1,0:T(8,128)(2,1)S(1)}, bf16[288,960]{1,0:T(8,128)(2,1)S(1)}, u32[]{:S(2)}, u32[]{:S(2)}) collective-permute-start(bf16[288,960]{1,0:T(8,128)(2,1)S(1)} %dynamic-slice_bitcast_fusion.2), channel_id=1, source_target_pairs={{0,4},{4,0},{8,12},{12,8},{16,20},{20,16},{24,28},{28,24},{1,5},{5... | collective-permute-start | bytes 1658888 | tf_op jit(solution)/shard_map/ppermute | solution.py:529
  561.9 13.2 %collective-permute-start.40 = (f32[2,2304]{1,0:T(2,128)S(1)}, f32[2,2304]{1,0:T(2,128)S(1)}, u32[]{:S(2)}, u32[]{:S(2)}) collective-permute-start(f32[2,2304]{1,0:T(2,128)S(1)} %add_add_fusion), channel_id=1, source_target_pairs={{0,4},{4,0},{8,12},{12,8},{16,20},{20,16},{24,28},{28,24},{1,5},{5... | collective-permute-start | bytes 55304 | tf_op jit(solution)/shard_map/ppermute | solution.py:594
  575.2 6.8 %collective-permute-start.41 = (f32[2,2304]{1,0:T(2,128)S(1)}, f32[2,2304]{1,0:T(2,128)S(1)}, u32[]{:S(2)}, u32[]{:S(2)}) collective-permute-start(f32[2,2304]{1,0:T(2,128)S(1)} %add.155), channel_id=1, source_target_pairs={{0,8},{4,12},{8,0},{12,4},{16,24},{20,28},{24,16},{28,20},{1,9},{5... | collective-permute-start | bytes 55304 | tf_op jit(solution)/shard_map/ppermute | solution.py:594
  582.0 6.6 %collective-permute-start.42 = (f32[2,2304]{1,0:T(2,128)S(1)}, f32[2,2304]{1,0:T(2,128)S(1)}, u32[]{:S(2)}, u32[]{:S(2)}) collective-permute-start(f32[2,2304]{1,0:T(2,128)S(1)} %add.156), channel_id=1, source_target_pairs={{0,16},{4,20},{8,24},{12,28},{16,0},{20,4},{24,8},{28,12},{1,17},{... | collective-permute-start | bytes 55304 | tf_op jit(solution)/shard_map/ppermute | solution.py:594
  591.2 3.0 copy-start.29
  (22 other events, 33.1 us)
Sparse Core Ops, SparseCore 0:
  58.7 66.7 all-gather.1
  204.2 85.5 reduce-scatter.5
  330.3 80.7 reduce-scatter.7
  417.8 66.7 reduce-scatter.9
  494.1 34.1 reduce-scatter.11
  556.0 81.6 reduce-scatter.13

commit v4 on v3

--- a/solution.py
+++ b/solution.py
@@ -56,10 +56,8 @@
         top = jnp.max(scores, axis=0, keepdims=True)
         expo = jnp.exp(scores - top)
         total = jnp.sum(expo, axis=0, keepdims=True)
-        probs = (expo * (1.0 / total)).astype(low)
-        out_ref[0, :, cols] = jnp.dot(
-            v_low[:, :kv], probs, preferred_element_type=full
-        ).astype(low)
+        mixed = jnp.dot(v_low[:, :kv], expo.astype(low), preferred_element_type=full)
+        out_ref[0, :, cols] = (mixed * (1.0 / total)).astype(low)
         lse_ref[0, :, cols] = top + jnp.log(total)
 
 
@@ -172,7 +170,7 @@
         copy.wait()
 
 
-def place(blocks, parts=1):
+def place(blocks, parts=1, limit=60):
     count = len(blocks)
     size = count // parts
     rows = sum(block.shape[0] for block in blocks[:parts])
@@ -188,7 +186,7 @@
             pltpu.SemaphoreType.DMA((count,)),
             pltpu.SemaphoreType.DMA((size,)),
         ],
-        compiler_params=pltpu.CompilerParams(vmem_limit_bytes=60 * 2**20),
+        compiler_params=pltpu.CompilerParams(vmem_limit_bytes=limit * 2**20),
         cost_estimate=SMALL,
         name="place",
     )(*blocks)
@@ -294,7 +292,7 @@
 
 
 def hidden_kernel(
-    own, core, chip, both, weight, tokens, gain, hidden_ref, scaled_ref, all_ref,
+    own, core, chip, both, weight, tokens, gain, hidden_ref, first_ref, second_ref, all_ref,
     squares_ref, held, arrived, left,
 ):
     step = pl.program_id(0)
@@ -313,7 +311,10 @@
     tile = hidden.shape[0]
     at = pl.multiple_of(step * tile, tile)
     hidden_ref[pl.ds(at, tile), :] = hidden
-    scaled_ref[pl.ds(at, tile), :] = (hidden * gain[...]).astype(low)
+    part = span // 2
+    halves = [(first_ref, slice(0, part)), (second_ref, slice(part, span))]
+    for ref, cut in halves:
+        ref[pl.ds(at, tile), :] = (hidden[:, cut] * gain[...]).astype(low)
     squares = jnp.sum(hidden * hidden, axis=0, keepdims=True)
 
     @pl.when(step == 0)
@@ -330,8 +331,9 @@
         high = total.astype(low)
         rest = (total - high.astype(full)).astype(low)
         cols = hidden_ref.shape[0]
-        scaled_ref[cols : cols + 8] = jnp.broadcast_to(high, (8, high.shape[1]))
-        scaled_ref[cols + 8 :] = jnp.broadcast_to(rest, (8, high.shape[1]))
+        for ref, cut in halves:
+            ref[cols : cols + 8] = jnp.broadcast_to(high[:, cut], (8, part))
+            ref[cols + 8 :] = jnp.broadcast_to(rest[:, cut], (8, part))
         out.wait()
 
 
@@ -343,14 +345,16 @@
     hbm = pl.BlockSpec(memory_space=pl.ANY)
     rows = lambda wide: pl.BlockSpec((tile, wide), lambda i: (i, 0))
     const = lambda shape: pl.BlockSpec(shape, lambda i: (0, 0))
-    hidden, scaled, whole = pl.pallas_call(
+    half = const((cols + 16, span // 2))
+    hidden, first, second, whole = pl.pallas_call(
         hidden_kernel,
         grid=(tiles,),
         in_specs=[hbm] * 4 + [rows(size * cols), rows(span), rows(1)],
-        out_specs=[const((cols, span)), const((cols + 16, span)), hbm],
+        out_specs=[const((cols, span)), half, half, hbm],
         out_shape=[
             jax.ShapeDtypeStruct((cols, span), full),
-            jax.ShapeDtypeStruct((cols + 16, span), low),
+            jax.ShapeDtypeStruct((cols + 16, span // 2), low),
+            jax.ShapeDtypeStruct((cols + 16, span // 2), low),
             jax.ShapeDtypeStruct((size, cols, span), low),
         ],
         scratch_shapes=[
@@ -363,20 +367,21 @@
         cost_estimate=SMALL,
         name="hidden_state",
     )(*blocks, weight, tokens, gain)
-    return hidden, scaled, whole.reshape(size * cols, span)
-
-
-def inner_kernel(
-    own, core, chip, both, w_gate, w_up, d_inner, inner_ref, grads_ref, mean_ref, factor_ref,
-    all_ref, held, rest, arrived, left,
-):
+    return hidden, first, second, whole.reshape(size * cols, span)
+
+
+def inner_kernel(*refs, half):
+    blocks, (w_gate, w_up, d_inner), refs = refs[:4], refs[4:7], refs[7:]
+    inner_ref, grads_ref, mean_ref, factor_ref, all_ref, held, rest, arrived, left = refs[5 * half :]
     step = pl.program_id(0)
-    out = pltpu.make_async_copy(held, all_ref, left.at[0])
     span = held.shape[2]
+    out = pltpu.make_async_copy(
+        held, all_ref.at[:, :, pl.ds(half * span, span)], left.at[0]
+    )
 
     @pl.when(step == 0)
     def _():
-        bring((own, core, chip, both), held, arrived, rest)
+        bring(blocks, held, arrived, rest)
         out.start()
         squares = [
             rest[j, 0:1].astype(full) + rest[j, 8:9].astype(full) for j in range(held.shape[0])
@@ -386,8 +391,8 @@
 
         mean_ref[...] = jnp.zeros_like(mean_ref)
 
-    wide = span // 4
-    for part in range(4):
+    wide = BLK
+    for part in range(span // wide):
         cut = slice(part * wide, (part + 1) * wide)
         scaled = held[:, :, cut].reshape(-1, wide)
         factor = factor_ref[:, cut]
@@ -408,27 +413,29 @@
         out.wait()
 
 
-def inner_part(blocks, w_gate, w_up, d_inner):
+def inner_part(half, blocks, w_gate, w_up, d_inner, before=()):
     tall, span = blocks[0].shape
     cols = tall - 16
     size = len(blocks)
     units = w_gate.shape[0]
     tile = units // 3
     hbm = pl.BlockSpec(memory_space=pl.ANY)
-    rows = lambda wide: pl.BlockSpec((tile, wide), lambda i: (i, 0))
-    row = pl.BlockSpec((1, span), lambda i: (0, 0))
-    inner, grads, mean, factor, whole = pl.pallas_call(
-        inner_kernel,
+    weight = pl.BlockSpec((tile, size * cols), lambda i: (i, 0))
+    part = pl.BlockSpec((tile, span), lambda i: (i, half))
+    row = pl.BlockSpec((1, span), lambda i: (0, half))
+    return pl.pallas_call(
+        lambda *refs: inner_kernel(*refs, half=half),
         grid=(units // tile,),
-        in_specs=[hbm] * 4 + [rows(size * cols), rows(size * cols), rows(span)],
-        out_specs=[rows(span), pl.BlockSpec((2, tile, span), lambda i: (0, i, 0)), row, row, hbm],
+        in_specs=[hbm] * 4 + [weight, weight, part] + [hbm] * len(before),
+        out_specs=[part, pl.BlockSpec((2, tile, span), lambda i: (0, i, half)), row, row, hbm],
         out_shape=[
-            jax.ShapeDtypeStruct((units, span), low),
-            jax.ShapeDtypeStruct((2, units, span), low),
-            jax.ShapeDtypeStruct((1, span), full),
-            jax.ShapeDtypeStruct((1, span), full),
-            jax.ShapeDtypeStruct((size, cols, span), low),
+            jax.ShapeDtypeStruct((units, 2 * span), low),
+            jax.ShapeDtypeStruct((2, units, 2 * span), low),
+            jax.ShapeDtypeStruct((1, 2 * span), full),
+            jax.ShapeDtypeStruct((1, 2 * span), full),
+            jax.ShapeDtypeStruct((size, cols, 2 * span), low),
         ],
+        input_output_aliases={7 + i: i for i in range(len(before))},
         scratch_shapes=[
             pltpu.VMEM((size, cols, span), low),
             pltpu.VMEM((size, 16, span), low),
@@ -438,8 +445,7 @@
         compiler_params=pltpu.CompilerParams(vmem_limit_bytes=60 * 2**20),
         cost_estimate=SMALL,
         name="inner_part",
-    )(*blocks, w_gate, w_up, d_inner)
-    return inner, grads.reshape(2 * units, span), mean, factor, whole.reshape(size * cols, span)
+    )(*blocks, w_gate, w_up, d_inner, *before)
 
 
 def to_rows(field, rows):
@@ -840,14 +846,27 @@
     attended_blocks = gather(attended.reshape(width_cols, span), out_tall)
 
     gain_own = own_gain(gain_ffn)
-    hidden, scaled, attended_all = hidden_state(attended_blocks, w_out.T, tokens_own, gain_own)
-    down_own = place([after(down_near[0], scaled), down_near[1], parts_all[0], parts_all[1]])
+    hidden, scaled_first, scaled_second, attended_all = hidden_state(
+        attended_blocks, w_out.T, tokens_own, gain_own
+    )
+    scaled_chip = swap(scaled_first, 2)
+
+    down_own = place(
+        [after(down_near[0], hidden), down_near[1], parts_all[0], parts_all[1]], limit=16
+    )
     d_inner = jnp.einsum("ef,te->ft", down_own, d_ffn, preferred_element_type=full).astype(low)
-    scaled_blocks = gather(scaled, d_inner)
-
+    scaled_chip = after(scaled_chip, d_inner)
+    scaled_first = [scaled_first, swap(scaled_first, 1), scaled_chip, swap(scaled_chip, 1)]
+    second_chip = swap(after(scaled_second, scaled_chip), 2)
+
+    first = stage(lambda: inner_part(0, scaled_first, w_gate.T, w_up.T, d_inner), d_inner)
+    second_chip = after(second_chip, first[2])
+    scaled_second = [scaled_second, swap(scaled_second, 1), second_chip, swap(second_chip, 1)]
     inner, ffn_grads, mean, factor, scaled_all = inner_part(
-        scaled_blocks, w_gate.T, w_up.T, d_inner
-    )
+        1, scaled_second, w_gate.T, w_up.T, d_inner, first
+    )
+    ffn_grads = ffn_grads.reshape(2 * hidden_cols, span)
+    scaled_all = scaled_all.reshape(width, span)
 
     third = 2 * hidden_cols // 3
     sum_most = GradSum(scaled_all, [ffn_grads], columns=2 * third)

time: 657 us -> 650 us (0.989)
    ppermute x37 -> x40, starting transfers between devices: 19.6 us -> 24.5 us  [swap(): return lax.ppermute(array, 'fsdp', [(i, i ^ j) for i in range(size)])]
    pallas_call x1 -> x2, Pallas kernels: 24.6 us -> 29.2 us  [inner_part(): pl.pallas_call(lambda *refs: inner_kernel(*refs, half=half), grid=(units...]
    ppermute x37 -> x40, waiting for transfers between devices: 108 us -> 103 us  [swap(): return lax.ppermute(array, 'fsdp', [(i, i ^ j) for i in range(size)])]
    unnamed x70 -> x78, local copies, waits for them, and re-layouts: 19.6 us -> 19 us
  transfers between devices with their start and end apart: 51 -> 54, of which waited for: 24 -> 28; matrix products, arithmetic and copies ran while one was open for 14% -> 13% of each run, Pallas kernels for 39% -> 41%
where the time goes in v4:
time: 650 us; the launch traced here: 641 us
  Pallas kernels  284 us (44%)
  waiting for transfers between devices  196 us (30%)
  local copies, waits for them, and re-layouts  41.7 us (6%)
  matrix products  41.3 us (6%)
  starting transfers between devices  38.2 us (6%)
  other arithmetic  25.1 us (4%)
  between operations  15.1 us (2%)
    ppermute x40, waiting for transfers between devices, swap(): return lax.ppermute(array, 'fsdp', [(i, i ^ j) for i in range(size)])  103 us
    pallas_call x8, Pallas kernels, half_product(): pl.pallas_call(lambda *refs: product_kernel(*refs, count=count, adds=adde...  65.3 us
    reduce_scatter x5, waiting for transfers between devices, line_scatter(): lax.psum_scatter(array, 'rep', scatter_dimension=0, tiled=True, axis_inde...  48.8 us
    pallas_call x6, Pallas kernels, feature_chunks(): pl.pallas_call(lambda *refs: chunks_kernel(*refs, count=len(weights), way...  46.7 us
    pallas_call x2, Pallas kernels, inner_part(): pl.pallas_call(lambda *refs: inner_kernel(*refs, half=half), grid=(units...  29.2 us
    pallas_call x3, Pallas kernels, token_chunks(): pl.pallas_call(lambda *refs: blocks_kernel(*refs, count=len(weights), add...  28.5 us
    pallas_call x1, Pallas kernels, attention_backward(): pl.pallas_call(backward_kernel, grid=(heads,), in_specs=[spec, spec, spec...  25.9 us
    ppermute x40, starting transfers between devices, swap(): return lax.ppermute(array, 'fsdp', [(i, i ^ j) for i in range(size)])  24.5 us
  transfers between devices with their start and end apart: 54, of which 28 were waited for; matrix products, arithmetic and copies ran while one was open for 13% of the time, Pallas kernels for 41%

profile of v4, /device:TPU:0, one launch (start us, length us, event | category | flops | bytes accessed | tf_op | source)
XLA Modules:
  0.0 641.3 jit_solution(3243317185916706560)
XLA Ops:
  14.7 2.7 spread.3
  17.4 6.1 fusion.13
  26.0 2.6 fusion.15
  28.6 8.5 %collective-permute-done.6.refs_1_ = bf16[256,2304]{1,0:T(8,128)(2,1)S(1)} collective-permute-done((bf16[256,2304]{1,0:T(8,128)(2,1)}, bf16[256,2304]{1,0:T(8,128)(2,1)S(1)}, u32[]{:S(2)}, u32[]{:S(2)}) %collective-permute-start.6) | collective-permute-done | bytes 1179680 | tf_op jit(solution)/shard_map/ppermute | solution.py:134
  42.9 4.4 spread.4
  51.0 2.6 fusion.17
  53.7 2.7 fusion.18
  61.8 20.6 %attention_forward.1 = (bf16[9,64,1024]{2,1,0:T(8,128)(2,1)}, bf16[9,64,1024]{2,1,0:T(8,128)(2,1)}, bf16[9,64,1024]{2,1,0:T(8,128)(2,1)}, bf16[9,64,1024]{2,1,0:T(8,128)(2,1)}, f32[9,1,1024]{2,1,0:T(1,128)}) custom-call(f32[9,64,512]{2,1,0:T(8,128)} %bitcast.181, f32[9,64,512]{2,1,0:T(8,128)} %bitcast.182, f32[9,64,512]{2,1,0:T(8,128)} %bitcast.183, ...), custom_call_target="tpu_custom_call" | custom-call | tf_op jit(solution)/shard_map/attention_forward/pallas_call | solution.py:72
  82.5 4.4 collective-permute-done.13.refs_3_
  93.7 3.6 spread.5
  99.4 6.5 %dynamic-slice_bitcast_fusion = (bf16[576,1440]{1,0:T(8,128)(2,1)}, bf16[576,1440]{1,0:T(8,128)(2,1)}) fusion(bf16[5760,576]{0,1:T(8,128)(2,1)} %param.27, s32[]{:T(128)S(6)} %select_n.105, s32[]{:T(128)S(6)} %select_n.103), kind=kLoop, calls=%fused_computation.22 | loop fusion | bytes 6635528 | tf_op jit(solution)/shard_map/dynamic_slice | solution.py:839
  105.9 11.5 %flip.2 = (bf16[2304,1440]{1,0:T(8,128)(2,1)}, bf16[2304,1440]{1,0:T(8,128)(2,1)}) custom-call(s32[1]{0:T(128)} %constant.133.clone.1.index, bf16[1440,2304]{1,0:T(8,128)(2,1)} %bitcast.148, bf16[1440,2304]{1,0:T(8,128)(2,1)} %bitcast.151), custom_call_target="tpu_custom_call" | custom-call | tf_op jit(solution)/shard_map/flip/pallas_call | solution.py:617
  117.3 5.6 flip.3.refs_1_
  128.3 9.3 %hidden_state.1 = (f32[576,1024]{1,0:T(8,128)}, bf16[592,512]{1,0:T(8,128)(2,1)}, bf16[592,512]{1,0:T(8,128)(2,1)}, bf16[4,576,1024]{2,1,0:T(8,128)(2,1)}) custom-call(bf16[576,1024]{1,0:T(8,128)(2,1)} %bitcast.180, bf16[576,1024]{1,0:T(8,128)(2,1)} %collective-permute-done.8.core, bf16[576,1024]{1,0:T(8,128)(2,1)} %collective-permute-done.9.chip, ...), custom_call_target="tpu_custom_call" | custom-call | tf_op jit(solution)/shard_map/hidden_state/pallas_call | solution.py:349
  140.7 3.1 place.4
  143.9 9.6 %convolution_convert_fusion.refs_6_ = bf16[1440,1024]{1,0:T(8,128)(2,1)} fusion(bf16[2304,1440]{1,0:T(8,128)(2,1)S(1)} %bitcast.135, bf16[1024,2304]{1,0:T(8,128)(2,1)S(1)} %bitcast.137), kind=kOutput, calls=%fused_computation.2 | convolution fusion | flops 6796247040 | bytes 14303232 | tf_op jit(solution)/shard_map/ef,te->ft/dot_general | solution.py:857
  156.4 14.6 %conditional.3 = ((bf16[1440,1024]{1,0:T(8,128)(2,1)}, bf16[2,1440,1024]{2,1,0:T(8,128)(2,1)}, f32[1,1024]{1,0:T(1,128)S(1)}, f32[1,1024]{1,0:T(1,128)S(1)}, bf16[4,576,1024]{2,1,0:T(8,128)(2,1)})) conditional(s32[]{:T(128)} %convert_element_type.91, () %tuple.83, (bf16[2304,1440]{0,1:T(8,128)(2,1)}, bf16[2304,1440]{0,1:T(8,128)(2,1)}, ...), branch_computations={%region_0.1_spmd, %region_1.2_spmd} | conditional | bytes 13574206 | solution.py:143
  156.4 14.6 %inner_part.2 = (bf16[1440,1024]{1,0:T(8,128)(2,1)}, bf16[2,1440,1024]{2,1,0:T(8,128)(2,1)}, f32[1,1024]{1,0:T(1,128)S(1)}, f32[1,1024]{1,0:T(1,128)S(1)}, bf16[4,576,1024]{2,1,0:T(8,128)(2,1)}) custom-call(bf16[592,512]{1,0:T(8,128)(2,1)} %get-tuple-element.34.refs_0_, bf16[592,512]{1,0:T(8,128)(2,1)} %get-tuple-element.35.refs_1_, ...), custom_call_target="tpu_custom_call" | custom-call | tf_op jit(solution)/shard_map/cond/branch_1_fun/inner_part/pallas_call | solution.py:426
  173.4 14.6 %inner_part.3 = (bf16[1440,1024]{1,0:T(8,128)(2,1)}, bf16[2,1440,1024]{2,1,0:T(8,128)(2,1)}, f32[1,1024]{1,0:T(1,128)S(1)}, f32[1,1024]{1,0:T(1,128)S(1)}, bf16[4,576,1024]{2,1,0:T(8,128)(2,1)}) custom-call(bf16[592,512]{1,0:T(8,128)(2,1)} %get-tuple-element.168.refs_0_, ...), custom_call_target="tpu_custom_call", output_to_operand_aliasing={{0}: (7, {}), {1}: (8, {}), {2}: (9, {}), {3}: (10, {}), {4... | custom-call | tf_op jit(solution)/shard_map/inner_part/pallas_call | solution.py:426
  188.0 9.0 %whole_product.1 = bf16[4,576,960]{2,1,0:T(8,128)(2,1)} custom-call(bf16[4,576,1024]{2,1,0:T(8,128)(2,1)} %get-tuple-element.179.act, bf16[2880,1024]{1,0:T(8,128)(2,1)} %bitcast.138), custom_call_target="tpu_custom_call" | custom-call | tf_op jit(solution)/shard_map/whole_product/pallas_call | solution.py:519
  198.3 9.3 %half_product.8 = bf16[4,1,288,1920]{3,2,1,0:T(8,128)(2,1)} custom-call(s32[1]{0:T(128)} %bitcast.56.refs_0_, bf16[4,2,288,1024]{3,2,1,0:T(8,128)(2,1)} %bitcast.143, bf16[2880,1024]{1,0:T(8,128)(2,1)} %bitcast.139), custom_call_target="tpu_custom_call" | custom-call | tf_op jit(solution)/shard_map/half_product/pallas_call | solution.py:493
  209.3 26.7 %conditional.4 = (bf16[592,1024]{1,0:T(8,128)(2,1)}, bf16[592,1024]{1,0:T(8,128)(2,1)}) conditional(s32[]{:T(128)} %convert_element_type.92, () %tuple.88, (bf16[2304,1440]{1,0:T(8,128)(2,1)}, bf16[2304,1440]{1,0:T(8,128)(2,1)}, bf16[2880,1024]{1,0:T(8,128)(2,1)}, f32[1,1024]{1,0:T(1,128)S(1)}) %tuple.145), branch_computations={%region_2.3_spmd, %region_3.4_spmd} | conditional | flops 7 | bytes 9699496 | solution.py:143
  209.8 13.8 %feature_chunks.6 = (bf16[592,1024]{1,0:T(8,128)(2,1)}, bf16[592,1024]{1,0:T(8,128)(2,1)}) custom-call(s32[2]{0:T(128)} %pad_add_fusion.refs_0_, bf16[2304,1440]{1,0:T(8,128)(2,1)} %get-tuple-element.41.refs_1_, bf16[2304,1440]{1,0:T(8,128)(2,1)} %get-tuple-element.42.refs_2_, bf16[2880,1024]{1,0:T(8,128)(2,1)} %get-tuple-element.43.refs_3_, ...), custom_call_target="tpu_custom_call" | custom-call | tf_op jit(solution)/shard_map/cond/branch_1_fun/feature_chunks/pallas_call | solution.py:669
  224.2 2.9 collective-permute-done.refs_4_
  227.1 8.9 %feature_chunks.7 = bf16[592,1024]{1,0:T(8,128)(2,1)} custom-call(s32[1]{0:T(128)} %bitcast.2.refs_0_, bf16[2304,1440]{1,0:T(8,128)(2,1)} %get-tuple-element.41.refs_1_, bf16[2304,1440]{1,0:T(8,128)(2,1)} %get-tuple-element.42.refs_2_, bf16[2880,1024]{1,0:T(8,128)(2,1)} %get-tuple-element.43.refs_3_, bf16[592,1024]{1,0:T(8,128)(2,1)} %collective-permute-done.refs_4_, ...), custom_call_target="tpu_custom_call" | custom-call | tf_op jit(solution)/shard_map/cond/branch_1_fun/feature_chunks/pallas_call | solution.py:669
  236.0 9.3 %feature_chunks.8.refs_0_ = f32[592,1024]{1,0:T(8,128)} custom-call(s32[1]{0:T(128)} %bitcast.14.refs_0_, bf16[2304,1440]{1,0:T(8,128)(2,1)} %get-tuple-element.159.refs_1_, bf16[2304,1440]{1,0:T(8,128)(2,1)} %get-tuple-element.177.refs_2_, bf16[2880,1024]{1,0:T(8,128)(2,1)} %bitcast.141, bf16[592,1024]{1,0:T(8,128)(2,1)} %get-tuple-element.183.refs_4_, ...), custom_call_target="tpu_custom_call" | custom-call | tf_op jit(solution)/shard_map/feature_chunks/pallas_call | solution.py:669
  245.3 18.1 %collective-permute-done.25.refs_2_ = bf16[1440,1024]{1,0:T(8,128)(2,1)} collective-permute-done((bf16[1440,1024]{1,0:T(8,128)(2,1)}, bf16[1440,1024]{1,0:T(8,128)(2,1)}, u32[]{:S(2)}, u32[]{:S(2)}) %collective-permute-start.25) | collective-permute-done | bytes 2949152 | tf_op jit(solution)/shard_map/ppermute | solution.py:134
  269.1 8.4 %place.5 = bf16[4,1440,1024]{2,1,0:T(8,128)(2,1)} custom-call(bf16[1440,1024]{1,0:T(8,128)(2,1)} %get-tuple-element.176.refs_0_, bf16[1440,1024]{1,0:T(8,128)(2,1)} %collective-permute-done.24.refs_1_, bf16[1440,1024]{1,0:T(8,128)(2,1)} %collective-permute-done.25.refs_2_, bf16[1440,1024]{1,0:T(8,128)(2,1)} %collective-permute-done.26.refs_3_), custom_call_target="tpu_custom_call" | custom-call | tf_op jit(solution)/shard_map/place/pallas_call | solution.py:179
  277.5 7.9 %half_product.9 = bf16[4,1,576,720]{3,2,1,0:T(8,128)(2,1)} custom-call(s32[1]{0:T(128)} %bitcast.56.refs_0_, bf16[4,2,720,1024]{3,2,1,0:T(8,128)(2,1)} %bitcast.145, bf16[576,1024]{1,0:T(8,128)(2,1)} %multiply_convert_fusion.refs_2_), custom_call_target="tpu_custom_call" | custom-call | tf_op jit(solution)/shard_map/half_product/pallas_call | solution.py:493
  285.4 7.4 %collective-permute-done.27.refs_1_ = bf16[592,1024]{1,0:T(8,128)(2,1)} collective-permute-done((bf16[592,1024]{1,0:T(8,128)(2,1)}, bf16[592,1024]{1,0:T(8,128)(2,1)}, u32[]{:S(2)}, u32[]{:S(2)}) %collective-permute-start.27) | collective-permute-done | bytes 1212448 | tf_op jit(solution)/shard_map/ppermute | solution.py:134
  292.8 6.2 attn_grad.1
  299.0 6.0 feature_chunks.9
  305.0 3.1 collective-permute-done.28.refs_3_
  309.0 3.9 feature_chunks.10
  313.0 10.1 %half_product.10 = bf16[4,1,288,1920]{3,2,1,0:T(8,128)(2,1)} custom-call(s32[1]{0:T(128)} %bitcast.59.refs_0_, bf16[4,2,288,1024]{3,2,1,0:T(8,128)(2,1)} %bitcast.144, bf16[2880,1024]{1,0:T(8,128)(2,1)} %bitcast.142, bf16[4,1,288,1920]{3,2,1,0:T(8,128)(2,1)} %collective-permute-done.29.refs_3_), custom_call_target="tpu_custom_call" | custom-call | tf_op jit(solution)/shard_map/half_product/pallas_call | solution.py:493
  328.9 4.8 feature_chunks.11
  333.7 5.5 half_product.11
  339.2 14.0 %collective-permute-done.31 = bf16[576,1024]{1,0:T(8,128)(2,1)S(1)} collective-permute-done((bf16[576,1024]{1,0:T(8,128)(2,1)S(1)}, bf16[576,1024]{1,0:T(8,128)(2,1)S(1)}, u32[]{:S(2)}, u32[]{:S(2)}) %collective-permute-start.31) | collective-permute-done | bytes 1179680 | tf_op jit(solution)/shard_map/ppermute | solution.py:134
  354.2 25.9 %attention_backward.1 = (bf16[9,64,1024]{2,1,0:T(8,128)(2,1)S(1)}, bf16[9,64,1024]{2,1,0:T(8,128)(2,1)S(1)}, bf16[9,64,1024]{2,1,0:T(8,128)(2,1)S(1)}) custom-call(bf16[9,64,1024]{2,1,0:T(8,128)(2,1)} %get-tuple-element.186.q_ref, bf16[9,64,1024]{2,1,0:T(8,128)(2,1)} %get-tuple-element.187.k_ref, bf16[9,64,1024]{2,1,0:T(8,128)(2,1)} %get-tuple-element.188.v_ref, ...), custom_call_target="tpu_custom_call" | custom-call | tf_op jit(solution)/shard_map/attention_backward/pallas_call | solution.py:119
  380.2 8.8 %half_product.12 = bf16[4,3,288,576]{3,2,1,0:T(8,128)(2,1)} custom-call(s32[1]{0:T(128)} %bitcast.56.refs_0_, bf16[4,2,288,1024]{3,2,1,0:T(8,128)(2,1)} %bitcast.133, bf16[576,1024]{1,0:T(8,128)(2,1)S(1)} %bitcast.154, bf16[576,1024]{1,0:T(8,128)(2,1)S(1)} %bitcast.157, bf16[576,1024]{1,0:T(8,128)(2,1)S(1)} %bitcast.160), custom_call_target="tpu_custom_call" | custom-call | tf_op jit(solution)/shard_map/half_product/pallas_call | solution.py:493
  389.0 13.1 %collective-permute-done.32.refs_3_ = bf16[4,1,576,720]{3,2,1,0:T(8,128)(2,1)} collective-permute-done((bf16[4,1,576,720]{3,2,1,0:T(8,128)(2,1)}, bf16[4,1,576,720]{3,2,1,0:T(8,128)(2,1)}, u32[]{:S(2)}, u32[]{:S(2)}) %collective-permute-start.32) | collective-permute-done | bytes 3317792 | tf_op jit(solution)/shard_map/ppermute | solution.py:535
  402.1 8.5 %half_product.13 = bf16[4,1,576,720]{3,2,1,0:T(8,128)(2,1)} custom-call(s32[1]{0:T(128)} %bitcast.59.refs_0_, bf16[4,2,720,1024]{3,2,1,0:T(8,128)(2,1)} %bitcast.146, bf16[576,1024]{1,0:T(8,128)(2,1)} %multiply_convert_fusion.refs_2_, bf16[4,1,576,720]{3,2,1,0:T(8,128)(2,1)} %collective-permute-done.32.refs_3_), custom_call_target="tpu_custom_call" | custom-call | tf_op jit(solution)/shard_map/half_product/pallas_call | solution.py:493
  413.8 52.5 %conditional.5 = (f32[256,2304]{1,0:T(8,128)}, bf16[256,2304]{1,0:T(8,128)(2,1)}) conditional(s32[]{:T(128)} %convert_element_type.94, () %tuple.98, (bf16[2304,576]{0,1:T(8,128)(2,1)}, bf16[2304,576]{0,1:T(8,128)(2,1)}, bf16[2304,576]{0,1:T(8,128)(2,1)}, bf16[576,1024]{1,0:T(8,128)(2,1)S(1)}, bf16[576,1024]{1,0:T(8,128)(2,1)S(1)}, ...), branch_computations={%region_4.5_spmd, %region_5.6_spmd} | conditional | flops 7 | bytes 14155984 | solution.py:143
  414.4 12.7 %token_chunks.3 = (bf16[256,2304]{1,0:T(8,128)(2,1)}, bf16[256,2304]{1,0:T(8,128)(2,1)}) custom-call(s32[2]{0:T(128)} %pad_add_fusion.1.refs_0_, bf16[576,2304]{1,0:T(8,128)(2,1)} %bitcast.163, bf16[576,2304]{1,0:T(8,128)(2,1)} %bitcast.166, bf16[576,2304]{1,0:T(8,128)(2,1)} %bitcast.169, bf16[576,1024]{1,0:T(8,128)(2,1)S(1)} %get-tuple-element.50.refs_4_, ...), custom_call_target="tpu_custom_call" | custom-call | tf_op jit(solution)/shard_map/cond/branch_1_fun/token_chunks/pallas_call | solution.py:754
  427.6 2.7 collective-permute-done.2.refs_7_
  430.3 7.7 %token_chunks.4 = bf16[256,2304]{1,0:T(8,128)(2,1)} custom-call(s32[1]{0:T(128)} %bitcast.6.refs_0_, bf16[576,2304]{1,0:T(8,128)(2,1)} %bitcast.164, bf16[576,2304]{1,0:T(8,128)(2,1)} %bitcast.167, bf16[576,2304]{1,0:T(8,128)(2,1)} %bitcast.170, bf16[576,1024]{1,0:T(8,128)(2,1)S(1)} %get-tuple-element.50.refs_4_, ...), custom_call_target="tpu_custom_call" | custom-call | tf_op jit(solution)/shard_map/cond/branch_1_fun/token_chunks/pallas_call | solution.py:754
  439.3 8.1 %token_chunks.5 = f32[256,2304]{1,0:T(8,128)} custom-call(s32[1]{0:T(128)} %bitcast.5.refs_0_, bf16[576,2304]{1,0:T(8,128)(2,1)} %bitcast.165, bf16[576,2304]{1,0:T(8,128)(2,1)} %bitcast.168, bf16[576,2304]{1,0:T(8,128)(2,1)} %bitcast.171, bf16[576,1024]{1,0:T(8,128)(2,1)S(1)} %get-tuple-element.50.refs_4_, bf16[576,1024]{1,0:T(8,128)(2,1)S(1)} %get-tuple-element.51.refs_5_, ...), custom_call_target="tpu_custom_call" | custom-call | tf_op jit(solution)/shard_map/cond/branch_1_fun/token_chunks/pallas_call | solution.py:754
  447.4 19.0 %collective-permute-done.4 = bf16[256,2304]{1,0:T(8,128)(2,1)} collective-permute-done((bf16[256,2304]{1,0:T(8,128)(2,1)}, bf16[256,2304]{1,0:T(8,128)(2,1)}, u32[]{:S(2)}, u32[]{:S(2)}) %collective-permute-start.4) | collective-permute-done | bytes 1179680 | tf_op jit(solution)/shard_map/cond/branch_1_fun/ppermute | solution.py:134
  466.3 5.7 half_product.14
  472.0 6.2 reduce-scatter.10.cloned.1.call-done
  478.3 12.7 %fusion.9 = bf16[576,1024]{1,0:T(8,128)(2,1)S(1)} fusion(f32[576,1024]{1,0:T(8,128)} %get-tuple-element.163.refs_3_, bf16[5760,576]{0,1:T(8,128)(2,1)} %param.27, bf16[5760,1024]{1,0:T(8,128)(2,1)} %bitcast.147), kind=kOutput, calls=%fused_computation.15 | convolution fusion | flops 6796541952 | bytes 21970944 | tf_op jit(solution)/shard_map/fe,ft->et/dot_general | solution.py:945
  495.1 3.5 fusion.7
  502.2 5.1 collective-permute-done.39.refs_3_
  509.4 2.9 bitcast_convert_fusion
  512.3 3.1 copy.34
  515.3 4.7 collective-permute-done.36.refs_3_
  524.4 4.9 fusion.6
  529.3 10.0 %collective-permute-done.46.refs_5_ = bf16[4,3,288,576]{3,2,1,0:T(8,128)(2,1)} collective-permute-done((bf16[4,3,288,576]{3,2,1,0:T(8,128)(2,1)}, bf16[4,3,288,576]{3,2,1,0:T(8,128)(2,1)}, u32[]{:S(2)}, u32[]{:S(2)}) %collective-permute-start.46) | collective-permute-done | bytes 3981344 | tf_op jit(solution)/shard_map/ppermute | solution.py:535
  539.3 9.5 %half_product.15 = bf16[4,3,288,576]{3,2,1,0:T(8,128)(2,1)} custom-call(s32[1]{0:T(128)} %bitcast.59.refs_0_, bf16[4,2,288,1024]{3,2,1,0:T(8,128)(2,1)} %bitcast.134, bf16[576,1024]{1,0:T(8,128)(2,1)S(1)} %bitcast.156, bf16[576,1024]{1,0:T(8,128)(2,1)S(1)} %bitcast.159, bf16[576,1024]{1,0:T(8,128)(2,1)} %bitcast.162, ...), custom_call_target="tpu_custom_call" | custom-call | tf_op jit(solution)/shard_map/half_product/pallas_call | solution.py:493
  557.4 10.8 %collective-permute-done.43 = f32[2,2304]{1,0:T(2,128)S(1)} collective-permute-done((f32[2,2304]{1,0:T(2,128)S(1)}, f32[2,2304]{1,0:T(2,128)S(1)}, u32[]{:S(2)}, u32[]{:S(2)}) %collective-permute-start.43) | collective-permute-done | bytes 18464 | tf_op jit(solution)/shard_map/ppermute | solution.py:600
  569.9 4.8 collective-permute-done.44
  577.0 5.2 collective-permute-done.45
  588.8 42.6 %reduce-scatter.14.cloned.1.call-done = bf16[1,3,288,576]{3,2,1,0:T(8,128)(2,1)} async-done(((bf16[4,3,288,576]{3,2,1,0:T(8,128)(2,1)}), bf16[1,3,288,576]{3,2,1,0:T(8,128)(2,1)}) %reduce-scatter.14.cloned.1.call-update) | async-done | bytes 995344 | tf_op jit(solution)/shard_map/reduce_scatter | solution.py:541
  631.4 2.6 fusion.10
  (220 shorter events, 104.3 us)
Async XLA Ops:
  7.2 131.0 %all-gather.2.cloned.1.call-start = ((), (), s32[]{:S(2)}) async-start(), calls=%async_computation.5 | async-start | bytes 3981312 | tf_op jit(solution)/shard_map/all_gather | solution.py:826
  7.2 3.9 collective-permute-start.5
  7.7 29.3 %collective-permute-start.6 = (bf16[256,2304]{1,0:T(8,128)(2,1)}, bf16[256,2304]{1,0:T(8,128)(2,1)S(1)}, u32[]{:S(2)}, u32[]{:S(2)}) collective-permute-start(bf16[256,2304]{1,0:T(8,128)(2,1)} %refs_1_.2), channel_id=1, source_target_pairs={{0,2},{1,3},{2,0},{3,1},{4,6},{5,7},{6,4},{7,5},{8,10},{9,11},{10,... | collective-permute-start | bytes 3538952 | tf_op jit(solution)/shard_map/ppermute | solution.py:134
  17.4 6.1 copy-start
  17.4 6.1 copy-start.18
  37.1 3.5 collective-permute-start.7
  38.4 17.9 %collective-permute-start.12 = (bf16[72,1440]{1,0:T(8,128)(2,1)S(1)}, bf16[72,1440]{1,0:T(8,128)(2,1)S(1)}, u32[]{:S(2)}, u32[]{:S(2)}) collective-permute-start(bf16[72,1440]{1,0:T(8,128)(2,1)S(1)} %get-tuple-element.152), channel_id=1, source_target_pairs={{0,2},{1,3},{2,0},{3,1},{4,6},{5,7},{6,4},{7,5},{8,10},{9,11},{10,... | collective-permute-start | bytes 622088 | tf_op jit(solution)/shard_map/ppermute | solution.py:134
  40.3 16.3 %collective-permute-start.11 = (bf16[72,1440]{1,0:T(8,128)(2,1)S(1)}, bf16[72,1440]{1,0:T(8,128)(2,1)S(1)}, u32[]{:S(2)}, u32[]{:S(2)}) collective-permute-start(bf16[72,1440]{1,0:T(8,128)(2,1)S(1)} %get-tuple-element.150), channel_id=1, source_target_pairs={{0,2},{1,3},{2,0},{3,1},{4,6},{5,7},{6,4},{7,5},{8,10},{9,11},{10,... | collective-permute-start | bytes 622088 | tf_op jit(solution)/shard_map/ppermute | solution.py:134
  53.7 5.0 copy-start.10
  56.3 1.5 collective-permute-start.19
  58.6 264.4 %reduce-scatter.6.cloned.1.call-start = ((), (), s32[]{:S(2)}) async-start(), calls=%async_computation.6 | async-start | bytes 5898240 | tf_op jit(solution)/shard_map/reduce_scatter | solution.py:541
  58.7 28.2 %collective-permute-start.13 = (bf16[256,2304]{1,0:T(8,128)(2,1)S(1)}, bf16[256,2304]{1,0:T(8,128)(2,1)S(1)}, u32[]{:S(2)}, u32[]{:S(2)}) collective-permute-start(bf16[256,2304]{1,0:T(8,128)(2,1)S(1)} %copy-done.10), channel_id=1, source_target_pairs={{0,2},{1,3},{2,0},{3,1},{4,6},{5,7},{6,4},{7,5},{8,10},{9,11},{10,... | collective-permute-start | bytes 3538952 | tf_op jit(solution)/shard_map/ppermute | solution.py:134
  60.6 29.4 %collective-permute-start.10 = (bf16[256,2304]{1,0:T(8,128)(2,1)S(1)}, bf16[256,2304]{1,0:T(8,128)(2,1)S(1)}, u32[]{:S(2)}, u32[]{:S(2)}) collective-permute-start(bf16[256,2304]{1,0:T(8,128)(2,1)S(1)} %copy-done.10), channel_id=1, source_target_pairs={{0,1},{1,0},{2,3},{3,2},{4,5},{5,4},{6,7},{7,6},{8,9},{9,8},{10,11... | collective-permute-start | bytes 3538952 | tf_op jit(solution)/shard_map/ppermute | solution.py:134
  86.9 4.0 collective-permute-start.14
  87.9 35.0 %collective-permute-start.9 = (bf16[576,1024]{1,0:T(8,128)(2,1)}, bf16[576,1024]{1,0:T(8,128)(2,1)}, u32[]{:S(2)}, u32[]{:S(2)}) collective-permute-start(bf16[576,1024]{1,0:T(8,128)(2,1)} %bitcast.178), channel_id=1, source_target_pairs={{0,2},{1,3},{2,0},{3,1},{4,6},{5,7},{6,4},{7,5},{8,10},{9,11},{10,... | collective-permute-start | bytes 3538952 | tf_op jit(solution)/shard_map/ppermute | solution.py:134
  89.7 35.6 %collective-permute-start.8 = (bf16[576,1024]{1,0:T(8,128)(2,1)}, bf16[576,1024]{1,0:T(8,128)(2,1)}, u32[]{:S(2)}, u32[]{:S(2)}) collective-permute-start(bf16[576,1024]{1,0:T(8,128)(2,1)} %bitcast.179), channel_id=1, source_target_pairs={{0,1},{1,0},{2,3},{3,2},{4,5},{5,4},{6,7},{7,6},{8,9},{9,8},{10,11... | collective-permute-start | bytes 3538952 | tf_op jit(solution)/shard_map/ppermute | solution.py:134
  99.4 166.0 %copy-start.6 = (f32[576,1024]{1,0:T(8,128)}, f32[576,1024]{1,0:T(8,128)S(1)}, u32[]{:S(2)}) copy-start(f32[576,1024]{1,0:T(8,128)S(1)} %get-tuple-element.190.refs_2_) | copy-start | bytes 7077892
  122.9 4.4 collective-permute-start.15
  123.6 17.0 %collective-permute-start.18 = (bf16[576,1440]{1,0:T(8,128)(2,1)}, bf16[576,1440]{1,0:T(8,128)(2,1)}, u32[]{:S(2)}, u32[]{:S(2)}) collective-permute-start(bf16[576,1440]{1,0:T(8,128)(2,1)} %get-tuple-element.225), channel_id=1, source_target_pairs={{0,1},{1,0},{2,3},{3,2},{4,5},{5,4},{6,7},{7,6},{8,9},{9,8},{10,11... | collective-permute-start | bytes 4976648 | tf_op jit(solution)/shard_map/ppermute | solution.py:134
  137.7 16.3 %collective-permute-start.17 = (bf16[592,512]{1,0:T(8,128)(2,1)}, bf16[592,512]{1,0:T(8,128)(2,1)}, u32[]{:S(2)}, u32[]{:S(2)}) collective-permute-start(bf16[592,512]{1,0:T(8,128)(2,1)} %get-tuple-element.165), channel_id=1, source_target_pairs={{0,2},{1,3},{2,0},{3,1},{4,6},{5,7},{6,4},{7,5},{8,10},{9,11},{10,... | collective-permute-start | bytes 1818632 | tf_op jit(solution)/shard_map/ppermute | solution.py:134
  138.0 17.6 %collective-permute-start.21 = (bf16[592,512]{1,0:T(8,128)(2,1)}, bf16[592,512]{1,0:T(8,128)(2,1)}, u32[]{:S(2)}, u32[]{:S(2)}) collective-permute-start(bf16[592,512]{1,0:T(8,128)(2,1)} %get-tuple-element.165), channel_id=1, source_target_pairs={{0,1},{1,0},{2,3},{3,2},{4,5},{5,4},{6,7},{7,6},{8,9},{9,8},{10,11... | collective-permute-start | bytes 1818632 | tf_op jit(solution)/shard_map/ppermute | solution.py:134
  138.2 5.6 slice-start
  143.8 10.2 %copy-start.31 = (bf16[592,512]{1,0:T(8,128)(2,1)S(1)}, bf16[592,512]{1,0:T(8,128)(2,1)}, u32[]{:S(2)}) copy-start(bf16[592,512]{1,0:T(8,128)(2,1)} %get-tuple-element.168.refs_0_) | copy-start | bytes 1818628
  154.0 2.4 collective-permute-start.22
  154.0 17.0 %collective-permute-start.20 = (bf16[592,512]{1,0:T(8,128)(2,1)S(1)}, bf16[592,512]{1,0:T(8,128)(2,1)}, u32[]{:S(2)}, u32[]{:S(2)}) collective-permute-start(bf16[592,512]{1,0:T(8,128)(2,1)S(1)} %copy-done.31), channel_id=1, source_target_pairs={{0,2},{1,3},{2,0},{3,1},{4,6},{5,7},{6,4},{7,5},{8,10},{9,11},{10,... | collective-permute-start | bytes 1818632 | tf_op jit(solution)/shard_map/ppermute | solution.py:134
  155.5 15.7 %collective-permute-start.16 = (bf16[592,512]{1,0:T(8,128)(2,1)S(1)}, bf16[592,512]{1,0:T(8,128)(2,1)}, u32[]{:S(2)}, u32[]{:S(2)}) collective-permute-start(bf16[592,512]{1,0:T(8,128)(2,1)S(1)} %copy-done.31), channel_id=1, source_target_pairs={{0,1},{1,0},{2,3},{3,2},{4,5},{5,4},{6,7},{7,6},{8,9},{9,8},{10,11... | collective-permute-start | bytes 1818632 | tf_op jit(solution)/shard_map/ppermute | solution.py:134
  171.0 2.4 collective-permute-start.23
  197.1 213.5 %reduce-scatter.8.cloned.1.call-start = ((), (), s32[]{:S(2)}) async-start(), calls=%async_computation.7 | async-start | bytes 5529600 | tf_op jit(solution)/shard_map/reduce_scatter | solution.py:541
  197.1 66.3 %collective-permute-start.25 = (bf16[1440,1024]{1,0:T(8,128)(2,1)}, bf16[1440,1024]{1,0:T(8,128)(2,1)}, u32[]{:S(2)}, u32[]{:S(2)}) collective-permute-start(bf16[1440,1024]{1,0:T(8,128)(2,1)} %get-tuple-element.176.refs_0_), channel_id=1, source_target_pairs={{0,2},{1,3},{2,0},{3,1},{4,6},{5,7},{6,4},{7,5},{8,10},{9,11},{10,... | collective-permute-start | bytes 8847368 | tf_op jit(solution)/shard_map/ppermute | solution.py:134
  207.6 105.3 %collective-permute-start.29 = (bf16[4,1,288,1920]{3,2,1,0:T(8,128)(2,1)}, bf16[4,1,288,1920]{3,2,1,0:T(8,128)(2,1)}, u32[]{:S(2)}, u32[]{:S(2)}) collective-permute-start(bf16[4,1,288,1920]{3,2,1,0:T(8,128)(2,1)} %half_product.8), channel_id=1, source_target_pairs={{0,4},{4,0},{8,12},{12,8},{16,20},{20,16},{24,28},{28,24},{1,5},{5... | collective-permute-start | bytes 13271048 | tf_op jit(solution)/shard_map/ppermute | solution.py:535
  209.3 57.5 %collective-permute-start.24 = (bf16[1440,1024]{1,0:T(8,128)(2,1)}, bf16[1440,1024]{1,0:T(8,128)(2,1)}, u32[]{:S(2)}, u32[]{:S(2)}) collective-permute-start(bf16[1440,1024]{1,0:T(8,128)(2,1)} %get-tuple-element.176.refs_0_), channel_id=1, source_target_pairs={{0,1},{1,0},{2,3},{3,2},{4,5},{5,4},{6,7},{7,6},{8,9},{9,8},{10,11... | collective-permute-start | bytes 8847368 | tf_op jit(solution)/shard_map/ppermute | solution.py:134
  223.6 3.5 collective-permute-start
  224.2 11.7 %collective-permute-start.1 = (bf16[592,1024]{1,0:T(8,128)(2,1)}, bf16[592,1024]{1,0:T(8,128)(2,1)}, u32[]{:S(2)}, u32[]{:S(2)}) collective-permute-start(bf16[592,1024]{1,0:T(8,128)(2,1)} %get-tuple-element.46), channel_id=1, source_target_pairs={{0,1},{1,0},{2,3},{3,2},{4,5},{5,4},{6,7},{7,6},{8,9},{9,8},{10,11... | collective-permute-start | bytes 3637256 | tf_op jit(solution)/shard_map/cond/branch_1_fun/ppermute | solution.py:134
  263.4 5.7 collective-permute-start.26
  263.4 29.4 %collective-permute-start.27 = (bf16[592,1024]{1,0:T(8,128)(2,1)}, bf16[592,1024]{1,0:T(8,128)(2,1)}, u32[]{:S(2)}, u32[]{:S(2)}) collective-permute-start(bf16[592,1024]{1,0:T(8,128)(2,1)} %get-tuple-element.189), channel_id=1, source_target_pairs={{0,2},{1,3},{2,0},{3,1},{4,6},{5,7},{6,4},{7,5},{8,10},{9,11},{10,... | collective-permute-start | bytes 3637256 | tf_op jit(solution)/shard_map/ppermute | solution.py:134
  305.0 3.1 collective-permute-start.28
  323.1 155.1 %reduce-scatter.10.cloned.1.call-start = ((), (), s32[]{:S(2)}) async-start(), calls=%async_computation.8 | async-start | bytes 4423680 | tf_op jit(solution)/shard_map/reduce_scatter | solution.py:541
  323.2 78.9 %collective-permute-start.32 = (bf16[4,1,576,720]{3,2,1,0:T(8,128)(2,1)}, bf16[4,1,576,720]{3,2,1,0:T(8,128)(2,1)}, u32[]{:S(2)}, u32[]{:S(2)}) collective-permute-start(bf16[4,1,576,720]{3,2,1,0:T(8,128)(2,1)} %half_product.9), channel_id=1, source_target_pairs={{0,4},{4,0},{8,12},{12,8},{16,20},{20,16},{24,28},{28,24},{1,5},{5... | collective-permute-start | bytes 9953288 | tf_op jit(solution)/shard_map/ppermute | solution.py:535
  324.8 3.1 collective-permute-start.30
  324.8 28.4 %collective-permute-start.31 = (bf16[576,1024]{1,0:T(8,128)(2,1)S(1)}, bf16[576,1024]{1,0:T(8,128)(2,1)S(1)}, u32[]{:S(2)}, u32[]{:S(2)}) collective-permute-start(bf16[576,1024]{1,0:T(8,128)(2,1)S(1)} %copy-done.23), channel_id=1, source_target_pairs={{0,2},{1,3},{2,0},{3,1},{4,6},{5,7},{6,4},{7,5},{8,10},{9,11},{10,... | collective-permute-start | bytes 3538952 | tf_op jit(solution)/shard_map/ppermute | solution.py:134
  380.2 8.9 %copy-start.16 = (bf16[9,64,1024]{2,1,0:T(8,128)(2,1)}, bf16[9,64,1024]{2,1,0:T(8,128)(2,1)S(1)}, u32[]{:S(2)}) copy-start(bf16[9,64,1024]{2,1,0:T(8,128)(2,1)S(1)} %get-tuple-element.204) | copy-start | bytes 3538948
  410.6 138.2 %reduce-scatter.12.cloned.1.call-start = ((), (), s32[]{:S(2)}) async-start(), calls=%async_computation.9 | async-start | bytes 1843200 | tf_op jit(solution)/shard_map/reduce_scatter | solution.py:541
  410.6 55.7 %collective-permute-start.33 = (bf16[4,1,288,576]{3,2,1,0:T(8,128)(2,1)}, bf16[4,1,288,576]{3,2,1,0:T(8,128)(2,1)}, u32[]{:S(2)}, u32[]{:S(2)}) collective-permute-start(bf16[4,1,288,576]{3,2,1,0:T(8,128)(2,1)} %half_product.11), channel_id=1, source_target_pairs={{0,4},{4,0},{8,12},{12,8},{16,20},{20,16},{24,28},{28,24},{1,5},{5... | collective-permute-start | bytes 3981320 | tf_op jit(solution)/shard_map/ppermute | solution.py:535
  412.6 126.7 %collective-permute-start.46 = (bf16[4,3,288,576]{3,2,1,0:T(8,128)(2,1)}, bf16[4,3,288,576]{3,2,1,0:T(8,128)(2,1)}, u32[]{:S(2)}, u32[]{:S(2)}) collective-permute-start(bf16[4,3,288,576]{3,2,1,0:T(8,128)(2,1)} %half_product.12), channel_id=1, source_target_pairs={{0,4},{4,0},{8,12},{12,8},{16,20},{20,16},{24,28},{28,24},{1,5},{5... | collective-permute-start | bytes 11943944 | tf_op jit(solution)/shard_map/ppermute | solution.py:535
  427.1 3.2 collective-permute-start.2
  427.1 12.2 %collective-permute-start.3 = (bf16[256,2304]{1,0:T(8,128)(2,1)}, bf16[256,2304]{1,0:T(8,128)(2,1)}, u32[]{:S(2)}, u32[]{:S(2)}) collective-permute-start(bf16[256,2304]{1,0:T(8,128)(2,1)} %get-tuple-element.55), channel_id=1, source_target_pairs={{0,1},{1,0},{2,3},{3,2},{4,5},{5,4},{6,7},{7,6},{8,9},{9,8},{10,11... | collective-permute-start | bytes 3538952 | tf_op jit(solution)/shard_map/cond/branch_1_fun/ppermute | solution.py:134
  438.0 28.3 %collective-permute-start.4 = (bf16[256,2304]{1,0:T(8,128)(2,1)}, bf16[256,2304]{1,0:T(8,128)(2,1)}, u32[]{:S(2)}, u32[]{:S(2)}) collective-permute-start(bf16[256,2304]{1,0:T(8,128)(2,1)} %token_chunks.4), channel_id=1, source_target_pairs={{0,2},{1,3},{2,0},{3,1},{4,6},{5,7},{6,4},{7,5},{8,10},{9,11},{10,... | collective-permute-start | bytes 3538952 | tf_op jit(solution)/shard_map/cond/branch_1_fun/ppermute | solution.py:134
  478.3 153.1 %reduce-scatter.14.cloned.1.call-start = ((), (), s32[]{:S(2)}) async-start(), calls=%async_computation.10 | async-start | bytes 5529600 | tf_op jit(solution)/shard_map/reduce_scatter | solution.py:541
  478.3 12.7 %copy-start.27 = (bf16[576,1024]{1,0:T(8,128)(2,1)S(1)}, bf16[576,1024]{1,0:T(8,128)(2,1)}, u32[]{:S(2)}) copy-start(bf16[576,1024]{1,0:T(8,128)(2,1)} %get-tuple-element.211) | copy-start | bytes 3538948
  491.9 7.3 %collective-permute-start.37 = (bf16[576,256]{1,0:T(8,128)(2,1)S(1)}, bf16[576,256]{1,0:T(8,128)(2,1)S(1)}, u32[]{:S(2)}, u32[]{:S(2)}) collective-permute-start(bf16[576,256]{1,0:T(8,128)(2,1)S(1)} %get-tuple-element.233), channel_id=1, source_target_pairs={{0,1},{1,0},{2,3},{3,2},{4,5},{5,4},{6,7},{7,6},{8,9},{9,8},{10,11... | collective-permute-start | bytes 884744 | tf_op jit(solution)/shard_map/ppermute | solution.py:134
  491.9 9.9 %collective-permute-start.38 = (bf16[576,256]{1,0:T(8,128)(2,1)S(1)}, bf16[576,256]{1,0:T(8,128)(2,1)}, u32[]{:S(2)}, u32[]{:S(2)}) collective-permute-start(bf16[576,256]{1,0:T(8,128)(2,1)S(1)} %get-tuple-element.232), channel_id=1, source_target_pairs={{0,2},{1,3},{2,0},{3,1},{4,6},{5,7},{6,4},{7,5},{8,10},{9,11},{10,... | collective-permute-start | bytes 884744 | tf_op jit(solution)/shard_map/ppermute | solution.py:134
  493.4 14.0 %collective-permute-start.39 = (bf16[576,256]{1,0:T(8,128)(2,1)S(1)}, bf16[576,256]{1,0:T(8,128)(2,1)}, u32[]{:S(2)}, u32[]{:S(2)}) collective-permute-start(bf16[576,256]{1,0:T(8,128)(2,1)S(1)} %get-tuple-element.231), channel_id=1, source_target_pairs={{0,3},{1,2},{2,1},{3,0},{4,7},{5,6},{6,5},{7,4},{8,11},{9,10},{10,... | collective-permute-start | bytes 884744 | tf_op jit(solution)/shard_map/ppermute | solution.py:134
  494.8 20.5 %collective-permute-start.34 = (bf16[576,256]{1,0:T(8,128)(2,1)}, bf16[576,256]{1,0:T(8,128)(2,1)}, u32[]{:S(2)}, u32[]{:S(2)}) collective-permute-start(bf16[576,256]{1,0:T(8,128)(2,1)} %get-tuple-element.237), channel_id=1, source_target_pairs={{0,1},{1,0},{2,3},{3,2},{4,5},{5,4},{6,7},{7,6},{8,9},{9,8},{10,11... | collective-permute-start | bytes 884744 | tf_op jit(solution)/shard_map/ppermute | solution.py:134
  499.2 8.2 %copy-start.33 = (bf16[576,256]{1,0:T(8,128)(2,1)}, bf16[576,256]{1,0:T(8,128)(2,1)S(1)}, u32[]{:S(2)}) copy-start(bf16[576,256]{1,0:T(8,128)(2,1)S(1)} %collective-permute-done.37.refs_1_) | copy-start | bytes 884740
  499.2 16.2 %collective-permute-start.35 = (bf16[576,256]{1,0:T(8,128)(2,1)}, bf16[576,256]{1,0:T(8,128)(2,1)}, u32[]{:S(2)}, u32[]{:S(2)}) collective-permute-start(bf16[576,256]{1,0:T(8,128)(2,1)} %get-tuple-element.236), channel_id=1, source_target_pairs={{0,2},{1,3},{2,0},{3,1},{4,6},{5,7},{6,4},{7,5},{8,10},{9,11},{10,... | collective-permute-start | bytes 884744 | tf_op jit(solution)/shard_map/ppermute | solution.py:134
  501.8 18.2 %collective-permute-start.36 = (bf16[576,256]{1,0:T(8,128)(2,1)}, bf16[576,256]{1,0:T(8,128)(2,1)}, u32[]{:S(2)}, u32[]{:S(2)}) collective-permute-start(bf16[576,256]{1,0:T(8,128)(2,1)} %get-tuple-element.235), channel_id=1, source_target_pairs={{0,3},{1,2},{2,1},{3,0},{4,7},{5,6},{6,5},{7,4},{8,11},{9,10},{10,... | collective-permute-start | bytes 884744 | tf_op jit(solution)/shard_map/ppermute | solution.py:134
  548.8 34.3 %copy-start.29 = (bf16[1,1,288,1920]{3,2,1,0:T(8,128)(2,1)S(1)}, bf16[1,1,288,1920]{3,2,1,0:T(8,128)(2,1)}, u32[]{:S(2)}) copy-start(bf16[1,1,288,1920]{3,2,1,0:T(8,128)(2,1)} %reduce-scatter.8.cloned.1.call-done) | copy-start | bytes 3317764
  550.2 3.7 collective-permute-start.40
  550.3 3.8 collective-permute-start.41
  551.7 3.3 collective-permute-start.42
  552.2 30.7 %collective-permute-start.47 = (bf16[288,960]{1,0:T(8,128)(2,1)S(1)}, bf16[288,960]{1,0:T(8,128)(2,1)S(1)}, u32[]{:S(2)}, u32[]{:S(2)}) collective-permute-start(bf16[288,960]{1,0:T(8,128)(2,1)S(1)} %dynamic-slice_bitcast_fusion.2), channel_id=1, source_target_pairs={{0,4},{4,0},{8,12},{12,8},{16,20},{20,16},{24,28},{28,24},{1,5},{5... | collective-permute-start | bytes 1658888 | tf_op jit(solution)/shard_map/ppermute | solution.py:535
  555.7 12.4 %collective-permute-start.43 = (f32[2,2304]{1,0:T(2,128)S(1)}, f32[2,2304]{1,0:T(2,128)S(1)}, u32[]{:S(2)}, u32[]{:S(2)}) collective-permute-start(f32[2,2304]{1,0:T(2,128)S(1)} %add_add_fusion), channel_id=1, source_target_pairs={{0,4},{4,0},{8,12},{12,8},{16,20},{20,16},{24,28},{28,24},{1,5},{5... | collective-permute-start | bytes 55304 | tf_op jit(solution)/shard_map/ppermute | solution.py:600
  568.2 6.5 %collective-permute-start.44 = (f32[2,2304]{1,0:T(2,128)S(1)}, f32[2,2304]{1,0:T(2,128)S(1)}, u32[]{:S(2)}, u32[]{:S(2)}) collective-permute-start(f32[2,2304]{1,0:T(2,128)S(1)} %add.155), channel_id=1, source_target_pairs={{0,8},{4,12},{8,0},{12,4},{16,24},{20,28},{24,16},{28,20},{1,9},{5... | collective-permute-start | bytes 55304 | tf_op jit(solution)/shard_map/ppermute | solution.py:600
  574.7 7.5 %collective-permute-start.45 = (f32[2,2304]{1,0:T(2,128)S(1)}, f32[2,2304]{1,0:T(2,128)S(1)}, u32[]{:S(2)}, u32[]{:S(2)}) collective-permute-start(f32[2,2304]{1,0:T(2,128)S(1)} %add.156), channel_id=1, source_target_pairs={{0,16},{4,20},{8,24},{12,28},{16,0},{20,4},{24,8},{28,12},{1,17},{... | collective-permute-start | bytes 55304 | tf_op jit(solution)/shard_map/ppermute | solution.py:600
  (29 other events, 60.1 us)
Sparse Core Ops, SparseCore 0:
  58.8 66.7 all-gather.1
  197.2 86.1 reduce-scatter.5
  323.2 81.5 reduce-scatter.7
  410.7 67.4 reduce-scatter.9
  481.1 34.0 reduce-scatter.11
  549.0 82.3 reduce-scatter.13

commit v5 on v4

--- a/solution.py
+++ b/solution.py
@@ -82,7 +82,7 @@
 
 
 def backward_kernel(
-    q_ref, k_ref, v_ref, g_ref, h_ref, lse_ref, cos_ref, sin_ref, dq_ref, dk_ref, dv_ref, dk_acc, dv_acc
+    q_ref, k_ref, v_ref, g_ref, h_ref, out_ref, lse_ref, cos_ref, sin_ref, dq_ref, dk_ref, dv_ref, dk_acc, dv_acc
 ):
     cosine, sine = cos_ref[...], sin_ref[...]
     span = q_ref.shape[2]
@@ -90,6 +90,7 @@
     k_low, v_low = k_ref[0], v_ref[0]
     grad = (g_ref[0] + h_ref[0].astype(full)).astype(low)
     k_rows, v_rows = k_low.T, v_low.T
+    deltas = jnp.sum(grad.astype(full) * out_ref[0].astype(full), axis=0, keepdims=True)
     dk_acc[...] = jnp.zeros_like(dk_acc)
     dv_acc[...] = jnp.zeros_like(dv_acc)
     for j in range(span // BLK):
@@ -100,8 +101,7 @@
         probs = jnp.exp(scores - lse_ref[0, :, cols])
         probs_low = probs.astype(low)
         d_probs = jnp.dot(v_rows[:kv], g_j, preferred_element_type=full)
-        delta = jnp.sum(probs * d_probs, axis=0, keepdims=True)
-        d_scores = (probs * (d_probs - delta)).astype(low)
+        d_scores = (probs * (d_probs - deltas[:, cols])).astype(low)
         dq = jnp.dot(k_low[:, :kv], d_scores, preferred_element_type=full) * (HD ** (-0.5))
         dq_ref[0, :, cols] = turn(dq, cosine[:, cols], -sine[:, cols]).astype(low)
         dk_acc[:, :kv] += lax.dot_general(q_j, d_scores, NT, preferred_element_type=full)
@@ -110,7 +110,7 @@
     dv_ref[0] = dv_acc[...].astype(low)
 
 
-def attention_backward(query, key, value, grad, rest, lse, cosine, sine):
+def attention_backward(query, key, value, grad, rest, attended, lse, cosine, sine):
     heads, _, span = query.shape
     spec = pl.BlockSpec((1, HD, span), lambda h: (h, 0, 0))
     table = pl.BlockSpec((HD // 2, span), lambda h: (0, 0))
@@ -119,14 +119,14 @@
     return pl.pallas_call(
         backward_kernel,
         grid=(heads,),
-        in_specs=[spec, spec, spec, spec, spec, row, table, table],
+        in_specs=[spec] * 6 + [row, table, table],
         out_specs=[spec, spec, spec],
         out_shape=[field, field, field],
         scratch_shapes=[pltpu.VMEM((HD, span), full), pltpu.VMEM((HD, span), full)],
         compiler_params=pltpu.CompilerParams(vmem_limit_bytes=60 * 2**20),
         cost_estimate=SMALL,
         name="attention_backward",
-    )(query, key, value, grad, rest, lse, cosine, sine)
+    )(query, key, value, grad, rest, attended, lse, cosine, sine)
 
 
 def swap(array, j):
@@ -630,7 +630,7 @@
 
 
 def chunks_kernel(index, *refs, count, ways, added, extra):
-    step = pl.program_id(0)
+    step = pl.program_id(1)
     weights, grads, refs = refs[:count], refs[count], refs[count + 1 :]
     plus, refs = refs[:added], refs[added:]
     row, outs = refs[:extra], refs[extra:]
@@ -665,19 +665,21 @@
     if earlier:
         index = after(index, *earlier)
     extra = () if extra is None else (extra,)
-    const = lambda shape: pl.BlockSpec(shape, lambda i, index: (0, 0))
+    tiles = 2
+    tile = lambda rows: pl.BlockSpec((rows, span // tiles), lambda i, k, index: (0, i))
     return pl.pallas_call(
         lambda *refs: chunks_kernel(
             *refs, count=len(weights), ways=len(partners), added=len(plus), extra=len(extra)
         ),
         grid_spec=pltpu.PrefetchScalarGridSpec(
             num_scalar_prefetch=1,
-            grid=(len(partners),),
+            grid=(tiles, len(partners)),
             in_specs=[
-                pl.BlockSpec((cols, w.shape[1]), lambda i, index: (index[i], 0)) for w in weights
+                pl.BlockSpec((cols, w.shape[1]), lambda i, k, index: (index[k], 0))
+                for w in weights
             ]
-            + [const(a.shape) for a in (grads, *plus, *extra)],
-            out_specs=[const((tall, span))] * len(partners),
+            + [tile(a.shape[0]) for a in (grads, *plus, *extra)],
+            out_specs=[tile(tall)] * len(partners),
         ),
         out_shape=[jax.ShapeDtypeStruct((tall, span), dtype)] * len(partners),
         compiler_params=pltpu.CompilerParams(vmem_limit_bytes=60 * 2**20),
@@ -898,10 +900,10 @@
 
     far, near = feature_chunks([out_tall], d_attn, (3, 1))
     far, near = swap(far, 1), swap(near, 1)
-    (chunk,) = feature_chunks([out_tall], d_attn, (2,), plus=[far])
+    token = sum_most.keep([far], sum_rest)
+    (chunk,) = feature_chunks([out_tall], d_attn, (2,), plus=[far], earlier=[token])
     across = swap(chunk, 2)
-    token = sum_most.keep([chunk], sum_rest)
-    (own,) = feature_chunks([out_tall], d_attn, (0,), plus=[near], dtype=full, earlier=[token])
+    (own,) = feature_chunks([out_tall], d_attn, (0,), plus=[near], dtype=full, earlier=[chunk])
     sum_out = GradSum(attended_all, [d_attn])
     token = sum_out.send([own])
     sum_out.transfer(token)
@@ -916,6 +918,7 @@
                 value_low,
                 own.reshape(heads, HD, span),
                 across.reshape(heads, HD, span),
+                attended,
                 lse,
                 cosine,
                 sine,

time: 650 us -> 646 us (level)
  Pallas kernels: 284 us -> 276 us
  transfers between devices with their start and end apart: 54 -> 54, of which waited for: 28 -> 27; matrix products, arithmetic and copies ran while one was open for 13% -> 13% of each run, Pallas kernels for 41% -> 40%
where the time goes in v5:
time: 646 us; the launch traced here: 637 us
  Pallas kernels  276 us (43%)
  waiting for transfers between devices  201 us (31%)
  matrix products  41.2 us (6%)
  local copies, waits for them, and re-layouts  40.9 us (6%)
  starting transfers between devices  37.9 us (6%)
  other arithmetic  25 us (4%)
  between operations  15.1 us (2%)
    ppermute x40, waiting for transfers between devices, swap(): return lax.ppermute(array, 'fsdp', [(i, i ^ j) for i in range(size)])  106 us
    pallas_call x8, Pallas kernels, half_product(): pl.pallas_call(lambda *refs: product_kernel(*refs, count=count, adds=adde...  65.4 us
    reduce_scatter x5, waiting for transfers between devices, line_scatter(): lax.psum_scatter(array, 'rep', scatter_dimension=0, tiled=True, axis_inde...  48.8 us
    pallas_call x6, Pallas kernels, feature_chunks(): pl.pallas_call(lambda *refs: chunks_kernel(*refs, count=len(weights), way...  44.2 us
    pallas_call x2, Pallas kernels, inner_part(): pl.pallas_call(lambda *refs: inner_kernel(*refs, half=half), grid=(units...  29.2 us
    pallas_call x3, Pallas kernels, token_chunks(): pl.pallas_call(lambda *refs: blocks_kernel(*refs, count=len(weights), add...  28.6 us
    ppermute x5, waiting for transfers between devices, neighbour(): lax.ppermute(array, 'rep', [(i, i ^ 1) for i in range(lax.axis_size('rep'...  24.4 us
    ppermute x40, starting transfers between devices, swap(): return lax.ppermute(array, 'fsdp', [(i, i ^ j) for i in range(size)])  24.3 us
  transfers between devices with their start and end apart: 54, of which 27 were waited for; matrix products, arithmetic and copies ran while one was open for 13% of the time, Pallas kernels for 40%

profile of v5, /device:TPU:0, one launch (start us, length us, event | category | flops | bytes accessed | tf_op | source)
XLA Modules:
  0.0 637.3 jit_solution(1627934180988072931)
XLA Ops:
  14.7 2.7 spread.3
  17.4 6.1 fusion.13
  26.0 2.6 fusion.15
  28.6 8.5 %collective-permute-done.6.refs_1_ = bf16[256,2304]{1,0:T(8,128)(2,1)S(1)} collective-permute-done((bf16[256,2304]{1,0:T(8,128)(2,1)}, bf16[256,2304]{1,0:T(8,128)(2,1)S(1)}, u32[]{:S(2)}, u32[]{:S(2)}) %collective-permute-start.6) | collective-permute-done | bytes 1179680 | tf_op jit(solution)/shard_map/ppermute | solution.py:134
  42.9 4.4 spread.4
  51.0 2.6 fusion.17
  53.6 2.6 fusion.18
  61.7 20.6 %attention_forward.1 = (bf16[9,64,1024]{2,1,0:T(8,128)(2,1)}, bf16[9,64,1024]{2,1,0:T(8,128)(2,1)}, bf16[9,64,1024]{2,1,0:T(8,128)(2,1)}, bf16[9,64,1024]{2,1,0:T(8,128)(2,1)}, f32[9,1,1024]{2,1,0:T(1,128)}) custom-call(f32[9,64,512]{2,1,0:T(8,128)} %bitcast.181, f32[9,64,512]{2,1,0:T(8,128)} %bitcast.182, f32[9,64,512]{2,1,0:T(8,128)} %bitcast.183, ...), custom_call_target="tpu_custom_call" | custom-call | tf_op jit(solution)/shard_map/attention_forward/pallas_call | solution.py:72
  82.4 4.4 collective-permute-done.13.refs_3_
  93.6 3.6 spread.5
  99.4 6.5 %dynamic-slice_bitcast_fusion = (bf16[576,1440]{1,0:T(8,128)(2,1)}, bf16[576,1440]{1,0:T(8,128)(2,1)}) fusion(bf16[5760,576]{0,1:T(8,128)(2,1)} %param.27, s32[]{:T(128)S(6)} %select_n.105, s32[]{:T(128)S(6)} %select_n.103), kind=kLoop, calls=%fused_computation.22 | loop fusion | bytes 6635528 | tf_op jit(solution)/shard_map/dynamic_slice | solution.py:841
  105.9 11.4 %flip.2 = (bf16[2304,1440]{1,0:T(8,128)(2,1)}, bf16[2304,1440]{1,0:T(8,128)(2,1)}) custom-call(s32[1]{0:T(128)} %constant.133.clone.1.index, bf16[1440,2304]{1,0:T(8,128)(2,1)} %bitcast.148, bf16[1440,2304]{1,0:T(8,128)(2,1)} %bitcast.151), custom_call_target="tpu_custom_call" | custom-call | tf_op jit(solution)/shard_map/flip/pallas_call | solution.py:617
  117.4 5.6 flip.3.refs_1_
  128.4 9.3 %hidden_state.1 = (f32[576,1024]{1,0:T(8,128)}, bf16[592,512]{1,0:T(8,128)(2,1)}, bf16[592,512]{1,0:T(8,128)(2,1)}, bf16[4,576,1024]{2,1,0:T(8,128)(2,1)}) custom-call(bf16[576,1024]{1,0:T(8,128)(2,1)} %bitcast.179, bf16[576,1024]{1,0:T(8,128)(2,1)} %collective-permute-done.8.core, bf16[576,1024]{1,0:T(8,128)(2,1)} %collective-permute-done.9.chip, ...), custom_call_target="tpu_custom_call" | custom-call | tf_op jit(solution)/shard_map/hidden_state/pallas_call | solution.py:349
  140.8 3.1 place.4
  143.9 9.5 %convolution_convert_fusion.refs_6_ = bf16[1440,1024]{1,0:T(8,128)(2,1)} fusion(bf16[2304,1440]{1,0:T(8,128)(2,1)S(1)} %bitcast.135, bf16[1024,2304]{1,0:T(8,128)(2,1)S(1)} %bitcast.137), kind=kOutput, calls=%fused_computation.2 | convolution fusion | flops 6796247040 | bytes 14303232 | tf_op jit(solution)/shard_map/ef,te->ft/dot_general | solution.py:859
  156.4 14.6 %conditional.3 = ((bf16[1440,1024]{1,0:T(8,128)(2,1)}, bf16[2,1440,1024]{2,1,0:T(8,128)(2,1)}, f32[1,1024]{1,0:T(1,128)S(1)}, f32[1,1024]{1,0:T(1,128)S(1)}, bf16[4,576,1024]{2,1,0:T(8,128)(2,1)})) conditional(s32[]{:T(128)} %convert_element_type.91, () %tuple.84, (bf16[2304,1440]{0,1:T(8,128)(2,1)}, bf16[2304,1440]{0,1:T(8,128)(2,1)}, ...), branch_computations={%region_0.1_spmd, %region_1.2_spmd} | conditional | bytes 13574206 | solution.py:143
  156.4 14.6 %inner_part.2 = (bf16[1440,1024]{1,0:T(8,128)(2,1)}, bf16[2,1440,1024]{2,1,0:T(8,128)(2,1)}, f32[1,1024]{1,0:T(1,128)S(1)}, f32[1,1024]{1,0:T(1,128)S(1)}, bf16[4,576,1024]{2,1,0:T(8,128)(2,1)}) custom-call(bf16[592,512]{1,0:T(8,128)(2,1)} %get-tuple-element.34.refs_0_, bf16[592,512]{1,0:T(8,128)(2,1)} %get-tuple-element.35.refs_1_, ...), custom_call_target="tpu_custom_call" | custom-call | tf_op jit(solution)/shard_map/cond/branch_1_fun/inner_part/pallas_call | solution.py:426
  173.5 14.6 %inner_part.3 = (bf16[1440,1024]{1,0:T(8,128)(2,1)}, bf16[2,1440,1024]{2,1,0:T(8,128)(2,1)}, f32[1,1024]{1,0:T(1,128)S(1)}, f32[1,1024]{1,0:T(1,128)S(1)}, bf16[4,576,1024]{2,1,0:T(8,128)(2,1)}) custom-call(bf16[592,512]{1,0:T(8,128)(2,1)} %get-tuple-element.169.refs_0_, ...), custom_call_target="tpu_custom_call", output_to_operand_aliasing={{0}: (7, {}), {1}: (8, {}), {2}: (9, {}), {3}: (10, {}), {4... | custom-call | tf_op jit(solution)/shard_map/inner_part/pallas_call | solution.py:426
  188.0 9.0 %whole_product.1 = bf16[4,576,960]{2,1,0:T(8,128)(2,1)} custom-call(bf16[4,576,1024]{2,1,0:T(8,128)(2,1)} %get-tuple-element.180.act, bf16[2880,1024]{1,0:T(8,128)(2,1)} %bitcast.138), custom_call_target="tpu_custom_call" | custom-call | tf_op jit(solution)/shard_map/whole_product/pallas_call | solution.py:519
  198.3 9.3 %half_product.8 = bf16[4,1,288,1920]{3,2,1,0:T(8,128)(2,1)} custom-call(s32[1]{0:T(128)} %bitcast.56.refs_0_, bf16[4,2,288,1024]{3,2,1,0:T(8,128)(2,1)} %bitcast.143, bf16[2880,1024]{1,0:T(8,128)(2,1)} %bitcast.139), custom_call_target="tpu_custom_call" | custom-call | tf_op jit(solution)/shard_map/half_product/pallas_call | solution.py:493
  209.2 25.6 %conditional.4 = (bf16[592,1024]{1,0:T(8,128)(2,1)}, bf16[592,1024]{1,0:T(8,128)(2,1)}) conditional(s32[]{:T(128)} %convert_element_type.92, () %tuple.89, (bf16[2304,1440]{1,0:T(8,128)(2,1)}, bf16[2304,1440]{1,0:T(8,128)(2,1)}, bf16[2880,1024]{1,0:T(8,128)(2,1)}, f32[1,1024]{1,0:T(1,128)S(1)}) %tuple.147), branch_computations={%region_2.3_spmd, %region_3.4_spmd} | conditional | flops 7 | bytes 9699496 | solution.py:143
  209.8 13.8 %feature_chunks.6 = (bf16[592,1024]{1,0:T(8,128)(2,1)}, bf16[592,1024]{1,0:T(8,128)(2,1)}) custom-call(s32[2]{0:T(128)} %pad_add_fusion.refs_0_, bf16[2304,1440]{1,0:T(8,128)(2,1)} %get-tuple-element.41.refs_1_, bf16[2304,1440]{1,0:T(8,128)(2,1)} %get-tuple-element.42.refs_2_, bf16[2880,1024]{1,0:T(8,128)(2,1)} %get-tuple-element.43.refs_3_, ...), custom_call_target="tpu_custom_call" | custom-call | tf_op jit(solution)/shard_map/cond/branch_1_fun/feature_chunks/pallas_call | solution.py:670
  224.1 2.9 collective-permute-done.refs_4_
  227.0 7.9 %feature_chunks.7 = bf16[592,1024]{1,0:T(8,128)(2,1)} custom-call(s32[1]{0:T(128)} %bitcast.2.refs_0_, bf16[2304,1440]{1,0:T(8,128)(2,1)} %get-tuple-element.41.refs_1_, bf16[2304,1440]{1,0:T(8,128)(2,1)} %get-tuple-element.42.refs_2_, bf16[2880,1024]{1,0:T(8,128)(2,1)} %get-tuple-element.43.refs_3_, bf16[592,1024]{1,0:T(8,128)(2,1)} %collective-permute-done.refs_4_, ...), custom_call_target="tpu_custom_call" | custom-call | tf_op jit(solution)/shard_map/cond/branch_1_fun/feature_chunks/pallas_call | solution.py:670
  234.9 8.3 %feature_chunks.8.refs_0_ = f32[592,1024]{1,0:T(8,128)} custom-call(s32[1]{0:T(128)} %bitcast.14.refs_0_, bf16[2304,1440]{1,0:T(8,128)(2,1)} %get-tuple-element.160.refs_1_, bf16[2304,1440]{1,0:T(8,128)(2,1)} %get-tuple-element.178.refs_2_, bf16[2880,1024]{1,0:T(8,128)(2,1)} %bitcast.141, bf16[592,1024]{1,0:T(8,128)(2,1)} %get-tuple-element.184.refs_4_, ...), custom_call_target="tpu_custom_call" | custom-call | tf_op jit(solution)/shard_map/feature_chunks/pallas_call | solution.py:670
  243.1 20.3 %collective-permute-done.25.refs_2_ = bf16[1440,1024]{1,0:T(8,128)(2,1)} collective-permute-done((bf16[1440,1024]{1,0:T(8,128)(2,1)}, bf16[1440,1024]{1,0:T(8,128)(2,1)}, u32[]{:S(2)}, u32[]{:S(2)}) %collective-permute-start.25) | collective-permute-done | bytes 2949152 | tf_op jit(solution)/shard_map/ppermute | solution.py:134
  269.2 8.5 %place.5 = bf16[4,1440,1024]{2,1,0:T(8,128)(2,1)} custom-call(bf16[1440,1024]{1,0:T(8,128)(2,1)} %get-tuple-element.177.refs_0_, bf16[1440,1024]{1,0:T(8,128)(2,1)} %collective-permute-done.24.refs_1_, bf16[1440,1024]{1,0:T(8,128)(2,1)} %collective-permute-done.25.refs_2_, bf16[1440,1024]{1,0:T(8,128)(2,1)} %collective-permute-done.26.refs_3_), custom_call_target="tpu_custom_call" | custom-call | tf_op jit(solution)/shard_map/place/pallas_call | solution.py:179
  277.7 7.9 %half_product.9 = bf16[4,1,576,720]{3,2,1,0:T(8,128)(2,1)} custom-call(s32[1]{0:T(128)} %bitcast.56.refs_0_, bf16[4,2,720,1024]{3,2,1,0:T(8,128)(2,1)} %bitcast.145, bf16[576,1024]{1,0:T(8,128)(2,1)} %multiply_convert_fusion.refs_2_), custom_call_target="tpu_custom_call" | custom-call | tf_op jit(solution)/shard_map/half_product/pallas_call | solution.py:493
  285.6 7.3 %collective-permute-done.27.refs_1_ = bf16[592,1024]{1,0:T(8,128)(2,1)} collective-permute-done((bf16[592,1024]{1,0:T(8,128)(2,1)}, bf16[592,1024]{1,0:T(8,128)(2,1)}, u32[]{:S(2)}, u32[]{:S(2)}) %collective-permute-start.27) | collective-permute-done | bytes 1212448 | tf_op jit(solution)/shard_map/ppermute | solution.py:134
  292.9 6.2 attn_grad.1
  299.0 6.7 %feature_chunks.9 = (bf16[576,1024]{1,0:T(8,128)(2,1)}, bf16[576,1024]{1,0:T(8,128)(2,1)}) custom-call(s32[2]{0:T(128)} %pad_add_fusion.2.refs_0_, bf16[2304,576]{1,0:T(8,128)(2,1)} %flip.3.refs_1_, bf16[576,1024]{1,0:T(8,128)(2,1)} %get-tuple-element.194.refs_2_), custom_call_target="tpu_custom_call" | custom-call | tf_op jit(solution)/shard_map/feature_chunks/pallas_call | solution.py:670
  305.7 3.1 collective-permute-done.28.refs_3_
  308.8 10.3 %half_product.10 = bf16[4,1,288,1920]{3,2,1,0:T(8,128)(2,1)} custom-call(s32[1]{0:T(128)} %bitcast.59.refs_0_, bf16[4,2,288,1024]{3,2,1,0:T(8,128)(2,1)} %bitcast.144, bf16[2880,1024]{1,0:T(8,128)(2,1)} %bitcast.142, bf16[4,1,288,1920]{3,2,1,0:T(8,128)(2,1)} %collective-permute-done.29.refs_3_), custom_call_target="tpu_custom_call" | custom-call | tf_op jit(solution)/shard_map/half_product/pallas_call | solution.py:493
  320.8 3.8 feature_chunks.10
  327.0 3.8 feature_chunks.11
  330.8 5.5 half_product.11
  336.3 16.9 %collective-permute-done.31 = bf16[576,1024]{1,0:T(8,128)(2,1)S(1)} collective-permute-done((bf16[576,1024]{1,0:T(8,128)(2,1)}, bf16[576,1024]{1,0:T(8,128)(2,1)S(1)}, u32[]{:S(2)}, u32[]{:S(2)}) %collective-permute-start.31) | collective-permute-done | bytes 1179680 | tf_op jit(solution)/shard_map/ppermute | solution.py:134
  354.2 20.6 %attention_backward.1 = (bf16[9,64,1024]{2,1,0:T(8,128)(2,1)S(1)}, bf16[9,64,1024]{2,1,0:T(8,128)(2,1)S(1)}, bf16[9,64,1024]{2,1,0:T(8,128)(2,1)S(1)}) custom-call(bf16[9,64,1024]{2,1,0:T(8,128)(2,1)} %get-tuple-element.187.q_ref, bf16[9,64,1024]{2,1,0:T(8,128)(2,1)} %get-tuple-element.188.k_ref, bf16[9,64,1024]{2,1,0:T(8,128)(2,1)} %get-tuple-element.189.v_ref, ...), custom_call_target="tpu_custom_call" | custom-call | tf_op jit(solution)/shard_map/attention_backward/pallas_call | solution.py:119
  374.8 8.9 %half_product.12 = bf16[4,3,288,576]{3,2,1,0:T(8,128)(2,1)} custom-call(s32[1]{0:T(128)} %bitcast.56.refs_0_, bf16[4,2,288,1024]{3,2,1,0:T(8,128)(2,1)} %bitcast.133, bf16[576,1024]{1,0:T(8,128)(2,1)S(1)} %bitcast.154, bf16[576,1024]{1,0:T(8,128)(2,1)S(1)} %bitcast.157, bf16[576,1024]{1,0:T(8,128)(2,1)S(1)} %bitcast.160), custom_call_target="tpu_custom_call" | custom-call | tf_op jit(solution)/shard_map/half_product/pallas_call | solution.py:493
  383.7 14.4 %collective-permute-done.32.refs_3_ = bf16[4,1,576,720]{3,2,1,0:T(8,128)(2,1)} collective-permute-done((bf16[4,1,576,720]{3,2,1,0:T(8,128)(2,1)}, bf16[4,1,576,720]{3,2,1,0:T(8,128)(2,1)}, u32[]{:S(2)}, u32[]{:S(2)}) %collective-permute-start.32) | collective-permute-done | bytes 3317792 | tf_op jit(solution)/shard_map/ppermute | solution.py:535
  398.1 8.4 %half_product.13 = bf16[4,1,576,720]{3,2,1,0:T(8,128)(2,1)} custom-call(s32[1]{0:T(128)} %bitcast.59.refs_0_, bf16[4,2,720,1024]{3,2,1,0:T(8,128)(2,1)} %bitcast.146, bf16[576,1024]{1,0:T(8,128)(2,1)} %multiply_convert_fusion.refs_2_, bf16[4,1,576,720]{3,2,1,0:T(8,128)(2,1)} %collective-permute-done.32.refs_3_), custom_call_target="tpu_custom_call" | custom-call | tf_op jit(solution)/shard_map/half_product/pallas_call | solution.py:493
  409.8 52.5 %conditional.5 = (f32[256,2304]{1,0:T(8,128)}, bf16[256,2304]{1,0:T(8,128)(2,1)}) conditional(s32[]{:T(128)} %convert_element_type.94, () %tuple.100, (bf16[2304,576]{0,1:T(8,128)(2,1)}, bf16[2304,576]{0,1:T(8,128)(2,1)}, bf16[2304,576]{0,1:T(8,128)(2,1)}, bf16[576,1024]{1,0:T(8,128)(2,1)S(1)}, bf16[576,1024]{1,0:T(8,128)(2,1)S(1)}, ...), branch_computations={%region_4.5_spmd, %region_5.6_spmd} | conditional | flops 7 | bytes 14155984 | solution.py:143
  410.4 12.7 %token_chunks.3 = (bf16[256,2304]{1,0:T(8,128)(2,1)}, bf16[256,2304]{1,0:T(8,128)(2,1)}) custom-call(s32[2]{0:T(128)} %pad_add_fusion.1.refs_0_, bf16[576,2304]{1,0:T(8,128)(2,1)} %bitcast.163, bf16[576,2304]{1,0:T(8,128)(2,1)} %bitcast.166, bf16[576,2304]{1,0:T(8,128)(2,1)} %bitcast.169, bf16[576,1024]{1,0:T(8,128)(2,1)S(1)} %get-tuple-element.50.refs_4_, ...), custom_call_target="tpu_custom_call" | custom-call | tf_op jit(solution)/shard_map/cond/branch_1_fun/token_chunks/pallas_call | solution.py:756
  423.6 2.7 collective-permute-done.2.refs_7_
  426.3 7.7 %token_chunks.4 = bf16[256,2304]{1,0:T(8,128)(2,1)} custom-call(s32[1]{0:T(128)} %bitcast.6.refs_0_, bf16[576,2304]{1,0:T(8,128)(2,1)} %bitcast.164, bf16[576,2304]{1,0:T(8,128)(2,1)} %bitcast.167, bf16[576,2304]{1,0:T(8,128)(2,1)} %bitcast.170, bf16[576,1024]{1,0:T(8,128)(2,1)S(1)} %get-tuple-element.50.refs_4_, ...), custom_call_target="tpu_custom_call" | custom-call | tf_op jit(solution)/shard_map/cond/branch_1_fun/token_chunks/pallas_call | solution.py:756
  435.2 8.1 %token_chunks.5 = f32[256,2304]{1,0:T(8,128)} custom-call(s32[1]{0:T(128)} %bitcast.5.refs_0_, bf16[576,2304]{1,0:T(8,128)(2,1)} %bitcast.165, bf16[576,2304]{1,0:T(8,128)(2,1)} %bitcast.168, bf16[576,2304]{1,0:T(8,128)(2,1)} %bitcast.171, bf16[576,1024]{1,0:T(8,128)(2,1)S(1)} %get-tuple-element.50.refs_4_, bf16[576,1024]{1,0:T(8,128)(2,1)S(1)} %get-tuple-element.51.refs_5_, ...), custom_call_target="tpu_custom_call" | custom-call | tf_op jit(solution)/shard_map/cond/branch_1_fun/token_chunks/pallas_call | solution.py:756
  443.3 19.0 %collective-permute-done.4 = bf16[256,2304]{1,0:T(8,128)(2,1)} collective-permute-done((bf16[256,2304]{1,0:T(8,128)(2,1)}, bf16[256,2304]{1,0:T(8,128)(2,1)}, u32[]{:S(2)}, u32[]{:S(2)}) %collective-permute-start.4) | collective-permute-done | bytes 1179680 | tf_op jit(solution)/shard_map/cond/branch_1_fun/ppermute | solution.py:134
  462.3 5.7 half_product.14
  468.0 6.2 reduce-scatter.10.cloned.1.call-done
  474.3 12.7 %fusion.9 = bf16[576,1024]{1,0:T(8,128)(2,1)S(1)} fusion(f32[576,1024]{1,0:T(8,128)} %get-tuple-element.164.refs_3_, bf16[5760,576]{0,1:T(8,128)(2,1)} %param.27, bf16[5760,1024]{1,0:T(8,128)(2,1)} %bitcast.147), kind=kOutput, calls=%fused_computation.15 | convolution fusion | flops 6796541952 | bytes 21970944 | tf_op jit(solution)/shard_map/fe,ft->et/dot_general | solution.py:948
  491.0 3.5 fusion.7
  498.2 5.1 collective-permute-done.39.refs_3_
  505.3 2.9 bitcast_convert_fusion
  508.2 3.1 copy.34
  511.3 4.6 collective-permute-done.36.refs_3_
  520.3 4.9 fusion.6
  525.2 10.1 %collective-permute-done.46.refs_5_ = bf16[4,3,288,576]{3,2,1,0:T(8,128)(2,1)} collective-permute-done((bf16[4,3,288,576]{3,2,1,0:T(8,128)(2,1)}, bf16[4,3,288,576]{3,2,1,0:T(8,128)(2,1)}, u32[]{:S(2)}, u32[]{:S(2)}) %collective-permute-start.46) | collective-permute-done | bytes 3981344 | tf_op jit(solution)/shard_map/ppermute | solution.py:535
  535.3 9.5 %half_product.15 = bf16[4,3,288,576]{3,2,1,0:T(8,128)(2,1)} custom-call(s32[1]{0:T(128)} %bitcast.59.refs_0_, bf16[4,2,288,1024]{3,2,1,0:T(8,128)(2,1)} %bitcast.134, bf16[576,1024]{1,0:T(8,128)(2,1)S(1)} %bitcast.156, bf16[576,1024]{1,0:T(8,128)(2,1)S(1)} %bitcast.159, bf16[576,1024]{1,0:T(8,128)(2,1)} %bitcast.162, ...), custom_call_target="tpu_custom_call" | custom-call | tf_op jit(solution)/shard_map/half_product/pallas_call | solution.py:493
  553.4 10.8 %collective-permute-done.43 = f32[2,2304]{1,0:T(2,128)S(1)} collective-permute-done((f32[2,2304]{1,0:T(2,128)S(1)}, f32[2,2304]{1,0:T(2,128)S(1)}, u32[]{:S(2)}, u32[]{:S(2)}) %collective-permute-start.43) | collective-permute-done | bytes 18464 | tf_op jit(solution)/shard_map/ppermute | solution.py:600
  565.9 4.9 collective-permute-done.44
  573.0 5.2 collective-permute-done.45
  584.7 42.6 %reduce-scatter.14.cloned.1.call-done = bf16[1,3,288,576]{3,2,1,0:T(8,128)(2,1)} async-done(((bf16[4,3,288,576]{3,2,1,0:T(8,128)(2,1)}), bf16[1,3,288,576]{3,2,1,0:T(8,128)(2,1)}) %reduce-scatter.14.cloned.1.call-update) | async-done | bytes 995344 | tf_op jit(solution)/shard_map/reduce_scatter | solution.py:541
  627.3 2.6 fusion.10
  (220 shorter events, 101.5 us)
Async XLA Ops:
  7.2 131.1 %all-gather.2.cloned.1.call-start = ((), (), s32[]{:S(2)}) async-start(), calls=%async_computation.5 | async-start | bytes 3981312 | tf_op jit(solution)/shard_map/all_gather | solution.py:828
  7.2 3.9 collective-permute-start.5
  7.7 29.3 %collective-permute-start.6 = (bf16[256,2304]{1,0:T(8,128)(2,1)}, bf16[256,2304]{1,0:T(8,128)(2,1)S(1)}, u32[]{:S(2)}, u32[]{:S(2)}) collective-permute-start(bf16[256,2304]{1,0:T(8,128)(2,1)} %refs_1_.2), channel_id=1, source_target_pairs={{0,2},{1,3},{2,0},{3,1},{4,6},{5,7},{6,4},{7,5},{8,10},{9,11},{10,... | collective-permute-start | bytes 3538952 | tf_op jit(solution)/shard_map/ppermute | solution.py:134
  17.4 6.1 copy-start
  17.4 6.1 copy-start.18
  37.1 3.5 collective-permute-start.7
  38.4 17.8 %collective-permute-start.12 = (bf16[72,1440]{1,0:T(8,128)(2,1)S(1)}, bf16[72,1440]{1,0:T(8,128)(2,1)S(1)}, u32[]{:S(2)}, u32[]{:S(2)}) collective-permute-start(bf16[72,1440]{1,0:T(8,128)(2,1)S(1)} %get-tuple-element.153), channel_id=1, source_target_pairs={{0,2},{1,3},{2,0},{3,1},{4,6},{5,7},{6,4},{7,5},{8,10},{9,11},{10,... | collective-permute-start | bytes 622088 | tf_op jit(solution)/shard_map/ppermute | solution.py:134
  40.3 16.2 %collective-permute-start.11 = (bf16[72,1440]{1,0:T(8,128)(2,1)S(1)}, bf16[72,1440]{1,0:T(8,128)(2,1)S(1)}, u32[]{:S(2)}, u32[]{:S(2)}) collective-permute-start(bf16[72,1440]{1,0:T(8,128)(2,1)S(1)} %get-tuple-element.151), channel_id=1, source_target_pairs={{0,2},{1,3},{2,0},{3,1},{4,6},{5,7},{6,4},{7,5},{8,10},{9,11},{10,... | collective-permute-start | bytes 622088 | tf_op jit(solution)/shard_map/ppermute | solution.py:134
  56.2 1.5 collective-permute-start.19
  58.5 260.5 %reduce-scatter.6.cloned.1.call-start = ((), (), s32[]{:S(2)}) async-start(), calls=%async_computation.6 | async-start | bytes 5898240 | tf_op jit(solution)/shard_map/reduce_scatter | solution.py:541
  58.6 28.2 %collective-permute-start.13 = (bf16[256,2304]{1,0:T(8,128)(2,1)S(1)}, bf16[256,2304]{1,0:T(8,128)(2,1)S(1)}, u32[]{:S(2)}, u32[]{:S(2)}) collective-permute-start(bf16[256,2304]{1,0:T(8,128)(2,1)S(1)} %copy-done.10), channel_id=1, source_target_pairs={{0,2},{1,3},{2,0},{3,1},{4,6},{5,7},{6,4},{7,5},{8,10},{9,11},{10,... | collective-permute-start | bytes 3538952 | tf_op jit(solution)/shard_map/ppermute | solution.py:134
  60.5 29.4 %collective-permute-start.10 = (bf16[256,2304]{1,0:T(8,128)(2,1)S(1)}, bf16[256,2304]{1,0:T(8,128)(2,1)S(1)}, u32[]{:S(2)}, u32[]{:S(2)}) collective-permute-start(bf16[256,2304]{1,0:T(8,128)(2,1)S(1)} %copy-done.10), channel_id=1, source_target_pairs={{0,1},{1,0},{2,3},{3,2},{4,5},{5,4},{6,7},{7,6},{8,9},{9,8},{10,11... | collective-permute-start | bytes 3538952 | tf_op jit(solution)/shard_map/ppermute | solution.py:134
  86.8 4.0 collective-permute-start.14
  87.8 35.1 %collective-permute-start.9 = (bf16[576,1024]{1,0:T(8,128)(2,1)}, bf16[576,1024]{1,0:T(8,128)(2,1)}, u32[]{:S(2)}, u32[]{:S(2)}) collective-permute-start(bf16[576,1024]{1,0:T(8,128)(2,1)} %bitcast.177), channel_id=1, source_target_pairs={{0,2},{1,3},{2,0},{3,1},{4,6},{5,7},{6,4},{7,5},{8,10},{9,11},{10,... | collective-permute-start | bytes 3538952 | tf_op jit(solution)/shard_map/ppermute | solution.py:134
  89.6 35.7 %collective-permute-start.8 = (bf16[576,1024]{1,0:T(8,128)(2,1)}, bf16[576,1024]{1,0:T(8,128)(2,1)}, u32[]{:S(2)}, u32[]{:S(2)}) collective-permute-start(bf16[576,1024]{1,0:T(8,128)(2,1)} %bitcast.178), channel_id=1, source_target_pairs={{0,1},{1,0},{2,3},{3,2},{4,5},{5,4},{6,7},{7,6},{8,9},{9,8},{10,11... | collective-permute-start | bytes 3538952 | tf_op jit(solution)/shard_map/ppermute | solution.py:134
  99.4 166.0 %copy-start.6 = (f32[576,1024]{1,0:T(8,128)}, f32[576,1024]{1,0:T(8,128)S(1)}, u32[]{:S(2)}) copy-start(f32[576,1024]{1,0:T(8,128)S(1)} %get-tuple-element.191.refs_2_) | copy-start | bytes 7077892
  122.9 4.4 collective-permute-start.15
  123.6 17.0 %collective-permute-start.18 = (bf16[576,1440]{1,0:T(8,128)(2,1)}, bf16[576,1440]{1,0:T(8,128)(2,1)}, u32[]{:S(2)}, u32[]{:S(2)}) collective-permute-start(bf16[576,1440]{1,0:T(8,128)(2,1)} %get-tuple-element.227), channel_id=1, source_target_pairs={{0,1},{1,0},{2,3},{3,2},{4,5},{5,4},{6,7},{7,6},{8,9},{9,8},{10,11... | collective-permute-start | bytes 4976648 | tf_op jit(solution)/shard_map/ppermute | solution.py:134
  137.7 16.3 %collective-permute-start.17 = (bf16[592,512]{1,0:T(8,128)(2,1)}, bf16[592,512]{1,0:T(8,128)(2,1)}, u32[]{:S(2)}, u32[]{:S(2)}) collective-permute-start(bf16[592,512]{1,0:T(8,128)(2,1)} %get-tuple-element.166), channel_id=1, source_target_pairs={{0,2},{1,3},{2,0},{3,1},{4,6},{5,7},{6,4},{7,5},{8,10},{9,11},{10,... | collective-permute-start | bytes 1818632 | tf_op jit(solution)/shard_map/ppermute | solution.py:134
  138.1 17.4 %collective-permute-start.21 = (bf16[592,512]{1,0:T(8,128)(2,1)}, bf16[592,512]{1,0:T(8,128)(2,1)}, u32[]{:S(2)}, u32[]{:S(2)}) collective-permute-start(bf16[592,512]{1,0:T(8,128)(2,1)} %get-tuple-element.166), channel_id=1, source_target_pairs={{0,1},{1,0},{2,3},{3,2},{4,5},{5,4},{6,7},{7,6},{8,9},{9,8},{10,11... | collective-permute-start | bytes 1818632 | tf_op jit(solution)/shard_map/ppermute | solution.py:134
  138.2 5.6 slice-start
  143.9 10.2 %copy-start.30 = (bf16[592,512]{1,0:T(8,128)(2,1)S(1)}, bf16[592,512]{1,0:T(8,128)(2,1)}, u32[]{:S(2)}) copy-start(bf16[592,512]{1,0:T(8,128)(2,1)} %get-tuple-element.169.refs_0_) | copy-start | bytes 1818628
  154.0 2.4 collective-permute-start.22
  154.1 17.0 %collective-permute-start.20 = (bf16[592,512]{1,0:T(8,128)(2,1)S(1)}, bf16[592,512]{1,0:T(8,128)(2,1)}, u32[]{:S(2)}, u32[]{:S(2)}) collective-permute-start(bf16[592,512]{1,0:T(8,128)(2,1)S(1)} %copy-done.30), channel_id=1, source_target_pairs={{0,2},{1,3},{2,0},{3,1},{4,6},{5,7},{6,4},{7,5},{8,10},{9,11},{10,... | collective-permute-start | bytes 1818632 | tf_op jit(solution)/shard_map/ppermute | solution.py:134
  155.5 15.7 %collective-permute-start.16 = (bf16[592,512]{1,0:T(8,128)(2,1)S(1)}, bf16[592,512]{1,0:T(8,128)(2,1)}, u32[]{:S(2)}, u32[]{:S(2)}) collective-permute-start(bf16[592,512]{1,0:T(8,128)(2,1)S(1)} %copy-done.30), channel_id=1, source_target_pairs={{0,1},{1,0},{2,3},{3,2},{4,5},{5,4},{6,7},{7,6},{8,9},{9,8},{10,11... | collective-permute-start | bytes 1818632 | tf_op jit(solution)/shard_map/ppermute | solution.py:134
  171.0 2.4 collective-permute-start.23
  197.1 209.4 %reduce-scatter.8.cloned.1.call-start = ((), (), s32[]{:S(2)}) async-start(), calls=%async_computation.7 | async-start | bytes 5529600 | tf_op jit(solution)/shard_map/reduce_scatter | solution.py:541
  197.1 66.3 %collective-permute-start.25 = (bf16[1440,1024]{1,0:T(8,128)(2,1)}, bf16[1440,1024]{1,0:T(8,128)(2,1)}, u32[]{:S(2)}, u32[]{:S(2)}) collective-permute-start(bf16[1440,1024]{1,0:T(8,128)(2,1)} %get-tuple-element.177.refs_0_), channel_id=1, source_target_pairs={{0,2},{1,3},{2,0},{3,1},{4,6},{5,7},{6,4},{7,5},{8,10},{9,11},{10,... | collective-permute-start | bytes 8847368 | tf_op jit(solution)/shard_map/ppermute | solution.py:134
  207.6 101.2 %collective-permute-start.29 = (bf16[4,1,288,1920]{3,2,1,0:T(8,128)(2,1)}, bf16[4,1,288,1920]{3,2,1,0:T(8,128)(2,1)}, u32[]{:S(2)}, u32[]{:S(2)}) collective-permute-start(bf16[4,1,288,1920]{3,2,1,0:T(8,128)(2,1)} %half_product.8), channel_id=1, source_target_pairs={{0,4},{4,0},{8,12},{12,8},{16,20},{20,16},{24,28},{28,24},{1,5},{5... | collective-permute-start | bytes 13271048 | tf_op jit(solution)/shard_map/ppermute | solution.py:535
  209.2 57.5 %collective-permute-start.24 = (bf16[1440,1024]{1,0:T(8,128)(2,1)}, bf16[1440,1024]{1,0:T(8,128)(2,1)}, u32[]{:S(2)}, u32[]{:S(2)}) collective-permute-start(bf16[1440,1024]{1,0:T(8,128)(2,1)} %get-tuple-element.177.refs_0_), channel_id=1, source_target_pairs={{0,1},{1,0},{2,3},{3,2},{4,5},{5,4},{6,7},{7,6},{8,9},{9,8},{10,11... | collective-permute-start | bytes 8847368 | tf_op jit(solution)/shard_map/ppermute | solution.py:134
  223.6 3.4 collective-permute-start
  224.1 10.8 %collective-permute-start.1 = (bf16[592,1024]{1,0:T(8,128)(2,1)}, bf16[592,1024]{1,0:T(8,128)(2,1)}, u32[]{:S(2)}, u32[]{:S(2)}) collective-permute-start(bf16[592,1024]{1,0:T(8,128)(2,1)} %get-tuple-element.46), channel_id=1, source_target_pairs={{0,1},{1,0},{2,3},{3,2},{4,5},{5,4},{6,7},{7,6},{8,9},{9,8},{10,11... | collective-permute-start | bytes 3637256 | tf_op jit(solution)/shard_map/cond/branch_1_fun/ppermute | solution.py:134
  263.5 5.7 collective-permute-start.26
  263.5 29.4 %collective-permute-start.27 = (bf16[592,1024]{1,0:T(8,128)(2,1)}, bf16[592,1024]{1,0:T(8,128)(2,1)}, u32[]{:S(2)}, u32[]{:S(2)}) collective-permute-start(bf16[592,1024]{1,0:T(8,128)(2,1)} %get-tuple-element.190), channel_id=1, source_target_pairs={{0,2},{1,3},{2,0},{3,1},{4,6},{5,7},{6,4},{7,5},{8,10},{9,11},{10,... | collective-permute-start | bytes 3637256 | tf_op jit(solution)/shard_map/ppermute | solution.py:134
  305.7 3.1 collective-permute-start.28
  308.8 10.3 %copy-start.23 = (bf16[576,1024]{1,0:T(8,128)(2,1)}, bf16[576,1024]{1,0:T(8,128)(2,1)S(1)}, u32[]{:S(2)}) copy-start(bf16[576,1024]{1,0:T(8,128)(2,1)S(1)} %collective-permute-done.28.refs_3_) | copy-start | bytes 3538948
  319.1 155.1 %reduce-scatter.10.cloned.1.call-start = ((), (), s32[]{:S(2)}) async-start(), calls=%async_computation.8 | async-start | bytes 4423680 | tf_op jit(solution)/shard_map/reduce_scatter | solution.py:541
  319.1 79.0 %collective-permute-start.32 = (bf16[4,1,576,720]{3,2,1,0:T(8,128)(2,1)}, bf16[4,1,576,720]{3,2,1,0:T(8,128)(2,1)}, u32[]{:S(2)}, u32[]{:S(2)}) collective-permute-start(bf16[4,1,576,720]{3,2,1,0:T(8,128)(2,1)} %half_product.9), channel_id=1, source_target_pairs={{0,4},{4,0},{8,12},{12,8},{16,20},{20,16},{24,28},{28,24},{1,5},{5... | collective-permute-start | bytes 9953288 | tf_op jit(solution)/shard_map/ppermute | solution.py:535
  320.8 5.1 collective-permute-start.30
  324.6 28.6 %collective-permute-start.31 = (bf16[576,1024]{1,0:T(8,128)(2,1)}, bf16[576,1024]{1,0:T(8,128)(2,1)S(1)}, u32[]{:S(2)}, u32[]{:S(2)}) collective-permute-start(bf16[576,1024]{1,0:T(8,128)(2,1)} %feature_chunks.10), channel_id=1, source_target_pairs={{0,2},{1,3},{2,0},{3,1},{4,6},{5,7},{6,4},{7,5},{8,10},{9,11},{10,... | collective-permute-start | bytes 3538952 | tf_op jit(solution)/shard_map/ppermute | solution.py:134
  374.8 8.9 %copy-start.16 = (bf16[9,64,1024]{2,1,0:T(8,128)(2,1)}, bf16[9,64,1024]{2,1,0:T(8,128)(2,1)S(1)}, u32[]{:S(2)}) copy-start(bf16[9,64,1024]{2,1,0:T(8,128)(2,1)S(1)} %get-tuple-element.206) | copy-start | bytes 3538948
  406.5 138.2 %reduce-scatter.12.cloned.1.call-start = ((), (), s32[]{:S(2)}) async-start(), calls=%async_computation.9 | async-start | bytes 1843200 | tf_op jit(solution)/shard_map/reduce_scatter | solution.py:541
  406.6 55.7 %collective-permute-start.33 = (bf16[4,1,288,576]{3,2,1,0:T(8,128)(2,1)}, bf16[4,1,288,576]{3,2,1,0:T(8,128)(2,1)}, u32[]{:S(2)}, u32[]{:S(2)}) collective-permute-start(bf16[4,1,288,576]{3,2,1,0:T(8,128)(2,1)} %half_product.11), channel_id=1, source_target_pairs={{0,4},{4,0},{8,12},{12,8},{16,20},{20,16},{24,28},{28,24},{1,5},{5... | collective-permute-start | bytes 3981320 | tf_op jit(solution)/shard_map/ppermute | solution.py:535
  408.6 126.7 %collective-permute-start.46 = (bf16[4,3,288,576]{3,2,1,0:T(8,128)(2,1)}, bf16[4,3,288,576]{3,2,1,0:T(8,128)(2,1)}, u32[]{:S(2)}, u32[]{:S(2)}) collective-permute-start(bf16[4,3,288,576]{3,2,1,0:T(8,128)(2,1)} %half_product.12), channel_id=1, source_target_pairs={{0,4},{4,0},{8,12},{12,8},{16,20},{20,16},{24,28},{28,24},{1,5},{5... | collective-permute-start | bytes 11943944 | tf_op jit(solution)/shard_map/ppermute | solution.py:535
  423.1 3.2 collective-permute-start.2
  423.1 12.1 %collective-permute-start.3 = (bf16[256,2304]{1,0:T(8,128)(2,1)}, bf16[256,2304]{1,0:T(8,128)(2,1)}, u32[]{:S(2)}, u32[]{:S(2)}) collective-permute-start(bf16[256,2304]{1,0:T(8,128)(2,1)} %get-tuple-element.55), channel_id=1, source_target_pairs={{0,1},{1,0},{2,3},{3,2},{4,5},{5,4},{6,7},{7,6},{8,9},{9,8},{10,11... | collective-permute-start | bytes 3538952 | tf_op jit(solution)/shard_map/cond/branch_1_fun/ppermute | solution.py:134
  434.0 28.3 %collective-permute-start.4 = (bf16[256,2304]{1,0:T(8,128)(2,1)}, bf16[256,2304]{1,0:T(8,128)(2,1)}, u32[]{:S(2)}, u32[]{:S(2)}) collective-permute-start(bf16[256,2304]{1,0:T(8,128)(2,1)} %token_chunks.4), channel_id=1, source_target_pairs={{0,2},{1,3},{2,0},{3,1},{4,6},{5,7},{6,4},{7,5},{8,10},{9,11},{10,... | collective-permute-start | bytes 3538952 | tf_op jit(solution)/shard_map/cond/branch_1_fun/ppermute | solution.py:134
  474.2 153.1 %reduce-scatter.14.cloned.1.call-start = ((), (), s32[]{:S(2)}) async-start(), calls=%async_computation.10 | async-start | bytes 5529600 | tf_op jit(solution)/shard_map/reduce_scatter | solution.py:541
  474.3 12.7 %copy-start.25 = (bf16[576,1024]{1,0:T(8,128)(2,1)S(1)}, bf16[576,1024]{1,0:T(8,128)(2,1)}, u32[]{:S(2)}) copy-start(bf16[576,1024]{1,0:T(8,128)(2,1)} %get-tuple-element.213) | copy-start | bytes 3538948
  487.8 7.3 %collective-permute-start.37 = (bf16[576,256]{1,0:T(8,128)(2,1)S(1)}, bf16[576,256]{1,0:T(8,128)(2,1)S(1)}, u32[]{:S(2)}, u32[]{:S(2)}) collective-permute-start(bf16[576,256]{1,0:T(8,128)(2,1)S(1)} %get-tuple-element.235), channel_id=1, source_target_pairs={{0,1},{1,0},{2,3},{3,2},{4,5},{5,4},{6,7},{7,6},{8,9},{9,8},{10,11... | collective-permute-start | bytes 884744 | tf_op jit(solution)/shard_map/ppermute | solution.py:134
  487.8 9.9 %collective-permute-start.38 = (bf16[576,256]{1,0:T(8,128)(2,1)S(1)}, bf16[576,256]{1,0:T(8,128)(2,1)}, u32[]{:S(2)}, u32[]{:S(2)}) collective-permute-start(bf16[576,256]{1,0:T(8,128)(2,1)S(1)} %get-tuple-element.234), channel_id=1, source_target_pairs={{0,2},{1,3},{2,0},{3,1},{4,6},{5,7},{6,4},{7,5},{8,10},{9,11},{10,... | collective-permute-start | bytes 884744 | tf_op jit(solution)/shard_map/ppermute | solution.py:134
  489.3 14.0 %collective-permute-start.39 = (bf16[576,256]{1,0:T(8,128)(2,1)S(1)}, bf16[576,256]{1,0:T(8,128)(2,1)}, u32[]{:S(2)}, u32[]{:S(2)}) collective-permute-start(bf16[576,256]{1,0:T(8,128)(2,1)S(1)} %get-tuple-element.233), channel_id=1, source_target_pairs={{0,3},{1,2},{2,1},{3,0},{4,7},{5,6},{6,5},{7,4},{8,11},{9,10},{10,... | collective-permute-start | bytes 884744 | tf_op jit(solution)/shard_map/ppermute | solution.py:134
  490.7 20.6 %collective-permute-start.34 = (bf16[576,256]{1,0:T(8,128)(2,1)}, bf16[576,256]{1,0:T(8,128)(2,1)}, u32[]{:S(2)}, u32[]{:S(2)}) collective-permute-start(bf16[576,256]{1,0:T(8,128)(2,1)} %get-tuple-element.239), channel_id=1, source_target_pairs={{0,1},{1,0},{2,3},{3,2},{4,5},{5,4},{6,7},{7,6},{8,9},{9,8},{10,11... | collective-permute-start | bytes 884744 | tf_op jit(solution)/shard_map/ppermute | solution.py:134
  495.1 8.2 %copy-start.32 = (bf16[576,256]{1,0:T(8,128)(2,1)}, bf16[576,256]{1,0:T(8,128)(2,1)S(1)}, u32[]{:S(2)}) copy-start(bf16[576,256]{1,0:T(8,128)(2,1)S(1)} %collective-permute-done.37.refs_1_) | copy-start | bytes 884740
  495.1 16.2 %collective-permute-start.35 = (bf16[576,256]{1,0:T(8,128)(2,1)}, bf16[576,256]{1,0:T(8,128)(2,1)}, u32[]{:S(2)}, u32[]{:S(2)}) collective-permute-start(bf16[576,256]{1,0:T(8,128)(2,1)} %get-tuple-element.238), channel_id=1, source_target_pairs={{0,2},{1,3},{2,0},{3,1},{4,6},{5,7},{6,4},{7,5},{8,10},{9,11},{10,... | collective-permute-start | bytes 884744 | tf_op jit(solution)/shard_map/ppermute | solution.py:134
  497.7 18.2 %collective-permute-start.36 = (bf16[576,256]{1,0:T(8,128)(2,1)}, bf16[576,256]{1,0:T(8,128)(2,1)}, u32[]{:S(2)}, u32[]{:S(2)}) collective-permute-start(bf16[576,256]{1,0:T(8,128)(2,1)} %get-tuple-element.237), channel_id=1, source_target_pairs={{0,3},{1,2},{2,1},{3,0},{4,7},{5,6},{6,5},{7,4},{8,11},{9,10},{10,... | collective-permute-start | bytes 884744 | tf_op jit(solution)/shard_map/ppermute | solution.py:134
  544.8 34.2 %copy-start.28 = (bf16[1,1,288,1920]{3,2,1,0:T(8,128)(2,1)S(1)}, bf16[1,1,288,1920]{3,2,1,0:T(8,128)(2,1)}, u32[]{:S(2)}) copy-start(bf16[1,1,288,1920]{3,2,1,0:T(8,128)(2,1)} %reduce-scatter.8.cloned.1.call-done) | copy-start | bytes 3317764
  546.1 3.7 collective-permute-start.40
  546.2 3.8 collective-permute-start.41
  547.6 3.3 collective-permute-start.42
  548.1 30.7 %collective-permute-start.47 = (bf16[288,960]{1,0:T(8,128)(2,1)S(1)}, bf16[288,960]{1,0:T(8,128)(2,1)S(1)}, u32[]{:S(2)}, u32[]{:S(2)}) collective-permute-start(bf16[288,960]{1,0:T(8,128)(2,1)S(1)} %dynamic-slice_bitcast_fusion.2), channel_id=1, source_target_pairs={{0,4},{4,0},{8,12},{12,8},{16,20},{20,16},{24,28},{28,24},{1,5},{5... | collective-permute-start | bytes 1658888 | tf_op jit(solution)/shard_map/ppermute | solution.py:535
  551.7 12.5 %collective-permute-start.43 = (f32[2,2304]{1,0:T(2,128)S(1)}, f32[2,2304]{1,0:T(2,128)S(1)}, u32[]{:S(2)}, u32[]{:S(2)}) collective-permute-start(f32[2,2304]{1,0:T(2,128)S(1)} %add_add_fusion), channel_id=1, source_target_pairs={{0,4},{4,0},{8,12},{12,8},{16,20},{20,16},{24,28},{28,24},{1,5},{5... | collective-permute-start | bytes 55304 | tf_op jit(solution)/shard_map/ppermute | solution.py:600
  564.2 6.6 %collective-permute-start.44 = (f32[2,2304]{1,0:T(2,128)S(1)}, f32[2,2304]{1,0:T(2,128)S(1)}, u32[]{:S(2)}, u32[]{:S(2)}) collective-permute-start(f32[2,2304]{1,0:T(2,128)S(1)} %add.155), channel_id=1, source_target_pairs={{0,8},{4,12},{8,0},{12,4},{16,24},{20,28},{24,16},{28,20},{1,9},{5... | collective-permute-start | bytes 55304 | tf_op jit(solution)/shard_map/ppermute | solution.py:600
  570.8 7.3 %collective-permute-start.45 = (f32[2,2304]{1,0:T(2,128)S(1)}, f32[2,2304]{1,0:T(2,128)S(1)}, u32[]{:S(2)}, u32[]{:S(2)}) collective-permute-start(f32[2,2304]{1,0:T(2,128)S(1)} %add.156), channel_id=1, source_target_pairs={{0,16},{4,20},{8,24},{12,28},{16,0},{20,4},{24,8},{28,12},{1,17},{... | collective-permute-start | bytes 55304 | tf_op jit(solution)/shard_map/ppermute | solution.py:600
  (29 other events, 64.2 us)
Sparse Core Ops, SparseCore 0:
  58.7 66.7 all-gather.1
  197.2 86.1 reduce-scatter.5
  319.2 81.5 reduce-scatter.7
  406.7 67.4 reduce-scatter.9
  477.0 34.0 reduce-scatter.11
  544.9 82.3 reduce-scatter.13

commit v6 on v5

--- a/solution.py
+++ b/solution.py
@@ -830,10 +830,11 @@
     )
     attended, query_low, key_low, value_low, lse = attention_forward(here, there, cosine, sine)
 
-    cotangent_blocks = [
-        cotangent, swap(cotangent, 1), cotangent_chip, swap(after(cotangent_chip, attended), 1)
-    ]
-    d_ffn, cotangent_own = spread(cotangent_blocks, (0, 1, 2, 3), gain_attn, False)
+    def spread_cotangent():
+        blocks = [cotangent, swap(cotangent, 1), cotangent_chip, swap(cotangent_chip, 1)]
+        return spread(blocks, (0, 1, 2, 3), gain_attn, False)
+
+    d_ffn, cotangent_own = stage(spread_cotangent, attended)
     d_ffn_own = (branch_scale * cotangent_own).astype(low)
     me_later = after(me, d_ffn)
 

time: 646 us -> 644 us (level)
    unnamed x78 -> x68, local copies, waits for them, and re-layouts: 18.2 us -> 10.9 us
  transfers between devices with their start and end apart: 54 -> 54, of which waited for: 27 -> 29; matrix products, arithmetic and copies ran while one was open for 13% -> 14% of each run, Pallas kernels for 40% -> 40%
where the time goes in v6:
time: 644 us; the launch traced here: 635 us
  Pallas kernels  279 us (43%)
  waiting for transfers between devices  205 us (32%)
  matrix products  41.3 us (6%)
  local copies, waits for them, and re-layouts  34.7 us (5%)
  starting transfers between devices  33.6 us (5%)
  other arithmetic  26.8 us (4%)
  between operations  15.1 us (2%)
    ppermute x40, waiting for transfers between devices, swap(): return lax.ppermute(array, 'fsdp', [(i, i ^ j) for i in range(size)])  109 us
    pallas_call x8, Pallas kernels, half_product(): pl.pallas_call(lambda *refs: product_kernel(*refs, count=count, adds=adde...  65.6 us
    reduce_scatter x5, waiting for transfers between devices, line_scatter(): lax.psum_scatter(array, 'rep', scatter_dimension=0, tiled=True, axis_inde...  48.3 us
    pallas_call x6, Pallas kernels, feature_chunks(): pl.pallas_call(lambda *refs: chunks_kernel(*refs, count=len(weights), way...  44.3 us
    pallas_call x2, Pallas kernels, inner_part(): pl.pallas_call(lambda *refs: inner_kernel(*refs, half=half), grid=(units...  29.1 us
    pallas_call x3, Pallas kernels, token_chunks(): pl.pallas_call(lambda *refs: blocks_kernel(*refs, count=len(weights), add...  28.5 us
    ppermute x5, waiting for transfers between devices, neighbour(): lax.ppermute(array, 'rep', [(i, i ^ 1) for i in range(lax.axis_size('rep'...  25.2 us
    ppermute x40, starting transfers between devices, swap(): return lax.ppermute(array, 'fsdp', [(i, i ^ j) for i in range(size)])  21.9 us
  transfers between devices with their start and end apart: 54, of which 29 were waited for; matrix products, arithmetic and copies ran while one was open for 14% of the time, Pallas kernels for 40%

profile of v6, /device:TPU:0, one launch (start us, length us, event | category | flops | bytes accessed | tf_op | source)
XLA Modules:
  0.0 634.9 jit_solution(15413921776847023489)
XLA Ops:
  14.7 2.7 spread.4
  17.4 6.1 fusion.13
  28.6 8.5 %collective-permute-done.8.refs_1_ = bf16[256,2304]{1,0:T(8,128)(2,1)S(1)} collective-permute-done((bf16[256,2304]{1,0:T(8,128)(2,1)}, bf16[256,2304]{1,0:T(8,128)(2,1)S(1)}, u32[]{:S(2)}, u32[]{:S(2)}) %collective-permute-start.8) | collective-permute-done | bytes 1179680 | tf_op jit(solution)/shard_map/ppermute | solution.py:134
  42.9 4.4 spread.5
  61.7 20.6 %attention_forward.1 = (bf16[9,64,1024]{2,1,0:T(8,128)(2,1)}, bf16[9,64,1024]{2,1,0:T(8,128)(2,1)}, bf16[9,64,1024]{2,1,0:T(8,128)(2,1)}, bf16[9,64,1024]{2,1,0:T(8,128)(2,1)}, f32[9,1,1024]{2,1,0:T(1,128)}) custom-call(f32[9,64,512]{2,1,0:T(8,128)} %bitcast.185, f32[9,64,512]{2,1,0:T(8,128)} %bitcast.186, f32[9,64,512]{2,1,0:T(8,128)} %bitcast.187, ...), custom_call_target="tpu_custom_call" | custom-call | tf_op jit(solution)/shard_map/attention_forward/pallas_call | solution.py:72
  82.7 4.8 collective-permute-done.14
  87.5 11.5 %conditional.4 = ((bf16[1024,2304]{1,0:T(8,128)(2,1)}, f32[576,1024]{1,0:T(8,128)})) conditional(s32[]{:T(128)} %convert_element_type.93, () %tuple.78, (bf16[256,2304]{1,0:T(8,128)(2,1)S(1)}, bf16[256,2304]{1,0:T(8,128)(2,1)S(1)}, f32[2304]{0:T(1024)}) %tuple.164), branch_computations={%region_0.1_spmd, %region_1.2_spmd} | conditional | flops 49 | bytes 14174888 | solution.py:143
  89.8 3.2 collective-permute-done.refs_2_
  93.2 5.8 spread.3
  99.0 5.1 dynamic-slice_bitcast_fusion
  104.1 11.5 %flip.2 = (bf16[2304,1440]{1,0:T(8,128)(2,1)}, bf16[2304,1440]{1,0:T(8,128)(2,1)}) custom-call(s32[1]{0:T(128)} %constant.149.clone.1.index, bf16[1440,2304]{1,0:T(8,128)(2,1)} %bitcast.150, bf16[1440,2304]{1,0:T(8,128)(2,1)} %bitcast.153), custom_call_target="tpu_custom_call" | custom-call | tf_op jit(solution)/shard_map/flip/pallas_call | solution.py:617
  115.6 5.6 flip.3.refs_1_
  125.3 9.3 %hidden_state.1 = (f32[576,1024]{1,0:T(8,128)}, bf16[592,512]{1,0:T(8,128)(2,1)}, bf16[592,512]{1,0:T(8,128)(2,1)}, bf16[4,576,1024]{2,1,0:T(8,128)(2,1)}) custom-call(bf16[576,1024]{1,0:T(8,128)(2,1)} %bitcast.181, bf16[576,1024]{1,0:T(8,128)(2,1)} %collective-permute-done.10.core, bf16[576,1024]{1,0:T(8,128)(2,1)} %collective-permute-done.11.chip, ...), custom_call_target="tpu_custom_call" | custom-call | tf_op jit(solution)/shard_map/hidden_state/pallas_call | solution.py:349
  138.1 3.0 place.4
  141.1 9.6 %convolution_convert_fusion.refs_6_ = bf16[1440,1024]{1,0:T(8,128)(2,1)} fusion(bf16[2304,1440]{1,0:T(8,128)(2,1)S(1)} %bitcast.139, bf16[1024,2304]{1,0:T(8,128)(2,1)S(1)} %bitcast.183), kind=kOutput, calls=%fused_computation.2 | convolution fusion | flops 6796247040 | bytes 14303232 | tf_op jit(solution)/shard_map/ef,te->ft/dot_general | solution.py:860
  153.2 15.4 %conditional.5 = ((bf16[1440,1024]{1,0:T(8,128)(2,1)S(1)}, bf16[2,1440,1024]{2,1,0:T(8,128)(2,1)}, f32[1,1024]{1,0:T(1,128)}, f32[1,1024]{1,0:T(1,128)}, bf16[4,576,1024]{2,1,0:T(8,128)(2,1)})) conditional(s32[]{:T(128)} %convert_element_type.95, () %tuple.93, (bf16[2304,1440]{0,1:T(8,128)(2,1)}, bf16[2304,1440]{0,1:T(8,128)(2,1)}, ...), branch_computations={%region_2.3_spmd, %region_3.4_spmd} | conditional | bytes 13574206 | solution.py:143
  154.1 14.6 %inner_part.2 = (bf16[1440,1024]{1,0:T(8,128)(2,1)S(1)}, bf16[2,1440,1024]{2,1,0:T(8,128)(2,1)}, f32[1,1024]{1,0:T(1,128)}, f32[1,1024]{1,0:T(1,128)}, bf16[4,576,1024]{2,1,0:T(8,128)(2,1)}) custom-call(bf16[592,512]{1,0:T(8,128)(2,1)} %get-tuple-element.43.refs_0_, bf16[592,512]{1,0:T(8,128)(2,1)} %get-tuple-element.44.refs_1_, ...), custom_call_target="tpu_custom_call" | custom-call | tf_op jit(solution)/shard_map/cond/branch_1_fun/inner_part/pallas_call | solution.py:426
  171.8 14.6 %inner_part.3 = (bf16[1440,1024]{1,0:T(8,128)(2,1)S(1)}, bf16[2,1440,1024]{2,1,0:T(8,128)(2,1)}, f32[1,1024]{1,0:T(1,128)}, f32[1,1024]{1,0:T(1,128)}, bf16[4,576,1024]{2,1,0:T(8,128)(2,1)}) custom-call(bf16[592,512]{1,0:T(8,128)(2,1)} %get-tuple-element.178.refs_0_, ...), custom_call_target="tpu_custom_call", output_to_operand_aliasing={{0}: (7, {}), {1}: (8, {}), {2}: (9, {}), {3}: (10, {}), {4... | custom-call | tf_op jit(solution)/shard_map/inner_part/pallas_call | solution.py:426
  186.3 9.0 %whole_product.1 = bf16[4,576,960]{2,1,0:T(8,128)(2,1)} custom-call(bf16[4,576,1024]{2,1,0:T(8,128)(2,1)} %get-tuple-element.189.act, bf16[2880,1024]{1,0:T(8,128)(2,1)} %bitcast.140), custom_call_target="tpu_custom_call" | custom-call | tf_op jit(solution)/shard_map/whole_product/pallas_call | solution.py:519
  196.5 9.3 %half_product.8 = bf16[4,1,288,1920]{3,2,1,0:T(8,128)(2,1)} custom-call(s32[1]{0:T(128)} %bitcast.60.refs_0_, bf16[4,2,288,1024]{3,2,1,0:T(8,128)(2,1)} %bitcast.145, bf16[2880,1024]{1,0:T(8,128)(2,1)} %bitcast.141), custom_call_target="tpu_custom_call" | custom-call | tf_op jit(solution)/shard_map/half_product/pallas_call | solution.py:493
  207.1 25.6 %conditional.6 = (bf16[592,1024]{1,0:T(8,128)(2,1)}, bf16[592,1024]{1,0:T(8,128)(2,1)}) conditional(s32[]{:T(128)} %convert_element_type.96, () %tuple.98, (bf16[2304,1440]{1,0:T(8,128)(2,1)}, bf16[2304,1440]{1,0:T(8,128)(2,1)}, bf16[2880,1024]{1,0:T(8,128)(2,1)}, f32[1,1024]{1,0:T(1,128)S(1)}) %tuple.165), branch_computations={%region_4.5_spmd, %region_5.6_spmd} | conditional | flops 7 | bytes 9699496 | solution.py:143
  207.7 13.7 %feature_chunks.6 = (bf16[592,1024]{1,0:T(8,128)(2,1)}, bf16[592,1024]{1,0:T(8,128)(2,1)}) custom-call(s32[2]{0:T(128)} %pad_add_fusion.refs_0_, bf16[2304,1440]{1,0:T(8,128)(2,1)} %get-tuple-element.50.refs_1_, bf16[2304,1440]{1,0:T(8,128)(2,1)} %get-tuple-element.51.refs_2_, bf16[2880,1024]{1,0:T(8,128)(2,1)} %get-tuple-element.52.refs_3_, ...), custom_call_target="tpu_custom_call" | custom-call | tf_op jit(solution)/shard_map/cond/branch_1_fun/feature_chunks/pallas_call | solution.py:670
  222.0 2.9 collective-permute-done.2.refs_4_
  224.8 7.9 %feature_chunks.7 = bf16[592,1024]{1,0:T(8,128)(2,1)} custom-call(s32[1]{0:T(128)} %bitcast.10.refs_0_, bf16[2304,1440]{1,0:T(8,128)(2,1)} %get-tuple-element.50.refs_1_, bf16[2304,1440]{1,0:T(8,128)(2,1)} %get-tuple-element.51.refs_2_, bf16[2880,1024]{1,0:T(8,128)(2,1)} %get-tuple-element.52.refs_3_, bf16[592,1024]{1,0:T(8,128)(2,1)} %collective-permute-done.2.refs_4_, ...), custom_call_target="tpu_custom_call" | custom-call | tf_op jit(solution)/shard_map/cond/branch_1_fun/feature_chunks/pallas_call | solution.py:670
  232.7 8.3 %feature_chunks.8.refs_0_ = f32[592,1024]{1,0:T(8,128)} custom-call(s32[1]{0:T(128)} %bitcast.22.refs_0_, bf16[2304,1440]{1,0:T(8,128)(2,1)} %get-tuple-element.169.refs_1_, bf16[2304,1440]{1,0:T(8,128)(2,1)} %get-tuple-element.187.refs_2_, bf16[2880,1024]{1,0:T(8,128)(2,1)} %bitcast.143, bf16[592,1024]{1,0:T(8,128)(2,1)} %get-tuple-element.193.refs_4_, ...), custom_call_target="tpu_custom_call" | custom-call | tf_op jit(solution)/shard_map/feature_chunks/pallas_call | solution.py:670
  241.0 20.6 %collective-permute-done.25.refs_2_ = bf16[1440,1024]{1,0:T(8,128)(2,1)} collective-permute-done((bf16[1440,1024]{1,0:T(8,128)(2,1)S(1)}, bf16[1440,1024]{1,0:T(8,128)(2,1)}, u32[]{:S(2)}, u32[]{:S(2)}) %collective-permute-start.25) | collective-permute-done | bytes 2949152 | tf_op jit(solution)/shard_map/ppermute | solution.py:134
  263.3 3.0 multiply_convert_fusion.refs_2_
  267.3 8.5 %place.5 = bf16[4,1440,1024]{2,1,0:T(8,128)(2,1)} custom-call(bf16[1440,1024]{1,0:T(8,128)(2,1)S(1)} %get-tuple-element.186.refs_0_, bf16[1440,1024]{1,0:T(8,128)(2,1)} %collective-permute-done.24.refs_1_, bf16[1440,1024]{1,0:T(8,128)(2,1)} %collective-permute-done.25.refs_2_, bf16[1440,1024]{1,0:T(8,128)(2,1)} %collective-permute-done.26.refs_3_), custom_call_target="tpu_custom_call" | custom-call | tf_op jit(solution)/shard_map/place/pallas_call | solution.py:179
  275.9 7.9 %half_product.9 = bf16[4,1,576,720]{3,2,1,0:T(8,128)(2,1)} custom-call(s32[1]{0:T(128)} %bitcast.60.refs_0_, bf16[4,2,720,1024]{3,2,1,0:T(8,128)(2,1)} %bitcast.147, bf16[576,1024]{1,0:T(8,128)(2,1)} %multiply_convert_fusion.refs_2_), custom_call_target="tpu_custom_call" | custom-call | tf_op jit(solution)/shard_map/half_product/pallas_call | solution.py:493
  283.8 7.2 %collective-permute-done.27.refs_1_ = bf16[592,1024]{1,0:T(8,128)(2,1)} collective-permute-done((bf16[592,1024]{1,0:T(8,128)(2,1)}, bf16[592,1024]{1,0:T(8,128)(2,1)}, u32[]{:S(2)}, u32[]{:S(2)}) %collective-permute-start.27) | collective-permute-done | bytes 1212448 | tf_op jit(solution)/shard_map/ppermute | solution.py:134
  291.0 6.2 attn_grad.1
  297.2 6.7 %feature_chunks.9 = (bf16[576,1024]{1,0:T(8,128)(2,1)}, bf16[576,1024]{1,0:T(8,128)(2,1)}) custom-call(s32[2]{0:T(128)} %pad_add_fusion.2.refs_0_, bf16[2304,576]{1,0:T(8,128)(2,1)} %flip.3.refs_1_, bf16[576,1024]{1,0:T(8,128)(2,1)} %get-tuple-element.203.refs_2_), custom_call_target="tpu_custom_call" | custom-call | tf_op jit(solution)/shard_map/feature_chunks/pallas_call | solution.py:670
  303.9 3.1 collective-permute-done.28.refs_3_
  306.9 10.3 %half_product.10 = bf16[4,1,288,1920]{3,2,1,0:T(8,128)(2,1)} custom-call(s32[1]{0:T(128)} %bitcast.63.refs_0_, bf16[4,2,288,1024]{3,2,1,0:T(8,128)(2,1)} %bitcast.146, bf16[2880,1024]{1,0:T(8,128)(2,1)} %bitcast.144, bf16[4,1,288,1920]{3,2,1,0:T(8,128)(2,1)} %collective-permute-done.29.refs_3_), custom_call_target="tpu_custom_call" | custom-call | tf_op jit(solution)/shard_map/half_product/pallas_call | solution.py:493
  318.9 3.8 feature_chunks.10
  324.6 3.8 feature_chunks.11
  328.4 5.5 half_product.11
  333.9 17.4 %collective-permute-done.31 = bf16[576,1024]{1,0:T(8,128)(2,1)S(1)} collective-permute-done((bf16[576,1024]{1,0:T(8,128)(2,1)}, bf16[576,1024]{1,0:T(8,128)(2,1)S(1)}, u32[]{:S(2)}, u32[]{:S(2)}) %collective-permute-start.31) | collective-permute-done | bytes 1179680 | tf_op jit(solution)/shard_map/ppermute | solution.py:134
  352.3 20.6 %attention_backward.1 = (bf16[9,64,1024]{2,1,0:T(8,128)(2,1)S(1)}, bf16[9,64,1024]{2,1,0:T(8,128)(2,1)S(1)}, bf16[9,64,1024]{2,1,0:T(8,128)(2,1)S(1)}) custom-call(bf16[9,64,1024]{2,1,0:T(8,128)(2,1)} %get-tuple-element.196.q_ref, bf16[9,64,1024]{2,1,0:T(8,128)(2,1)} %get-tuple-element.197.k_ref, bf16[9,64,1024]{2,1,0:T(8,128)(2,1)} %get-tuple-element.198.v_ref, ...), custom_call_target="tpu_custom_call" | custom-call | tf_op jit(solution)/shard_map/attention_backward/pallas_call | solution.py:119
  372.9 8.9 %half_product.12 = bf16[4,3,288,576]{3,2,1,0:T(8,128)(2,1)} custom-call(s32[1]{0:T(128)} %bitcast.60.refs_0_, bf16[4,2,288,1024]{3,2,1,0:T(8,128)(2,1)} %bitcast.137, bf16[576,1024]{1,0:T(8,128)(2,1)S(1)} %bitcast.156, bf16[576,1024]{1,0:T(8,128)(2,1)S(1)} %bitcast.159, bf16[576,1024]{1,0:T(8,128)(2,1)S(1)} %bitcast.162), custom_call_target="tpu_custom_call" | custom-call | tf_op jit(solution)/shard_map/half_product/pallas_call | solution.py:493
  381.8 14.5 %collective-permute-done.32.refs_3_ = bf16[4,1,576,720]{3,2,1,0:T(8,128)(2,1)} collective-permute-done((bf16[4,1,576,720]{3,2,1,0:T(8,128)(2,1)}, bf16[4,1,576,720]{3,2,1,0:T(8,128)(2,1)}, u32[]{:S(2)}, u32[]{:S(2)}) %collective-permute-start.32) | collective-permute-done | bytes 3317792 | tf_op jit(solution)/shard_map/ppermute | solution.py:535
  396.3 8.4 %half_product.13 = bf16[4,1,576,720]{3,2,1,0:T(8,128)(2,1)} custom-call(s32[1]{0:T(128)} %bitcast.63.refs_0_, bf16[4,2,720,1024]{3,2,1,0:T(8,128)(2,1)} %bitcast.148, bf16[576,1024]{1,0:T(8,128)(2,1)} %multiply_convert_fusion.refs_2_, bf16[4,1,576,720]{3,2,1,0:T(8,128)(2,1)} %collective-permute-done.32.refs_3_), custom_call_target="tpu_custom_call" | custom-call | tf_op jit(solution)/shard_map/half_product/pallas_call | solution.py:493
  407.9 52.5 %conditional.7 = (f32[256,2304]{1,0:T(8,128)}, bf16[256,2304]{1,0:T(8,128)(2,1)}) conditional(s32[]{:T(128)} %convert_element_type.98, () %tuple.109, (bf16[2304,576]{0,1:T(8,128)(2,1)}, bf16[2304,576]{0,1:T(8,128)(2,1)}, bf16[2304,576]{0,1:T(8,128)(2,1)}, bf16[576,1024]{1,0:T(8,128)(2,1)S(1)}, bf16[576,1024]{1,0:T(8,128)(2,1)S(1)}, ...), branch_computations={%region_6.7_spmd, %region_7.8_spmd} | conditional | flops 7 | bytes 14155984 | solution.py:143
  408.4 12.7 %token_chunks.3 = (bf16[256,2304]{1,0:T(8,128)(2,1)}, bf16[256,2304]{1,0:T(8,128)(2,1)}) custom-call(s32[2]{0:T(128)} %pad_add_fusion.1.refs_0_, bf16[576,2304]{1,0:T(8,128)(2,1)} %bitcast.165, bf16[576,2304]{1,0:T(8,128)(2,1)} %bitcast.168, bf16[576,2304]{1,0:T(8,128)(2,1)} %bitcast.171, bf16[576,1024]{1,0:T(8,128)(2,1)S(1)} %get-tuple-element.59.refs_4_, ...), custom_call_target="tpu_custom_call" | custom-call | tf_op jit(solution)/shard_map/cond/branch_1_fun/token_chunks/pallas_call | solution.py:756
  421.7 2.7 collective-permute-done.4.refs_7_
  424.3 7.7 %token_chunks.4 = bf16[256,2304]{1,0:T(8,128)(2,1)} custom-call(s32[1]{0:T(128)} %bitcast.14.refs_0_, bf16[576,2304]{1,0:T(8,128)(2,1)} %bitcast.166, bf16[576,2304]{1,0:T(8,128)(2,1)} %bitcast.169, bf16[576,2304]{1,0:T(8,128)(2,1)} %bitcast.172, bf16[576,1024]{1,0:T(8,128)(2,1)S(1)} %get-tuple-element.59.refs_4_, ...), custom_call_target="tpu_custom_call" | custom-call | tf_op jit(solution)/shard_map/cond/branch_1_fun/token_chunks/pallas_call | solution.py:756
  432.6 8.1 %token_chunks.5 = f32[256,2304]{1,0:T(8,128)} custom-call(s32[1]{0:T(128)} %bitcast.13.refs_0_, bf16[576,2304]{1,0:T(8,128)(2,1)} %bitcast.167, bf16[576,2304]{1,0:T(8,128)(2,1)} %bitcast.170, bf16[576,2304]{1,0:T(8,128)(2,1)} %bitcast.173, bf16[576,1024]{1,0:T(8,128)(2,1)S(1)} %get-tuple-element.59.refs_4_, ...), custom_call_target="tpu_custom_call" | custom-call | tf_op jit(solution)/shard_map/cond/branch_1_fun/token_chunks/pallas_call | solution.py:756
  440.7 19.6 %collective-permute-done.6 = bf16[256,2304]{1,0:T(8,128)(2,1)} collective-permute-done((bf16[256,2304]{1,0:T(8,128)(2,1)}, bf16[256,2304]{1,0:T(8,128)(2,1)}, u32[]{:S(2)}, u32[]{:S(2)}) %collective-permute-start.6) | collective-permute-done | bytes 1179680 | tf_op jit(solution)/shard_map/cond/branch_1_fun/ppermute | solution.py:134
  460.3 5.7 half_product.14
  466.1 5.6 reduce-scatter.10.cloned.1.call-done
  471.8 12.7 %fusion.9 = bf16[576,1024]{1,0:T(8,128)(2,1)S(1)} fusion(f32[576,1024]{1,0:T(8,128)} %get-tuple-element.173.refs_3_, bf16[5760,576]{0,1:T(8,128)(2,1)} %param.29, bf16[5760,1024]{1,0:T(8,128)(2,1)} %bitcast.149), kind=kOutput, calls=%fused_computation.15 | convolution fusion | flops 6796541952 | bytes 21970944 | tf_op jit(solution)/shard_map/fe,ft->et/dot_general | solution.py:949
  488.6 3.5 fusion.7
  495.7 5.1 collective-permute-done.39.refs_3_
  502.9 2.9 bitcast_convert_fusion
  505.7 3.1 copy.34
  508.8 4.7 collective-permute-done.36.refs_3_
  517.9 4.9 fusion.6
  522.7 10.7 %collective-permute-done.46.refs_5_ = bf16[4,3,288,576]{3,2,1,0:T(8,128)(2,1)} collective-permute-done((bf16[4,3,288,576]{3,2,1,0:T(8,128)(2,1)}, bf16[4,3,288,576]{3,2,1,0:T(8,128)(2,1)}, u32[]{:S(2)}, u32[]{:S(2)}) %collective-permute-start.46) | collective-permute-done | bytes 3981344 | tf_op jit(solution)/shard_map/ppermute | solution.py:535
  533.5 9.5 %half_product.15 = bf16[4,3,288,576]{3,2,1,0:T(8,128)(2,1)} custom-call(s32[1]{0:T(128)} %bitcast.63.refs_0_, bf16[4,2,288,1024]{3,2,1,0:T(8,128)(2,1)} %bitcast.138, bf16[576,1024]{1,0:T(8,128)(2,1)S(1)} %bitcast.158, bf16[576,1024]{1,0:T(8,128)(2,1)S(1)} %bitcast.161, bf16[576,1024]{1,0:T(8,128)(2,1)} %bitcast.164, ...), custom_call_target="tpu_custom_call" | custom-call | tf_op jit(solution)/shard_map/half_product/pallas_call | solution.py:493
  550.9 11.5 %collective-permute-done.43 = f32[2,2304]{1,0:T(2,128)S(1)} collective-permute-done((f32[2,2304]{1,0:T(2,128)S(1)}, f32[2,2304]{1,0:T(2,128)S(1)}, u32[]{:S(2)}, u32[]{:S(2)}) %collective-permute-start.43) | collective-permute-done | bytes 18464 | tf_op jit(solution)/shard_map/ppermute | solution.py:600
  564.0 5.0 collective-permute-done.44
  570.5 5.2 collective-permute-done.45
  582.3 42.6 %reduce-scatter.14.cloned.1.call-done = bf16[1,3,288,576]{3,2,1,0:T(8,128)(2,1)} async-done(((bf16[4,3,288,576]{3,2,1,0:T(8,128)(2,1)}), bf16[1,3,288,576]{3,2,1,0:T(8,128)(2,1)}) %reduce-scatter.14.cloned.1.call-update) | async-done | bytes 995344 | tf_op jit(solution)/shard_map/reduce_scatter | solution.py:541
  624.9 2.6 fusion.10
  (216 shorter events, 96.9 us)
Async XLA Ops:
  7.2 128.5 %all-gather.2.cloned.1.call-start = ((), (), s32[]{:S(2)}) async-start(), calls=%async_computation.5 | async-start | bytes 3981312 | tf_op jit(solution)/shard_map/all_gather | solution.py:828
  7.2 3.9 collective-permute-start.7
  7.7 29.3 %collective-permute-start.8 = (bf16[256,2304]{1,0:T(8,128)(2,1)}, bf16[256,2304]{1,0:T(8,128)(2,1)S(1)}, u32[]{:S(2)}, u32[]{:S(2)}) collective-permute-start(bf16[256,2304]{1,0:T(8,128)(2,1)} %refs_1_.1), channel_id=1, source_target_pairs={{0,2},{1,3},{2,0},{3,1},{4,6},{5,7},{6,4},{7,5},{8,10},{9,11},{10,... | collective-permute-start | bytes 3538952 | tf_op jit(solution)/shard_map/ppermute | solution.py:134
  17.4 6.1 copy-start
  17.4 6.1 copy-start.10
  37.1 3.5 collective-permute-start.9
  38.4 17.8 %collective-permute-start.13 = (bf16[72,1440]{1,0:T(8,128)(2,1)S(1)}, bf16[72,1440]{1,0:T(8,128)(2,1)S(1)}, u32[]{:S(2)}, u32[]{:S(2)}) collective-permute-start(bf16[72,1440]{1,0:T(8,128)(2,1)S(1)} %get-tuple-element.163), channel_id=1, source_target_pairs={{0,2},{1,3},{2,0},{3,1},{4,6},{5,7},{6,4},{7,5},{8,10},{9,11},{10,... | collective-permute-start | bytes 622088 | tf_op jit(solution)/shard_map/ppermute | solution.py:134
  40.3 16.2 %collective-permute-start.12 = (bf16[72,1440]{1,0:T(8,128)(2,1)S(1)}, bf16[72,1440]{1,0:T(8,128)(2,1)S(1)}, u32[]{:S(2)}, u32[]{:S(2)}) collective-permute-start(bf16[72,1440]{1,0:T(8,128)(2,1)S(1)} %get-tuple-element.161), channel_id=1, source_target_pairs={{0,2},{1,3},{2,0},{3,1},{4,6},{5,7},{6,4},{7,5},{8,10},{9,11},{10,... | collective-permute-start | bytes 622088 | tf_op jit(solution)/shard_map/ppermute | solution.py:134
  56.2 1.5 collective-permute-start.19
  58.5 258.7 %reduce-scatter.6.cloned.1.call-start = ((), (), s32[]{:S(2)}) async-start(), calls=%async_computation.6 | async-start | bytes 5898240 | tf_op jit(solution)/shard_map/reduce_scatter | solution.py:541
  58.6 28.9 %collective-permute-start.14 = (bf16[256,2304]{1,0:T(8,128)(2,1)S(1)}, bf16[256,2304]{1,0:T(8,128)(2,1)S(1)}, u32[]{:S(2)}, u32[]{:S(2)}) collective-permute-start(bf16[256,2304]{1,0:T(8,128)(2,1)S(1)} %copy-done.17), channel_id=1, source_target_pairs={{0,2},{1,3},{2,0},{3,1},{4,6},{5,7},{6,4},{7,5},{8,10},{9,11},{10,... | collective-permute-start | bytes 3538952 | tf_op jit(solution)/shard_map/ppermute | solution.py:134
  82.4 38.8 %collective-permute-start.11 = (bf16[576,1024]{1,0:T(8,128)(2,1)}, bf16[576,1024]{1,0:T(8,128)(2,1)}, u32[]{:S(2)}, u32[]{:S(2)}) collective-permute-start(bf16[576,1024]{1,0:T(8,128)(2,1)} %bitcast.179), channel_id=1, source_target_pairs={{0,2},{1,3},{2,0},{3,1},{4,6},{5,7},{6,4},{7,5},{8,10},{9,11},{10,... | collective-permute-start | bytes 3538952 | tf_op jit(solution)/shard_map/ppermute | solution.py:134
  82.7 40.6 %collective-permute-start.10 = (bf16[576,1024]{1,0:T(8,128)(2,1)}, bf16[576,1024]{1,0:T(8,128)(2,1)}, u32[]{:S(2)}, u32[]{:S(2)}) collective-permute-start(bf16[576,1024]{1,0:T(8,128)(2,1)} %bitcast.180), channel_id=1, source_target_pairs={{0,1},{1,0},{2,3},{3,2},{4,5},{5,4},{6,7},{7,6},{8,9},{9,8},{10,11... | collective-permute-start | bytes 3538952 | tf_op jit(solution)/shard_map/ppermute | solution.py:134
  88.5 4.5 collective-permute-start
  88.5 4.7 collective-permute-start.1
  121.2 4.2 collective-permute-start.15
  121.6 16.5 %collective-permute-start.18 = (bf16[576,1440]{1,0:T(8,128)(2,1)}, bf16[576,1440]{1,0:T(8,128)(2,1)S(1)}, u32[]{:S(2)}, u32[]{:S(2)}) collective-permute-start(bf16[576,1440]{1,0:T(8,128)(2,1)} %get-tuple-element.236), channel_id=1, source_target_pairs={{0,1},{1,0},{2,3},{3,2},{4,5},{5,4},{6,7},{7,6},{8,9},{9,8},{10,11... | collective-permute-start | bytes 4976648 | tf_op jit(solution)/shard_map/ppermute | solution.py:134
  134.7 16.3 %collective-permute-start.17 = (bf16[592,512]{1,0:T(8,128)(2,1)}, bf16[592,512]{1,0:T(8,128)(2,1)}, u32[]{:S(2)}, u32[]{:S(2)}) collective-permute-start(bf16[592,512]{1,0:T(8,128)(2,1)} %get-tuple-element.175), channel_id=1, source_target_pairs={{0,2},{1,3},{2,0},{3,1},{4,6},{5,7},{6,4},{7,5},{8,10},{9,11},{10,... | collective-permute-start | bytes 1818632 | tf_op jit(solution)/shard_map/ppermute | solution.py:134
  135.6 16.7 %collective-permute-start.21 = (bf16[592,512]{1,0:T(8,128)(2,1)}, bf16[592,512]{1,0:T(8,128)(2,1)}, u32[]{:S(2)}, u32[]{:S(2)}) collective-permute-start(bf16[592,512]{1,0:T(8,128)(2,1)} %get-tuple-element.175), channel_id=1, source_target_pairs={{0,1},{1,0},{2,3},{3,2},{4,5},{5,4},{6,7},{7,6},{8,9},{9,8},{10,11... | collective-permute-start | bytes 1818632 | tf_op jit(solution)/shard_map/ppermute | solution.py:134
  141.1 10.1 %copy-start.23 = (bf16[592,512]{1,0:T(8,128)(2,1)S(1)}, bf16[592,512]{1,0:T(8,128)(2,1)}, u32[]{:S(2)}) copy-start(bf16[592,512]{1,0:T(8,128)(2,1)} %get-tuple-element.178.refs_0_) | copy-start | bytes 1818628
  151.0 2.2 collective-permute-start.22
  151.2 17.4 %collective-permute-start.20 = (bf16[592,512]{1,0:T(8,128)(2,1)S(1)}, bf16[592,512]{1,0:T(8,128)(2,1)}, u32[]{:S(2)}, u32[]{:S(2)}) collective-permute-start(bf16[592,512]{1,0:T(8,128)(2,1)S(1)} %copy-done.23), channel_id=1, source_target_pairs={{0,2},{1,3},{2,0},{3,1},{4,6},{5,7},{6,4},{7,5},{8,10},{9,11},{10,... | collective-permute-start | bytes 1818632 | tf_op jit(solution)/shard_map/ppermute | solution.py:134
  152.4 16.6 %collective-permute-start.16 = (bf16[592,512]{1,0:T(8,128)(2,1)S(1)}, bf16[592,512]{1,0:T(8,128)(2,1)}, u32[]{:S(2)}, u32[]{:S(2)}) collective-permute-start(bf16[592,512]{1,0:T(8,128)(2,1)S(1)} %copy-done.23), channel_id=1, source_target_pairs={{0,1},{1,0},{2,3},{3,2},{4,5},{5,4},{6,7},{7,6},{8,9},{9,8},{10,11... | collective-permute-start | bytes 1818632 | tf_op jit(solution)/shard_map/ppermute | solution.py:134
  168.6 2.3 collective-permute-start.23
  195.4 209.3 %reduce-scatter.8.cloned.1.call-start = ((), (), s32[]{:S(2)}) async-start(), calls=%async_computation.7 | async-start | bytes 5529600 | tf_op jit(solution)/shard_map/reduce_scatter | solution.py:541
  195.4 66.2 %collective-permute-start.25 = (bf16[1440,1024]{1,0:T(8,128)(2,1)S(1)}, bf16[1440,1024]{1,0:T(8,128)(2,1)}, u32[]{:S(2)}, u32[]{:S(2)}) collective-permute-start(bf16[1440,1024]{1,0:T(8,128)(2,1)S(1)} %get-tuple-element.186.refs_0_), channel_id=1, source_target_pairs={{0,2},{1,3},{2,0},{3,1},{4,6},{5,7},{6,4},{7,5},{8,10},{9,11},{10,... | collective-permute-start | bytes 8847368 | tf_op jit(solution)/shard_map/ppermute | solution.py:134
  196.5 10.6 %copy-start.30 = (f32[1,1024]{1,0:T(1,128)S(1)}, f32[1,1024]{1,0:T(1,128)}, u32[]{:S(2)}) copy-start(f32[1,1024]{1,0:T(1,128)} %get-tuple-element.192.refs_5_) | copy-start | bytes 12292
  205.8 101.1 %collective-permute-start.29 = (bf16[4,1,288,1920]{3,2,1,0:T(8,128)(2,1)}, bf16[4,1,288,1920]{3,2,1,0:T(8,128)(2,1)}, u32[]{:S(2)}, u32[]{:S(2)}) collective-permute-start(bf16[4,1,288,1920]{3,2,1,0:T(8,128)(2,1)} %half_product.8), channel_id=1, source_target_pairs={{0,4},{4,0},{8,12},{12,8},{16,20},{20,16},{24,28},{28,24},{1,5},{5... | collective-permute-start | bytes 13271048 | tf_op jit(solution)/shard_map/ppermute | solution.py:535
  207.1 59.3 %collective-permute-start.24 = (bf16[1440,1024]{1,0:T(8,128)(2,1)S(1)}, bf16[1440,1024]{1,0:T(8,128)(2,1)}, u32[]{:S(2)}, u32[]{:S(2)}) collective-permute-start(bf16[1440,1024]{1,0:T(8,128)(2,1)S(1)} %get-tuple-element.186.refs_0_), channel_id=1, source_target_pairs={{0,1},{1,0},{2,3},{3,2},{4,5},{5,4},{6,7},{7,6},{8,9},{9,8},{10,11... | collective-permute-start | bytes 8847368 | tf_op jit(solution)/shard_map/ppermute | solution.py:134
  221.4 3.4 collective-permute-start.2
  222.0 10.8 %collective-permute-start.3 = (bf16[592,1024]{1,0:T(8,128)(2,1)}, bf16[592,1024]{1,0:T(8,128)(2,1)}, u32[]{:S(2)}, u32[]{:S(2)}) collective-permute-start(bf16[592,1024]{1,0:T(8,128)(2,1)} %get-tuple-element.55), channel_id=1, source_target_pairs={{0,1},{1,0},{2,3},{3,2},{4,5},{5,4},{6,7},{7,6},{8,9},{9,8},{10,11... | collective-permute-start | bytes 3637256 | tf_op jit(solution)/shard_map/cond/branch_1_fun/ppermute | solution.py:134
  261.6 5.7 collective-permute-start.26
  261.6 29.4 %collective-permute-start.27 = (bf16[592,1024]{1,0:T(8,128)(2,1)}, bf16[592,1024]{1,0:T(8,128)(2,1)}, u32[]{:S(2)}, u32[]{:S(2)}) collective-permute-start(bf16[592,1024]{1,0:T(8,128)(2,1)} %get-tuple-element.199), channel_id=1, source_target_pairs={{0,2},{1,3},{2,0},{3,1},{4,6},{5,7},{6,4},{7,5},{8,10},{9,11},{10,... | collective-permute-start | bytes 3637256 | tf_op jit(solution)/shard_map/ppermute | solution.py:134
  275.9 15.1 %copy-start.32 = (f32[1,1024]{1,0:T(1,128)S(1)}, f32[1,1024]{1,0:T(1,128)}, u32[]{:S(2)}) copy-start(f32[1,1024]{1,0:T(1,128)} %get-tuple-element.202.refs_5_) | copy-start | bytes 12292
  303.9 3.1 collective-permute-start.28
  306.9 10.3 %copy-start.14 = (bf16[576,1024]{1,0:T(8,128)(2,1)}, bf16[576,1024]{1,0:T(8,128)(2,1)S(1)}, u32[]{:S(2)}) copy-start(bf16[576,1024]{1,0:T(8,128)(2,1)S(1)} %collective-permute-done.28.refs_3_) | copy-start | bytes 3538948
  317.3 154.4 %reduce-scatter.10.cloned.1.call-start = ((), (), s32[]{:S(2)}) async-start(), calls=%async_computation.8 | async-start | bytes 4423680 | tf_op jit(solution)/shard_map/reduce_scatter | solution.py:541
  317.4 79.0 %collective-permute-start.32 = (bf16[4,1,576,720]{3,2,1,0:T(8,128)(2,1)}, bf16[4,1,576,720]{3,2,1,0:T(8,128)(2,1)}, u32[]{:S(2)}, u32[]{:S(2)}) collective-permute-start(bf16[4,1,576,720]{3,2,1,0:T(8,128)(2,1)} %half_product.9), channel_id=1, source_target_pairs={{0,4},{4,0},{8,12},{12,8},{16,20},{20,16},{24,28},{28,24},{1,5},{5... | collective-permute-start | bytes 9953288 | tf_op jit(solution)/shard_map/ppermute | solution.py:535
  318.9 4.7 collective-permute-start.30
  322.7 28.6 %collective-permute-start.31 = (bf16[576,1024]{1,0:T(8,128)(2,1)}, bf16[576,1024]{1,0:T(8,128)(2,1)S(1)}, u32[]{:S(2)}, u32[]{:S(2)}) collective-permute-start(bf16[576,1024]{1,0:T(8,128)(2,1)} %feature_chunks.10), channel_id=1, source_target_pairs={{0,2},{1,3},{2,0},{3,1},{4,6},{5,7},{6,4},{7,5},{8,10},{9,11},{10,... | collective-permute-start | bytes 3538952 | tf_op jit(solution)/shard_map/ppermute | solution.py:134
  372.9 8.9 %copy-start.8 = (bf16[9,64,1024]{2,1,0:T(8,128)(2,1)}, bf16[9,64,1024]{2,1,0:T(8,128)(2,1)S(1)}, u32[]{:S(2)}) copy-start(bf16[9,64,1024]{2,1,0:T(8,128)(2,1)S(1)} %get-tuple-element.215) | copy-start | bytes 3538948
  404.7 138.3 %reduce-scatter.12.cloned.1.call-start = ((), (), s32[]{:S(2)}) async-start(), calls=%async_computation.9 | async-start | bytes 1843200 | tf_op jit(solution)/shard_map/reduce_scatter | solution.py:541
  404.8 55.6 %collective-permute-start.33 = (bf16[4,1,288,576]{3,2,1,0:T(8,128)(2,1)}, bf16[4,1,288,576]{3,2,1,0:T(8,128)(2,1)}, u32[]{:S(2)}, u32[]{:S(2)}) collective-permute-start(bf16[4,1,288,576]{3,2,1,0:T(8,128)(2,1)} %half_product.11), channel_id=1, source_target_pairs={{0,4},{4,0},{8,12},{12,8},{16,20},{20,16},{24,28},{28,24},{1,5},{5... | collective-permute-start | bytes 3981320 | tf_op jit(solution)/shard_map/ppermute | solution.py:535
  406.7 126.8 %collective-permute-start.46 = (bf16[4,3,288,576]{3,2,1,0:T(8,128)(2,1)}, bf16[4,3,288,576]{3,2,1,0:T(8,128)(2,1)}, u32[]{:S(2)}, u32[]{:S(2)}) collective-permute-start(bf16[4,3,288,576]{3,2,1,0:T(8,128)(2,1)} %half_product.12), channel_id=1, source_target_pairs={{0,4},{4,0},{8,12},{12,8},{16,20},{20,16},{24,28},{28,24},{1,5},{5... | collective-permute-start | bytes 11943944 | tf_op jit(solution)/shard_map/ppermute | solution.py:535
  421.2 3.2 collective-permute-start.4
  421.2 11.4 %collective-permute-start.5 = (bf16[256,2304]{1,0:T(8,128)(2,1)}, bf16[256,2304]{1,0:T(8,128)(2,1)}, u32[]{:S(2)}, u32[]{:S(2)}) collective-permute-start(bf16[256,2304]{1,0:T(8,128)(2,1)} %get-tuple-element.64), channel_id=1, source_target_pairs={{0,1},{1,0},{2,3},{3,2},{4,5},{5,4},{6,7},{7,6},{8,9},{9,8},{10,11... | collective-permute-start | bytes 3538952 | tf_op jit(solution)/shard_map/cond/branch_1_fun/ppermute | solution.py:134
  432.0 28.3 %collective-permute-start.6 = (bf16[256,2304]{1,0:T(8,128)(2,1)}, bf16[256,2304]{1,0:T(8,128)(2,1)}, u32[]{:S(2)}, u32[]{:S(2)}) collective-permute-start(bf16[256,2304]{1,0:T(8,128)(2,1)} %token_chunks.4), channel_id=1, source_target_pairs={{0,2},{1,3},{2,0},{3,1},{4,6},{5,7},{6,4},{7,5},{8,10},{9,11},{10,... | collective-permute-start | bytes 3538952 | tf_op jit(solution)/shard_map/cond/branch_1_fun/ppermute | solution.py:134
  471.7 153.2 %reduce-scatter.14.cloned.1.call-start = ((), (), s32[]{:S(2)}) async-start(), calls=%async_computation.10 | async-start | bytes 5529600 | tf_op jit(solution)/shard_map/reduce_scatter | solution.py:541
  471.8 12.7 %copy-start.16 = (bf16[576,1024]{1,0:T(8,128)(2,1)S(1)}, bf16[576,1024]{1,0:T(8,128)(2,1)}, u32[]{:S(2)}) copy-start(bf16[576,1024]{1,0:T(8,128)(2,1)} %get-tuple-element.222) | copy-start | bytes 3538948
  485.4 7.3 %collective-permute-start.37 = (bf16[576,256]{1,0:T(8,128)(2,1)S(1)}, bf16[576,256]{1,0:T(8,128)(2,1)S(1)}, u32[]{:S(2)}, u32[]{:S(2)}) collective-permute-start(bf16[576,256]{1,0:T(8,128)(2,1)S(1)} %get-tuple-element.244), channel_id=1, source_target_pairs={{0,1},{1,0},{2,3},{3,2},{4,5},{5,4},{6,7},{7,6},{8,9},{9,8},{10,11... | collective-permute-start | bytes 884744 | tf_op jit(solution)/shard_map/ppermute | solution.py:134
  485.4 9.9 %collective-permute-start.38 = (bf16[576,256]{1,0:T(8,128)(2,1)S(1)}, bf16[576,256]{1,0:T(8,128)(2,1)}, u32[]{:S(2)}, u32[]{:S(2)}) collective-permute-start(bf16[576,256]{1,0:T(8,128)(2,1)S(1)} %get-tuple-element.243), channel_id=1, source_target_pairs={{0,2},{1,3},{2,0},{3,1},{4,6},{5,7},{6,4},{7,5},{8,10},{9,11},{10,... | collective-permute-start | bytes 884744 | tf_op jit(solution)/shard_map/ppermute | solution.py:134
  486.8 14.0 %collective-permute-start.39 = (bf16[576,256]{1,0:T(8,128)(2,1)S(1)}, bf16[576,256]{1,0:T(8,128)(2,1)}, u32[]{:S(2)}, u32[]{:S(2)}) collective-permute-start(bf16[576,256]{1,0:T(8,128)(2,1)S(1)} %get-tuple-element.242), channel_id=1, source_target_pairs={{0,3},{1,2},{2,1},{3,0},{4,7},{5,6},{6,5},{7,4},{8,11},{9,10},{10,... | collective-permute-start | bytes 884744 | tf_op jit(solution)/shard_map/ppermute | solution.py:134
  488.3 20.5 %collective-permute-start.34 = (bf16[576,256]{1,0:T(8,128)(2,1)}, bf16[576,256]{1,0:T(8,128)(2,1)}, u32[]{:S(2)}, u32[]{:S(2)}) collective-permute-start(bf16[576,256]{1,0:T(8,128)(2,1)} %get-tuple-element.248), channel_id=1, source_target_pairs={{0,1},{1,0},{2,3},{3,2},{4,5},{5,4},{6,7},{7,6},{8,9},{9,8},{10,11... | collective-permute-start | bytes 884744 | tf_op jit(solution)/shard_map/ppermute | solution.py:134
  492.6 8.2 %copy-start.27 = (bf16[576,256]{1,0:T(8,128)(2,1)}, bf16[576,256]{1,0:T(8,128)(2,1)S(1)}, u32[]{:S(2)}) copy-start(bf16[576,256]{1,0:T(8,128)(2,1)S(1)} %collective-permute-done.37.refs_1_) | copy-start | bytes 884740
  492.6 16.1 %collective-permute-start.35 = (bf16[576,256]{1,0:T(8,128)(2,1)}, bf16[576,256]{1,0:T(8,128)(2,1)}, u32[]{:S(2)}, u32[]{:S(2)}) collective-permute-start(bf16[576,256]{1,0:T(8,128)(2,1)} %get-tuple-element.247), channel_id=1, source_target_pairs={{0,2},{1,3},{2,0},{3,1},{4,6},{5,7},{6,4},{7,5},{8,10},{9,11},{10,... | collective-permute-start | bytes 884744 | tf_op jit(solution)/shard_map/ppermute | solution.py:134
  495.3 18.2 %collective-permute-start.36 = (bf16[576,256]{1,0:T(8,128)(2,1)}, bf16[576,256]{1,0:T(8,128)(2,1)}, u32[]{:S(2)}, u32[]{:S(2)}) collective-permute-start(bf16[576,256]{1,0:T(8,128)(2,1)} %get-tuple-element.246), channel_id=1, source_target_pairs={{0,3},{1,2},{2,1},{3,0},{4,7},{5,6},{6,5},{7,4},{8,11},{9,10},{10,... | collective-permute-start | bytes 884744 | tf_op jit(solution)/shard_map/ppermute | solution.py:134
  543.0 33.6 %copy-start.21 = (bf16[1,1,288,1920]{3,2,1,0:T(8,128)(2,1)S(1)}, bf16[1,1,288,1920]{3,2,1,0:T(8,128)(2,1)}, u32[]{:S(2)}) copy-start(bf16[1,1,288,1920]{3,2,1,0:T(8,128)(2,1)} %reduce-scatter.8.cloned.1.call-done) | copy-start | bytes 3317764
  544.4 3.5 collective-permute-start.40
  544.4 3.8 collective-permute-start.41
  545.6 3.3 collective-permute-start.42
  546.3 30.0 %collective-permute-start.47 = (bf16[288,960]{1,0:T(8,128)(2,1)S(1)}, bf16[288,960]{1,0:T(8,128)(2,1)S(1)}, u32[]{:S(2)}, u32[]{:S(2)}) collective-permute-start(bf16[288,960]{1,0:T(8,128)(2,1)S(1)} %dynamic-slice_bitcast_fusion.2), channel_id=1, source_target_pairs={{0,4},{4,0},{8,12},{12,8},{16,20},{20,16},{24,28},{28,24},{1,5},{5... | collective-permute-start | bytes 1658888 | tf_op jit(solution)/shard_map/ppermute | solution.py:535
  549.7 12.7 %collective-permute-start.43 = (f32[2,2304]{1,0:T(2,128)S(1)}, f32[2,2304]{1,0:T(2,128)S(1)}, u32[]{:S(2)}, u32[]{:S(2)}) collective-permute-start(f32[2,2304]{1,0:T(2,128)S(1)} %add_add_fusion), channel_id=1, source_target_pairs={{0,4},{4,0},{8,12},{12,8},{16,20},{20,16},{24,28},{28,24},{1,5},{5... | collective-permute-start | bytes 55304 | tf_op jit(solution)/shard_map/ppermute | solution.py:600
  562.4 6.6 %collective-permute-start.44 = (f32[2,2304]{1,0:T(2,128)S(1)}, f32[2,2304]{1,0:T(2,128)S(1)}, u32[]{:S(2)}, u32[]{:S(2)}) collective-permute-start(f32[2,2304]{1,0:T(2,128)S(1)} %add.151), channel_id=1, source_target_pairs={{0,8},{4,12},{8,0},{12,4},{16,24},{20,28},{24,16},{28,20},{1,9},{5... | collective-permute-start | bytes 55304 | tf_op jit(solution)/shard_map/ppermute | solution.py:600
  569.1 6.7 %collective-permute-start.45 = (f32[2,2304]{1,0:T(2,128)S(1)}, f32[2,2304]{1,0:T(2,128)S(1)}, u32[]{:S(2)}, u32[]{:S(2)}) collective-permute-start(f32[2,2304]{1,0:T(2,128)S(1)} %add.152), channel_id=1, source_target_pairs={{0,16},{4,20},{8,24},{12,28},{16,0},{20,4},{24,8},{28,12},{1,17},{... | collective-permute-start | bytes 55304 | tf_op jit(solution)/shard_map/ppermute | solution.py:600
  (26 other events, 61.4 us)
Sparse Core Ops, SparseCore 0:
  58.7 66.7 all-gather.1
  195.5 85.7 reduce-scatter.5
  317.4 80.9 reduce-scatter.7
  404.9 66.7 reduce-scatter.9
  474.6 34.0 reduce-scatter.11
  543.2 81.7 reduce-scatter.13
